TPU v7x, 32 devices: a whole 2x2x4 slice. The times are simulated.
32 devices in a mesh: grp: 2 (over x), lon: 16 (over z, y, core).
Axes of the slice: x: 2, y: 2, z: 4, core: 2. Of those that a mesh axis runs over, the one named last changes fastest.
Arguments:
- grid_latent: bfloat16 [65536, 512], P(('grp', 'lon')), parts along dimension 0, may hold values from -6 to 6
- mesh_latent: bfloat16 [8192, 512], P(('grp', 'lon')), parts along dimension 0, may hold values from -6 to 6
- edge_latent: bfloat16 [98304, 512], P(('grp', 'lon')), parts along dimension 0, may hold values from -6 to 6
- mesh_cotangent: bfloat16 [8192, 512], P(('grp', 'lon')), parts along dimension 0, may hold values from -6 to 6
- edge_src: int32 [98304], P(('grp', 'lon')), parts along dimension 0, may hold values from 0 to 767, as said below
- edge_dst: int32 [98304], P(('grp', 'lon')), parts along dimension 0, may hold values from 0 to 255
- tile_count: int32 [32], P(('grp', 'lon')), parts along dimension 0, may hold values from 1 to 12, as said below
- send_rows: int32 [32, 16, 48], P(('grp', 'lon')), parts along dimension 0, may hold values from -1 to 2047, as said below
- w_edge_in: bfloat16 [1536, 512], replicated, may hold values from -0.15625 to 0.15625
- w_edge_out: bfloat16 [512, 512], replicated, may hold values from -0.25 to 0.25
- w_node_in: bfloat16 [1024, 512], replicated, may hold values from -0.1875 to 0.1875
- w_node_out: bfloat16 [512, 512], replicated, may hold values from -0.25 to 0.25
Outputs:
- grid_grad: bfloat16 [65536, 512], P(('grp', 'lon')), parts along dimension 0
- edge_grad: bfloat16 [98304, 512], P(('grp', 'lon')), parts along dimension 0
- mesh_grad: bfloat16 [8192, 512], P(('grp', 'lon')), parts along dimension 0
- grad_edge_in: float32 [3072, 512], P(('grp', 'lon')), parts along dimension 0
- grad_edge_out: float32 [1024, 512], P(('grp', 'lon')), parts along dimension 0
- grad_node_in: float32 [2048, 512], P(('grp', 'lon')), parts along dimension 0
- grad_node_out: float32 [1024, 512], P(('grp', 'lon')), parts along dimension 0
There are 2 independent parts, one for each index of `grp`. A program takes and returns all parts, laid end to end along the dimension named above; an argument that names none is the same for every part. Nothing has to cross between parts.
Inputs may be any that keep to these rules, and one draw needn't show every extreme that they name: send_rows[p, d, s] is a row of device p's 2048 grid rows sent to device d, or -1 for an empty slot; the live entries of each list come first and are distinct. Lists are non-empty only between sectors at most 3 apart around the loop (full at distance 2 or less), except for one receiving device that gets full lists of 48 from every device. `edge_src`: every edge reads a live slot p * 48 + s of its device's received rows. `tile_count`: some device has all 12 tiles live.
All inputs are finite; a program needn't handle non-finite values.
Results may differ from a plain program's by a relative error of at most 0.015.
Values may be sent and summed in bfloat16 or wider, within the bound.
No kernel may reach another device: no remote copies, remote signals or barrier semaphores. Data moves between devices by JAX's collectives and lax.ppermute only.
A program may use at most 192 MiB of HBM per device.

v0:
```python
import jax
import jax.numpy as jnp
from jax import lax
from jax.sharding import PartitionSpec as P

TILE = 256


def layer_norm(values):
    centered = values - jnp.mean(values, axis=1, keepdims=True)
    inverse = lax.rsqrt(jnp.mean(centered * centered, axis=1, keepdims=True) + 1e-05)
    return (centered * inverse, inverse)


def norm_back(normed, inverse, upstream):
    first = jnp.mean(upstream, axis=1, keepdims=True)
    second = jnp.mean(upstream * normed, axis=1, keepdims=True)
    return inverse * (upstream - first - normed * second)


def silu_slope(values):
    sigma = jax.nn.sigmoid(values)
    return sigma * (1.0 + values * (1.0 - sigma))


def contract_rows(left, right):
    return lax.dot_general(
        left, right, (((0,), (0,)), ((), ())), preferred_element_type=jnp.float32
    )


def contract_cols(left, right):
    return lax.dot_general(
        left, right, (((1,), (1,)), ((), ())), preferred_element_type=jnp.float32
    )


def on_device(
    grid_latent,
    mesh_latent,
    edge_latent,
    mesh_cotangent,
    edge_src,
    edge_dst,
    tile_count,
    send_rows,
    w_edge_in,
    w_edge_out,
    w_node_in,
    w_node_out,
):
    latent_width = edge_latent.shape[1]
    grid_count = grid_latent.shape[0]
    mesh_count = mesh_latent.shape[0]
    edge_count = edge_latent.shape[0]
    rows_list = send_rows[0]
    is_live = rows_list >= 0
    picked = jnp.take(grid_latent, jnp.clip(rows_list, 0, grid_count - 1), axis=0)
    outgoing = jnp.where(is_live[:, :, None], picked, jnp.zeros_like(picked))
    arrived = lax.all_to_all(outgoing, "lon", split_axis=0, concat_axis=0, tiled=True)
    received = arrived.reshape(-1, latent_width)
    slot_count = received.shape[0]
    edge_live = (jnp.arange(edge_count, dtype=jnp.int32) < tile_count[0] * TILE).astype(jnp.float32)
    sender_rows = jnp.take(received, edge_src, axis=0)
    onehot = (edge_dst[:, None] == jnp.arange(mesh_count, dtype=jnp.int32)[None, :]).astype(
        jnp.bfloat16
    )
    receiver_rows = jnp.dot(onehot, mesh_latent, preferred_element_type=jnp.float32).astype(
        jnp.bfloat16
    )
    joined = jnp.concatenate([edge_latent, sender_rows, receiver_rows], axis=1)
    edge_pre = jnp.dot(joined, w_edge_in, preferred_element_type=jnp.float32)
    edge_hidden = jax.nn.silu(edge_pre).astype(jnp.bfloat16)
    edge_proj = jnp.dot(edge_hidden, w_edge_out, preferred_element_type=jnp.float32)
    edge_norm, edge_inverse = layer_norm(edge_proj)
    edge_new = ((edge_latent.astype(jnp.float32) + edge_norm) * edge_live[:, None]).astype(
        jnp.bfloat16
    )
    aggregate = contract_rows(onehot, edge_new).astype(jnp.bfloat16)
    node_in = jnp.concatenate([mesh_latent, aggregate], axis=1)
    node_pre = jnp.dot(node_in, w_node_in, preferred_element_type=jnp.float32)
    node_hidden = jax.nn.silu(node_pre).astype(jnp.bfloat16)
    node_proj = jnp.dot(node_hidden, w_node_out, preferred_element_type=jnp.float32)
    node_norm, node_inverse = layer_norm(node_proj)
    upstream = mesh_cotangent.astype(jnp.float32)
    d_node_proj = norm_back(node_norm, node_inverse, upstream).astype(jnp.bfloat16)
    grad_node_out = contract_rows(node_hidden, d_node_proj)
    d_node_pre = (contract_cols(d_node_proj, w_node_out) * silu_slope(node_pre)).astype(
        jnp.bfloat16
    )
    grad_node_in = contract_rows(node_in, d_node_pre)
    d_node_in = contract_cols(d_node_pre, w_node_in)
    d_aggregate = d_node_in[:, latent_width:].astype(jnp.bfloat16)
    d_edge_new = (
        jnp.dot(onehot, d_aggregate, preferred_element_type=jnp.float32) * edge_live[:, None]
    )
    d_edge_proj = norm_back(edge_norm, edge_inverse, d_edge_new).astype(jnp.bfloat16)
    grad_edge_out = contract_rows(edge_hidden, d_edge_proj)
    d_edge_pre = (contract_cols(d_edge_proj, w_edge_out) * silu_slope(edge_pre)).astype(
        jnp.bfloat16
    )
    grad_edge_in = contract_rows(joined, d_edge_pre)
    d_joined = contract_cols(d_edge_pre, w_edge_in)
    edge_grad = (d_edge_new + d_joined[:, :latent_width]).astype(jnp.bfloat16)
    d_sender = d_joined[:, latent_width : 2 * latent_width].astype(jnp.bfloat16)
    d_receiver = d_joined[:, 2 * latent_width :].astype(jnp.bfloat16)
    mesh_grad = (upstream + d_node_in[:, :latent_width] + contract_rows(onehot, d_receiver)).astype(
        jnp.bfloat16
    )
    d_slots = jax.ops.segment_sum(
        d_sender.astype(jnp.float32), edge_src, num_segments=slot_count
    ).astype(jnp.bfloat16)
    returned = lax.all_to_all(
        d_slots.reshape(arrived.shape), "lon", split_axis=0, concat_axis=0, tiled=True
    )
    targets = jnp.where(is_live, rows_list, grid_count).reshape(-1)
    grid_grad = jax.ops.segment_sum(
        returned.reshape(-1, latent_width).astype(jnp.float32), targets, num_segments=grid_count + 1
    )[:grid_count].astype(jnp.bfloat16)
    totals = (
        lax.psum_scatter(
            grad_edge_in.astype(jnp.bfloat16), "lon", scatter_dimension=0, tiled=True
        ).astype(jnp.float32),
        lax.psum_scatter(
            grad_edge_out.astype(jnp.bfloat16), "lon", scatter_dimension=0, tiled=True
        ).astype(jnp.float32),
        lax.psum_scatter(
            grad_node_in.astype(jnp.bfloat16), "lon", scatter_dimension=0, tiled=True
        ).astype(jnp.float32),
        lax.psum_scatter(
            grad_node_out.astype(jnp.bfloat16), "lon", scatter_dimension=0, tiled=True
        ).astype(jnp.float32),
    )
    return (grid_grad, edge_grad, mesh_grad, totals[0], totals[1], totals[2], totals[3])


def solution(mesh):
    placed = (
        P(("grp", "lon"), None),
        P(("grp", "lon"), None),
        P(("grp", "lon"), None),
        P(("grp", "lon"), None),
        P(("grp", "lon")),
        P(("grp", "lon")),
        P(("grp", "lon")),
        P(("grp", "lon"), None, None),
        P(),
        P(),
        P(),
        P(),
    )
    return jax.shard_map(
        on_device,
        mesh=mesh,
        in_specs=placed,
        out_specs=(
            P(("grp", "lon"), None),
            P(("grp", "lon"), None),
            P(("grp", "lon"), None),
            P(("grp", "lon"), None),
            P(("grp", "lon"), None),
            P(("grp", "lon"), None),
            P(("grp", "lon"), None),
        ),
        check_vma=False,
    )
```

profile of v0, /device:TPU:0, one launch (start us, length us, event | category | flops | bytes accessed | tf_op | source)
XLA Modules:
  0.0 326.7 jit_solution(2413618624711039259)
XLA Ops:
  13.4 7.4 %all-to-all-start = ((bf16[16,48,512]{2,1,0:T(8,128)(2,1)}), bf16[16,48,512]{2,1,0:T(8,128)(2,1)S(1)}, u32[]{:S(2)}, u32[]{:S(2)}) async-start(bf16[16,48,512]{2,1,0:T(8,128)(2,1)} %select_select_fusion), calls=%async_computation | async-start | bytes 1572864 | tf_op jit(solution)/shard_map/all_to_all | solution.py:60
  22.2 4.7 %copy.25 = bf16[3072,512]{0,1:T(8,128)(2,1)} copy(bf16[3072,512]{1,0:T(8,128)(2,1)} %param.14) | data formatting | bytes 6291456 | tf_op args[2]
  30.2 9.3 %all-to-all-done = bf16[16,48,512]{2,1,0:T(8,128)(2,1)S(1)} async-done(((bf16[16,48,512]{2,1,0:T(8,128)(2,1)}), bf16[16,48,512]{2,1,0:T(8,128)(2,1)S(1)}, u32[]{:S(2)}, u32[]{:S(2)}) %all-to-all-start) | async-done | bytes 786464 | tf_op jit(solution)/shard_map/all_to_all | solution.py:60
  39.5 13.2 %gather_fusion.1 = bf16[3072,512]{1,0:T(8,128)(2,1)} fusion(bf16[768,512]{1,0:T(8,128)(2,1)S(1)} %bitcast.35, s32[3072]{0:T(1024)S(1)} %fusion.36), kind=kCustom, calls=%fused_computation.1 | custom fusion | bytes 6303744 | tf_op jit(solution)/shard_map/jit(_take)/gather | solution.py:64
  52.7 4.8 %copy.24 = bf16[3072,512]{0,1:T(8,128)(2,1)} copy(bf16[3072,512]{1,0:T(8,128)(2,1)} %gather_fusion.1) | data formatting | bytes 6291456 | tf_op jit(solution)/shard_map/jit(_take)/gather | solution.py:64
  61.3 7.7 %multiply_convert_fusion.3 = (bf16[3072,512]{1,0:T(8,128)(2,1)S(1)}, f32[3072,512]{1,0:T(8,128)}) fusion(bf16[1536,512]{1,0:T(8,128)(2,1)S(1)} %copy-done.10, bf16[3072,512]{0,1:T(8,128)(2,1)S(1)} %copy-done.4, bf16[3072,512]{0,1:T(8,128)(2,1)S(1)} %broadcast_select_fusion, bf16[3072,512]{0,1:T(8,128)(2,1)S(1)} %copy-done.7), kind=kOutput, calls=%fused_computation.13 | convolution fusion | flops 4868014080 | bytes 20447232 | tf_op jit(solution)/shard_map/dot_general | solution.py:72
  78.6 5.5 %multiply_reduce_fusion.2 = (f32[3072]{0:T(1024)S(1)}, f32[3072]{0:T(1024)S(1)}, f32[3072,512]{0,1:T(8,128)S(1)}) fusion(f32[3072]{0:T(1024)S(1)} %fusion.35, f32[3072]{0:T(1024)S(1)} %add_rsqrt_fusion, f32[3072,512]{0,1:T(8,128)} %copy-done.2, f32[3072]{0:T(1024)S(1)} %broadcast_multiply_fusion.2, f32[256,1024]{1,0:T(8,128)S(1)} %fusion.46, ...), kind=kOutput, calls=%fused_computation.16 | convolution fusion | flops 815523840 | bytes 12918784 | tf_op jit(solution)/shard_map/dot_general | solution.py:95
  84.1 4.4 %multiply_convert_fusion.1 = bf16[3072,512]{0,1:T(8,128)(2,1)} fusion(f32[3072,512]{0,1:T(8,128)S(1)} %get-tuple-element.31, f32[3072,512]{0,1:T(8,128)S(1)} %bitcast.37, f32[3072]{0:T(1024)S(1)} %broadcast_multiply_fusion, f32[3072]{0:T(1024)S(1)} %broadcast_multiply_fusion.1, f32[3072]{0:T(1024)S(1)} %fusion.35, f32[3072]{0:T(1024)} %copy-done.25, ...), kind=kLoop, calls=%fused_computation.9 | loop fusion | flops 12582912 | bytes 15790080 | tf_op jit(solution)/shard_map/convert_element_type | solution.py:97
  88.6 4.6 %convolution_convert_fusion.2 = bf16[512,512]{1,0:T(8,128)(2,1)} fusion(bf16[3072,512]{1,0:T(8,128)(2,1)S(1)} %copy-done.6, bf16[3072,512]{0,1:T(8,128)(2,1)} %multiply_convert_fusion.1), kind=kOutput, calls=%fused_computation.38 | convolution fusion | flops 1610874880 | bytes 6815744 | tf_op jit(solution)/shard_map/dot_general | solution.py:27
  93.4 7.7 %multiply_convert_fusion = bf16[3072,512]{1,0:T(8,128)(2,1)} fusion(f32[3072,512]{1,0:T(8,128)} %get-tuple-element.26, bf16[3072,512]{0,1:T(8,128)(2,1)} %multiply_convert_fusion.1, bf16[512,512]{1,0:T(8,128)(2,1)S(1)} %copy-done.16), kind=kOutput, calls=%fused_computation.8 | convolution fusion | flops 1624768512 | bytes 13107200 | tf_op jit(solution)/shard_map/dot_general | solution.py:33
  102.8 11.2 %fusion.10 = bf16[1536,512]{1,0:T(8,128)(2,1)} fusion(bf16[3072,512]{1,0:T(8,128)(2,1)} %multiply_convert_fusion, bf16[3072,512]{0,1:T(8,128)(2,1)} %convolution_convert_fusion, bf16[3072,512]{0,1:T(8,128)(2,1)} %copy-done.8, bf16[3072,512]{0,1:T(8,128)(2,1)} %copy.25), kind=kOutput, calls=%fused_computation.29 | convolution fusion | flops 4860936192 | bytes 14155776 | tf_op jit(solution)/shard_map/dot_general | solution.py:27
  114.0 14.1 %fusion.45 = (bf16[3072,1536]{1,0:T(8,128)(2,1)}, f32[3072,1536]{1,0:T(8,128)}) fusion(bf16[3072,512]{1,0:T(8,128)(2,1)} %multiply_convert_fusion, bf16[1536,512]{1,0:T(8,128)(2,1)S(1)} %copy-done.11), kind=kOutput, calls=%fused_computation.88 | convolution fusion | flops 4836556800 | bytes 33030144 | tf_op jit(solution)/shard_map/dot_general | solution.py:33
  128.1 19.8 %scatter_custom_fusion = f32[768,512]{1,0:T(8,128)S(1)} fusion(s32[3072]{0:T(1024)} %param.16, bf16[3072,1536]{1,0:T(8,128)(2,1)} %get-tuple-element.32, f32[]{:T(128)} %constant.29.clone.1), kind=kCustom, calls=%fused_computation.6 | custom fusion | flops 3145728 | bytes 4719104 | tf_op jit(solution)/shard_map/scatter-add | solution.py:110
  148.9 5.4 %all-to-all-start.1 = ((bf16[16,48,512]{2,1,0:T(8,128)(2,1)}), bf16[16,48,512]{2,1,0:T(8,128)(2,1)S(1)}, u32[]{:S(2)}, u32[]{:S(2)}) async-start(bf16[16,48,512]{2,1,0:T(8,128)(2,1)} %bitcast.39), calls=%async_computation.1 | async-start | bytes 1572864 | tf_op jit(solution)/shard_map/all_to_all | solution.py:113
  154.4 6.1 %slice.35 = f32[3072,512]{1,0:T(8,128)} slice(f32[3072,1536]{1,0:T(8,128)} %get-tuple-element.33), slice={[0:3072], [0:512]} | slice | bytes 12582912 | tf_op jit(solution)/shard_map/slice | solution.py:104
  160.5 6.6 %copy.29 = f32[3072,512]{0,1:T(8,128)} copy(f32[3072,512]{1,0:T(8,128)} %slice.35) | data formatting | bytes 12582912
  167.1 7.8 %add_convert_fusion = bf16[3072,512]{0,1:T(8,128)(2,1)} fusion(f32[3072,512]{0,1:T(8,128)} %copy.29, f32[3072,512]{0,1:T(8,128)} %copy-done.3, f32[3072]{0:T(1024)S(1)} %fusion.35), kind=kLoop, calls=%fused_computation.5 | loop fusion | flops 4718592 | bytes 15740928 | tf_op jit(solution)/shard_map/convert_element_type | solution.py:104
  174.9 4.7 %copy.28 = bf16[3072,512]{1,0:T(8,128)(2,1)} copy(bf16[3072,512]{0,1:T(8,128)(2,1)} %add_convert_fusion) | data formatting | bytes 6291456
  179.6 4.4 %fusion.26 = bf16[256,512]{1,0:T(8,128)(2,1)} fusion(bf16[3072,1536]{1,0:T(8,128)(2,1)} %get-tuple-element.32, s32[3072]{0:T(1024)S(1)} %copy-done.23, bf16[256,512]{1,0:T(8,128)(2,1)S(1)} %copy-done.14, f32[256,1024]{1,0:T(8,128)} %copy-done.9), kind=kOutput, calls=%fused_computation.44 | convolution fusion | flops 806617088 | bytes 4206592 | tf_op jit(solution)/shard_map/dot_general | solution.py:27
  185.4 10.6 %reduce-scatter.7.cloned.1.call-done = bf16[32,512]{1,0:T(8,128)(2,1)} async-done(((bf16[512,512]{1,0:T(8,128)(2,1)}), bf16[32,512]{1,0:T(8,128)(2,1)}) %reduce-scatter.7.cloned.1.call-update) | async-done | bytes 32784 | tf_op jit(solution)/shard_map/reduce_scatter | solution.py:124
  197.4 9.4 %scatter_custom_fusion.1 = f32[2049,512]{1,0:T(8,128)} fusion(s32[768]{0:T(1024)S(1)} %fusion.37, f32[]{:T(128)} %constant.29.clone.1, bf16[768,512]{1,0:T(8,128)(2,1)S(1)} %bitcast.38), kind=kCustom, calls=%fused_computation.30 | custom fusion | flops 786432 | bytes 4982788 | tf_op jit(solution)/shard_map/scatter-add | solution.py:117
  206.8 3.8 %slice.52 = bf16[2048,512]{1,0:T(8,128)(2,1)} slice(f32[2049,512]{1,0:T(8,128)} %scatter_custom_fusion.1), slice={[0:2048], [0:512]} | slice | bytes 4194304 | tf_op jit(solution)/shard_map/slice | solution.py:117
  210.6 45.4 %reduce-scatter.9.cloned.1.call-done = bf16[64,512]{1,0:T(8,128)(2,1)} async-done(((bf16[1024,512]{1,0:T(8,128)(2,1)}), bf16[64,512]{1,0:T(8,128)(2,1)}) %reduce-scatter.9.cloned.1.call-update) | async-done | bytes 65552 | tf_op jit(solution)/shard_map/reduce_scatter | solution.py:127
  257.5 61.1 %reduce-scatter.5.cloned.1.call-done = bf16[96,512]{1,0:T(8,128)(2,1)} async-done(((bf16[1536,512]{1,0:T(8,128)(2,1)}), bf16[96,512]{1,0:T(8,128)(2,1)}) %reduce-scatter.5.cloned.1.call-update) | async-done | bytes 98320 | tf_op jit(solution)/shard_map/reduce_scatter | solution.py:121
  (115 shorter events, 32.1 us)
Async XLA Ops:
  7.2 13.7 %copy-start.24 = (s32[1,16,48]{2,1,0:T(8,128)S(1)}, s32[1,16,48]{2,1,0:T(8,128)}, u32[]{:S(2)}) copy-start(s32[1,16,48]{2,1,0:T(8,128)} %param.19) | copy-start | bytes 9220
  12.2 14.7 %copy-start.26 = (s32[3072]{0:T(1024)S(1)}, s32[3072]{0:T(1024)}, u32[]{:S(2)}) copy-start(s32[3072]{0:T(1024)} %param.16) | copy-start | bytes 36868
  12.2 14.7 %copy-start.17 = (bf16[256,512]{1,0:T(8,128)(2,1)S(1)}, bf16[256,512]{1,0:T(8,128)(2,1)}, u32[]{:S(2)}) copy-start(bf16[256,512]{1,0:T(8,128)(2,1)} %param.13) | copy-start | bytes 786436
  12.3 14.7 %copy-start.22 = (s32[3072]{0:T(1024)S(1)}, s32[3072]{0:T(1024)}, u32[]{:S(2)}) copy-start(s32[3072]{0:T(1024)} %param.17) | copy-start | bytes 36868
  13.4 26.1 %all-to-all-start = ((bf16[16,48,512]{2,1,0:T(8,128)(2,1)}), bf16[16,48,512]{2,1,0:T(8,128)(2,1)S(1)}, u32[]{:S(2)}, u32[]{:S(2)}) async-start(bf16[16,48,512]{2,1,0:T(8,128)(2,1)} %select_select_fusion), calls=%async_computation | async-start | bytes 1572864 | tf_op jit(solution)/shard_map/all_to_all | solution.py:60
  20.8 163.2 %reduce-scatter.11.cloned.1.call-start = ((), (), s32[]{:S(2)}) async-start(), calls=%async_computation.9 | async-start | bytes 557056 | tf_op jit(solution)/shard_map/reduce_scatter | solution.py:130
  52.7 7.1 %copy-start.10 = (bf16[1536,512]{1,0:T(8,128)(2,1)S(1)}, bf16[1536,512]{1,0:T(8,128)(2,1)}, u32[]{:S(2)}) copy-start(bf16[1536,512]{1,0:T(8,128)(2,1)} %param.20) | copy-start | bytes 4718596
  61.3 7.7 %copy-start.8 = (bf16[3072,512]{0,1:T(8,128)(2,1)}, bf16[3072,512]{0,1:T(8,128)(2,1)S(1)}, u32[]{:S(2)}) copy-start(bf16[3072,512]{0,1:T(8,128)(2,1)S(1)} %broadcast_select_fusion) | copy-start | bytes 9437188
  61.3 7.7 %copy-start.15 = (bf16[512,512]{1,0:T(8,128)(2,1)S(1)}, bf16[512,512]{1,0:T(8,128)(2,1)}, u32[]{:S(2)}) copy-start(bf16[512,512]{1,0:T(8,128)(2,1)} %param.21) | copy-start | bytes 1572868
  71.0 7.5 %copy-start.21 = (f32[3072]{0:T(1024)}, f32[3072]{0:T(1024)S(1)}, u32[]{:S(2)}) copy-start(f32[3072]{0:T(1024)S(1)} %broadcast_multiply_fusion.2) | copy-start | bytes 36868
  71.9 6.7 %copy-start.25 = (f32[3072]{0:T(1024)}, f32[3072]{0:T(1024)S(1)}, u32[]{:S(2)}) copy-start(f32[3072]{0:T(1024)S(1)} %add_rsqrt_fusion) | copy-start | bytes 36868
  76.6 7.4 %copy-start.19 = (bf16[256,512]{1,0:T(8,128)(2,1)}, bf16[256,512]{1,0:T(8,128)(2,1)S(1)}, u32[]{:S(2)}) copy-start(bf16[256,512]{1,0:T(8,128)(2,1)S(1)} %fusion.25) | copy-start | bytes 786436
  77.8 118.2 %reduce-scatter.7.cloned.1.call-start = ((), (), s32[]{:S(2)}) async-start(), calls=%async_computation.7 | async-start | bytes 557056 | tf_op jit(solution)/shard_map/reduce_scatter | solution.py:124
  78.1 6.0 %slice-start = ((s8[6291456]{0:T(1024)(128)(4,1)}), s8[4194304]{0:T(1024)(128)(4,1)S(1)}, s32[]{:S(2)}) async-start(s8[6291456]{0:T(1024)(128)(4,1)} %bitcast.36), calls=%async_computation.10 | async-start | bytes 8388608
  78.6 5.5 %slice-start.1 = ((s8[6291456]{0:T(1024)(128)(4,1)}), s8[2097152]{0:T(1024)(128)(4,1)S(1)}, s32[]{:S(2)}) async-start(s8[6291456]{0:T(1024)(128)(4,1)} %bitcast.36), calls=%async_computation.11 | async-start | bytes 4194304
  93.3 162.7 %reduce-scatter.9.cloned.1.call-start = ((), (), s32[]{:S(2)}) async-start(), calls=%async_computation.8 | async-start | bytes 1114112 | tf_op jit(solution)/shard_map/reduce_scatter | solution.py:127
  93.4 7.7 %copy-start.18 = (bf16[256,512]{1,0:T(8,128)(2,1)S(1)}, bf16[256,512]{1,0:T(8,128)(2,1)}, u32[]{:S(2)}) copy-start(bf16[256,512]{1,0:T(8,128)(2,1)} %param.13) | copy-start | bytes 786436
  93.4 7.7 %copy-start.20 = (bf16[256,512]{1,0:T(8,128)(2,1)S(1)}, bf16[256,512]{1,0:T(8,128)(2,1)}, u32[]{:S(2)}) copy-start(bf16[256,512]{1,0:T(8,128)(2,1)} %copy-done.19) | copy-start | bytes 786436
  93.4 7.7 %copy-start.30 = (bf16[256,512]{1,0:T(8,128)(2,1)S(1)}, bf16[256,512]{1,0:T(8,128)(2,1)}, u32[]{:S(2)}) copy-start(bf16[256,512]{1,0:T(8,128)(2,1)} %copy-done.29) | copy-start | bytes 786436
  102.6 11.5 %copy-start.11 = (bf16[1536,512]{1,0:T(8,128)(2,1)S(1)}, bf16[1536,512]{1,0:T(8,128)(2,1)}, u32[]{:S(2)}) copy-start(bf16[1536,512]{1,0:T(8,128)(2,1)} %param.20) | copy-start | bytes 4718596
  102.6 216.0 %reduce-scatter.5.cloned.1.call-start = ((), (), s32[]{:S(2)}) async-start(), calls=%async_computation.6 | async-start | bytes 1671168 | tf_op jit(solution)/shard_map/reduce_scatter | solution.py:121
  128.1 26.3 %copy-start.27 = (s32[768,1]{0,1:T(1,128)S(1)}, s32[768,1]{0,1:T(1,128)}, u32[]{:S(2)}) copy-start(s32[768,1]{0,1:T(1,128)} %squeeze.4) | copy-start | bytes 9220
  148.9 48.5 %all-to-all-start.1 = ((bf16[16,48,512]{2,1,0:T(8,128)(2,1)}), bf16[16,48,512]{2,1,0:T(8,128)(2,1)S(1)}, u32[]{:S(2)}, u32[]{:S(2)}) async-start(bf16[16,48,512]{2,1,0:T(8,128)(2,1)} %bitcast.39), calls=%async_computation.1 | async-start | bytes 1572864 | tf_op jit(solution)/shard_map/all_to_all | solution.py:113
  179.6 140.5 %copy-start.1 = (bf16[2048,512]{1,0:T(8,128)(2,1)S(1)}, bf16[2048,512]{1,0:T(8,128)(2,1)}, u32[]{:S(2)}) copy-start(bf16[2048,512]{1,0:T(8,128)(2,1)} %param.12) | copy-start | bytes 6291460
  (15 other events, 53.1 us)
Sparse Core Ops, SparseCore 0:
  78.0 56.5 reduce-scatter.10
  138.5 57.4 reduce-scatter.6
  199.6 56.3 reduce-scatter.8
  260.0 58.5 reduce-scatter.4
where the time goes:
time: 328 us; the launch traced here: 327 us
  waiting for transfers between devices  126 us (38%)
  matrix products  66.6 us (20%)
  other arithmetic  55.6 us (17%)
  local copies, waits for them, and re-layouts  49.7 us (15%)
  between operations  14.9 us (5%)
  starting transfers between devices  13.4 us (4%)
    reduce_scatter x1, waiting for transfers between devices, on_device(): lax.psum_scatter(grad_edge_in.astype(jnp.bfloat16), 'lon', scatter_dimens...  61.1 us
    reduce_scatter x1, waiting for transfers between devices, on_device(): lax.psum_scatter(grad_node_in.astype(jnp.bfloat16), 'lon', scatter_dimens...  45.4 us
    dot_general x6, matrix products, contract_rows(): lax.dot_general(left, right, (((0,), (0,)), ((), ())), preferred_element_...  24.8 us
    dot_general x4, matrix products, contract_cols(): lax.dot_general(left, right, (((1,), (1,)), ((), ())), preferred_element_...  22.6 us
    scatter-add x1, other arithmetic, on_device(): jax.ops.segment_sum(d_sender.astype(jnp.float32), edge_src, num_segments=...  19.8 us
    unnamed x69, local copies, waits for them, and re-layouts  18.4 us
    gather x2, local copies, waits for them, and re-layouts, on_device(): sender_rows = jnp.take(received, edge_src, axis=0)  18 us
    reduce_scatter x1, waiting for transfers between devices, on_device(): lax.psum_scatter(grad_edge_out.astype(jnp.bfloat16), 'lon', scatter_dimen...  10.6 us
  transfers between devices with their start and end apart: 6, of which 4 were waited for; matrix products, arithmetic and copies ran while one was open for 39% of the time, Pallas kernels for 0%

commit v1 on v0

v1 whole, which is shorter than its diff:
```python
import functools

import jax
import jax.numpy as jnp
from jax import lax
from jax.experimental import pallas as pl
from jax.experimental.pallas import tpu as pltpu
from jax.sharding import PartitionSpec as P

TILE = 256
NEAR = 3
SHIFTS = (0, 1, 2, 3, -1, -2, -3)
BF16 = jnp.bfloat16
F32 = jnp.float32
VMEM_BYTES = 56 * 1024 * 1024


def dot(left, right):
    return lax.dot_general(left, right, (((1,), (0,)), ((), ())), preferred_element_type=F32)


def contract_rows(left, right):
    return lax.dot_general(left, right, (((0,), (0,)), ((), ())), preferred_element_type=F32)


def contract_cols(left, right):
    return lax.dot_general(left, right, (((1,), (1,)), ((), ())), preferred_element_type=F32)


def layer_norm(values):
    centered = values - jnp.mean(values, axis=1, keepdims=True)
    inverse = lax.rsqrt(jnp.mean(centered * centered, axis=1, keepdims=True) + 1e-05)
    return (centered * inverse, inverse)


def norm_back(normed, inverse, upstream):
    first = jnp.mean(upstream, axis=1, keepdims=True)
    second = jnp.mean(upstream * normed, axis=1, keepdims=True)
    return inverse * (upstream - first - normed * second)


def silu_and_slope(values):
    sigma = 0.5 + 0.5 * jnp.tanh(0.5 * values)
    hidden = values * sigma
    return (hidden, sigma + hidden * (1.0 - sigma))


def as_column(row):
    count = row.shape[1]
    down = lax.broadcasted_iota(jnp.int32, (count, count), 0)
    along = lax.broadcasted_iota(jnp.int32, (count, count), 1)
    picked = jnp.where(down == along, row.astype(F32), 0.0)
    return jnp.sum(picked, axis=1, keepdims=True).astype(jnp.int32)


def hot_rows(row, width):
    column = as_column(row)
    along = lax.broadcasted_iota(jnp.int32, (row.shape[1], width), 1)
    return (column == along).astype(F32).astype(BF16)


def hot_columns(row, height):
    down = lax.broadcasted_iota(jnp.int32, (height, row.shape[1]), 0)
    return (row == down).astype(F32).astype(BF16)


def list_hots(me, rows_ref, grid_count):
    peers, cap = rows_ref.shape
    pieces = []
    for shift in SHIFTS:
        target = lax.rem(me + shift + peers, peers)
        pieces.append(hot_rows(rows_ref[pl.ds(target, 1), :], grid_count))
    peer = lax.broadcasted_iota(jnp.int32, (peers, cap), 0)
    ahead = lax.rem(peer - me + peers, peers)
    apart = jnp.minimum(ahead, peers - ahead)
    far = jnp.max(jnp.where(apart > NEAR, rows_ref[...].astype(F32), -1.0), axis=0, keepdims=True)
    pieces.append(hot_rows(far.astype(jnp.int32), grid_count))
    return jnp.concatenate(pieces, axis=0)


def gather_kernel(me_ref, rows_ref, grid_ref, *out_refs):
    cap = rows_ref.shape[1]
    hots = list_hots(me_ref[0], rows_ref, grid_ref.shape[0])
    picked = dot(hots, grid_ref[...]).astype(BF16)
    for place, out_ref in enumerate(out_refs):
        out_ref[...] = picked[place * cap : (place + 1) * cap]


def scatter_kernel(me_ref, rows_ref, *refs):
    list_refs, out_ref = refs[:-1], refs[-1]
    hots = list_hots(me_ref[0], rows_ref, out_ref.shape[0])
    values = jnp.concatenate([ref[...].astype(BF16) for ref in list_refs], axis=0)
    out_ref[...] = contract_rows(hots, values).astype(BF16)


def local_kernel(dst_ref, edge_ref, mesh_ref, w_edge_ref, w_receiver_ref, out_ref, mesh_proj):
    @pl.when(pl.program_id(0) == 0)
    def _():
        mesh_proj[...] = dot(mesh_ref[...], w_receiver_ref[...]).astype(BF16)

    onehot = hot_rows(dst_ref[0], mesh_ref.shape[0])
    out_ref[...] = (
        dot(edge_ref[...], w_edge_ref[...]) + dot(onehot, mesh_proj[...])
    ).astype(BF16)


def split_out(me, peers, send_ref, keep_ref, parts):
    upper = peers // 4
    for upper_bits in range(upper):
        for low_bits in range(4):
            owner = me ^ (4 * upper_bits + low_bits)
            target = send_ref if low_bits % 2 else keep_ref
            start = 0
            for ref, share, live in parts:
                offset = pl.multiple_of(owner * share, 16)
                piece = ref[pl.ds(offset, share), :]
                if live:
                    ahead = lax.rem(owner - me + peers, peers)
                    apart = jnp.minimum(ahead, peers - ahead)
                    piece = jnp.where(apart > NEAR, piece.astype(F32), 0.0)
                target[low_bits // 2, upper_bits, start : start + share, :] = piece.astype(BF16)
                start += share


def forward_kernel(
    peers, me_ref, count_ref, src_ref, dst_ref, local_ref, edge_ref, *refs
):
    lists = refs[:10]
    (w_sender_ref, w_out_ref, w_node_in_ref, w_node_out_ref, mesh_ref, cotangent_ref) = refs[10:16]
    (received_ref, hidden_ref, slope_ref, norm_ref, inverse_ref) = refs[16:21]
    (send_ref, keep_ref, d_aggregate_ref, d_mesh_ref) = refs[21:25]
    (slot_proj, aggregate, grad_in, grad_out) = refs[25:]
    step = pl.program_id(0)
    me = me_ref[0]
    cap = lists[0].shape[0]
    width = edge_ref.shape[1]
    upper = peers // 4

    @pl.when(step == 0)
    def _():
        aggregate[...] = jnp.zeros_like(aggregate)
        w_sender = w_sender_ref[...]

        def place(owner, rows, projected):
            offset = pl.multiple_of(owner * cap, 16)
            received_ref[pl.ds(offset, cap), :] = rows
            slot_proj[pl.ds(offset, cap), :] = projected

        far = (lists[7], lists[8], lists[9])
        for ref, low_bits in zip(far, ((0,), (2,), (1, 3))):
            rows = ref[...]
            projected = dot(rows, w_sender).astype(BF16)
            at = 0
            for low in low_bits:
                for upper_bits in range(upper):
                    owner = me ^ (4 * upper_bits + low)
                    place(owner, rows[at : at + cap], projected[at : at + cap])
                    at += cap
        rows = jnp.concatenate([ref[...] for ref in lists[:7]], axis=0)
        projected = dot(rows, w_sender).astype(BF16)
        for spot, shift in enumerate(SHIFTS):
            owner = lax.rem(me - shift + peers, peers)
            place(owner, rows[spot * cap : (spot + 1) * cap], projected[spot * cap : (spot + 1) * cap])

    @pl.when(step < count_ref[0])
    def _():
        onehot = hot_rows(src_ref[0], slot_proj.shape[0])
        pre = local_ref[...].astype(F32) + dot(onehot, slot_proj[...])
        hidden, slope = silu_and_slope(pre)
        hidden = hidden.astype(BF16)
        hidden_ref[...] = hidden
        slope_ref[...] = slope.astype(BF16)
        normed, inverse = layer_norm(dot(hidden, w_out_ref[...]))
        norm_ref[...] = normed.astype(BF16)
        inverse_ref[...] = inverse
        edge_new = (edge_ref[...].astype(F32) + normed).astype(BF16)
        aggregate[...] += dot(hot_columns(dst_ref[0], aggregate.shape[0]), edge_new)

    @pl.when(step == pl.num_programs(0) - 1)
    def _():
        mesh = mesh_ref[...]
        summed = aggregate[...].astype(BF16)
        node_pre = dot(mesh, w_node_in_ref[:width, :]) + dot(summed, w_node_in_ref[width:, :])
        hidden, slope = silu_and_slope(node_pre)
        hidden = hidden.astype(BF16)
        normed, inverse = layer_norm(dot(hidden, w_node_out_ref[...]))
        upstream = cotangent_ref[...].astype(F32)
        d_proj = norm_back(normed, inverse, upstream).astype(BF16)
        d_pre = (contract_cols(d_proj, w_node_out_ref[...]) * slope).astype(BF16)
        d_mesh_ref[...] = upstream + contract_cols(d_pre, w_node_in_ref[:width, :])
        d_aggregate_ref[...] = contract_cols(d_pre, w_node_in_ref[width:, :]).astype(BF16)
        grad_out[...] = contract_rows(hidden, d_proj)
        grad_in[:width, :] = contract_rows(mesh, d_pre)
        grad_in[width:, :] = contract_rows(summed, d_pre)
        split_out(
            me,
            peers,
            send_ref,
            keep_ref,
            ((grad_in, grad_in.shape[0] // peers, False), (grad_out, grad_out.shape[0] // peers, False)),
        )


def slots_kernel(peers, me_ref, count_ref, src_ref, dst_ref, *refs):
    (hidden_ref, slope_ref, norm_ref, inverse_ref, d_aggregate_ref) = refs[:5]
    (received_ref, w_sender_ref, w_out_ref) = refs[5:8]
    (d_pre_ref, grad_sender_ref, send_ref, keep_ref) = refs[8:12]
    near_refs = refs[12:19]
    (slot_sum, grad_out, d_slots) = refs[19:]
    step = pl.program_id(0)
    me = me_ref[0]

    @pl.when(step == 0)
    def _():
        slot_sum[...] = jnp.zeros_like(slot_sum)
        grad_out[...] = jnp.zeros_like(grad_out)

    @pl.when(step < count_ref[0])
    def _():
        onehot = hot_rows(dst_ref[0], d_aggregate_ref.shape[0])
        upstream = dot(onehot, d_aggregate_ref[...])
        d_proj = norm_back(norm_ref[...].astype(F32), inverse_ref[...], upstream).astype(BF16)
        grad_out[...] += contract_rows(hidden_ref[...], d_proj)
        d_pre = (contract_cols(d_proj, w_out_ref[...]) * slope_ref[...].astype(F32)).astype(BF16)
        d_pre_ref[...] = d_pre
        slot_sum[...] += dot(hot_columns(src_ref[0], slot_sum.shape[0]), d_pre)

    @pl.when(step == pl.num_programs(0) - 1)
    def _():
        summed = slot_sum[...].astype(BF16)
        grad_sender_ref[...] = contract_rows(received_ref[...], summed)
        d_slots[...] = contract_cols(summed, w_sender_ref[...]).astype(BF16)
        cap = near_refs[0].shape[0]
        for shift, ref in zip(SHIFTS, near_refs):
            owner = lax.rem(me - shift + peers, peers)
            ref[...] = d_slots[pl.ds(pl.multiple_of(owner * cap, 16), cap), :]
        split_out(
            me,
            peers,
            send_ref,
            keep_ref,
            ((grad_out, grad_out.shape[0] // peers, False), (d_slots, cap, True)),
        )


def edges_kernel(peers, me_ref, count_ref, dst_ref, *refs):
    (edge_ref, d_pre_ref, d_aggregate_ref, d_mesh_ref, mesh_ref, grad_sender_ref) = refs[:6]
    (w_edge_ref, w_receiver_ref) = refs[6:8]
    (edge_grad_ref, mesh_grad_ref, send_ref, keep_ref) = refs[8:12]
    (grad_in, mesh_sum) = refs[12:]
    step = pl.program_id(0)
    width = edge_ref.shape[1]

    @pl.when(step == 0)
    def _():
        grad_in[:width, :] = jnp.zeros((width, grad_in.shape[1]), F32)
        mesh_sum[...] = jnp.zeros_like(mesh_sum)

    @pl.when(step < count_ref[0])
    def _():
        d_pre = d_pre_ref[...]
        onehot = hot_rows(dst_ref[0], d_aggregate_ref.shape[0])
        upstream = dot(onehot, d_aggregate_ref[...])
        edge_grad_ref[...] = (upstream + contract_cols(d_pre, w_edge_ref[...])).astype(BF16)
        grad_in[:width, :] += contract_rows(edge_ref[...], d_pre)
        mesh_sum[...] += dot(hot_columns(dst_ref[0], mesh_sum.shape[0]), d_pre)

    @pl.when(step >= count_ref[0])
    def _():
        edge_grad_ref[...] = jnp.zeros_like(edge_grad_ref)

    @pl.when(step == pl.num_programs(0) - 1)
    def _():
        summed = mesh_sum[...].astype(BF16)
        mesh_grad_ref[...] = (d_mesh_ref[...] + contract_cols(summed, w_receiver_ref[...])).astype(BF16)
        grad_in[width : 2 * width, :] = grad_sender_ref[...]
        grad_in[2 * width :, :] = contract_rows(mesh_ref[...], summed)
        split_out(me_ref[0], peers, send_ref, keep_ref, ((grad_in, grad_in.shape[0] // peers, False),))


def by_xor(peers, bits):
    return [(peer, peer ^ bits) for peer in range(peers)]


def by_shift(peers, shift):
    return [(peer, (peer + shift) % peers) for peer in range(peers)]


def send(values, perm):
    return lax.ppermute(values, "lon", perm)


def add(left, right):
    return (left.astype(F32) + right.astype(F32)).astype(BF16)


def reduce_scatter(peers, outgoing, kept):
    arrived = send(outgoing, by_xor(peers, 1))
    next_out = add(kept[1], arrived[1])
    next_kept = add(kept[0], arrived[0])
    arrived = send(next_out, by_xor(peers, 2))
    pieces = [add(next_kept[place], arrived[place]) for place in range(peers // 4)]
    total = pieces[0].astype(F32)
    for place in range(1, peers // 4):
        total = total + send(pieces[place], by_xor(peers, 4 * place)).astype(F32)
    return total


def whole(shape):
    return pl.BlockSpec(shape, lambda *_: (0,) * len(shape))


def on_device(
    grid_latent,
    mesh_latent,
    edge_latent,
    mesh_cotangent,
    edge_src,
    edge_dst,
    tile_count,
    send_rows,
    w_edge_in,
    w_edge_out,
    w_node_in,
    w_node_out,
):
    peers = lax.axis_size("lon")
    me = lax.axis_index("lon").astype(jnp.int32).reshape(1)
    upper = peers // 4
    rows = send_rows[0]
    cap = rows.shape[1]
    slots = peers * cap
    edges, width = edge_latent.shape
    mesh_count = mesh_latent.shape[0]
    grid_count = grid_latent.shape[0]
    tiles = edges // TILE
    src = edge_src.reshape(tiles, 1, TILE)
    dst = edge_dst.reshape(tiles, 1, TILE)
    smem = pl.BlockSpec(memory_space=pltpu.SMEM)
    params = pltpu.CompilerParams(vmem_limit_bytes=VMEM_BYTES)
    one_list = jax.ShapeDtypeStruct((cap, width), BF16)
    square = (width, width)

    def tile_of(last):
        return pl.BlockSpec((TILE, last), lambda step, *_: (step, 0))

    index_tile = pl.BlockSpec((1, 1, TILE), lambda step, *_: (step, 0, 0))

    def weight(place):
        return pl.BlockSpec(square, lambda *_: (place, 0))

    def halves(share):
        shape = (2, upper, share, width)
        return [jax.ShapeDtypeStruct(shape, BF16)] * 2, [whole(shape)] * 2

    lists = pl.pallas_call(
        gather_kernel,
        in_specs=[smem, whole(rows.shape), whole(grid_latent.shape)],
        out_specs=[whole((cap, width))] * 8,
        out_shape=[one_list] * 8,
        compiler_params=params,
        name="gather_lists",
    )(me, rows, grid_latent)

    near = [lists[0]] + [
        send(lists[place], by_shift(peers, SHIFTS[place])) for place in range(1, 7)
    ]
    far_own = jnp.concatenate(
        [lists[7]] + [send(lists[7], by_xor(peers, 4 * bits)) for bits in range(1, upper)], axis=0
    )
    far_next = send(far_own, by_xor(peers, 2))
    far_core = send(jnp.concatenate([far_own, far_next], axis=0), by_xor(peers, 1))

    local = pl.pallas_call(
        local_kernel,
        grid=(tiles,),
        in_specs=[index_tile, tile_of(width), whole(mesh_latent.shape), weight(0), weight(2)],
        out_specs=tile_of(width),
        out_shape=jax.ShapeDtypeStruct((edges, width), BF16),
        scratch_shapes=[pltpu.VMEM((mesh_count, width), BF16)],
        compiler_params=params,
        cost_estimate=pl.CostEstimate(
            flops=2 * edges * width * (width + mesh_count), bytes_accessed=4 * edges * width, transcendentals=0
        ),
        name="edge_local",
    )(dst, edge_latent, mesh_latent, w_edge_in, w_edge_in)

    node_shape, node_spec = halves(w_node_in.shape[0] // peers + w_node_out.shape[0] // peers)
    (received, hidden, slope, norm, inverse, node_send, node_keep, d_aggregate, d_mesh) = pl.pallas_call(
        functools.partial(forward_kernel, peers),
        grid=(tiles,),
        in_specs=[smem, smem, index_tile, index_tile, tile_of(width), tile_of(width)]
        + [whole((cap, width))] * 7
        + [whole((upper * cap, width))] * 2
        + [whole((2 * upper * cap, width))]
        + [weight(1)]
        + [whole(w.shape) for w in (w_edge_out, w_node_in, w_node_out, mesh_latent, mesh_cotangent)],
        out_specs=[whole((slots, width))]
        + [tile_of(width)] * 3
        + [tile_of(1)]
        + node_spec
        + [whole((mesh_count, width))] * 2,
        out_shape=[jax.ShapeDtypeStruct((slots, width), BF16)]
        + [jax.ShapeDtypeStruct((edges, width), BF16)] * 3
        + [jax.ShapeDtypeStruct((edges, 1), F32)]
        + node_shape
        + [jax.ShapeDtypeStruct((mesh_count, width), BF16), jax.ShapeDtypeStruct((mesh_count, width), F32)],
        scratch_shapes=[
            pltpu.VMEM((slots, width), BF16),
            pltpu.VMEM((mesh_count, width), F32),
            pltpu.VMEM(w_node_in.shape, F32),
            pltpu.VMEM(w_node_out.shape, F32),
        ],
        compiler_params=params,
        name="forward",
    )(
        me,
        tile_count,
        src,
        dst,
        local,
        edge_latent,
        *near,
        far_own,
        far_next,
        far_core,
        w_edge_in,
        w_edge_out,
        w_node_in,
        w_node_out,
        mesh_latent,
        mesh_cotangent,
    )

    slot_shape, slot_spec = halves(w_edge_out.shape[0] // peers + cap)
    results = pl.pallas_call(
        functools.partial(slots_kernel, peers),
        grid=(tiles,),
        in_specs=[smem, smem, index_tile, index_tile]
        + [tile_of(width)] * 3
        + [tile_of(1), whole((mesh_count, width)), whole((slots, width)), weight(1), whole(square)],
        out_specs=[tile_of(width), whole(square)] + slot_spec + [whole((cap, width))] * 7,
        out_shape=[jax.ShapeDtypeStruct((edges, width), BF16), jax.ShapeDtypeStruct(square, F32)]
        + slot_shape
        + [one_list] * 7,
        scratch_shapes=[
            pltpu.VMEM((slots, width), F32),
            pltpu.VMEM(square, F32),
            pltpu.VMEM((slots, width), BF16),
        ],
        compiler_params=params,
        cost_estimate=pl.CostEstimate(
            flops=2 * edges * width * (mesh_count + 2 * width + slots),
            bytes_accessed=8 * edges * width,
            transcendentals=0,
        ),
        name="backward_slots",
    )(me, tile_count, src, dst, hidden, slope, norm, inverse, d_aggregate, received, w_edge_in, w_edge_out)
    (d_pre, grad_sender, slot_send, slot_keep), returns = results[:4], results[4:]
    returned = [returns[0]] + [
        send(returns[place], by_shift(peers, -SHIFTS[place])) for place in range(1, 7)
    ]

    edge_shape, edge_spec = halves(w_edge_in.shape[0] // peers)
    edge_grad, mesh_grad, edge_send, edge_keep = pl.pallas_call(
        functools.partial(edges_kernel, peers),
        grid=(tiles,),
        in_specs=[smem, smem, index_tile, tile_of(width), tile_of(width)]
        + [whole((mesh_count, width))] * 3
        + [whole(square), weight(0), weight(2)],
        out_specs=[tile_of(width), whole((mesh_count, width))] + edge_spec,
        out_shape=[
            jax.ShapeDtypeStruct((edges, width), BF16),
            jax.ShapeDtypeStruct((mesh_count, width), BF16),
        ]
        + edge_shape,
        scratch_shapes=[pltpu.VMEM(w_edge_in.shape, F32), pltpu.VMEM((mesh_count, width), F32)],
        compiler_params=params,
        cost_estimate=pl.CostEstimate(
            flops=2 * edges * width * (2 * mesh_count + 2 * width),
            bytes_accessed=6 * edges * width,
            transcendentals=0,
        ),
        name="backward_edges",
    )(
        me,
        tile_count,
        dst,
        edge_latent,
        d_pre,
        d_aggregate,
        d_mesh,
        mesh_latent,
        grad_sender,
        w_edge_in,
        w_edge_in,
    )

    node_total = reduce_scatter(peers, node_send, node_keep)
    slot_total = reduce_scatter(peers, slot_send, slot_keep)
    edge_total = reduce_scatter(peers, edge_send, edge_keep)
    node_rows = w_node_in.shape[0] // peers
    out_rows = w_edge_out.shape[0] // peers
    grid_grad = pl.pallas_call(
        scatter_kernel,
        in_specs=[smem, whole(rows.shape)] + [whole((cap, width))] * 8,
        out_specs=whole(grid_latent.shape),
        out_shape=jax.ShapeDtypeStruct((grid_count, width), BF16),
        compiler_params=params,
        name="scatter_lists",
    )(me, rows, *returned, slot_total[out_rows:])
    return (
        grid_grad,
        edge_grad,
        mesh_grad,
        edge_total,
        slot_total[:out_rows],
        node_total[:node_rows],
        node_total[node_rows:],
    )


def solution(mesh):
    rows = P(("grp", "lon"), None)
    flat = P(("grp", "lon"))
    return jax.shard_map(
        on_device,
        mesh=mesh,
        in_specs=(rows, rows, rows, rows, flat, flat, flat, P(("grp", "lon"), None, None)) + (P(),) * 4,
        out_specs=(rows,) * 7,
        check_vma=False,
    )
```

time: 328 us -> 153 us (0.47)
  the two profiles are of different devices: /device:TPU:0 before, /device:TPU:10 now
where the time goes in v1:
time: 153 us; the launch traced here: 152 us
  Pallas kernels  70.1 us (46%)
  starting transfers between devices  37.4 us (24%)
  waiting for transfers between devices  36.2 us (24%)
  local copies, waits for them, and re-layouts  4.87 us (3%)
  between operations  1.76 us (1%)
  other arithmetic  1.69 us (1%)
    ppermute x32, starting transfers between devices, send(): return lax.ppermute(values, 'lon', perm)  37.4 us
    ppermute x32, waiting for transfers between devices, send(): return lax.ppermute(values, 'lon', perm)  36.2 us
    pallas_call x1, Pallas kernels, on_device(): pl.pallas_call(functools.partial(forward_kernel, peers), grid=(tiles,), i...  20.7 us
    pallas_call x1, Pallas kernels, on_device(): pl.pallas_call(functools.partial(slots_kernel, peers), grid=(tiles,), in_...  17.9 us
    pallas_call x1, Pallas kernels, on_device(): pl.pallas_call(functools.partial(edges_kernel, peers), grid=(tiles,), in_...  13.5 us
    pallas_call x1, Pallas kernels, on_device(): pl.pallas_call(local_kernel, grid=(tiles,), in_specs=[index_tile, tile_of...  11 us
    pallas_call x1, Pallas kernels, on_device(): pl.pallas_call(scatter_kernel, in_specs=[smem, whole(rows.shape)] + [whol...  3.81 us
    pallas_call x1, Pallas kernels, on_device(): pl.pallas_call(gather_kernel, in_specs=[smem, whole(rows.shape), whole(gr...  3.3 us
  transfers between devices with their start and end apart: 32, of which 10 were waited for; matrix products, arithmetic and copies ran while one was open for 3% of the time, Pallas kernels for 19%

profile of v1, /device:TPU:10, one launch (start us, length us, event | category | flops | bytes accessed | tf_op | source)
XLA Modules:
  0.0 152.0 jit_solution(18064939559248931326)
XLA Ops:
  0.6 3.3 %gather_lists.1 = (bf16[48,512]{1,0:T(8,128)(2,1)}, bf16[48,512]{1,0:T(8,128)(2,1)}, bf16[48,512]{1,0:T(8,128)(2,1)}, bf16[48,512]{1,0:T(8,128)(2,1)}, bf16[48,5...) custom-call(s32[1]{0:T(128)} %bitcast.me_ref, ...), custom_call_target="tpu_custom_call" | custom-call | tf_op jit(solution)/shard_map/gather_lists/pallas_call | solution.py:356
  4.4 2.6 %collective-permute-start.7 = (bf16[48,512]{1,0:T(8,128)(2,1)}, bf16[48,512]{1,0:T(8,128)(2,1)S(1)}, u32[]{:S(2)}, u32[]{:S(2)}) collective-permute-start(bf16[48,512]{1,0:T(8,128)(2,1)} %get-tuple-element.46), channel_id=1, source_target_pairs={{0,8},{1,9},{2,10},{3,11},{4,12},{5,13},{6,14},{7,15},{8,0},{9,1},... | collective-permute-start | bytes 147464 | tf_op jit(solution)/shard_map/ppermute | solution.py:290
  8.3 2.4 %collective-permute-done.7 = bf16[48,512]{1,0:T(8,128)(2,1)S(1)} collective-permute-done((bf16[48,512]{1,0:T(8,128)(2,1)}, bf16[48,512]{1,0:T(8,128)(2,1)S(1)}, u32[]{:S(2)}, u32[]{:S(2)}) %collective-permute-start.7) | collective-permute-done | bytes 49184 | tf_op jit(solution)/shard_map/ppermute | solution.py:290
  11.8 1.6 %collective-permute-start.9 = (bf16[192,512]{1,0:T(8,128)(2,1)S(1)}, bf16[192,512]{1,0:T(8,128)(2,1)S(1)}, u32[]{:S(2)}, u32[]{:S(2)}) collective-permute-start(bf16[192,512]{1,0:T(8,128)(2,1)S(1)} %get-tuple-element.87.refs_7_), channel_id=1, source_target_pairs={{0,2},{1,3},{2,0},{3,1},{4,6},{5,7},{6,4},{7,5},{8,10},{9,11},{10,... | collective-permute-start | bytes 589832 | tf_op jit(solution)/shard_map/ppermute | solution.py:290
  13.4 4.2 %collective-permute-done.9.refs_8_ = bf16[192,512]{1,0:T(8,128)(2,1)S(1)} collective-permute-done((bf16[192,512]{1,0:T(8,128)(2,1)S(1)}, bf16[192,512]{1,0:T(8,128)(2,1)S(1)}, u32[]{:S(2)}, u32[]{:S(2)}) %collective-permute-start.9) | collective-permute-done | bytes 196640 | tf_op jit(solution)/shard_map/ppermute | solution.py:290
  19.7 2.2 %collective-permute-start.2 = (bf16[48,512]{1,0:T(8,128)(2,1)}, bf16[48,512]{1,0:T(8,128)(2,1)S(1)}, u32[]{:S(2)}, u32[]{:S(2)}) collective-permute-start(bf16[48,512]{1,0:T(8,128)(2,1)} %get-tuple-element.42), channel_id=1, source_target_pairs={{0,3},{1,4},{2,5},{3,6},{4,7},{5,8},{6,9},{7,10},{8,11},{9,12},{10... | collective-permute-start | bytes 147464 | tf_op jit(solution)/shard_map/ppermute | solution.py:290
  23.5 1.7 %collective-permute-start.4 = (bf16[48,512]{1,0:T(8,128)(2,1)}, bf16[48,512]{1,0:T(8,128)(2,1)S(1)}, u32[]{:S(2)}, u32[]{:S(2)}) collective-permute-start(bf16[48,512]{1,0:T(8,128)(2,1)} %get-tuple-element.44), channel_id=1, source_target_pairs={{0,14},{1,15},{2,0},{3,1},{4,2},{5,3},{6,4},{7,5},{8,6},{9,7},{10,... | collective-permute-start | bytes 147464 | tf_op jit(solution)/shard_map/ppermute | solution.py:290
  25.2 2.9 %collective-permute-start.5 = (bf16[48,512]{1,0:T(8,128)(2,1)}, bf16[48,512]{1,0:T(8,128)(2,1)S(1)}, u32[]{:S(2)}, u32[]{:S(2)}) collective-permute-start(bf16[48,512]{1,0:T(8,128)(2,1)} %get-tuple-element.45), channel_id=1, source_target_pairs={{0,13},{1,14},{2,15},{3,0},{4,1},{5,2},{6,3},{7,4},{8,5},{9,6},{10... | collective-permute-start | bytes 147464 | tf_op jit(solution)/shard_map/ppermute | solution.py:290
  28.2 11.0 %edge_local.1.local_ref = bf16[3072,512]{1,0:T(8,128)(2,1)} custom-call(s32[12,1,256]{2,1,0:T(1,128)} %bitcast.103, bf16[3072,512]{1,0:T(8,128)(2,1)} %refs_0_.1, bf16[256,512]{1,0:T(8,128)(2,1)} %refs_4_.1, bf16[1536,512]{1,0:T(8,128)(2,1)} %refs_7_.3, bf16[1536,512]{1,0:T(8,128)(2,1)} %refs_7_.3), custom_call_target="tpu_custom_call" | custom-call | flops 2415919104 | bytes 6291456 | tf_op jit(solution)/shard_map/edge_local/pallas_call | solution.py:374
  40.7 20.7 %forward.1 = (bf16[768,512]{1,0:T(8,128)(2,1)}, bf16[3072,512]{1,0:T(8,128)(2,1)}, bf16[3072,512]{1,0:T(8,128)(2,1)}, bf16[3072,512]{1,0:T(8,128)(2,1)}, f32[307...) custom-call(s32[1]{0:T(128)} %bitcast.me_ref, ...), custom_call_target="tpu_custom_call" | custom-call | tf_op jit(solution)/shard_map/forward/pallas_call | solution.py:389
  61.3 17.9 %backward_slots.1 = (bf16[3072,512]{1,0:T(8,128)(2,1)}, f32[512,512]{1,0:T(8,128)}, bf16[2,4,80,512]{3,2,1,0:T(8,128)(2,1)}, bf16[2,4,80,512]{3,2,1,0:T(8,128)(2...) custom-call(s32[1]{0:T(128)} %bitcast.me_ref, ...), custom_call_target="tpu_custom_call" | custom-call | flops 6442450944 | bytes 12582912 | tf_op jit(solution)/shard_map/backward_slots/pallas_call | solution.py:436
  79.2 5.0 %collective-permute-start.17 = (bf16[2,4,80,512]{3,2,1,0:T(8,128)(2,1)}, bf16[2,4,80,512]{3,2,1,0:T(8,128)(2,1)S(1)}, u32[]{:S(2)}, u32[]{:S(2)}) collective-permute-start(bf16[2,4,80,512]{3,2,1,0:T(8,128)(2,1)} %get-tuple-element.61), channel_id=1, source_target_pairs={{0,1},{1,0},{2,3},{3,2},{4,5},{5,4},{6,7},{7,6},{8,9},{9,8},{10,11... | collective-permute-start | bytes 1966088 | tf_op jit(solution)/shard_map/ppermute | solution.py:290
  84.3 13.5 %backward_edges.1 = (bf16[3072,512]{1,0:T(8,128)(2,1)}, bf16[256,512]{1,0:T(8,128)(2,1)}, bf16[2,4,96,512]{3,2,1,0:T(8,128)(2,1)}, bf16[2,4,96,512]{3,2,1,0:T(8,128)(2,1)}) custom-call(s32[1]{0:T(128)} %bitcast.me_ref, s32[1]{0:T(128)S(6)} %copy.26.count_ref, s32[12,1,256]{2,1,0:T(1,128)} %bitcast.106, bf16[3072,512]{1,0:T(8,128)(2,1)} %refs_0_.1, ...), custom_call_target="tpu_custom_call" | custom-call | flops 4831838208 | bytes 9437184 | tf_op jit(solution)/shard_map/backward_edges/pallas_call | solution.py:465
  97.8 1.7 %collective-permute-start.22 = (bf16[2,4,96,512]{3,2,1,0:T(8,128)(2,1)}, bf16[2,4,96,512]{3,2,1,0:T(8,128)(2,1)S(1)}, u32[]{:S(2)}, u32[]{:S(2)}) collective-permute-start(bf16[2,4,96,512]{3,2,1,0:T(8,128)(2,1)} %get-tuple-element.68), channel_id=1, source_target_pairs={{0,1},{1,0},{2,3},{3,2},{4,5},{5,4},{6,7},{7,6},{8,9},{9,8},{10,11... | collective-permute-start | bytes 2359304 | tf_op jit(solution)/shard_map/ppermute | solution.py:290
  100.3 10.1 %collective-permute-done.18 = bf16[4,80,512]{2,1,0:T(8,128)(2,1)S(1)} collective-permute-done((bf16[4,80,512]{2,1,0:T(8,128)(2,1)S(1)}, bf16[4,80,512]{2,1,0:T(8,128)(2,1)S(1)}, u32[]{:S(2)}, u32[]{:S(2)}) %collective-permute-start.18) | collective-permute-done | bytes 327712 | tf_op jit(solution)/shard_map/ppermute | solution.py:290
  112.1 3.4 %collective-permute-start.21 = (bf16[80,512]{1,0:T(8,128)(2,1)S(1)}, bf16[80,512]{1,0:T(8,128)(2,1)S(1)}, u32[]{:S(2)}, u32[]{:S(2)}) collective-permute-start(bf16[80,512]{1,0:T(8,128)(2,1)S(1)} %get-tuple-element.84), channel_id=1, source_target_pairs={{0,12},{1,13},{2,14},{3,15},{4,8},{5,9},{6,10},{7,11},{8,4},{9,5},... | collective-permute-start | bytes 245768 | tf_op jit(solution)/shard_map/ppermute | solution.py:290
  117.7 4.1 %collective-permute-done.21 = bf16[80,512]{1,0:T(8,128)(2,1)S(1)} collective-permute-done((bf16[80,512]{1,0:T(8,128)(2,1)S(1)}, bf16[80,512]{1,0:T(8,128)(2,1)S(1)}, u32[]{:S(2)}, u32[]{:S(2)}) %collective-permute-start.21) | collective-permute-done | bytes 81952 | tf_op jit(solution)/shard_map/ppermute | solution.py:290
  121.8 1.9 %collective-permute-start.23 = (bf16[4,96,512]{2,1,0:T(8,128)(2,1)S(1)}, bf16[4,96,512]{2,1,0:T(8,128)(2,1)S(1)}, u32[]{:S(2)}, u32[]{:S(2)}) collective-permute-start(bf16[4,96,512]{2,1,0:T(8,128)(2,1)S(1)} %get-tuple-element.74), channel_id=1, source_target_pairs={{0,2},{1,3},{2,0},{3,1},{4,6},{5,7},{6,4},{7,5},{8,10},{9,11},{10,... | collective-permute-start | bytes 1179656 | tf_op jit(solution)/shard_map/ppermute | solution.py:290
  125.7 3.8 %scatter_lists.1 = bf16[2048,512]{1,0:T(8,128)(2,1)} custom-call(s32[1]{0:T(128)} %bitcast.me_ref, s32[16,48]{1,0:T(8,128)} %bitcast.108, bf16[48,512]{1,0:T(8,128)(2,1)} %get-tuple-element.53.refs_0_, bf16[48,512]{1,0:T(8,128)(2,1)} %copy-done.12, bf16[48,512]{1,0:T(8,128)(2,1)} %copy-done.13, bf16[48,512]{1,0:T(8,128)(2,1)} %copy-done.14, ...), custom_call_target="tpu_custom_call" | custom-call | tf_op jit(solution)/shard_map/scatter_lists/pallas_call | solution.py:504
  129.6 2.1 %collective-permute-start.29 = (bf16[96,512]{1,0:T(8,128)(2,1)S(1)}, bf16[96,512]{1,0:T(8,128)(2,1)S(1)}, u32[]{:S(2)}, u32[]{:S(2)}) collective-permute-start(bf16[96,512]{1,0:T(8,128)(2,1)S(1)} %get-tuple-element.77), channel_id=1, source_target_pairs={{0,4},{1,5},{2,6},{3,7},{4,0},{5,1},{6,2},{7,3},{8,12},{9,13},{10,... | collective-permute-start | bytes 294920 | tf_op jit(solution)/shard_map/ppermute | solution.py:290
  133.3 2.9 %collective-permute-start.24 = (bf16[96,512]{1,0:T(8,128)(2,1)S(1)}, bf16[96,512]{1,0:T(8,128)(2,1)S(1)}, u32[]{:S(2)}, u32[]{:S(2)}) collective-permute-start(bf16[96,512]{1,0:T(8,128)(2,1)S(1)} %get-tuple-element.80), channel_id=1, source_target_pairs={{0,4},{1,5},{2,6},{3,7},{4,0},{5,1},{6,2},{7,3},{8,12},{9,13},{10,... | collective-permute-start | bytes 294920 | tf_op jit(solution)/shard_map/ppermute | solution.py:290
  136.2 1.5 %collective-permute-start.26 = (bf16[96,512]{1,0:T(8,128)(2,1)S(1)}, bf16[96,512]{1,0:T(8,128)(2,1)S(1)}, u32[]{:S(2)}, u32[]{:S(2)}) collective-permute-start(bf16[96,512]{1,0:T(8,128)(2,1)S(1)} %get-tuple-element.81), channel_id=1, source_target_pairs={{0,12},{1,13},{2,14},{3,15},{4,8},{5,9},{6,10},{7,11},{8,4},{9,5},... | collective-permute-start | bytes 294920 | tf_op jit(solution)/shard_map/ppermute | solution.py:290
  138.9 8.6 %collective-permute-done.31 = bf16[96,512]{1,0:T(8,128)(2,1)S(1)} collective-permute-done((bf16[96,512]{1,0:T(8,128)(2,1)S(1)}, bf16[96,512]{1,0:T(8,128)(2,1)S(1)}, u32[]{:S(2)}, u32[]{:S(2)}) %collective-permute-start.31) | collective-permute-done | bytes 98336 | tf_op jit(solution)/shard_map/ppermute | solution.py:290
  148.8 2.5 %collective-permute-done.26 = bf16[96,512]{1,0:T(8,128)(2,1)S(1)} collective-permute-done((bf16[96,512]{1,0:T(8,128)(2,1)S(1)}, bf16[96,512]{1,0:T(8,128)(2,1)S(1)}, u32[]{:S(2)}, u32[]{:S(2)}) %collective-permute-start.26) | collective-permute-done | bytes 98336 | tf_op jit(solution)/shard_map/ppermute | solution.py:290
  (114 shorter events, 18.9 us)
Async XLA Ops:
  17.6 22.3 %collective-permute-start.10 = (bf16[384,512]{1,0:T(8,128)(2,1)S(1)}, bf16[384,512]{1,0:T(8,128)(2,1)S(1)}, u32[]{:S(2)}, u32[]{:S(2)}) collective-permute-start(bf16[384,512]{1,0:T(8,128)(2,1)S(1)} %constant_dynamic-update-slice_fusion.4), channel_id=1, source_target_pairs={{0,1},{1,0},{2,3},{3,2},{4,5},{5,4},{6,7},{7,6},{8,9},{9,8},{10,11... | collective-permute-start | bytes 1179656 | tf_op jit(solution)/shard_map/ppermute | solution.py:290
  18.1 7.1 %collective-permute-start.1 = (bf16[48,512]{1,0:T(8,128)(2,1)}, bf16[48,512]{1,0:T(8,128)(2,1)S(1)}, u32[]{:S(2)}, u32[]{:S(2)}) collective-permute-start(bf16[48,512]{1,0:T(8,128)(2,1)} %get-tuple-element.41), channel_id=1, source_target_pairs={{0,2},{1,3},{2,4},{3,5},{4,6},{5,7},{6,8},{7,9},{8,10},{9,11},{10,... | collective-permute-start | bytes 147464 | tf_op jit(solution)/shard_map/ppermute | solution.py:290
  19.7 20.1 %collective-permute-start.2 = (bf16[48,512]{1,0:T(8,128)(2,1)}, bf16[48,512]{1,0:T(8,128)(2,1)S(1)}, u32[]{:S(2)}, u32[]{:S(2)}) collective-permute-start(bf16[48,512]{1,0:T(8,128)(2,1)} %get-tuple-element.42), channel_id=1, source_target_pairs={{0,3},{1,4},{2,5},{3,6},{4,7},{5,8},{6,9},{7,10},{8,11},{9,12},{10... | collective-permute-start | bytes 147464 | tf_op jit(solution)/shard_map/ppermute | solution.py:290
  21.9 18.0 %collective-permute-start.3 = (bf16[48,512]{1,0:T(8,128)(2,1)}, bf16[48,512]{1,0:T(8,128)(2,1)S(1)}, u32[]{:S(2)}, u32[]{:S(2)}) collective-permute-start(bf16[48,512]{1,0:T(8,128)(2,1)} %get-tuple-element.43), channel_id=1, source_target_pairs={{0,15},{1,0},{2,1},{3,2},{4,3},{5,4},{6,5},{7,6},{8,7},{9,8},{10,9... | collective-permute-start | bytes 147464 | tf_op jit(solution)/shard_map/ppermute | solution.py:290
  23.5 16.3 %collective-permute-start.4 = (bf16[48,512]{1,0:T(8,128)(2,1)}, bf16[48,512]{1,0:T(8,128)(2,1)S(1)}, u32[]{:S(2)}, u32[]{:S(2)}) collective-permute-start(bf16[48,512]{1,0:T(8,128)(2,1)} %get-tuple-element.44), channel_id=1, source_target_pairs={{0,14},{1,15},{2,0},{3,1},{4,2},{5,3},{6,4},{7,5},{8,6},{9,7},{10,... | collective-permute-start | bytes 147464 | tf_op jit(solution)/shard_map/ppermute | solution.py:290
  25.2 14.6 %collective-permute-start.5 = (bf16[48,512]{1,0:T(8,128)(2,1)}, bf16[48,512]{1,0:T(8,128)(2,1)S(1)}, u32[]{:S(2)}, u32[]{:S(2)}) collective-permute-start(bf16[48,512]{1,0:T(8,128)(2,1)} %get-tuple-element.45), channel_id=1, source_target_pairs={{0,13},{1,14},{2,15},{3,0},{4,1},{5,2},{6,3},{7,4},{8,5},{9,6},{10... | collective-permute-start | bytes 147464 | tf_op jit(solution)/shard_map/ppermute | solution.py:290
  79.2 20.3 %collective-permute-start.17 = (bf16[2,4,80,512]{3,2,1,0:T(8,128)(2,1)}, bf16[2,4,80,512]{3,2,1,0:T(8,128)(2,1)S(1)}, u32[]{:S(2)}, u32[]{:S(2)}) collective-permute-start(bf16[2,4,80,512]{3,2,1,0:T(8,128)(2,1)} %get-tuple-element.61), channel_id=1, source_target_pairs={{0,1},{1,0},{2,3},{3,2},{4,5},{5,4},{6,7},{7,6},{8,9},{9,8},{10,11... | collective-permute-start | bytes 1966088 | tf_op jit(solution)/shard_map/ppermute | solution.py:290
  84.2 15.8 %collective-permute-start.27 = (bf16[2,4,96,512]{3,2,1,0:T(8,128)(2,1)S(1)}, bf16[2,4,96,512]{3,2,1,0:T(8,128)(2,1)S(1)}, u32[]{:S(2)}, u32[]{:S(2)}) collective-permute-start(bf16[2,4,96,512]{3,2,1,0:T(8,128)(2,1)S(1)} %copy-done.18), channel_id=1, source_target_pairs={{0,1},{1,0},{2,3},{3,2},{4,5},{5,4},{6,7},{7,6},{8,9},{9,8},{10,11... | collective-permute-start | bytes 2359304 | tf_op jit(solution)/shard_map/ppermute | solution.py:290
  97.8 14.3 %collective-permute-start.22 = (bf16[2,4,96,512]{3,2,1,0:T(8,128)(2,1)}, bf16[2,4,96,512]{3,2,1,0:T(8,128)(2,1)S(1)}, u32[]{:S(2)}, u32[]{:S(2)}) collective-permute-start(bf16[2,4,96,512]{3,2,1,0:T(8,128)(2,1)} %get-tuple-element.68), channel_id=1, source_target_pairs={{0,1},{1,0},{2,3},{3,2},{4,5},{5,4},{6,7},{7,6},{8,9},{9,8},{10,11... | collective-permute-start | bytes 2359304 | tf_op jit(solution)/shard_map/ppermute | solution.py:290
  99.7 10.6 %collective-permute-start.18 = (bf16[4,80,512]{2,1,0:T(8,128)(2,1)S(1)}, bf16[4,80,512]{2,1,0:T(8,128)(2,1)S(1)}, u32[]{:S(2)}, u32[]{:S(2)}) collective-permute-start(bf16[4,80,512]{2,1,0:T(8,128)(2,1)S(1)} %get-tuple-element.76), channel_id=1, source_target_pairs={{0,2},{1,3},{2,0},{3,1},{4,6},{5,7},{6,4},{7,5},{8,10},{9,11},{10,... | collective-permute-start | bytes 983048 | tf_op jit(solution)/shard_map/ppermute | solution.py:290
  99.8 12.1 %collective-permute-start.11 = (bf16[48,512]{1,0:T(8,128)(2,1)S(1)}, bf16[48,512]{1,0:T(8,128)(2,1)S(1)}, u32[]{:S(2)}, u32[]{:S(2)}) collective-permute-start(bf16[48,512]{1,0:T(8,128)(2,1)S(1)} %copy-done.24), channel_id=1, source_target_pairs={{0,15},{1,0},{2,1},{3,2},{4,3},{5,4},{6,5},{7,6},{8,7},{9,8},{10,9... | collective-permute-start | bytes 147464 | tf_op jit(solution)/shard_map/ppermute | solution.py:290
  99.9 12.1 %collective-permute-start.12 = (bf16[48,512]{1,0:T(8,128)(2,1)S(1)}, bf16[48,512]{1,0:T(8,128)(2,1)S(1)}, u32[]{:S(2)}, u32[]{:S(2)}) collective-permute-start(bf16[48,512]{1,0:T(8,128)(2,1)S(1)} %copy-done.23), channel_id=1, source_target_pairs={{0,14},{1,15},{2,0},{3,1},{4,2},{5,3},{6,4},{7,5},{8,6},{9,7},{10,... | collective-permute-start | bytes 147464 | tf_op jit(solution)/shard_map/ppermute | solution.py:290
  100.0 15.7 %collective-permute-start.13 = (bf16[48,512]{1,0:T(8,128)(2,1)S(1)}, bf16[48,512]{1,0:T(8,128)(2,1)S(1)}, u32[]{:S(2)}, u32[]{:S(2)}) collective-permute-start(bf16[48,512]{1,0:T(8,128)(2,1)S(1)} %copy-done.22), channel_id=1, source_target_pairs={{0,13},{1,14},{2,15},{3,0},{4,1},{5,2},{6,3},{7,4},{8,5},{9,6},{10... | collective-permute-start | bytes 147464 | tf_op jit(solution)/shard_map/ppermute | solution.py:290
  110.4 19.1 %collective-permute-start.28 = (bf16[4,96,512]{2,1,0:T(8,128)(2,1)S(1)}, bf16[4,96,512]{2,1,0:T(8,128)(2,1)S(1)}, u32[]{:S(2)}, u32[]{:S(2)}) collective-permute-start(bf16[4,96,512]{2,1,0:T(8,128)(2,1)S(1)} %get-tuple-element.72), channel_id=1, source_target_pairs={{0,2},{1,3},{2,0},{3,1},{4,6},{5,7},{6,4},{7,5},{8,10},{9,11},{10,... | collective-permute-start | bytes 1179656 | tf_op jit(solution)/shard_map/ppermute | solution.py:290
  112.1 9.7 %collective-permute-start.21 = (bf16[80,512]{1,0:T(8,128)(2,1)S(1)}, bf16[80,512]{1,0:T(8,128)(2,1)S(1)}, u32[]{:S(2)}, u32[]{:S(2)}) collective-permute-start(bf16[80,512]{1,0:T(8,128)(2,1)S(1)} %get-tuple-element.84), channel_id=1, source_target_pairs={{0,12},{1,13},{2,14},{3,15},{4,8},{5,9},{6,10},{7,11},{8,4},{9,5},... | collective-permute-start | bytes 245768 | tf_op jit(solution)/shard_map/ppermute | solution.py:290
  115.7 9.3 %collective-permute-start.14 = (bf16[48,512]{1,0:T(8,128)(2,1)S(1)}, bf16[48,512]{1,0:T(8,128)(2,1)S(1)}, u32[]{:S(2)}, u32[]{:S(2)}) collective-permute-start(bf16[48,512]{1,0:T(8,128)(2,1)S(1)} %copy-done.21), channel_id=1, source_target_pairs={{0,1},{1,2},{2,3},{3,4},{4,5},{5,6},{6,7},{7,8},{8,9},{9,10},{10,1... | collective-permute-start | bytes 147464 | tf_op jit(solution)/shard_map/ppermute | solution.py:290
  117.0 8.1 %collective-permute-start.15 = (bf16[48,512]{1,0:T(8,128)(2,1)S(1)}, bf16[48,512]{1,0:T(8,128)(2,1)S(1)}, u32[]{:S(2)}, u32[]{:S(2)}) collective-permute-start(bf16[48,512]{1,0:T(8,128)(2,1)S(1)} %copy-done.20), channel_id=1, source_target_pairs={{0,2},{1,3},{2,4},{3,5},{4,6},{5,7},{6,8},{7,9},{8,10},{9,11},{10,... | collective-permute-start | bytes 147464 | tf_op jit(solution)/shard_map/ppermute | solution.py:290
  117.7 7.3 %collective-permute-start.16 = (bf16[48,512]{1,0:T(8,128)(2,1)S(1)}, bf16[48,512]{1,0:T(8,128)(2,1)S(1)}, u32[]{:S(2)}, u32[]{:S(2)}) collective-permute-start(bf16[48,512]{1,0:T(8,128)(2,1)S(1)} %copy-done.19), channel_id=1, source_target_pairs={{0,3},{1,4},{2,5},{3,6},{4,7},{5,8},{6,9},{7,10},{8,11},{9,12},{10... | collective-permute-start | bytes 147464 | tf_op jit(solution)/shard_map/ppermute | solution.py:290
  121.8 11.4 %collective-permute-start.23 = (bf16[4,96,512]{2,1,0:T(8,128)(2,1)S(1)}, bf16[4,96,512]{2,1,0:T(8,128)(2,1)S(1)}, u32[]{:S(2)}, u32[]{:S(2)}) collective-permute-start(bf16[4,96,512]{2,1,0:T(8,128)(2,1)S(1)} %get-tuple-element.74), channel_id=1, source_target_pairs={{0,2},{1,3},{2,0},{3,1},{4,6},{5,7},{6,4},{7,5},{8,10},{9,11},{10,... | collective-permute-start | bytes 1179656 | tf_op jit(solution)/shard_map/ppermute | solution.py:290
  131.7 7.1 %collective-permute-start.30 = (bf16[96,512]{1,0:T(8,128)(2,1)S(1)}, bf16[96,512]{1,0:T(8,128)(2,1)S(1)}, u32[]{:S(2)}, u32[]{:S(2)}) collective-permute-start(bf16[96,512]{1,0:T(8,128)(2,1)S(1)} %get-tuple-element.79), channel_id=1, source_target_pairs={{0,8},{1,9},{2,10},{3,11},{4,12},{5,13},{6,14},{7,15},{8,0},{9,1},... | collective-permute-start | bytes 294920 | tf_op jit(solution)/shard_map/ppermute | solution.py:290
  131.7 15.7 %collective-permute-start.31 = (bf16[96,512]{1,0:T(8,128)(2,1)S(1)}, bf16[96,512]{1,0:T(8,128)(2,1)S(1)}, u32[]{:S(2)}, u32[]{:S(2)}) collective-permute-start(bf16[96,512]{1,0:T(8,128)(2,1)S(1)} %get-tuple-element.78), channel_id=1, source_target_pairs={{0,12},{1,13},{2,14},{3,15},{4,8},{5,9},{6,10},{7,11},{8,4},{9,5},... | collective-permute-start | bytes 294920 | tf_op jit(solution)/shard_map/ppermute | solution.py:290
  133.3 15.5 %collective-permute-start.24 = (bf16[96,512]{1,0:T(8,128)(2,1)S(1)}, bf16[96,512]{1,0:T(8,128)(2,1)S(1)}, u32[]{:S(2)}, u32[]{:S(2)}) collective-permute-start(bf16[96,512]{1,0:T(8,128)(2,1)S(1)} %get-tuple-element.80), channel_id=1, source_target_pairs={{0,4},{1,5},{2,6},{3,7},{4,0},{5,1},{6,2},{7,3},{8,12},{9,13},{10,... | collective-permute-start | bytes 294920 | tf_op jit(solution)/shard_map/ppermute | solution.py:290
  136.2 12.6 %collective-permute-start.25 = (bf16[96,512]{1,0:T(8,128)(2,1)S(1)}, bf16[96,512]{1,0:T(8,128)(2,1)S(1)}, u32[]{:S(2)}, u32[]{:S(2)}) collective-permute-start(bf16[96,512]{1,0:T(8,128)(2,1)S(1)} %get-tuple-element.82), channel_id=1, source_target_pairs={{0,8},{1,9},{2,10},{3,11},{4,12},{5,13},{6,14},{7,15},{8,0},{9,1},... | collective-permute-start | bytes 294920 | tf_op jit(solution)/shard_map/ppermute | solution.py:290
  136.2 15.0 %collective-permute-start.26 = (bf16[96,512]{1,0:T(8,128)(2,1)S(1)}, bf16[96,512]{1,0:T(8,128)(2,1)S(1)}, u32[]{:S(2)}, u32[]{:S(2)}) collective-permute-start(bf16[96,512]{1,0:T(8,128)(2,1)S(1)} %get-tuple-element.81), channel_id=1, source_target_pairs={{0,12},{1,13},{2,14},{3,15},{4,8},{5,9},{6,10},{7,11},{8,4},{9,5},... | collective-permute-start | bytes 294920 | tf_op jit(solution)/shard_map/ppermute | solution.py:290
  (33 other events, 333.3 us)

commit v2 on v1

--- a/solution.py
+++ b/solution.py
@@ -8,6 +8,9 @@
 from jax.sharding import PartitionSpec as P
 
 TILE = 256
+STEP = 1024
+SUB = 512
+LANES = 128
 NEAR = 3
 SHIFTS = (0, 1, 2, 3, -1, -2, -3)
 BF16 = jnp.bfloat16
@@ -47,14 +50,19 @@
 
 def as_column(row):
     count = row.shape[1]
-    down = lax.broadcasted_iota(jnp.int32, (count, count), 0)
-    along = lax.broadcasted_iota(jnp.int32, (count, count), 1)
-    picked = jnp.where(down == along, row.astype(F32), 0.0)
-    return jnp.sum(picked, axis=1, keepdims=True).astype(jnp.int32)
-
-
-def hot_rows(row, width):
-    column = as_column(row)
+    block = min(count, LANES)
+    down = lax.broadcasted_iota(jnp.int32, (block, block), 0)
+    along = lax.broadcasted_iota(jnp.int32, (block, block), 1)
+    columns = []
+    for start in range(0, count, block):
+        piece = row[:, start : start + block].astype(F32)
+        picked = jnp.where(down == along, piece, 0.0)
+        columns.append(jnp.sum(picked, axis=1, keepdims=True))
+    return jnp.concatenate(columns, axis=0).astype(jnp.int32)
+
+
+def hot_rows(row, width, first=0):
+    column = as_column(row) - first
     along = lax.broadcasted_iota(jnp.int32, (row.shape[1], width), 1)
     return (column == along).astype(F32).astype(BF16)
 
@@ -64,44 +72,72 @@
     return (row == down).astype(F32).astype(BF16)
 
 
-def list_hots(me, rows_ref, grid_count):
+def live_only(row, first, count):
+    place = first + lax.broadcasted_iota(jnp.int32, row.shape, 1)
+    return jnp.where(place < count, row, -1)
+
+
+def list_hots(me, rows_ref, grid_count, first):
     peers, cap = rows_ref.shape
     pieces = []
     for shift in SHIFTS:
         target = lax.rem(me + shift + peers, peers)
-        pieces.append(hot_rows(rows_ref[pl.ds(target, 1), :], grid_count))
+        pieces.append(hot_rows(rows_ref[pl.ds(target, 1), :], grid_count, first))
     peer = lax.broadcasted_iota(jnp.int32, (peers, cap), 0)
     ahead = lax.rem(peer - me + peers, peers)
     apart = jnp.minimum(ahead, peers - ahead)
     far = jnp.max(jnp.where(apart > NEAR, rows_ref[...].astype(F32), -1.0), axis=0, keepdims=True)
-    pieces.append(hot_rows(far.astype(jnp.int32), grid_count))
+    pieces.append(hot_rows(far.astype(jnp.int32), grid_count, first))
     return jnp.concatenate(pieces, axis=0)
 
 
-def gather_kernel(me_ref, rows_ref, grid_ref, *out_refs):
+def gather_kernel(me_ref, rows_ref, grid_ref, *refs):
+    out_refs, total = refs[:-1], refs[-1]
     cap = rows_ref.shape[1]
-    hots = list_hots(me_ref[0], rows_ref, grid_ref.shape[0])
-    picked = dot(hots, grid_ref[...]).astype(BF16)
-    for place, out_ref in enumerate(out_refs):
-        out_ref[...] = picked[place * cap : (place + 1) * cap]
-
-
-def scatter_kernel(me_ref, rows_ref, *refs):
-    list_refs, out_ref = refs[:-1], refs[-1]
-    hots = list_hots(me_ref[0], rows_ref, out_ref.shape[0])
-    values = jnp.concatenate([ref[...].astype(BF16) for ref in list_refs], axis=0)
+    step = pl.program_id(0)
+    part = grid_ref.shape[0]
+
+    @pl.when(step == 0)
+    def _():
+        total[...] = jnp.zeros_like(total)
+
+    total[...] += dot(list_hots(me_ref[0], rows_ref, part, step * part), grid_ref[...])
+
+    @pl.when(step == pl.num_programs(0) - 1)
+    def _():
+        for place, out_ref in enumerate(out_refs):
+            out_ref[...] = total[place * cap : (place + 1) * cap, :].astype(BF16)
+
+
+def scatter_kernel(skip, me_ref, rows_ref, *refs):
+    list_refs, far_refs, out_ref = refs[:7], refs[7:-1], refs[-1]
+    part = out_ref.shape[0]
+    cap = rows_ref.shape[1]
+    hots = list_hots(me_ref[0], rows_ref, part, pl.program_id(0) * part)
+    far = far_refs[0][skip:, :].astype(F32)
+    for ref in far_refs[1:]:
+        far = far + ref[skip:, :].astype(F32)
+    values = jnp.concatenate([ref[...] for ref in list_refs] + [far.astype(BF16)], axis=0)
     out_ref[...] = contract_rows(hots, values).astype(BF16)
 
 
-def local_kernel(dst_ref, edge_ref, mesh_ref, w_edge_ref, w_receiver_ref, out_ref, mesh_proj):
+def halves_of(ref):
+    rows = ref.shape[-1] if len(ref.shape) == 3 else ref.shape[0]
+    return [(start, slice(start, start + SUB)) for start in range(0, rows, SUB)]
+
+
+def local_kernel(dst_ref, edge_ref, mesh_ref, w_edge_ref, w_receiver_ref, *refs):
+    out_ref, mesh_proj = refs[-2:]
+
     @pl.when(pl.program_id(0) == 0)
     def _():
         mesh_proj[...] = dot(mesh_ref[...], w_receiver_ref[...]).astype(BF16)
 
-    onehot = hot_rows(dst_ref[0], mesh_ref.shape[0])
-    out_ref[...] = (
-        dot(edge_ref[...], w_edge_ref[...]) + dot(onehot, mesh_proj[...])
-    ).astype(BF16)
+    for start, part in halves_of(edge_ref):
+        onehot = hot_rows(dst_ref[0, :, part], mesh_ref.shape[0])
+        out_ref[part, :] = (
+            dot(edge_ref[part, :], w_edge_ref[...]) + dot(onehot, mesh_proj[...])
+        ).astype(BF16)
 
 
 def split_out(me, peers, send_ref, keep_ref, parts):
@@ -162,19 +198,27 @@
             owner = lax.rem(me - shift + peers, peers)
             place(owner, rows[spot * cap : (spot + 1) * cap], projected[spot * cap : (spot + 1) * cap])
 
-    @pl.when(step < count_ref[0])
-    def _():
-        onehot = hot_rows(src_ref[0], slot_proj.shape[0])
-        pre = local_ref[...].astype(F32) + dot(onehot, slot_proj[...])
-        hidden, slope = silu_and_slope(pre)
-        hidden = hidden.astype(BF16)
-        hidden_ref[...] = hidden
-        slope_ref[...] = slope.astype(BF16)
-        normed, inverse = layer_norm(dot(hidden, w_out_ref[...]))
-        norm_ref[...] = normed.astype(BF16)
-        inverse_ref[...] = inverse
-        edge_new = (edge_ref[...].astype(F32) + normed).astype(BF16)
-        aggregate[...] += dot(hot_columns(dst_ref[0], aggregate.shape[0]), edge_new)
+    @pl.when(step * STEP < count_ref[0] * TILE)
+    def _():
+        parts = halves_of(edge_ref)
+        pres = []
+        for start, part in parts:
+            onehot = hot_rows(src_ref[0, :, part], slot_proj.shape[0])
+            pres.append(local_ref[part, :].astype(F32) + dot(onehot, slot_proj[...]))
+        projs = []
+        for (start, part), pre in zip(parts, pres):
+            hidden, slope = silu_and_slope(pre)
+            hidden = hidden.astype(BF16)
+            hidden_ref[part, :] = hidden
+            slope_ref[part, :] = slope.astype(BF16)
+            projs.append(dot(hidden, w_out_ref[...]))
+        for (start, part), proj in zip(parts, projs):
+            normed, inverse = layer_norm(proj)
+            norm_ref[part, :] = normed.astype(BF16)
+            inverse_ref[part, :] = inverse
+            edge_new = (edge_ref[part, :].astype(F32) + normed).astype(BF16)
+            receivers = live_only(dst_ref[0, :, part], step * STEP + start, count_ref[0] * TILE)
+            aggregate[...] += dot(hot_columns(receivers, aggregate.shape[0]), edge_new)
 
     @pl.when(step == pl.num_programs(0) - 1)
     def _():
@@ -215,15 +259,25 @@
         slot_sum[...] = jnp.zeros_like(slot_sum)
         grad_out[...] = jnp.zeros_like(grad_out)
 
-    @pl.when(step < count_ref[0])
-    def _():
-        onehot = hot_rows(dst_ref[0], d_aggregate_ref.shape[0])
-        upstream = dot(onehot, d_aggregate_ref[...])
-        d_proj = norm_back(norm_ref[...].astype(F32), inverse_ref[...], upstream).astype(BF16)
-        grad_out[...] += contract_rows(hidden_ref[...], d_proj)
-        d_pre = (contract_cols(d_proj, w_out_ref[...]) * slope_ref[...].astype(F32)).astype(BF16)
-        d_pre_ref[...] = d_pre
-        slot_sum[...] += dot(hot_columns(src_ref[0], slot_sum.shape[0]), d_pre)
+    @pl.when(step * STEP < count_ref[0] * TILE)
+    def _():
+        parts = halves_of(hidden_ref)
+        upstreams = []
+        for start, part in parts:
+            receivers = live_only(dst_ref[0, :, part], step * STEP + start, count_ref[0] * TILE)
+            onehot = hot_rows(receivers, d_aggregate_ref.shape[0])
+            upstreams.append(dot(onehot, d_aggregate_ref[...]))
+        d_projs = []
+        d_hiddens = []
+        for (start, part), upstream in zip(parts, upstreams):
+            d_proj = norm_back(norm_ref[part, :].astype(F32), inverse_ref[part, :], upstream).astype(BF16)
+            d_projs.append(d_proj)
+            d_hiddens.append(contract_cols(d_proj, w_out_ref[...]))
+        for (start, part), d_proj, d_hidden in zip(parts, d_projs, d_hiddens):
+            grad_out[...] += contract_rows(hidden_ref[part, :], d_proj)
+            d_pre = (d_hidden * slope_ref[part, :].astype(F32)).astype(BF16)
+            d_pre_ref[part, :] = d_pre
+            slot_sum[...] += dot(hot_columns(src_ref[0, :, part], slot_sum.shape[0]), d_pre)
 
     @pl.when(step == pl.num_programs(0) - 1)
     def _():
@@ -256,16 +310,18 @@
         grad_in[:width, :] = jnp.zeros((width, grad_in.shape[1]), F32)
         mesh_sum[...] = jnp.zeros_like(mesh_sum)
 
-    @pl.when(step < count_ref[0])
-    def _():
-        d_pre = d_pre_ref[...]
-        onehot = hot_rows(dst_ref[0], d_aggregate_ref.shape[0])
-        upstream = dot(onehot, d_aggregate_ref[...])
-        edge_grad_ref[...] = (upstream + contract_cols(d_pre, w_edge_ref[...])).astype(BF16)
-        grad_in[:width, :] += contract_rows(edge_ref[...], d_pre)
-        mesh_sum[...] += dot(hot_columns(dst_ref[0], mesh_sum.shape[0]), d_pre)
-
-    @pl.when(step >= count_ref[0])
+    @pl.when(step * STEP < count_ref[0] * TILE)
+    def _():
+        for start, part in halves_of(edge_ref):
+            d_pre = d_pre_ref[part, :]
+            receivers = live_only(dst_ref[0, :, part], step * STEP + start, count_ref[0] * TILE)
+            onehot = hot_rows(receivers, d_aggregate_ref.shape[0])
+            upstream = dot(onehot, d_aggregate_ref[...])
+            edge_grad_ref[part, :] = (upstream + contract_cols(d_pre, w_edge_ref[...])).astype(BF16)
+            grad_in[:width, :] += contract_rows(edge_ref[part, :], d_pre)
+            mesh_sum[...] += dot(hot_columns(receivers, mesh_sum.shape[0]), d_pre)
+
+    @pl.when(step * STEP >= count_ref[0] * TILE)
     def _():
         edge_grad_ref[...] = jnp.zeros_like(edge_grad_ref)
 
@@ -294,15 +350,26 @@
     return (left.astype(F32) + right.astype(F32)).astype(BF16)
 
 
-def reduce_scatter(peers, outgoing, kept):
+def core_sum(peers, outgoing, kept):
     arrived = send(outgoing, by_xor(peers, 1))
-    next_out = add(kept[1], arrived[1])
-    next_kept = add(kept[0], arrived[0])
-    arrived = send(next_out, by_xor(peers, 2))
-    pieces = [add(next_kept[place], arrived[place]) for place in range(peers // 4)]
-    total = pieces[0].astype(F32)
-    for place in range(1, peers // 4):
-        total = total + send(pieces[place], by_xor(peers, 4 * place)).astype(F32)
+    return add(kept[1], arrived[1]), add(kept[0], arrived[0])
+
+
+def next_sum(peers, outgoing, kept):
+    arrived = send(outgoing, by_xor(peers, 2))
+    return [add(kept[place], arrived[place]) for place in range(peers // 4)]
+
+
+def last_hop(peers, pieces):
+    return [pieces[0]] + [
+        send(pieces[place], by_xor(peers, 4 * place)) for place in range(1, peers // 4)
+    ]
+
+
+def total_of(terms, start, stop):
+    total = terms[0][start:stop].astype(F32)
+    for term in terms[1:]:
+        total = total + term[start:stop].astype(F32)
     return total
 
 
@@ -333,18 +400,18 @@
     edges, width = edge_latent.shape
     mesh_count = mesh_latent.shape[0]
     grid_count = grid_latent.shape[0]
-    tiles = edges // TILE
-    src = edge_src.reshape(tiles, 1, TILE)
-    dst = edge_dst.reshape(tiles, 1, TILE)
+    tiles = edges // STEP
+    src = edge_src.reshape(tiles, 1, STEP)
+    dst = edge_dst.reshape(tiles, 1, STEP)
     smem = pl.BlockSpec(memory_space=pltpu.SMEM)
     params = pltpu.CompilerParams(vmem_limit_bytes=VMEM_BYTES)
     one_list = jax.ShapeDtypeStruct((cap, width), BF16)
     square = (width, width)
 
     def tile_of(last):
-        return pl.BlockSpec((TILE, last), lambda step, *_: (step, 0))
-
-    index_tile = pl.BlockSpec((1, 1, TILE), lambda step, *_: (step, 0, 0))
+        return pl.BlockSpec((STEP, last), lambda step, *_: (step, 0))
+
+    index_tile = pl.BlockSpec((1, 1, STEP), lambda step, *_: (step, 0, 0))
 
     def weight(place):
         return pl.BlockSpec(square, lambda *_: (place, 0))
@@ -353,37 +420,54 @@
         shape = (2, upper, share, width)
         return [jax.ShapeDtypeStruct(shape, BF16)] * 2, [whole(shape)] * 2
 
+    grid_part = grid_count // 4
     lists = pl.pallas_call(
         gather_kernel,
-        in_specs=[smem, whole(rows.shape), whole(grid_latent.shape)],
+        grid=(4,),
+        in_specs=[smem, whole(rows.shape), pl.BlockSpec((grid_part, width), lambda step: (step, 0))],
         out_specs=[whole((cap, width))] * 8,
         out_shape=[one_list] * 8,
+        scratch_shapes=[pltpu.VMEM((8 * cap, width), F32)],
         compiler_params=params,
         name="gather_lists",
     )(me, rows, grid_latent)
 
+    def local_part(first, count, *before):
+        return pl.pallas_call(
+            local_kernel,
+            grid=(count,),
+            in_specs=[
+                pl.BlockSpec((1, 1, STEP), lambda step: (first + step, 0, 0)),
+                pl.BlockSpec((STEP, width), lambda step: (first + step, 0)),
+                whole(mesh_latent.shape),
+                weight(0),
+                weight(2),
+            ]
+            + [pl.BlockSpec(memory_space=pl.ANY)] * len(before),
+            out_specs=pl.BlockSpec((STEP, width), lambda step: (first + step, 0)),
+            out_shape=jax.ShapeDtypeStruct((edges, width), BF16),
+            scratch_shapes=[pltpu.VMEM((mesh_count, width), BF16)],
+            input_output_aliases={5: 0} if before else {},
+            compiler_params=params,
+            cost_estimate=pl.CostEstimate(
+                flops=2 * count * STEP * width * (width + mesh_count),
+                bytes_accessed=4 * count * STEP * width,
+                transcendentals=0,
+            ),
+            name="edge_local",
+        )(receivers, edge_latent, mesh_latent, w_edge_in, w_edge_in, *before)
+
+    hops = [send(lists[7], by_xor(peers, 4 * bits)) for bits in range(1, upper)]
     near = [lists[0]] + [
         send(lists[place], by_shift(peers, SHIFTS[place])) for place in range(1, 7)
     ]
-    far_own = jnp.concatenate(
-        [lists[7]] + [send(lists[7], by_xor(peers, 4 * bits)) for bits in range(1, upper)], axis=0
-    )
+    far_own = jnp.concatenate([lists[7]] + hops, axis=0)
+    far_own, receivers = lax.optimization_barrier((far_own, dst))
     far_next = send(far_own, by_xor(peers, 2))
+    local = local_part(0, tiles - 1)
+    far_next, near, local = lax.optimization_barrier((far_next, near, local))
     far_core = send(jnp.concatenate([far_own, far_next], axis=0), by_xor(peers, 1))
-
-    local = pl.pallas_call(
-        local_kernel,
-        grid=(tiles,),
-        in_specs=[index_tile, tile_of(width), whole(mesh_latent.shape), weight(0), weight(2)],
-        out_specs=tile_of(width),
-        out_shape=jax.ShapeDtypeStruct((edges, width), BF16),
-        scratch_shapes=[pltpu.VMEM((mesh_count, width), BF16)],
-        compiler_params=params,
-        cost_estimate=pl.CostEstimate(
-            flops=2 * edges * width * (width + mesh_count), bytes_accessed=4 * edges * width, transcendentals=0
-        ),
-        name="edge_local",
-    )(dst, edge_latent, mesh_latent, w_edge_in, w_edge_in)
+    local = local_part(tiles - 1, 1, local)
 
     node_shape, node_spec = halves(w_node_in.shape[0] // peers + w_node_out.shape[0] // peers)
     (received, hidden, slope, norm, inverse, node_send, node_keep, d_aggregate, d_mesh) = pl.pallas_call(
@@ -432,6 +516,7 @@
         mesh_cotangent,
     )
 
+    node_next, node_kept = core_sum(peers, node_send, node_keep)
     slot_shape, slot_spec = halves(w_edge_out.shape[0] // peers + cap)
     results = pl.pallas_call(
         functools.partial(slots_kernel, peers),
@@ -457,6 +542,11 @@
         name="backward_slots",
     )(me, tile_count, src, dst, hidden, slope, norm, inverse, d_aggregate, received, w_edge_in, w_edge_out)
     (d_pre, grad_sender, slot_send, slot_keep), returns = results[:4], results[4:]
+    (node_next, node_kept, d_pre, slot_send, slot_keep, returns) = lax.optimization_barrier(
+        (node_next, node_kept, d_pre, slot_send, slot_keep, returns)
+    )
+    node_pieces = next_sum(peers, node_next, node_kept)
+    slot_next, slot_kept = core_sum(peers, slot_send, slot_keep)
     returned = [returns[0]] + [
         send(returns[place], by_shift(peers, -SHIFTS[place])) for place in range(1, 7)
     ]
@@ -496,27 +586,36 @@
         w_edge_in,
     )
 
-    node_total = reduce_scatter(peers, node_send, node_keep)
-    slot_total = reduce_scatter(peers, slot_send, slot_keep)
-    edge_total = reduce_scatter(peers, edge_send, edge_keep)
+    (node_pieces, slot_next, slot_kept, edge_send, edge_keep) = lax.optimization_barrier(
+        (node_pieces, slot_next, slot_kept, edge_send, edge_keep)
+    )
+    slot_pieces = next_sum(peers, slot_next, slot_kept)
+    node_terms = last_hop(peers, node_pieces)
+    edge_next, edge_kept = core_sum(peers, edge_send, edge_keep)
+    slot_terms = last_hop(peers, slot_pieces)
+    edge_pieces = next_sum(peers, edge_next, edge_kept)
+    edge_terms = last_hop(peers, edge_pieces)
     node_rows = w_node_in.shape[0] // peers
     out_rows = w_edge_out.shape[0] // peers
     grid_grad = pl.pallas_call(
-        scatter_kernel,
-        in_specs=[smem, whole(rows.shape)] + [whole((cap, width))] * 8,
-        out_specs=whole(grid_latent.shape),
+        functools.partial(scatter_kernel, out_rows),
+        grid=(4,),
+        in_specs=[smem, whole(rows.shape)]
+        + [whole((cap, width))] * 7
+        + [whole((out_rows + cap, width))] * upper,
+        out_specs=pl.BlockSpec((grid_part, width), lambda step: (step, 0)),
         out_shape=jax.ShapeDtypeStruct((grid_count, width), BF16),
         compiler_params=params,
         name="scatter_lists",
-    )(me, rows, *returned, slot_total[out_rows:])
+    )(me, rows, *returned, *slot_terms)
     return (
         grid_grad,
         edge_grad,
         mesh_grad,
-        edge_total,
-        slot_total[:out_rows],
-        node_total[:node_rows],
-        node_total[node_rows:],
+        total_of(edge_terms, 0, w_edge_in.shape[0] // peers),
+        total_of(slot_terms, 0, out_rows),
+        total_of(node_terms, 0, node_rows),
+        total_of(node_terms, node_rows, node_rows + w_node_out.shape[0] // peers),
     )
 
 

time: 153 us -> 129 us (0.84)
  the two profiles are of different devices: /device:TPU:10 before, /device:TPU:0 now
where the time goes in v2:
time: 129 us
  Pallas kernels  54.7 us (42%)
  starting transfers between devices  45.4 us (35%)
  waiting for transfers between devices  20.7 us (16%)
  other arithmetic  4.45 us (3%)
  local copies, waits for them, and re-layouts  2.14 us (2%)
  between operations  1.77 us (1%)
    ppermute x32, starting transfers between devices, send(): return lax.ppermute(values, 'lon', perm)  45.4 us
    ppermute x32, waiting for transfers between devices, send(): return lax.ppermute(values, 'lon', perm)  20.7 us
    pallas_call x1, Pallas kernels, on_device(): pl.pallas_call(functools.partial(forward_kernel, peers), grid=(tiles,), i...  14.7 us
    pallas_call x1, Pallas kernels, on_device(): pl.pallas_call(functools.partial(slots_kernel, peers), grid=(tiles,), in_...  12.1 us
    pallas_call x1, Pallas kernels, on_device(): pl.pallas_call(functools.partial(edges_kernel, peers), grid=(tiles,), in_...  9.62 us
    pallas_call x2, Pallas kernels, local_part(): pl.pallas_call(local_kernel, grid=(count,), in_specs=[pl.BlockSpec((1, 1,...  9.36 us
    pallas_call x1, Pallas kernels, on_device(): pl.pallas_call(functools.partial(scatter_kernel, out_rows), grid=(4,), in...  4.54 us
    pallas_call x1, Pallas kernels, on_device(): pl.pallas_call(gather_kernel, grid=(4,), in_specs=[smem, whole(rows.shape...  4.38 us
  transfers between devices with their start and end apart: 32, of which 7 were waited for; matrix products, arithmetic and copies ran while one was open for 3% of the time, Pallas kernels for 28%

profile of v2, /device:TPU:0, one launch (start us, length us, event | category | flops | bytes accessed | tf_op | source)
XLA Modules:
  0.0 129.1 jit_solution(9325211663228208258)
XLA Ops:
  0.6 4.4 %gather_lists.1 = (bf16[48,512]{1,0:T(8,128)(2,1)}, bf16[48,512]{1,0:T(8,128)(2,1)}, bf16[48,512]{1,0:T(8,128)(2,1)}, bf16[48,512]{1,0:T(8,128)(2,1)}, bf16[48,5...) custom-call(s32[1]{0:T(128)} %bitcast.me_ref, ...), custom_call_target="tpu_custom_call" | custom-call | tf_op jit(solution)/shard_map/gather_lists/pallas_call | solution.py:424
  5.0 5.1 %collective-permute-start.2 = (bf16[48,512]{1,0:T(8,128)(2,1)}, bf16[48,512]{1,0:T(8,128)(2,1)S(1)}, u32[]{:S(2)}, u32[]{:S(2)}) collective-permute-start(bf16[48,512]{1,0:T(8,128)(2,1)} %get-tuple-element.70), channel_id=1, source_target_pairs={{0,12},{1,13},{2,14},{3,15},{4,8},{5,9},{6,10},{7,11},{8,4},{9,5},... | collective-permute-start | bytes 147464 | tf_op jit(solution)/shard_map/ppermute | solution.py:346
  10.7 1.7 %collective-permute-start.5 = (bf16[48,512]{1,0:T(8,128)(2,1)}, bf16[48,512]{1,0:T(8,128)(2,1)S(1)}, u32[]{:S(2)}, u32[]{:S(2)}) collective-permute-start(bf16[48,512]{1,0:T(8,128)(2,1)} %get-tuple-element.75), channel_id=1, source_target_pairs={{0,2},{1,3},{2,4},{3,5},{4,6},{5,7},{6,8},{7,9},{8,10},{9,11},{10,... | collective-permute-start | bytes 147464 | tf_op jit(solution)/shard_map/ppermute | solution.py:346
  12.6 2.7 %collective-permute-done.1 = bf16[48,512]{1,0:T(8,128)(2,1)S(1)} collective-permute-done((bf16[48,512]{1,0:T(8,128)(2,1)}, bf16[48,512]{1,0:T(8,128)(2,1)S(1)}, u32[]{:S(2)}, u32[]{:S(2)}) %collective-permute-start.1) | collective-permute-done | bytes 49184 | tf_op jit(solution)/shard_map/ppermute | solution.py:346
  17.7 3.5 %collective-permute-start.7 = (bf16[48,512]{1,0:T(8,128)(2,1)}, bf16[48,512]{1,0:T(8,128)(2,1)S(1)}, u32[]{:S(2)}, u32[]{:S(2)}) collective-permute-start(bf16[48,512]{1,0:T(8,128)(2,1)} %get-tuple-element.77), channel_id=1, source_target_pairs={{0,15},{1,0},{2,1},{3,2},{4,3},{5,4},{6,5},{7,6},{8,7},{9,8},{10,9... | collective-permute-start | bytes 147464 | tf_op jit(solution)/shard_map/ppermute | solution.py:346
  22.7 5.5 %edge_local.2.refs_0_ = bf16[3072,512]{1,0:T(8,128)(2,1)} custom-call(s32[3,1,1024]{2,1,0:T(1,128)} %bitcast.66, bf16[3072,512]{1,0:T(8,128)(2,1)} %refs_0_.1, bf16[256,512]{1,0:T(8,128)(2,1)} %refs_4_.1, bf16[1536,512]{1,0:T(8,128)(2,1)} %refs_7_.3, bf16[1536,512]{1,0:T(8,128)(2,1)} %refs_7_.3), custom_call_target="tpu_custom_call" | custom-call | flops 1610612736 | bytes 4194304 | tf_op jit(solution)/shard_map/edge_local/pallas_call | solution.py:436
  29.4 3.9 %edge_local.3.local_ref = bf16[3072,512]{1,0:T(8,128)(2,1)} custom-call(s32[3,1,1024]{2,1,0:T(1,128)} %bitcast.67, bf16[3072,512]{1,0:T(8,128)(2,1)} %refs_0_.1, bf16[256,512]{1,0:T(8,128)(2,1)} %refs_4_.1, bf16[1536,512]{1,0:T(8,128)(2,1)} %refs_7_.3, bf16[1536,512]{1,0:T(8,128)(2,1)} %refs_7_.3, ...), custom_call_target="tpu_custom_call", output_to_operand_aliasing={{}: (5, {})} | custom-call | flops 805306368 | bytes 2097152 | tf_op jit(solution)/shard_map/edge_local/pallas_call | solution.py:436
  34.1 14.7 %forward.1 = (bf16[768,512]{1,0:T(8,128)(2,1)}, bf16[3072,512]{1,0:T(8,128)(2,1)}, bf16[3072,512]{1,0:T(8,128)(2,1)}, bf16[3072,512]{1,0:T(8,128)(2,1)}, f32[307...) custom-call(s32[1]{0:T(128)} %bitcast.me_ref, ...), custom_call_target="tpu_custom_call" | custom-call | tf_op jit(solution)/shard_map/forward/pallas_call | solution.py:473
  49.0 12.1 %backward_slots.1 = (bf16[3072,512]{1,0:T(8,128)(2,1)}, f32[512,512]{1,0:T(8,128)}, bf16[2,4,80,512]{3,2,1,0:T(8,128)(2,1)}, bf16[2,4,80,512]{3,2,1,0:T(8,128)(2...) custom-call(s32[1]{0:T(128)} %bitcast.me_ref, ...), custom_call_target="tpu_custom_call" | custom-call | flops 6442450944 | bytes 12582912 | tf_op jit(solution)/shard_map/backward_slots/pallas_call | solution.py:521
  61.4 1.7 %collective-permute-start.18 = (bf16[4,96,512]{2,1,0:T(8,128)(2,1)S(1)}, bf16[4,96,512]{2,1,0:T(8,128)(2,1)S(1)}, u32[]{:S(2)}, u32[]{:S(2)}) collective-permute-start(bf16[4,96,512]{2,1,0:T(8,128)(2,1)S(1)} %get-tuple-element.115), channel_id=1, source_target_pairs={{0,2},{1,3},{2,0},{3,1},{4,6},{5,7},{6,4},{7,5},{8,10},{9,11},{10,... | collective-permute-start | bytes 1179656 | tf_op jit(solution)/shard_map/ppermute | solution.py:346
  63.3 9.6 %backward_edges.1 = (bf16[3072,512]{1,0:T(8,128)(2,1)}, bf16[256,512]{1,0:T(8,128)(2,1)}, bf16[2,4,96,512]{3,2,1,0:T(8,128)(2,1)}, bf16[2,4,96,512]{3,2,1,0:T(8,128)(2,1)}) custom-call(s32[1]{0:T(128)} %bitcast.me_ref, s32[1]{0:T(128)S(6)} %copy.21.count_ref, s32[3,1,1024]{2,1,0:T(1,128)} %bitcast.70, bf16[3072,512]{1,0:T(8,128)(2,1)} %refs_0_.1, ...), custom_call_target="tpu_custom_call" | custom-call | flops 4831838208 | bytes 9437184 | tf_op jit(solution)/shard_map/backward_edges/pallas_call | solution.py:555
  74.4 7.3 %collective-permute-start.29 = (bf16[96,512]{1,0:T(8,128)(2,1)S(1)}, bf16[96,512]{1,0:T(8,128)(2,1)S(1)}, u32[]{:S(2)}, u32[]{:S(2)}) collective-permute-start(bf16[96,512]{1,0:T(8,128)(2,1)S(1)} %get-tuple-element.130), channel_id=1, source_target_pairs={{0,4},{1,5},{2,6},{3,7},{4,0},{5,1},{6,2},{7,3},{8,12},{9,13},{10,... | collective-permute-start | bytes 294920 | tf_op jit(solution)/shard_map/ppermute | solution.py:346
  82.4 1.6 %collective-permute-start.31 = (bf16[96,512]{1,0:T(8,128)(2,1)S(1)}, bf16[96,512]{1,0:T(8,128)(2,1)S(1)}, u32[]{:S(2)}, u32[]{:S(2)}) collective-permute-start(bf16[96,512]{1,0:T(8,128)(2,1)S(1)} %get-tuple-element.132), channel_id=1, source_target_pairs={{0,12},{1,13},{2,14},{3,15},{4,8},{5,9},{6,10},{7,11},{8,4},{9,5},... | collective-permute-start | bytes 294920 | tf_op jit(solution)/shard_map/ppermute | solution.py:346
  84.0 2.3 %collective-permute-start.12 = (bf16[48,512]{1,0:T(8,128)(2,1)S(1)}, bf16[48,512]{1,0:T(8,128)(2,1)S(1)}, u32[]{:S(2)}, u32[]{:S(2)}) collective-permute-start(bf16[48,512]{1,0:T(8,128)(2,1)S(1)} %copy-done.28), channel_id=1, source_target_pairs={{0,15},{1,0},{2,1},{3,2},{4,3},{5,4},{6,5},{7,6},{8,7},{9,8},{10,9... | collective-permute-start | bytes 147464 | tf_op jit(solution)/shard_map/ppermute | solution.py:346
  86.3 3.6 %collective-permute-start.13 = (bf16[48,512]{1,0:T(8,128)(2,1)S(1)}, bf16[48,512]{1,0:T(8,128)(2,1)S(1)}, u32[]{:S(2)}, u32[]{:S(2)}) collective-permute-start(bf16[48,512]{1,0:T(8,128)(2,1)S(1)} %copy-done.27), channel_id=1, source_target_pairs={{0,14},{1,15},{2,0},{3,1},{4,2},{5,3},{6,4},{7,5},{8,6},{9,7},{10,... | collective-permute-start | bytes 147464 | tf_op jit(solution)/shard_map/ppermute | solution.py:346
  90.0 1.8 %collective-permute-done.30 = bf16[96,512]{1,0:T(8,128)(2,1)S(1)} collective-permute-done((bf16[96,512]{1,0:T(8,128)(2,1)S(1)}, bf16[96,512]{1,0:T(8,128)(2,1)S(1)}, u32[]{:S(2)}, u32[]{:S(2)}) %collective-permute-start.30) | collective-permute-done | bytes 98336 | tf_op jit(solution)/shard_map/ppermute | solution.py:346
  95.5 6.9 %collective-permute-done.20 = bf16[4,80,512]{2,1,0:T(8,128)(2,1)S(1)} collective-permute-done((bf16[4,80,512]{2,1,0:T(8,128)(2,1)S(1)}, bf16[4,80,512]{2,1,0:T(8,128)(2,1)S(1)}, u32[]{:S(2)}, u32[]{:S(2)}) %collective-permute-start.20) | collective-permute-done | bytes 327712 | tf_op jit(solution)/shard_map/ppermute | solution.py:346
  104.0 2.6 %collective-permute-start.22 = (bf16[80,512]{1,0:T(8,128)(2,1)S(1)}, bf16[80,512]{1,0:T(8,128)(2,1)S(1)}, u32[]{:S(2)}, u32[]{:S(2)}) collective-permute-start(bf16[80,512]{1,0:T(8,128)(2,1)S(1)} %get-tuple-element.147), channel_id=1, source_target_pairs={{0,8},{1,9},{2,10},{3,11},{4,12},{5,13},{6,14},{7,15},{8,0},{9,1},... | collective-permute-start | bytes 245768 | tf_op jit(solution)/shard_map/ppermute | solution.py:346
  106.7 4.6 %collective-permute-done.25 = bf16[4,96,512]{2,1,0:T(8,128)(2,1)S(1)} collective-permute-done((bf16[4,96,512]{2,1,0:T(8,128)(2,1)S(1)}, bf16[4,96,512]{2,1,0:T(8,128)(2,1)S(1)}, u32[]{:S(2)}, u32[]{:S(2)}) %collective-permute-start.25) | collective-permute-done | bytes 393248 | tf_op jit(solution)/shard_map/ppermute | solution.py:346
  111.3 1.9 %collective-permute-start.21 = (bf16[80,512]{1,0:T(8,128)(2,1)S(1)}, bf16[80,512]{1,0:T(8,128)(2,1)S(1)}, u32[]{:S(2)}, u32[]{:S(2)}) collective-permute-start(bf16[80,512]{1,0:T(8,128)(2,1)S(1)} %get-tuple-element.148), channel_id=1, source_target_pairs={{0,4},{1,5},{2,6},{3,7},{4,0},{5,1},{6,2},{7,3},{8,12},{9,13},{10,... | collective-permute-start | bytes 245768 | tf_op jit(solution)/shard_map/ppermute | solution.py:346
  115.1 2.2 %collective-permute-start.28 = (bf16[96,512]{1,0:T(8,128)(2,1)S(1)}, bf16[96,512]{1,0:T(8,128)(2,1)S(1)}, u32[]{:S(2)}, u32[]{:S(2)}) collective-permute-start(bf16[96,512]{1,0:T(8,128)(2,1)S(1)} %get-tuple-element.140), channel_id=1, source_target_pairs={{0,12},{1,13},{2,14},{3,15},{4,8},{5,9},{6,10},{7,11},{8,4},{9,5},... | collective-permute-start | bytes 294920 | tf_op jit(solution)/shard_map/ppermute | solution.py:346
  118.8 1.6 %collective-permute-done.16.refs_5_ = bf16[48,512]{1,0:T(8,128)(2,1)S(1)} collective-permute-done((bf16[48,512]{1,0:T(8,128)(2,1)S(1)}, bf16[48,512]{1,0:T(8,128)(2,1)S(1)}, u32[]{:S(2)}, u32[]{:S(2)}) %collective-permute-start.16) | collective-permute-done | bytes 49184 | tf_op jit(solution)/shard_map/ppermute | solution.py:346
  121.0 4.5 %scatter_lists.1 = bf16[2048,512]{1,0:T(8,128)(2,1)} custom-call(s32[1]{0:T(128)} %bitcast.me_ref, s32[16,48]{1,0:T(8,128)} %bitcast.72, bf16[48,512]{1,0:T(8,128)(2,1)} %get-tuple-element.107.refs_0_, bf16[48,512]{1,0:T(8,128)(2,1)} %copy-done.16, bf16[48,512]{1,0:T(8,128)(2,1)} %copy-done.17, bf16[48,512]{1,0:T(8,128)(2,1)} %copy-done.18, ...), custom_call_target="tpu_custom_call" | custom-call | tf_op jit(solution)/shard_map/scatter_lists/pallas_call | solution.py:600
  125.6 2.8 %collective-permute-done.27 = bf16[96,512]{1,0:T(8,128)(2,1)S(1)} collective-permute-done((bf16[96,512]{1,0:T(8,128)(2,1)S(1)}, bf16[96,512]{1,0:T(8,128)(2,1)S(1)}, u32[]{:S(2)}, u32[]{:S(2)}) %collective-permute-start.27) | collective-permute-done | bytes 98336 | tf_op jit(solution)/shard_map/ppermute | solution.py:346
  (117 shorter events, 18.6 us)
Async XLA Ops:
  5.0 7.5 %collective-permute-start.2 = (bf16[48,512]{1,0:T(8,128)(2,1)}, bf16[48,512]{1,0:T(8,128)(2,1)S(1)}, u32[]{:S(2)}, u32[]{:S(2)}) collective-permute-start(bf16[48,512]{1,0:T(8,128)(2,1)} %get-tuple-element.70), channel_id=1, source_target_pairs={{0,12},{1,13},{2,14},{3,15},{4,8},{5,9},{6,10},{7,11},{8,4},{9,5},... | collective-permute-start | bytes 147464 | tf_op jit(solution)/shard_map/ppermute | solution.py:346
  10.7 10.5 %collective-permute-start.4 = (bf16[48,512]{1,0:T(8,128)(2,1)}, bf16[48,512]{1,0:T(8,128)(2,1)S(1)}, u32[]{:S(2)}, u32[]{:S(2)}) collective-permute-start(bf16[48,512]{1,0:T(8,128)(2,1)} %get-tuple-element.74), channel_id=1, source_target_pairs={{0,1},{1,2},{2,3},{3,4},{4,5},{5,6},{6,7},{7,8},{8,9},{9,10},{10,1... | collective-permute-start | bytes 147464 | tf_op jit(solution)/shard_map/ppermute | solution.py:346
  10.7 12.0 %collective-permute-start.5 = (bf16[48,512]{1,0:T(8,128)(2,1)}, bf16[48,512]{1,0:T(8,128)(2,1)S(1)}, u32[]{:S(2)}, u32[]{:S(2)}) collective-permute-start(bf16[48,512]{1,0:T(8,128)(2,1)} %get-tuple-element.75), channel_id=1, source_target_pairs={{0,2},{1,3},{2,4},{3,5},{4,6},{5,7},{6,8},{7,9},{8,10},{9,11},{10,... | collective-permute-start | bytes 147464 | tf_op jit(solution)/shard_map/ppermute | solution.py:346
  16.1 12.2 %collective-permute-start.3 = (bf16[192,512]{1,0:T(8,128)(2,1)S(1)}, bf16[192,512]{1,0:T(8,128)(2,1)S(1)}, u32[]{:S(2)}, u32[]{:S(2)}) collective-permute-start(bf16[192,512]{1,0:T(8,128)(2,1)S(1)} %pad_maximum_fusion.1.refs_7_), channel_id=1, source_target_pairs={{0,2},{1,3},{2,0},{3,1},{4,6},{5,7},{6,4},{7,5},{8,10},{9,11},{10,... | collective-permute-start | bytes 589832 | tf_op jit(solution)/shard_map/ppermute | solution.py:346
  17.7 10.5 %collective-permute-start.6 = (bf16[48,512]{1,0:T(8,128)(2,1)}, bf16[48,512]{1,0:T(8,128)(2,1)S(1)}, u32[]{:S(2)}, u32[]{:S(2)}) collective-permute-start(bf16[48,512]{1,0:T(8,128)(2,1)} %get-tuple-element.76), channel_id=1, source_target_pairs={{0,3},{1,4},{2,5},{3,6},{4,7},{5,8},{6,9},{7,10},{8,11},{9,12},{10... | collective-permute-start | bytes 147464 | tf_op jit(solution)/shard_map/ppermute | solution.py:346
  17.7 10.5 %collective-permute-start.7 = (bf16[48,512]{1,0:T(8,128)(2,1)}, bf16[48,512]{1,0:T(8,128)(2,1)S(1)}, u32[]{:S(2)}, u32[]{:S(2)}) collective-permute-start(bf16[48,512]{1,0:T(8,128)(2,1)} %get-tuple-element.77), channel_id=1, source_target_pairs={{0,15},{1,0},{2,1},{3,2},{4,3},{5,4},{6,5},{7,6},{8,7},{9,8},{10,9... | collective-permute-start | bytes 147464 | tf_op jit(solution)/shard_map/ppermute | solution.py:346
  48.8 12.3 %collective-permute-start.11 = (bf16[2,4,96,512]{3,2,1,0:T(8,128)(2,1)}, bf16[2,4,96,512]{3,2,1,0:T(8,128)(2,1)S(1)}, u32[]{:S(2)}, u32[]{:S(2)}) collective-permute-start(bf16[2,4,96,512]{3,2,1,0:T(8,128)(2,1)} %get-tuple-element.90), channel_id=1, source_target_pairs={{0,1},{1,0},{2,3},{3,2},{4,5},{5,4},{6,7},{7,6},{8,9},{9,8},{10,11... | collective-permute-start | bytes 2359304 | tf_op jit(solution)/shard_map/ppermute | solution.py:346
  61.4 11.6 %collective-permute-start.18 = (bf16[4,96,512]{2,1,0:T(8,128)(2,1)S(1)}, bf16[4,96,512]{2,1,0:T(8,128)(2,1)S(1)}, u32[]{:S(2)}, u32[]{:S(2)}) collective-permute-start(bf16[4,96,512]{2,1,0:T(8,128)(2,1)S(1)} %get-tuple-element.115), channel_id=1, source_target_pairs={{0,2},{1,3},{2,0},{3,1},{4,6},{5,7},{6,4},{7,5},{8,10},{9,11},{10,... | collective-permute-start | bytes 1179656 | tf_op jit(solution)/shard_map/ppermute | solution.py:346
  63.1 10.0 %collective-permute-start.19 = (bf16[2,4,80,512]{3,2,1,0:T(8,128)(2,1)}, bf16[2,4,80,512]{3,2,1,0:T(8,128)(2,1)S(1)}, u32[]{:S(2)}, u32[]{:S(2)}) collective-permute-start(bf16[2,4,80,512]{3,2,1,0:T(8,128)(2,1)} %get-tuple-element.117), channel_id=1, source_target_pairs={{0,1},{1,0},{2,3},{3,2},{4,5},{5,4},{6,7},{7,6},{8,9},{9,8},{10,11... | collective-permute-start | bytes 1966088 | tf_op jit(solution)/shard_map/ppermute | solution.py:346
  74.0 19.8 %collective-permute-start.24 = (bf16[2,4,96,512]{3,2,1,0:T(8,128)(2,1)S(1)}, bf16[2,4,96,512]{3,2,1,0:T(8,128)(2,1)S(1)}, u32[]{:S(2)}, u32[]{:S(2)}) collective-permute-start(bf16[2,4,96,512]{3,2,1,0:T(8,128)(2,1)S(1)} %copy-done.22), channel_id=1, source_target_pairs={{0,1},{1,0},{2,3},{3,2},{4,5},{5,4},{6,7},{7,6},{8,9},{9,8},{10,11... | collective-permute-start | bytes 2359304 | tf_op jit(solution)/shard_map/ppermute | solution.py:346
  74.4 12.0 %collective-permute-start.29 = (bf16[96,512]{1,0:T(8,128)(2,1)S(1)}, bf16[96,512]{1,0:T(8,128)(2,1)S(1)}, u32[]{:S(2)}, u32[]{:S(2)}) collective-permute-start(bf16[96,512]{1,0:T(8,128)(2,1)S(1)} %get-tuple-element.130), channel_id=1, source_target_pairs={{0,4},{1,5},{2,6},{3,7},{4,0},{5,1},{6,2},{7,3},{8,12},{9,13},{10,... | collective-permute-start | bytes 294920 | tf_op jit(solution)/shard_map/ppermute | solution.py:346
  81.7 10.1 %collective-permute-start.30 = (bf16[96,512]{1,0:T(8,128)(2,1)S(1)}, bf16[96,512]{1,0:T(8,128)(2,1)S(1)}, u32[]{:S(2)}, u32[]{:S(2)}) collective-permute-start(bf16[96,512]{1,0:T(8,128)(2,1)S(1)} %get-tuple-element.131), channel_id=1, source_target_pairs={{0,8},{1,9},{2,10},{3,11},{4,12},{5,13},{6,14},{7,15},{8,0},{9,1},... | collective-permute-start | bytes 294920 | tf_op jit(solution)/shard_map/ppermute | solution.py:346
  82.4 9.4 %collective-permute-start.31 = (bf16[96,512]{1,0:T(8,128)(2,1)S(1)}, bf16[96,512]{1,0:T(8,128)(2,1)S(1)}, u32[]{:S(2)}, u32[]{:S(2)}) collective-permute-start(bf16[96,512]{1,0:T(8,128)(2,1)S(1)} %get-tuple-element.132), channel_id=1, source_target_pairs={{0,12},{1,13},{2,14},{3,15},{4,8},{5,9},{6,10},{7,11},{8,4},{9,5},... | collective-permute-start | bytes 294920 | tf_op jit(solution)/shard_map/ppermute | solution.py:346
  84.0 18.5 %collective-permute-start.12 = (bf16[48,512]{1,0:T(8,128)(2,1)S(1)}, bf16[48,512]{1,0:T(8,128)(2,1)S(1)}, u32[]{:S(2)}, u32[]{:S(2)}) collective-permute-start(bf16[48,512]{1,0:T(8,128)(2,1)S(1)} %copy-done.28), channel_id=1, source_target_pairs={{0,15},{1,0},{2,1},{3,2},{4,3},{5,4},{6,5},{7,6},{8,7},{9,8},{10,9... | collective-permute-start | bytes 147464 | tf_op jit(solution)/shard_map/ppermute | solution.py:346
  86.3 17.7 %collective-permute-start.13 = (bf16[48,512]{1,0:T(8,128)(2,1)S(1)}, bf16[48,512]{1,0:T(8,128)(2,1)S(1)}, u32[]{:S(2)}, u32[]{:S(2)}) collective-permute-start(bf16[48,512]{1,0:T(8,128)(2,1)S(1)} %copy-done.27), channel_id=1, source_target_pairs={{0,14},{1,15},{2,0},{3,1},{4,2},{5,3},{6,4},{7,5},{8,6},{9,7},{10,... | collective-permute-start | bytes 147464 | tf_op jit(solution)/shard_map/ppermute | solution.py:346
  91.8 21.5 %collective-permute-start.14 = (bf16[48,512]{1,0:T(8,128)(2,1)S(1)}, bf16[48,512]{1,0:T(8,128)(2,1)S(1)}, u32[]{:S(2)}, u32[]{:S(2)}) collective-permute-start(bf16[48,512]{1,0:T(8,128)(2,1)S(1)} %copy-done.26), channel_id=1, source_target_pairs={{0,13},{1,14},{2,15},{3,0},{4,1},{5,2},{6,3},{7,4},{8,5},{9,6},{10... | collective-permute-start | bytes 147464 | tf_op jit(solution)/shard_map/ppermute | solution.py:346
  91.8 10.6 %collective-permute-start.20 = (bf16[4,80,512]{2,1,0:T(8,128)(2,1)S(1)}, bf16[4,80,512]{2,1,0:T(8,128)(2,1)S(1)}, u32[]{:S(2)}, u32[]{:S(2)}) collective-permute-start(bf16[4,80,512]{2,1,0:T(8,128)(2,1)S(1)} %get-tuple-element.124), channel_id=1, source_target_pairs={{0,2},{1,3},{2,0},{3,1},{4,6},{5,7},{6,4},{7,5},{8,10},{9,11},{10,... | collective-permute-start | bytes 983048 | tf_op jit(solution)/shard_map/ppermute | solution.py:346
  94.1 17.2 %collective-permute-start.25 = (bf16[4,96,512]{2,1,0:T(8,128)(2,1)S(1)}, bf16[4,96,512]{2,1,0:T(8,128)(2,1)S(1)}, u32[]{:S(2)}, u32[]{:S(2)}) collective-permute-start(bf16[4,96,512]{2,1,0:T(8,128)(2,1)S(1)} %get-tuple-element.134), channel_id=1, source_target_pairs={{0,2},{1,3},{2,0},{3,1},{4,6},{5,7},{6,4},{7,5},{8,10},{9,11},{10,... | collective-permute-start | bytes 1179656 | tf_op jit(solution)/shard_map/ppermute | solution.py:346
  102.4 12.1 %collective-permute-start.15 = (bf16[48,512]{1,0:T(8,128)(2,1)S(1)}, bf16[48,512]{1,0:T(8,128)(2,1)S(1)}, u32[]{:S(2)}, u32[]{:S(2)}) collective-permute-start(bf16[48,512]{1,0:T(8,128)(2,1)S(1)} %copy-done.25), channel_id=1, source_target_pairs={{0,1},{1,2},{2,3},{3,4},{4,5},{5,6},{6,7},{7,8},{8,9},{9,10},{10,1... | collective-permute-start | bytes 147464 | tf_op jit(solution)/shard_map/ppermute | solution.py:346
  102.5 12.0 %collective-permute-start.23 = (bf16[80,512]{1,0:T(8,128)(2,1)S(1)}, bf16[80,512]{1,0:T(8,128)(2,1)S(1)}, u32[]{:S(2)}, u32[]{:S(2)}) collective-permute-start(bf16[80,512]{1,0:T(8,128)(2,1)S(1)} %get-tuple-element.146), channel_id=1, source_target_pairs={{0,12},{1,13},{2,14},{3,15},{4,8},{5,9},{6,10},{7,11},{8,4},{9,5},... | collective-permute-start | bytes 245768 | tf_op jit(solution)/shard_map/ppermute | solution.py:346
  104.0 11.0 %collective-permute-start.22 = (bf16[80,512]{1,0:T(8,128)(2,1)S(1)}, bf16[80,512]{1,0:T(8,128)(2,1)S(1)}, u32[]{:S(2)}, u32[]{:S(2)}) collective-permute-start(bf16[80,512]{1,0:T(8,128)(2,1)S(1)} %get-tuple-element.147), channel_id=1, source_target_pairs={{0,8},{1,9},{2,10},{3,11},{4,12},{5,13},{6,14},{7,15},{8,0},{9,1},... | collective-permute-start | bytes 245768 | tf_op jit(solution)/shard_map/ppermute | solution.py:346
  114.6 11.0 %collective-permute-start.26 = (bf16[96,512]{1,0:T(8,128)(2,1)S(1)}, bf16[96,512]{1,0:T(8,128)(2,1)S(1)}, u32[]{:S(2)}, u32[]{:S(2)}) collective-permute-start(bf16[96,512]{1,0:T(8,128)(2,1)S(1)} %get-tuple-element.139), channel_id=1, source_target_pairs={{0,4},{1,5},{2,6},{3,7},{4,0},{5,1},{6,2},{7,3},{8,12},{9,13},{10,... | collective-permute-start | bytes 294920 | tf_op jit(solution)/shard_map/ppermute | solution.py:346
  115.1 10.5 %collective-permute-start.28 = (bf16[96,512]{1,0:T(8,128)(2,1)S(1)}, bf16[96,512]{1,0:T(8,128)(2,1)S(1)}, u32[]{:S(2)}, u32[]{:S(2)}) collective-permute-start(bf16[96,512]{1,0:T(8,128)(2,1)S(1)} %get-tuple-element.140), channel_id=1, source_target_pairs={{0,12},{1,13},{2,14},{3,15},{4,8},{5,9},{6,10},{7,11},{8,4},{9,5},... | collective-permute-start | bytes 294920 | tf_op jit(solution)/shard_map/ppermute | solution.py:346
  117.3 11.1 %collective-permute-start.27 = (bf16[96,512]{1,0:T(8,128)(2,1)S(1)}, bf16[96,512]{1,0:T(8,128)(2,1)S(1)}, u32[]{:S(2)}, u32[]{:S(2)}) collective-permute-start(bf16[96,512]{1,0:T(8,128)(2,1)S(1)} %get-tuple-element.141), channel_id=1, source_target_pairs={{0,8},{1,9},{2,10},{3,11},{4,12},{5,13},{6,14},{7,15},{8,0},{9,1},... | collective-permute-start | bytes 294920 | tf_op jit(solution)/shard_map/ppermute | solution.py:346
  (37 other events, 376.7 us)

commit v3 on v2

--- a/solution.py
+++ b/solution.py
@@ -12,7 +12,6 @@
 SUB = 512
 LANES = 128
 NEAR = 3
-SHIFTS = (0, 1, 2, 3, -1, -2, -3)
 BF16 = jnp.bfloat16
 F32 = jnp.float32
 VMEM_BYTES = 56 * 1024 * 1024
@@ -77,11 +76,41 @@
     return jnp.where(place < count, row, -1)
 
 
+def near_peers(me, peers):
+    after = lax.rem(me + 2, peers)
+    before = lax.rem(me + peers - 2, peers)
+    across = lax.rem(me + peers - 3 + 6 * (me & 1), peers)
+    return (me, me ^ 1, after, after ^ 1, before, before ^ 1, across)
+
+
+def write_near(refs, cap, lists):
+    mine, other, after, before, across = refs
+    mine[...] = lists[0]
+    other[...] = lists[1]
+    after[:cap, :] = lists[2]
+    after[cap:, :] = lists[3]
+    before[:cap, :] = lists[4]
+    before[cap:, :] = lists[5]
+    across[...] = lists[6]
+
+
+def read_near(refs, cap):
+    mine, other, from_before, from_after, across, core_before, core_after = refs
+    return [
+        mine[...],
+        other[...],
+        from_after[:cap, :],
+        core_after[cap:, :],
+        from_before[:cap, :],
+        core_before[cap:, :],
+        across[...],
+    ]
+
+
 def list_hots(me, rows_ref, grid_count, first):
     peers, cap = rows_ref.shape
     pieces = []
-    for shift in SHIFTS:
-        target = lax.rem(me + shift + peers, peers)
+    for target in near_peers(me, peers):
         pieces.append(hot_rows(rows_ref[pl.ds(target, 1), :], grid_count, first))
     peer = lax.broadcasted_iota(jnp.int32, (peers, cap), 0)
     ahead = lax.rem(peer - me + peers, peers)
@@ -92,32 +121,35 @@
 
 
 def gather_kernel(me_ref, rows_ref, grid_ref, *refs):
-    out_refs, total = refs[:-1], refs[-1]
+    near_refs, far_ref, total = refs[:5], refs[5], refs[6]
     cap = rows_ref.shape[1]
     step = pl.program_id(0)
     part = grid_ref.shape[0]
+    found = dot(list_hots(me_ref[0], rows_ref, part, step * part), grid_ref[...])
 
     @pl.when(step == 0)
     def _():
-        total[...] = jnp.zeros_like(total)
-
-    total[...] += dot(list_hots(me_ref[0], rows_ref, part, step * part), grid_ref[...])
+        total[...] = found
 
     @pl.when(step == pl.num_programs(0) - 1)
     def _():
-        for place, out_ref in enumerate(out_refs):
-            out_ref[...] = total[place * cap : (place + 1) * cap, :].astype(BF16)
+        rows = (total[...] + found).astype(BF16)
+        lists = [rows[at : at + cap] for at in range(0, 8 * cap, cap)]
+        write_near(near_refs, cap, lists)
+        for at in range(0, far_ref.shape[0], cap):
+            far_ref[at : at + cap, :] = lists[7]
 
 
 def scatter_kernel(skip, me_ref, rows_ref, *refs):
-    list_refs, far_refs, out_ref = refs[:7], refs[7:-1], refs[-1]
+    near_refs, far_ref, out_ref = refs[:7], refs[7], refs[8]
     part = out_ref.shape[0]
-    cap = rows_ref.shape[1]
+    peers, cap = rows_ref.shape
+    share = skip + cap
     hots = list_hots(me_ref[0], rows_ref, part, pl.program_id(0) * part)
-    far = far_refs[0][skip:, :].astype(F32)
-    for ref in far_refs[1:]:
-        far = far + ref[skip:, :].astype(F32)
-    values = jnp.concatenate([ref[...] for ref in list_refs] + [far.astype(BF16)], axis=0)
+    far = jnp.zeros((cap, out_ref.shape[1]), F32)
+    for at in range(skip, far_ref.shape[0], share):
+        far = far + far_ref[at : at + cap, :].astype(F32)
+    values = jnp.concatenate(read_near(near_refs, cap) + [far.astype(BF16)], axis=0)
     out_ref[...] = contract_rows(hots, values).astype(BF16)
 
 
@@ -141,36 +173,33 @@
 
 
 def split_out(me, peers, send_ref, keep_ref, parts):
-    upper = peers // 4
-    for upper_bits in range(upper):
-        for low_bits in range(4):
-            owner = me ^ (4 * upper_bits + low_bits)
-            target = send_ref if low_bits % 2 else keep_ref
-            start = 0
-            for ref, share, live in parts:
-                offset = pl.multiple_of(owner * share, 16)
-                piece = ref[pl.ds(offset, share), :]
-                if live:
+    for low in range(4):
+        target = send_ref if low % 2 else keep_ref
+        at = 0
+        for upper in range(peers // 4):
+            owner = 4 * upper + ((me & 3) ^ low)
+            for ref, share, far in parts:
+                piece = ref[pl.ds(pl.multiple_of(owner * share, 16), share), :]
+                if far:
                     ahead = lax.rem(owner - me + peers, peers)
                     apart = jnp.minimum(ahead, peers - ahead)
                     piece = jnp.where(apart > NEAR, piece.astype(F32), 0.0)
-                target[low_bits // 2, upper_bits, start : start + share, :] = piece.astype(BF16)
-                start += share
+                target[low // 2, at : at + share, :] = piece.astype(BF16)
+                at += share
 
 
 def forward_kernel(
     peers, me_ref, count_ref, src_ref, dst_ref, local_ref, edge_ref, *refs
 ):
-    lists = refs[:10]
-    (w_sender_ref, w_out_ref, w_node_in_ref, w_node_out_ref, mesh_ref, cotangent_ref) = refs[10:16]
-    (received_ref, hidden_ref, slope_ref, norm_ref, inverse_ref) = refs[16:21]
-    (send_ref, keep_ref, d_aggregate_ref, d_mesh_ref) = refs[21:25]
-    (slot_proj, aggregate, grad_in, grad_out) = refs[25:]
+    near_refs, far_refs = refs[:7], refs[7:11]
+    (w_sender_ref, w_out_ref, w_node_in_ref, w_node_out_ref, mesh_ref, cotangent_ref) = refs[11:17]
+    (received_ref, hidden_ref, slope_ref, norm_ref, inverse_ref) = refs[17:22]
+    (send_ref, keep_ref, d_aggregate_ref, d_mesh_ref) = refs[22:26]
+    (slot_proj, aggregate, grad_in, grad_out) = refs[26:]
     step = pl.program_id(0)
     me = me_ref[0]
-    cap = lists[0].shape[0]
+    cap = near_refs[0].shape[0]
     width = edge_ref.shape[1]
-    upper = peers // 4
 
     @pl.when(step == 0)
     def _():
@@ -182,20 +211,15 @@
             received_ref[pl.ds(offset, cap), :] = rows
             slot_proj[pl.ds(offset, cap), :] = projected
 
-        far = (lists[7], lists[8], lists[9])
-        for ref, low_bits in zip(far, ((0,), (2,), (1, 3))):
+        for low, ref in enumerate(far_refs):
             rows = ref[...]
             projected = dot(rows, w_sender).astype(BF16)
-            at = 0
-            for low in low_bits:
-                for upper_bits in range(upper):
-                    owner = me ^ (4 * upper_bits + low)
-                    place(owner, rows[at : at + cap], projected[at : at + cap])
-                    at += cap
-        rows = jnp.concatenate([ref[...] for ref in lists[:7]], axis=0)
+            for upper in range(peers // 4):
+                span = slice(upper * cap, (upper + 1) * cap)
+                place(4 * upper + ((me & 3) ^ low), rows[span], projected[span])
+        rows = jnp.concatenate(read_near(near_refs, cap), axis=0)
         projected = dot(rows, w_sender).astype(BF16)
-        for spot, shift in enumerate(SHIFTS):
-            owner = lax.rem(me - shift + peers, peers)
+        for spot, owner in enumerate(near_peers(me, peers)):
             place(owner, rows[spot * cap : (spot + 1) * cap], projected[spot * cap : (spot + 1) * cap])
 
     @pl.when(step * STEP < count_ref[0] * TILE)
@@ -249,8 +273,8 @@
     (hidden_ref, slope_ref, norm_ref, inverse_ref, d_aggregate_ref) = refs[:5]
     (received_ref, w_sender_ref, w_out_ref) = refs[5:8]
     (d_pre_ref, grad_sender_ref, send_ref, keep_ref) = refs[8:12]
-    near_refs = refs[12:19]
-    (slot_sum, grad_out, d_slots) = refs[19:]
+    near_refs = refs[12:17]
+    (slot_sum, grad_out, d_slots) = refs[17:]
     step = pl.program_id(0)
     me = me_ref[0]
 
@@ -285,9 +309,10 @@
         grad_sender_ref[...] = contract_rows(received_ref[...], summed)
         d_slots[...] = contract_cols(summed, w_sender_ref[...]).astype(BF16)
         cap = near_refs[0].shape[0]
-        for shift, ref in zip(SHIFTS, near_refs):
-            owner = lax.rem(me - shift + peers, peers)
-            ref[...] = d_slots[pl.ds(pl.multiple_of(owner * cap, 16), cap), :]
+        owners = near_peers(me, peers)
+        write_near(
+            near_refs, cap, [d_slots[pl.ds(pl.multiple_of(owner * cap, 16), cap), :] for owner in owners]
+        )
         split_out(
             me,
             peers,
@@ -334,6 +359,10 @@
         split_out(me_ref[0], peers, send_ref, keep_ref, ((grad_in, grad_in.shape[0] // peers, False),))
 
 
+def send(values, perm):
+    return lax.ppermute(values, "lon", perm)
+
+
 def by_xor(peers, bits):
     return [(peer, peer ^ bits) for peer in range(peers)]
 
@@ -342,8 +371,30 @@
     return [(peer, (peer + shift) % peers) for peer in range(peers)]
 
 
-def send(values, perm):
-    return lax.ppermute(values, "lon", perm)
+def across_chips(peers):
+    return [(peer, (peer + (3 if peer % 2 else -3)) % peers) for peer in range(peers)]
+
+
+def exchange_upper(peers, values):
+    groups = [list(range(low, peers, 4)) for low in range(4)]
+    return lax.all_to_all(
+        values, "lon", split_axis=0, concat_axis=0, axis_index_groups=groups, tiled=True
+    )
+
+
+def exchange_near(peers, lists):
+    mine, other, after, before, across = lists
+    return [
+        mine,
+        send(other, by_xor(peers, 1)),
+        send(after, by_shift(peers, 2)),
+        send(before, by_shift(peers, -2)),
+        send(across, across_chips(peers)),
+    ]
+
+
+def core_near(peers, near):
+    return list(near) + [send(near[2], by_xor(peers, 1)), send(near[3], by_xor(peers, 1))]
 
 
 def add(left, right):
@@ -356,21 +407,12 @@
 
 
 def next_sum(peers, outgoing, kept):
-    arrived = send(outgoing, by_xor(peers, 2))
-    return [add(kept[place], arrived[place]) for place in range(peers // 4)]
-
-
-def last_hop(peers, pieces):
-    return [pieces[0]] + [
-        send(pieces[place], by_xor(peers, 4 * place)) for place in range(1, peers // 4)
-    ]
-
-
-def total_of(terms, start, stop):
-    total = terms[0][start:stop].astype(F32)
-    for term in terms[1:]:
-        total = total + term[start:stop].astype(F32)
-    return total
+    return add(kept, send(outgoing, by_xor(peers, 2)))
+
+
+def total_of(peers, terms, start, stop):
+    blocks = terms.reshape(peers // 4, -1, terms.shape[1])
+    return jnp.sum(blocks[:, start:stop].astype(F32), axis=0)
 
 
 def whole(shape):
@@ -405,7 +447,6 @@
     dst = edge_dst.reshape(tiles, 1, STEP)
     smem = pl.BlockSpec(memory_space=pltpu.SMEM)
     params = pltpu.CompilerParams(vmem_limit_bytes=VMEM_BYTES)
-    one_list = jax.ShapeDtypeStruct((cap, width), BF16)
     square = (width, width)
 
     def tile_of(last):
@@ -417,16 +458,20 @@
         return pl.BlockSpec(square, lambda *_: (place, 0))
 
     def halves(share):
-        shape = (2, upper, share, width)
+        shape = (2, upper * share, width)
         return [jax.ShapeDtypeStruct(shape, BF16)] * 2, [whole(shape)] * 2
 
-    grid_part = grid_count // 4
+    grid_part = grid_count // 2
+    near_rows = (cap, cap, 2 * cap, 2 * cap, cap)
+    near_specs = [whole((count, width)) for count in near_rows]
+    near_shapes = [jax.ShapeDtypeStruct((count, width), BF16) for count in near_rows]
+    core_specs = near_specs + [whole((2 * cap, width))] * 2
     lists = pl.pallas_call(
         gather_kernel,
-        grid=(4,),
+        grid=(2,),
         in_specs=[smem, whole(rows.shape), pl.BlockSpec((grid_part, width), lambda step: (step, 0))],
-        out_specs=[whole((cap, width))] * 8,
-        out_shape=[one_list] * 8,
+        out_specs=near_specs + [whole((upper * cap, width))],
+        out_shape=near_shapes + [jax.ShapeDtypeStruct((upper * cap, width), BF16)],
         scratch_shapes=[pltpu.VMEM((8 * cap, width), F32)],
         compiler_params=params,
         name="gather_lists",
@@ -457,16 +502,15 @@
             name="edge_local",
         )(receivers, edge_latent, mesh_latent, w_edge_in, w_edge_in, *before)
 
-    hops = [send(lists[7], by_xor(peers, 4 * bits)) for bits in range(1, upper)]
-    near = [lists[0]] + [
-        send(lists[place], by_shift(peers, SHIFTS[place])) for place in range(1, 7)
-    ]
-    far_own = jnp.concatenate([lists[7]] + hops, axis=0)
+    far_own = exchange_upper(peers, lists[5])
+    near = exchange_near(peers, lists[:5])
     far_own, receivers = lax.optimization_barrier((far_own, dst))
     far_next = send(far_own, by_xor(peers, 2))
+    far_core = send(far_own, by_xor(peers, 1))
     local = local_part(0, tiles - 1)
-    far_next, near, local = lax.optimization_barrier((far_next, near, local))
-    far_core = send(jnp.concatenate([far_own, far_next], axis=0), by_xor(peers, 1))
+    far_next, far_core, near, local = lax.optimization_barrier((far_next, far_core, near, local))
+    near = core_near(peers, near)
+    far_both = send(far_next, by_xor(peers, 1))
     local = local_part(tiles - 1, 1, local)
 
     node_shape, node_spec = halves(w_node_in.shape[0] // peers + w_node_out.shape[0] // peers)
@@ -474,9 +518,8 @@
         functools.partial(forward_kernel, peers),
         grid=(tiles,),
         in_specs=[smem, smem, index_tile, index_tile, tile_of(width), tile_of(width)]
-        + [whole((cap, width))] * 7
-        + [whole((upper * cap, width))] * 2
-        + [whole((2 * upper * cap, width))]
+        + core_specs
+        + [whole((upper * cap, width))] * 4
         + [weight(1)]
         + [whole(w.shape) for w in (w_edge_out, w_node_in, w_node_out, mesh_latent, mesh_cotangent)],
         out_specs=[whole((slots, width))]
@@ -506,8 +549,9 @@
         edge_latent,
         *near,
         far_own,
+        far_core,
         far_next,
-        far_core,
+        far_both,
         w_edge_in,
         w_edge_out,
         w_node_in,
@@ -524,10 +568,10 @@
         in_specs=[smem, smem, index_tile, index_tile]
         + [tile_of(width)] * 3
         + [tile_of(1), whole((mesh_count, width)), whole((slots, width)), weight(1), whole(square)],
-        out_specs=[tile_of(width), whole(square)] + slot_spec + [whole((cap, width))] * 7,
+        out_specs=[tile_of(width), whole(square)] + slot_spec + near_specs,
         out_shape=[jax.ShapeDtypeStruct((edges, width), BF16), jax.ShapeDtypeStruct(square, F32)]
         + slot_shape
-        + [one_list] * 7,
+        + near_shapes,
         scratch_shapes=[
             pltpu.VMEM((slots, width), F32),
             pltpu.VMEM(square, F32),
@@ -547,9 +591,7 @@
     )
     node_pieces = next_sum(peers, node_next, node_kept)
     slot_next, slot_kept = core_sum(peers, slot_send, slot_keep)
-    returned = [returns[0]] + [
-        send(returns[place], by_shift(peers, -SHIFTS[place])) for place in range(1, 7)
-    ]
+    returned = exchange_near(peers, returns)
 
     edge_shape, edge_spec = halves(w_edge_in.shape[0] // peers)
     edge_grad, mesh_grad, edge_send, edge_keep = pl.pallas_call(
@@ -590,32 +632,33 @@
         (node_pieces, slot_next, slot_kept, edge_send, edge_keep)
     )
     slot_pieces = next_sum(peers, slot_next, slot_kept)
-    node_terms = last_hop(peers, node_pieces)
     edge_next, edge_kept = core_sum(peers, edge_send, edge_keep)
-    slot_terms = last_hop(peers, slot_pieces)
+    node_terms = exchange_upper(peers, node_pieces)
+    returned = core_near(peers, returned)
     edge_pieces = next_sum(peers, edge_next, edge_kept)
-    edge_terms = last_hop(peers, edge_pieces)
+    slot_terms = exchange_upper(peers, slot_pieces)
+    edge_terms = exchange_upper(peers, edge_pieces)
     node_rows = w_node_in.shape[0] // peers
     out_rows = w_edge_out.shape[0] // peers
     grid_grad = pl.pallas_call(
         functools.partial(scatter_kernel, out_rows),
-        grid=(4,),
+        grid=(2,),
         in_specs=[smem, whole(rows.shape)]
-        + [whole((cap, width))] * 7
-        + [whole((out_rows + cap, width))] * upper,
+        + core_specs
+        + [whole((upper * (out_rows + cap), width))],
         out_specs=pl.BlockSpec((grid_part, width), lambda step: (step, 0)),
         out_shape=jax.ShapeDtypeStruct((grid_count, width), BF16),
         compiler_params=params,
         name="scatter_lists",
-    )(me, rows, *returned, *slot_terms)
+    )(me, rows, *returned, slot_terms)
     return (
         grid_grad,
         edge_grad,
         mesh_grad,
-        total_of(edge_terms, 0, w_edge_in.shape[0] // peers),
-        total_of(slot_terms, 0, out_rows),
-        total_of(node_terms, 0, node_rows),
-        total_of(node_terms, node_rows, node_rows + w_node_out.shape[0] // peers),
+        total_of(peers, edge_terms, 0, w_edge_in.shape[0] // peers),
+        total_of(peers, slot_terms, 0, out_rows),
+        total_of(peers, node_terms, 0, node_rows),
+        total_of(peers, node_terms, node_rows, node_rows + w_node_out.shape[0] // peers),
     )
 
 

time: 129 us -> 137 us (1.062)
  starting transfers between devices: 45.4 us -> 36.2 us
  waiting for transfers between devices: 20.7 us -> 29.7 us
  Pallas kernels: 54.7 us -> 60.9 us
  other arithmetic: 4.45 us -> 6.62 us
    ppermute x32 -> x21, starting transfers between devices: 45.4 us -> 18.7 us  [send(): return lax.ppermute(values, 'lon', perm)]
    all_to_all x0 -> x4, starting transfers between devices: none -> 17.5 us  [exchange_upper(): lax.all_to_all(values, 'lon', split_axis=0, concat_axis=0, axis_index_gro...]
    all_to_all x0 -> x4, waiting for transfers between devices: none -> 14.8 us  [exchange_upper(): lax.all_to_all(values, 'lon', split_axis=0, concat_axis=0, axis_index_gro...]
    ppermute x32 -> x21, waiting for transfers between devices: 20.7 us -> 14.9 us  [send(): return lax.ppermute(values, 'lon', perm)]
    reduce_sum x0 -> x4, other arithmetic: none -> 3.62 us  [total_of(): return jnp.sum(blocks[:, start:stop].astype(F32), axis=0)]
    pallas_call x1, Pallas kernels: 12.1 us -> 15.5 us  [on_device(): pl.pallas_call(functools.partial(slots_kernel, peers), grid=(tiles,), in_...]
    pallas_call x1, Pallas kernels: 14.7 us -> 17.6 us  [on_device(): pl.pallas_call(functools.partial(forward_kernel, peers), grid=(tiles,), i...]
    add x4 -> x0, other arithmetic: 2.72 us -> none  [total_of(): total = total + term[start:stop].astype(F32)]
  transfers between devices with their start and end apart: 32 -> 25, of which waited for: 7 -> 6; matrix products, arithmetic and copies ran while one was open for 3% -> 4% of each run, Pallas kernels for 28% -> 29%
where the time goes in v3:
time: 137 us
  Pallas kernels  60.9 us (44%)
  starting transfers between devices  36.2 us (26%)
  waiting for transfers between devices  29.7 us (22%)
  other arithmetic  6.62 us (5%)
  between operations  1.67 us (1%)
  local copies, waits for them, and re-layouts  1.65 us (1%)
    ppermute x21, starting transfers between devices, send(): return lax.ppermute(values, 'lon', perm)  18.7 us
    pallas_call x1, Pallas kernels, on_device(): pl.pallas_call(functools.partial(forward_kernel, peers), grid=(tiles,), i...  17.6 us
    all_to_all x4, starting transfers between devices, exchange_upper(): lax.all_to_all(values, 'lon', split_axis=0, concat_axis=0, axis_index_gro...  17.5 us
    pallas_call x1, Pallas kernels, on_device(): pl.pallas_call(functools.partial(slots_kernel, peers), grid=(tiles,), in_...  15.5 us
    ppermute x21, waiting for transfers between devices, send(): return lax.ppermute(values, 'lon', perm)  14.9 us
    all_to_all x4, waiting for transfers between devices, exchange_upper(): lax.all_to_all(values, 'lon', split_axis=0, concat_axis=0, axis_index_gro...  14.8 us
    pallas_call x1, Pallas kernels, on_device(): pl.pallas_call(functools.partial(edges_kernel, peers), grid=(tiles,), in_...  11.1 us
    pallas_call x2, Pallas kernels, local_part(): pl.pallas_call(local_kernel, grid=(count,), in_specs=[pl.BlockSpec((1, 1,...  9.33 us
  transfers between devices with their start and end apart: 25, of which 6 were waited for; matrix products, arithmetic and copies ran while one was open for 4% of the time, Pallas kernels for 29%

profile of v3, /device:TPU:0, one launch (start us, length us, event | category | flops | bytes accessed | tf_op | source)
XLA Modules:
  0.0 136.8 jit_solution(13563705800667468957)
XLA Ops:
  0.6 3.4 %gather_lists.1 = (bf16[48,512]{1,0:T(8,128)(2,1)}, bf16[48,512]{1,0:T(8,128)(2,1)}, bf16[96,512]{1,0:T(8,128)(2,1)}, bf16[96,512]{1,0:T(8,128)(2,1)}, bf16[48,5...) custom-call(s32[1]{0:T(128)} %bitcast.me_ref, s32[16,48]{1,0:T(8,128)} %bitcast.35, bf16[2048,512]{1,0:T(8,128)(2,1)} %grid_ref.1), custom_call_target="tpu_custom_call" | custom-call | tf_op jit(solution)/shard_map/gather_lists/pallas_call | solution.py:469
  4.1 6.3 %all-to-all-start = ((bf16[4,48,512]{2,1,0:T(8,128)(2,1)}), bf16[4,48,512]{2,1,0:T(8,128)(2,1)S(1)}, u32[]{:S(2)}, u32[]{:S(2)}) async-start(bf16[4,48,512]{2,1,0:T(8,128)(2,1)} %bitcast.29), calls=%async_computation | async-start | bytes 393216 | tf_op jit(solution)/shard_map/all_to_all | solution.py:380
  10.4 7.5 %all-to-all-done = bf16[4,48,512]{2,1,0:T(8,128)(2,1)S(1)} async-done(((bf16[4,48,512]{2,1,0:T(8,128)(2,1)}), bf16[4,48,512]{2,1,0:T(8,128)(2,1)S(1)}, u32[]{:S(2)}, u32[]{:S(2)}) %all-to-all-start) | async-done | bytes 196640 | tf_op jit(solution)/shard_map/all_to_all | solution.py:380
  17.9 1.5 %collective-permute-start = (bf16[192,512]{1,0:T(8,128)(2,1)S(1)}, bf16[192,512]{1,0:T(8,128)(2,1)S(1)}, u32[]{:S(2)}, u32[]{:S(2)}) collective-permute-start(bf16[192,512]{1,0:T(8,128)(2,1)S(1)} %bitcast.27), channel_id=1, source_target_pairs={{0,2},{1,3},{2,0},{3,1},{4,6},{5,7},{6,4},{7,5},{8,10},{9,11},{10,... | collective-permute-start | bytes 589832 | tf_op jit(solution)/shard_map/ppermute | solution.py:363
  19.4 1.2 collective-permute-start.5
  21.2 4.2 %collective-permute-start.4 = (bf16[96,512]{1,0:T(8,128)(2,1)}, bf16[96,512]{1,0:T(8,128)(2,1)S(1)}, u32[]{:S(2)}, u32[]{:S(2)}) collective-permute-start(bf16[96,512]{1,0:T(8,128)(2,1)} %get-tuple-element.66), channel_id=1, source_target_pairs={{0,14},{1,15},{2,0},{3,1},{4,2},{5,3},{6,4},{7,5},{8,6},{9,7},{10,... | collective-permute-start | bytes 294920 | tf_op jit(solution)/shard_map/ppermute | solution.py:363
  25.4 5.5 %edge_local.2.refs_0_ = bf16[3072,512]{1,0:T(8,128)(2,1)} custom-call(s32[3,1,1024]{2,1,0:T(1,128)} %bitcast.30, bf16[3072,512]{1,0:T(8,128)(2,1)} %refs_0_.1, bf16[256,512]{1,0:T(8,128)(2,1)} %refs_4_.1, bf16[1536,512]{1,0:T(8,128)(2,1)} %refs_7_.3, bf16[1536,512]{1,0:T(8,128)(2,1)} %refs_7_.3), custom_call_target="tpu_custom_call" | custom-call | flops 1610612736 | bytes 4194304 | tf_op jit(solution)/shard_map/edge_local/pallas_call | solution.py:481
  32.3 3.9 %edge_local.3.local_ref = bf16[3072,512]{1,0:T(8,128)(2,1)} custom-call(s32[3,1,1024]{2,1,0:T(1,128)} %bitcast.31, bf16[3072,512]{1,0:T(8,128)(2,1)} %refs_0_.1, bf16[256,512]{1,0:T(8,128)(2,1)} %refs_4_.1, bf16[1536,512]{1,0:T(8,128)(2,1)} %refs_7_.3, bf16[1536,512]{1,0:T(8,128)(2,1)} %refs_7_.3, ...), custom_call_target="tpu_custom_call", output_to_operand_aliasing={{}: (5, {})} | custom-call | flops 805306368 | bytes 2097152 | tf_op jit(solution)/shard_map/edge_local/pallas_call | solution.py:481
  36.9 17.6 %forward.1 = (bf16[768,512]{1,0:T(8,128)(2,1)}, bf16[3072,512]{1,0:T(8,128)(2,1)}, bf16[3072,512]{1,0:T(8,128)(2,1)}, bf16[3072,512]{1,0:T(8,128)(2,1)}, f32[307...) custom-call(s32[1]{0:T(128)} %bitcast.me_ref, ...), custom_call_target="tpu_custom_call" | custom-call | tf_op jit(solution)/shard_map/forward/pallas_call | solution.py:517
  55.0 15.5 %backward_slots.1 = (bf16[3072,512]{1,0:T(8,128)(2,1)}, f32[512,512]{1,0:T(8,128)}, bf16[2,320,512]{2,1,0:T(8,128)(2,1)}, bf16[2,320,512]{2,1,0:T(8,128)(2,1)}, ...) custom-call(s32[1]{0:T(128)} %bitcast.me_ref, ...), custom_call_target="tpu_custom_call" | custom-call | flops 6442450944 | bytes 12582912 | tf_op jit(solution)/shard_map/backward_slots/pallas_call | solution.py:565
  71.0 11.1 %backward_edges.1 = (bf16[3072,512]{1,0:T(8,128)(2,1)}, bf16[256,512]{1,0:T(8,128)(2,1)}, bf16[2,384,512]{2,1,0:T(8,128)(2,1)}, bf16[2,384,512]{2,1,0:T(8,128)(2,1)}) custom-call(s32[1]{0:T(128)} %bitcast.me_ref, s32[1]{0:T(128)S(6)} %copy.21.count_ref, s32[3,1,1024]{2,1,0:T(1,128)} %bitcast.34, bf16[3072,512]{1,0:T(8,128)(2,1)} %refs_0_.1, ...), custom_call_target="tpu_custom_call" | custom-call | flops 4831838208 | bytes 9437184 | tf_op jit(solution)/shard_map/backward_edges/pallas_call | solution.py:597
  83.7 3.5 %all-to-all-start.3 = ((bf16[4,96,512]{2,1,0:T(8,128)(2,1)}), bf16[4,96,512]{2,1,0:T(8,128)(2,1)S(1)}, u32[]{:S(2)}, u32[]{:S(2)}) async-start(bf16[4,96,512]{2,1,0:T(8,128)(2,1)} %bitcast.15), calls=%async_computation.3 | async-start | bytes 786432 | tf_op jit(solution)/shard_map/all_to_all | solution.py:380
  87.6 1.9 %collective-permute-start.20 = (bf16[384,512]{1,0:T(8,128)(2,1)S(1)}, bf16[384,512]{1,0:T(8,128)(2,1)S(1)}, u32[]{:S(2)}, u32[]{:S(2)}) collective-permute-start(bf16[384,512]{1,0:T(8,128)(2,1)S(1)} %fusion.4), channel_id=1, source_target_pairs={{0,2},{1,3},{2,0},{3,1},{4,6},{5,7},{6,4},{7,5},{8,10},{9,11},{10,... | collective-permute-start | bytes 1179656 | tf_op jit(solution)/shard_map/ppermute | solution.py:363
  89.5 8.4 %collective-permute-done.18 = bf16[320,512]{1,0:T(8,128)(2,1)S(1)} collective-permute-done((bf16[320,512]{1,0:T(8,128)(2,1)S(1)}, bf16[320,512]{1,0:T(8,128)(2,1)S(1)}, u32[]{:S(2)}, u32[]{:S(2)}) %collective-permute-start.18) | collective-permute-done | bytes 327712 | tf_op jit(solution)/shard_map/ppermute | solution.py:363
  99.4 4.3 %all-to-all-start.1 = ((bf16[4,80,512]{2,1,0:T(8,128)(2,1)}), bf16[4,80,512]{2,1,0:T(8,128)(2,1)S(1)}, u32[]{:S(2)}, u32[]{:S(2)}) async-start(bf16[4,80,512]{2,1,0:T(8,128)(2,1)} %bitcast.10), calls=%async_computation.1 | async-start | bytes 655360 | tf_op jit(solution)/shard_map/all_to_all | solution.py:380
  103.7 1.8 %collective-permute-done.20 = bf16[384,512]{1,0:T(8,128)(2,1)S(1)} collective-permute-done((bf16[384,512]{1,0:T(8,128)(2,1)S(1)}, bf16[384,512]{1,0:T(8,128)(2,1)S(1)}, u32[]{:S(2)}, u32[]{:S(2)}) %collective-permute-start.20) | collective-permute-done | bytes 393248 | tf_op jit(solution)/shard_map/ppermute | solution.py:363
  105.4 0.9 fusion
  106.3 6.5 %all-to-all-done.1 = bf16[4,80,512]{2,1,0:T(8,128)(2,1)S(1)} async-done(((bf16[4,80,512]{2,1,0:T(8,128)(2,1)}), bf16[4,80,512]{2,1,0:T(8,128)(2,1)S(1)}, u32[]{:S(2)}, u32[]{:S(2)}) %all-to-all-start.1) | async-done | bytes 327712 | tf_op jit(solution)/shard_map/all_to_all | solution.py:380
  112.9 3.5 %all-to-all-start.2 = ((bf16[4,96,512]{2,1,0:T(8,128)(2,1)}), bf16[4,96,512]{2,1,0:T(8,128)(2,1)S(1)}, u32[]{:S(2)}, u32[]{:S(2)}) async-start(bf16[4,96,512]{2,1,0:T(8,128)(2,1)} %bitcast.14), calls=%async_computation.2 | async-start | bytes 786432 | tf_op jit(solution)/shard_map/all_to_all | solution.py:380
  117.0 4.2 %collective-permute-start.12 = (bf16[96,512]{1,0:T(8,128)(2,1)S(1)}, bf16[96,512]{1,0:T(8,128)(2,1)S(1)}, u32[]{:S(2)}, u32[]{:S(2)}) collective-permute-start(bf16[96,512]{1,0:T(8,128)(2,1)S(1)} %copy-done.21), channel_id=1, source_target_pairs={{0,14},{1,15},{2,0},{3,1},{4,2},{5,3},{6,4},{7,5},{8,6},{9,7},{10,... | collective-permute-start | bytes 294920 | tf_op jit(solution)/shard_map/ppermute | solution.py:363
  121.1 2.0 %collective-permute-start.13 = (bf16[48,512]{1,0:T(8,128)(2,1)S(1)}, bf16[48,512]{1,0:T(8,128)(2,1)S(1)}, u32[]{:S(2)}, u32[]{:S(2)}) collective-permute-start(bf16[48,512]{1,0:T(8,128)(2,1)S(1)} %copy-done.23), channel_id=1, source_target_pairs={{0,13},{1,4},{2,15},{3,6},{4,1},{5,8},{6,3},{7,10},{8,5},{9,12},{1... | collective-permute-start | bytes 147464 | tf_op jit(solution)/shard_map/ppermute | solution.py:363
  123.2 4.7 %collective-permute-done.11.refs_2_ = bf16[96,512]{1,0:T(8,128)(2,1)S(1)} collective-permute-done((bf16[96,512]{1,0:T(8,128)(2,1)S(1)}, bf16[96,512]{1,0:T(8,128)(2,1)S(1)}, u32[]{:S(2)}, u32[]{:S(2)}) %collective-permute-start.11) | collective-permute-done | bytes 98336 | tf_op jit(solution)/shard_map/ppermute | solution.py:363
  130.5 4.0 %scatter_lists.1 = bf16[2048,512]{1,0:T(8,128)(2,1)} custom-call(s32[1]{0:T(128)} %bitcast.me_ref, s32[16,48]{1,0:T(8,128)} %bitcast.36, bf16[48,512]{1,0:T(8,128)(2,1)} %get-tuple-element.92.refs_0_, bf16[48,512]{1,0:T(8,128)(2,1)} %copy-done.18, bf16[96,512]{1,0:T(8,128)(2,1)} %copy-done.12, bf16[96,512]{1,0:T(8,128)(2,1)} %copy-done.13, ...), custom_call_target="tpu_custom_call" | custom-call | tf_op jit(solution)/shard_map/scatter_lists/pallas_call | solution.py:643
  134.5 1.6 %convert_reduce_fusion.3 = f32[32,512]{1,0:T(8,128)} fusion(bf16[4,80,512]{2,1,0:T(8,128)(2,1)} %copy-done), kind=kLoop, calls=%fused_computation.19 | loop fusion | flops 114688 | bytes 196608 | tf_op jit(solution)/shard_map/reduce_sum | solution.py:415
  (93 shorter events, 10.2 us)
Async XLA Ops:
  4.1 13.8 %all-to-all-start = ((bf16[4,48,512]{2,1,0:T(8,128)(2,1)}), bf16[4,48,512]{2,1,0:T(8,128)(2,1)S(1)}, u32[]{:S(2)}, u32[]{:S(2)}) async-start(bf16[4,48,512]{2,1,0:T(8,128)(2,1)} %bitcast.29), calls=%async_computation | async-start | bytes 393216 | tf_op jit(solution)/shard_map/all_to_all | solution.py:380
  10.4 10.8 %collective-permute-start.2 = (bf16[48,512]{1,0:T(8,128)(2,1)}, bf16[48,512]{1,0:T(8,128)(2,1)S(1)}, u32[]{:S(2)}, u32[]{:S(2)}) collective-permute-start(bf16[48,512]{1,0:T(8,128)(2,1)} %get-tuple-element.64), channel_id=1, source_target_pairs={{0,1},{1,0},{2,3},{3,2},{4,5},{5,4},{6,7},{7,6},{8,9},{9,8},{10,11... | collective-permute-start | bytes 147464 | tf_op jit(solution)/shard_map/ppermute | solution.py:363
  17.9 13.0 %collective-permute-start.1 = (bf16[192,512]{1,0:T(8,128)(2,1)S(1)}, bf16[192,512]{1,0:T(8,128)(2,1)S(1)}, u32[]{:S(2)}, u32[]{:S(2)}) collective-permute-start(bf16[192,512]{1,0:T(8,128)(2,1)S(1)} %bitcast.26), channel_id=1, source_target_pairs={{0,1},{1,0},{2,3},{3,2},{4,5},{5,4},{6,7},{7,6},{8,9},{9,8},{10,11... | collective-permute-start | bytes 589832 | tf_op jit(solution)/shard_map/ppermute | solution.py:363
  17.9 13.0 %collective-permute-start = (bf16[192,512]{1,0:T(8,128)(2,1)S(1)}, bf16[192,512]{1,0:T(8,128)(2,1)S(1)}, u32[]{:S(2)}, u32[]{:S(2)}) collective-permute-start(bf16[192,512]{1,0:T(8,128)(2,1)S(1)} %bitcast.27), channel_id=1, source_target_pairs={{0,2},{1,3},{2,0},{3,1},{4,6},{5,7},{6,4},{7,5},{8,10},{9,11},{10,... | collective-permute-start | bytes 589832 | tf_op jit(solution)/shard_map/ppermute | solution.py:363
  19.4 11.4 %collective-permute-start.5 = (bf16[48,512]{1,0:T(8,128)(2,1)}, bf16[48,512]{1,0:T(8,128)(2,1)S(1)}, u32[]{:S(2)}, u32[]{:S(2)}) collective-permute-start(bf16[48,512]{1,0:T(8,128)(2,1)} %get-tuple-element.67), channel_id=1, source_target_pairs={{0,13},{1,4},{2,15},{3,6},{4,1},{5,8},{6,3},{7,10},{8,5},{9,12},{1... | collective-permute-start | bytes 147464 | tf_op jit(solution)/shard_map/ppermute | solution.py:363
  20.7 10.2 %collective-permute-start.3 = (bf16[96,512]{1,0:T(8,128)(2,1)}, bf16[96,512]{1,0:T(8,128)(2,1)S(1)}, u32[]{:S(2)}, u32[]{:S(2)}) collective-permute-start(bf16[96,512]{1,0:T(8,128)(2,1)} %get-tuple-element.65), channel_id=1, source_target_pairs={{0,2},{1,3},{2,4},{3,5},{4,6},{5,7},{6,8},{7,9},{8,10},{9,11},{10,... | collective-permute-start | bytes 294920 | tf_op jit(solution)/shard_map/ppermute | solution.py:363
  21.2 9.7 %collective-permute-start.4 = (bf16[96,512]{1,0:T(8,128)(2,1)}, bf16[96,512]{1,0:T(8,128)(2,1)S(1)}, u32[]{:S(2)}, u32[]{:S(2)}) collective-permute-start(bf16[96,512]{1,0:T(8,128)(2,1)} %get-tuple-element.66), channel_id=1, source_target_pairs={{0,14},{1,15},{2,0},{3,1},{4,2},{5,3},{6,4},{7,5},{8,6},{9,7},{10,... | collective-permute-start | bytes 294920 | tf_op jit(solution)/shard_map/ppermute | solution.py:363
  31.0 5.3 %collective-permute-start.8 = (bf16[192,512]{1,0:T(8,128)(2,1)S(1)}, bf16[192,512]{1,0:T(8,128)(2,1)S(1)}, u32[]{:S(2)}, u32[]{:S(2)}) collective-permute-start(bf16[192,512]{1,0:T(8,128)(2,1)S(1)} %collective-permute-done.refs_9_), channel_id=1, source_target_pairs={{0,1},{1,0},{2,3},{3,2},{4,5},{5,4},{6,7},{7,6},{8,9},{9,8},{10,11... | collective-permute-start | bytes 589832 | tf_op jit(solution)/shard_map/ppermute | solution.py:363
  31.0 5.1 %collective-permute-start.6 = (bf16[96,512]{1,0:T(8,128)(2,1)S(1)}, bf16[96,512]{1,0:T(8,128)(2,1)S(1)}, u32[]{:S(2)}, u32[]{:S(2)}) collective-permute-start(bf16[96,512]{1,0:T(8,128)(2,1)S(1)} %collective-permute-done.3.refs_2_), channel_id=1, source_target_pairs={{0,1},{1,0},{2,3},{3,2},{4,5},{5,4},{6,7},{7,6},{8,9},{9,8},{10,11... | collective-permute-start | bytes 294920 | tf_op jit(solution)/shard_map/ppermute | solution.py:363
  31.5 4.7 %collective-permute-start.7 = (bf16[96,512]{1,0:T(8,128)(2,1)S(1)}, bf16[96,512]{1,0:T(8,128)(2,1)S(1)}, u32[]{:S(2)}, u32[]{:S(2)}) collective-permute-start(bf16[96,512]{1,0:T(8,128)(2,1)S(1)} %collective-permute-done.4.refs_3_), channel_id=1, source_target_pairs={{0,1},{1,0},{2,3},{3,2},{4,5},{5,4},{6,7},{7,6},{8,9},{9,8},{10,11... | collective-permute-start | bytes 294920 | tf_op jit(solution)/shard_map/ppermute | solution.py:363
  54.5 16.0 %collective-permute-start.9 = (bf16[2,384,512]{2,1,0:T(8,128)(2,1)}, bf16[2,384,512]{2,1,0:T(8,128)(2,1)S(1)}, u32[]{:S(2)}, u32[]{:S(2)}) collective-permute-start(bf16[2,384,512]{2,1,0:T(8,128)(2,1)} %get-tuple-element.77), channel_id=1, source_target_pairs={{0,1},{1,0},{2,3},{3,2},{4,5},{5,4},{6,7},{7,6},{8,9},{9,8},{10,11... | collective-permute-start | bytes 2359304 | tf_op jit(solution)/shard_map/ppermute | solution.py:363
  70.7 11.4 %collective-permute-start.16 = (bf16[384,512]{1,0:T(8,128)(2,1)S(1)}, bf16[384,512]{1,0:T(8,128)(2,1)S(1)}, u32[]{:S(2)}, u32[]{:S(2)}) collective-permute-start(bf16[384,512]{1,0:T(8,128)(2,1)S(1)} %get-tuple-element.98), channel_id=1, source_target_pairs={{0,2},{1,3},{2,0},{3,1},{4,6},{5,7},{6,4},{7,5},{8,10},{9,11},{10,... | collective-permute-start | bytes 1179656 | tf_op jit(solution)/shard_map/ppermute | solution.py:363
  70.8 12.1 %collective-permute-start.17 = (bf16[2,320,512]{2,1,0:T(8,128)(2,1)}, bf16[2,320,512]{2,1,0:T(8,128)(2,1)S(1)}, u32[]{:S(2)}, u32[]{:S(2)}) collective-permute-start(bf16[2,320,512]{2,1,0:T(8,128)(2,1)} %get-tuple-element.100), channel_id=1, source_target_pairs={{0,1},{1,0},{2,3},{3,2},{4,5},{5,4},{6,7},{7,6},{8,9},{9,8},{10,11... | collective-permute-start | bytes 1966088 | tf_op jit(solution)/shard_map/ppermute | solution.py:363
  83.4 4.1 %collective-permute-start.19 = (bf16[2,384,512]{2,1,0:T(8,128)(2,1)S(1)}, bf16[2,384,512]{2,1,0:T(8,128)(2,1)S(1)}, u32[]{:S(2)}, u32[]{:S(2)}) collective-permute-start(bf16[2,384,512]{2,1,0:T(8,128)(2,1)S(1)} %copy-done.20), channel_id=1, source_target_pairs={{0,1},{1,0},{2,3},{3,2},{4,5},{5,4},{6,7},{7,6},{8,9},{9,8},{10,11... | collective-permute-start | bytes 2359304 | tf_op jit(solution)/shard_map/ppermute | solution.py:363
  83.7 15.7 %all-to-all-start.3 = ((bf16[4,96,512]{2,1,0:T(8,128)(2,1)}), bf16[4,96,512]{2,1,0:T(8,128)(2,1)S(1)}, u32[]{:S(2)}, u32[]{:S(2)}) async-start(bf16[4,96,512]{2,1,0:T(8,128)(2,1)} %bitcast.15), calls=%async_computation.3 | async-start | bytes 786432 | tf_op jit(solution)/shard_map/all_to_all | solution.py:380
  87.2 10.6 %collective-permute-start.18 = (bf16[320,512]{1,0:T(8,128)(2,1)S(1)}, bf16[320,512]{1,0:T(8,128)(2,1)S(1)}, u32[]{:S(2)}, u32[]{:S(2)}) collective-permute-start(bf16[320,512]{1,0:T(8,128)(2,1)S(1)} %get-tuple-element.107), channel_id=1, source_target_pairs={{0,2},{1,3},{2,0},{3,1},{4,6},{5,7},{6,4},{7,5},{8,10},{9,11},{10,... | collective-permute-start | bytes 983048 | tf_op jit(solution)/shard_map/ppermute | solution.py:363
  87.6 17.9 %collective-permute-start.20 = (bf16[384,512]{1,0:T(8,128)(2,1)S(1)}, bf16[384,512]{1,0:T(8,128)(2,1)S(1)}, u32[]{:S(2)}, u32[]{:S(2)}) collective-permute-start(bf16[384,512]{1,0:T(8,128)(2,1)S(1)} %fusion.4), channel_id=1, source_target_pairs={{0,2},{1,3},{2,0},{3,1},{4,6},{5,7},{6,4},{7,5},{8,10},{9,11},{10,... | collective-permute-start | bytes 1179656 | tf_op jit(solution)/shard_map/ppermute | solution.py:363
  99.4 13.4 %all-to-all-start.1 = ((bf16[4,80,512]{2,1,0:T(8,128)(2,1)}), bf16[4,80,512]{2,1,0:T(8,128)(2,1)S(1)}, u32[]{:S(2)}, u32[]{:S(2)}) async-start(bf16[4,80,512]{2,1,0:T(8,128)(2,1)} %bitcast.10), calls=%async_computation.1 | async-start | bytes 655360 | tf_op jit(solution)/shard_map/all_to_all | solution.py:380
  112.9 23.2 %all-to-all-start.2 = ((bf16[4,96,512]{2,1,0:T(8,128)(2,1)}), bf16[4,96,512]{2,1,0:T(8,128)(2,1)S(1)}, u32[]{:S(2)}, u32[]{:S(2)}) async-start(bf16[4,96,512]{2,1,0:T(8,128)(2,1)} %bitcast.14), calls=%async_computation.2 | async-start | bytes 786432 | tf_op jit(solution)/shard_map/all_to_all | solution.py:380
  116.3 11.6 %collective-permute-start.11 = (bf16[96,512]{1,0:T(8,128)(2,1)S(1)}, bf16[96,512]{1,0:T(8,128)(2,1)S(1)}, u32[]{:S(2)}, u32[]{:S(2)}) collective-permute-start(bf16[96,512]{1,0:T(8,128)(2,1)S(1)} %copy-done.22), channel_id=1, source_target_pairs={{0,2},{1,3},{2,4},{3,5},{4,6},{5,7},{6,8},{7,9},{8,10},{9,11},{10,... | collective-permute-start | bytes 294920 | tf_op jit(solution)/shard_map/ppermute | solution.py:363
  117.0 11.0 %collective-permute-start.12 = (bf16[96,512]{1,0:T(8,128)(2,1)S(1)}, bf16[96,512]{1,0:T(8,128)(2,1)S(1)}, u32[]{:S(2)}, u32[]{:S(2)}) collective-permute-start(bf16[96,512]{1,0:T(8,128)(2,1)S(1)} %copy-done.21), channel_id=1, source_target_pairs={{0,14},{1,15},{2,0},{3,1},{4,2},{5,3},{6,4},{7,5},{8,6},{9,7},{10,... | collective-permute-start | bytes 294920 | tf_op jit(solution)/shard_map/ppermute | solution.py:363
  121.1 8.7 %collective-permute-start.10 = (bf16[48,512]{1,0:T(8,128)(2,1)S(1)}, bf16[48,512]{1,0:T(8,128)(2,1)S(1)}, u32[]{:S(2)}, u32[]{:S(2)}) collective-permute-start(bf16[48,512]{1,0:T(8,128)(2,1)S(1)} %copy-done.24), channel_id=1, source_target_pairs={{0,1},{1,0},{2,3},{3,2},{4,5},{5,4},{6,7},{7,6},{8,9},{9,8},{10,11... | collective-permute-start | bytes 147464 | tf_op jit(solution)/shard_map/ppermute | solution.py:363
  121.1 8.6 %collective-permute-start.13 = (bf16[48,512]{1,0:T(8,128)(2,1)S(1)}, bf16[48,512]{1,0:T(8,128)(2,1)S(1)}, u32[]{:S(2)}, u32[]{:S(2)}) collective-permute-start(bf16[48,512]{1,0:T(8,128)(2,1)S(1)} %copy-done.23), channel_id=1, source_target_pairs={{0,13},{1,4},{2,15},{3,6},{4,1},{5,8},{6,3},{7,10},{8,5},{9,12},{1... | collective-permute-start | bytes 147464 | tf_op jit(solution)/shard_map/ppermute | solution.py:363
  127.9 1.9 %collective-permute-start.15 = (bf16[96,512]{1,0:T(8,128)(2,1)S(1)}, bf16[96,512]{1,0:T(8,128)(2,1)S(1)}, u32[]{:S(2)}, u32[]{:S(2)}) collective-permute-start(bf16[96,512]{1,0:T(8,128)(2,1)S(1)} %collective-permute-done.12.refs_3_), channel_id=1, source_target_pairs={{0,1},{1,0},{2,3},{3,2},{4,5},{5,4},{6,7},{7,6},{8,9},{9,8},{10,11... | collective-permute-start | bytes 294920 | tf_op jit(solution)/shard_map/ppermute | solution.py:363
  (26 other events, 223.9 us)

commit v4 on v3

--- a/solution.py
+++ b/solution.py
@@ -136,19 +136,17 @@
         rows = (total[...] + found).astype(BF16)
         lists = [rows[at : at + cap] for at in range(0, 8 * cap, cap)]
         write_near(near_refs, cap, lists)
-        for at in range(0, far_ref.shape[0], cap):
-            far_ref[at : at + cap, :] = lists[7]
+        far_ref[...] = lists[7]
 
 
 def scatter_kernel(skip, me_ref, rows_ref, *refs):
-    near_refs, far_ref, out_ref = refs[:7], refs[7], refs[8]
+    near_refs, far_refs, out_ref = refs[:7], refs[7:-1], refs[-1]
     part = out_ref.shape[0]
-    peers, cap = rows_ref.shape
-    share = skip + cap
+    cap = rows_ref.shape[1]
     hots = list_hots(me_ref[0], rows_ref, part, pl.program_id(0) * part)
-    far = jnp.zeros((cap, out_ref.shape[1]), F32)
-    for at in range(skip, far_ref.shape[0], share):
-        far = far + far_ref[at : at + cap, :].astype(F32)
+    far = far_refs[0][skip:, :].astype(F32)
+    for ref in far_refs[1:]:
+        far = far + ref[skip:, :].astype(F32)
     values = jnp.concatenate(read_near(near_refs, cap) + [far.astype(BF16)], axis=0)
     out_ref[...] = contract_rows(hots, values).astype(BF16)
 
@@ -177,7 +175,7 @@
         target = send_ref if low % 2 else keep_ref
         at = 0
         for upper in range(peers // 4):
-            owner = 4 * upper + ((me & 3) ^ low)
+            owner = me ^ (4 * upper + low)
             for ref, share, far in parts:
                 piece = ref[pl.ds(pl.multiple_of(owner * share, 16), share), :]
                 if far:
@@ -216,7 +214,7 @@
             projected = dot(rows, w_sender).astype(BF16)
             for upper in range(peers // 4):
                 span = slice(upper * cap, (upper + 1) * cap)
-                place(4 * upper + ((me & 3) ^ low), rows[span], projected[span])
+                place(me ^ (4 * upper + low), rows[span], projected[span])
         rows = jnp.concatenate(read_near(near_refs, cap), axis=0)
         projected = dot(rows, w_sender).astype(BF16)
         for spot, owner in enumerate(near_peers(me, peers)):
@@ -269,19 +267,13 @@
         )
 
 
-def slots_kernel(peers, me_ref, count_ref, src_ref, dst_ref, *refs):
-    (hidden_ref, slope_ref, norm_ref, inverse_ref, d_aggregate_ref) = refs[:5]
-    (received_ref, w_sender_ref, w_out_ref) = refs[5:8]
-    (d_pre_ref, grad_sender_ref, send_ref, keep_ref) = refs[8:12]
-    near_refs = refs[12:17]
-    (slot_sum, grad_out, d_slots) = refs[17:]
+def out_kernel(me_ref, count_ref, dst_ref, *refs):
+    (hidden_ref, norm_ref, inverse_ref, d_aggregate_ref, d_proj_ref, grad_ref) = refs
     step = pl.program_id(0)
-    me = me_ref[0]
 
     @pl.when(step == 0)
     def _():
-        slot_sum[...] = jnp.zeros_like(slot_sum)
-        grad_out[...] = jnp.zeros_like(grad_out)
+        grad_ref[...] = jnp.zeros_like(grad_ref)
 
     @pl.when(step * STEP < count_ref[0] * TILE)
     def _():
@@ -291,17 +283,33 @@
             receivers = live_only(dst_ref[0, :, part], step * STEP + start, count_ref[0] * TILE)
             onehot = hot_rows(receivers, d_aggregate_ref.shape[0])
             upstreams.append(dot(onehot, d_aggregate_ref[...]))
-        d_projs = []
-        d_hiddens = []
         for (start, part), upstream in zip(parts, upstreams):
             d_proj = norm_back(norm_ref[part, :].astype(F32), inverse_ref[part, :], upstream).astype(BF16)
-            d_projs.append(d_proj)
-            d_hiddens.append(contract_cols(d_proj, w_out_ref[...]))
-        for (start, part), d_proj, d_hidden in zip(parts, d_projs, d_hiddens):
-            grad_out[...] += contract_rows(hidden_ref[part, :], d_proj)
+            d_proj_ref[part, :] = d_proj
+            grad_ref[...] += contract_rows(hidden_ref[part, :], d_proj)
+
+
+def slots_kernel(peers, me_ref, count_ref, src_ref, *refs):
+    (d_proj_ref, slope_ref, received_ref, w_sender_ref, w_out_ref, grad_out_ref) = refs[:6]
+    (d_pre_ref, grad_sender_ref, send_ref, keep_ref) = refs[6:10]
+    near_refs = refs[10:15]
+    (slot_sum, d_slots) = refs[15:]
+    step = pl.program_id(0)
+    me = me_ref[0]
+
+    @pl.when(step == 0)
+    def _():
+        slot_sum[...] = jnp.zeros_like(slot_sum)
+
+    @pl.when(step * STEP < count_ref[0] * TILE)
+    def _():
+        parts = halves_of(d_proj_ref)
+        d_hiddens = [contract_cols(d_proj_ref[part, :], w_out_ref[...]) for start, part in parts]
+        for (start, part), d_hidden in zip(parts, d_hiddens):
             d_pre = (d_hidden * slope_ref[part, :].astype(F32)).astype(BF16)
             d_pre_ref[part, :] = d_pre
-            slot_sum[...] += dot(hot_columns(src_ref[0, :, part], slot_sum.shape[0]), d_pre)
+            senders = live_only(src_ref[0, :, part], step * STEP + start, count_ref[0] * TILE)
+            slot_sum[...] += dot(hot_columns(senders, slot_sum.shape[0]), d_pre)
 
     @pl.when(step == pl.num_programs(0) - 1)
     def _():
@@ -318,7 +326,7 @@
             peers,
             send_ref,
             keep_ref,
-            ((grad_out, grad_out.shape[0] // peers, False), (d_slots, cap, True)),
+            ((grad_out_ref, grad_out_ref.shape[0] // peers, False), (d_slots, cap, True)),
         )
 
 
@@ -375,18 +383,11 @@
     return [(peer, (peer + (3 if peer % 2 else -3)) % peers) for peer in range(peers)]
 
 
-def exchange_upper(peers, values):
-    groups = [list(range(low, peers, 4)) for low in range(4)]
-    return lax.all_to_all(
-        values, "lon", split_axis=0, concat_axis=0, axis_index_groups=groups, tiled=True
-    )
-
-
 def exchange_near(peers, lists):
     mine, other, after, before, across = lists
     return [
         mine,
-        send(other, by_xor(peers, 1)),
+        other,
         send(after, by_shift(peers, 2)),
         send(before, by_shift(peers, -2)),
         send(across, across_chips(peers)),
@@ -394,7 +395,9 @@
 
 
 def core_near(peers, near):
-    return list(near) + [send(near[2], by_xor(peers, 1)), send(near[3], by_xor(peers, 1))]
+    mine, other, after, before, across = near
+    swap = by_xor(peers, 1)
+    return [mine, send(other, swap), after, before, across, send(after, swap), send(before, swap)]
 
 
 def add(left, right):
@@ -410,9 +413,38 @@
     return add(kept, send(outgoing, by_xor(peers, 2)))
 
 
-def total_of(peers, terms, start, stop):
-    blocks = terms.reshape(peers // 4, -1, terms.shape[1])
-    return jnp.sum(blocks[:, start:stop].astype(F32), axis=0)
+def last_terms(peers, pieces):
+    count = peers // 4
+    share = pieces.shape[0] // count
+    terms = [pieces[:share]]
+    for place in range(1, count):
+        piece = pieces[place * share : (place + 1) * share]
+        terms.append(send(piece, by_xor(peers, 4 * place)))
+    return terms
+
+
+def halve_first(peers, pieces):
+    count = peers // 4
+    share = pieces.shape[0] // count
+    blocks = pieces.reshape(count // 2, 2, share, -1)
+    return blocks[:, 0].reshape(-1, pieces.shape[1]), blocks[:, 1].reshape(-1, pieces.shape[1])
+
+
+def node_last(peers, pieces):
+    count = peers // 8
+    share = pieces.shape[0] // count
+    terms = [pieces[:share]]
+    for place in range(1, count):
+        piece = pieces[place * share : (place + 1) * share]
+        terms.append(send(piece, by_xor(peers, 8 * place)))
+    return terms
+
+
+def total_of(terms, start, stop):
+    total = terms[0][start:stop].astype(F32)
+    for term in terms[1:]:
+        total = total + term[start:stop].astype(F32)
+    return total
 
 
 def whole(shape):
@@ -470,48 +502,37 @@
         gather_kernel,
         grid=(2,),
         in_specs=[smem, whole(rows.shape), pl.BlockSpec((grid_part, width), lambda step: (step, 0))],
-        out_specs=near_specs + [whole((upper * cap, width))],
-        out_shape=near_shapes + [jax.ShapeDtypeStruct((upper * cap, width), BF16)],
+        out_specs=near_specs + [whole((cap, width))],
+        out_shape=near_shapes + [jax.ShapeDtypeStruct((cap, width), BF16)],
         scratch_shapes=[pltpu.VMEM((8 * cap, width), F32)],
         compiler_params=params,
         name="gather_lists",
     )(me, rows, grid_latent)
 
-    def local_part(first, count, *before):
-        return pl.pallas_call(
-            local_kernel,
-            grid=(count,),
-            in_specs=[
-                pl.BlockSpec((1, 1, STEP), lambda step: (first + step, 0, 0)),
-                pl.BlockSpec((STEP, width), lambda step: (first + step, 0)),
-                whole(mesh_latent.shape),
-                weight(0),
-                weight(2),
-            ]
-            + [pl.BlockSpec(memory_space=pl.ANY)] * len(before),
-            out_specs=pl.BlockSpec((STEP, width), lambda step: (first + step, 0)),
-            out_shape=jax.ShapeDtypeStruct((edges, width), BF16),
-            scratch_shapes=[pltpu.VMEM((mesh_count, width), BF16)],
-            input_output_aliases={5: 0} if before else {},
-            compiler_params=params,
-            cost_estimate=pl.CostEstimate(
-                flops=2 * count * STEP * width * (width + mesh_count),
-                bytes_accessed=4 * count * STEP * width,
-                transcendentals=0,
-            ),
-            name="edge_local",
-        )(receivers, edge_latent, mesh_latent, w_edge_in, w_edge_in, *before)
-
-    far_own = exchange_upper(peers, lists[5])
+    hops = [send(lists[5], by_xor(peers, 4 * place)) for place in range(1, upper)]
     near = exchange_near(peers, lists[:5])
+    far_own = jnp.concatenate([lists[5]] + hops, axis=0)
     far_own, receivers = lax.optimization_barrier((far_own, dst))
     far_next = send(far_own, by_xor(peers, 2))
     far_core = send(far_own, by_xor(peers, 1))
-    local = local_part(0, tiles - 1)
+    local = pl.pallas_call(
+        local_kernel,
+        grid=(tiles,),
+        in_specs=[index_tile, tile_of(width), whole(mesh_latent.shape), weight(0), weight(2)],
+        out_specs=tile_of(width),
+        out_shape=jax.ShapeDtypeStruct((edges, width), BF16),
+        scratch_shapes=[pltpu.VMEM((mesh_count, width), BF16)],
+        compiler_params=params,
+        cost_estimate=pl.CostEstimate(
+            flops=2 * edges * width * (width + mesh_count),
+            bytes_accessed=4 * edges * width,
+            transcendentals=0,
+        ),
+        name="edge_local",
+    )(receivers, edge_latent, mesh_latent, w_edge_in, w_edge_in)
     far_next, far_core, near, local = lax.optimization_barrier((far_next, far_core, near, local))
     near = core_near(peers, near)
     far_both = send(far_next, by_xor(peers, 1))
-    local = local_part(tiles - 1, 1, local)
 
     node_shape, node_spec = halves(w_node_in.shape[0] // peers + w_node_out.shape[0] // peers)
     (received, hidden, slope, norm, inverse, node_send, node_keep, d_aggregate, d_mesh) = pl.pallas_call(
@@ -561,37 +582,51 @@
     )
 
     node_next, node_kept = core_sum(peers, node_send, node_keep)
+    d_proj, grad_out = pl.pallas_call(
+        out_kernel,
+        grid=(tiles,),
+        in_specs=[smem, smem, index_tile]
+        + [tile_of(width)] * 2
+        + [tile_of(1), whole((mesh_count, width))],
+        out_specs=[tile_of(width), whole(square)],
+        out_shape=[jax.ShapeDtypeStruct((edges, width), BF16), jax.ShapeDtypeStruct(square, F32)],
+        compiler_params=params,
+        cost_estimate=pl.CostEstimate(
+            flops=2 * edges * width * (mesh_count + width), bytes_accessed=6 * edges * width, transcendentals=0
+        ),
+        name="backward_out",
+    )(me, tile_count, dst, hidden, norm, inverse, d_aggregate)
+    node_next, node_kept, d_proj, grad_out = lax.optimization_barrier(
+        (node_next, node_kept, d_proj, grad_out)
+    )
+    node_pieces = next_sum(peers, node_next, node_kept)
+
     slot_shape, slot_spec = halves(w_edge_out.shape[0] // peers + cap)
     results = pl.pallas_call(
         functools.partial(slots_kernel, peers),
         grid=(tiles,),
-        in_specs=[smem, smem, index_tile, index_tile]
-        + [tile_of(width)] * 3
-        + [tile_of(1), whole((mesh_count, width)), whole((slots, width)), weight(1), whole(square)],
+        in_specs=[smem, smem, index_tile]
+        + [tile_of(width)] * 2
+        + [whole((slots, width)), weight(1), whole(square), whole(square)],
         out_specs=[tile_of(width), whole(square)] + slot_spec + near_specs,
         out_shape=[jax.ShapeDtypeStruct((edges, width), BF16), jax.ShapeDtypeStruct(square, F32)]
         + slot_shape
         + near_shapes,
-        scratch_shapes=[
-            pltpu.VMEM((slots, width), F32),
-            pltpu.VMEM(square, F32),
-            pltpu.VMEM((slots, width), BF16),
-        ],
+        scratch_shapes=[pltpu.VMEM((slots, width), F32), pltpu.VMEM((slots, width), BF16)],
         compiler_params=params,
         cost_estimate=pl.CostEstimate(
-            flops=2 * edges * width * (mesh_count + 2 * width + slots),
-            bytes_accessed=8 * edges * width,
-            transcendentals=0,
+            flops=2 * edges * width * (width + slots), bytes_accessed=6 * edges * width, transcendentals=0
         ),
         name="backward_slots",
-    )(me, tile_count, src, dst, hidden, slope, norm, inverse, d_aggregate, received, w_edge_in, w_edge_out)
+    )(me, tile_count, src, d_proj, slope, received, w_edge_in, w_edge_out, grad_out)
     (d_pre, grad_sender, slot_send, slot_keep), returns = results[:4], results[4:]
-    (node_next, node_kept, d_pre, slot_send, slot_keep, returns) = lax.optimization_barrier(
-        (node_next, node_kept, d_pre, slot_send, slot_keep, returns)
+    (node_pieces, d_pre, slot_send, slot_keep, returns) = lax.optimization_barrier(
+        (node_pieces, d_pre, slot_send, slot_keep, returns)
     )
-    node_pieces = next_sum(peers, node_next, node_kept)
     slot_next, slot_kept = core_sum(peers, slot_send, slot_keep)
     returned = exchange_near(peers, returns)
+    node_kept, node_next = halve_first(peers, node_pieces)
+    node_pieces = add(node_kept, send(node_next, by_xor(peers, 4)))
 
     edge_shape, edge_spec = halves(w_edge_in.shape[0] // peers)
     edge_grad, mesh_grad, edge_send, edge_keep = pl.pallas_call(
@@ -628,16 +663,16 @@
         w_edge_in,
     )
 
-    (node_pieces, slot_next, slot_kept, edge_send, edge_keep) = lax.optimization_barrier(
-        (node_pieces, slot_next, slot_kept, edge_send, edge_keep)
+    (node_pieces, slot_next, slot_kept, returned, edge_send, edge_keep) = lax.optimization_barrier(
+        (node_pieces, slot_next, slot_kept, returned, edge_send, edge_keep)
     )
     slot_pieces = next_sum(peers, slot_next, slot_kept)
     edge_next, edge_kept = core_sum(peers, edge_send, edge_keep)
-    node_terms = exchange_upper(peers, node_pieces)
+    node_terms = node_last(peers, node_pieces)
     returned = core_near(peers, returned)
     edge_pieces = next_sum(peers, edge_next, edge_kept)
-    slot_terms = exchange_upper(peers, slot_pieces)
-    edge_terms = exchange_upper(peers, edge_pieces)
+    slot_terms = last_terms(peers, slot_pieces)
+    edge_terms = last_terms(peers, edge_pieces)
     node_rows = w_node_in.shape[0] // peers
     out_rows = w_edge_out.shape[0] // peers
     grid_grad = pl.pallas_call(
@@ -645,20 +680,20 @@
         grid=(2,),
         in_specs=[smem, whole(rows.shape)]
         + core_specs
-        + [whole((upper * (out_rows + cap), width))],
+        + [whole((out_rows + cap, width))] * upper,
         out_specs=pl.BlockSpec((grid_part, width), lambda step: (step, 0)),
         out_shape=jax.ShapeDtypeStruct((grid_count, width), BF16),
         compiler_params=params,
         name="scatter_lists",
-    )(me, rows, *returned, slot_terms)
+    )(me, rows, *returned, *slot_terms)
     return (
         grid_grad,
         edge_grad,
         mesh_grad,
-        total_of(peers, edge_terms, 0, w_edge_in.shape[0] // peers),
-        total_of(peers, slot_terms, 0, out_rows),
-        total_of(peers, node_terms, 0, node_rows),
-        total_of(peers, node_terms, node_rows, node_rows + w_node_out.shape[0] // peers),
+        total_of(edge_terms, 0, w_edge_in.shape[0] // peers),
+        total_of(slot_terms, 0, out_rows),
+        total_of(node_terms, 0, node_rows),
+        total_of(node_terms, node_rows, node_rows + w_node_out.shape[0] // peers),
     )
 
 

time: 137 us -> 119 us (0.87)
  waiting for transfers between devices: 29.7 us -> 17 us
  Pallas kernels: 60.9 us -> 56.3 us
  other arithmetic: 6.62 us -> 4.37 us
    ppermute x21 -> x32, starting transfers between devices: 18.7 us -> 36.3 us  [send(): return lax.ppermute(values, 'lon', perm)]
    all_to_all x4 -> x0, starting transfers between devices: 17.5 us -> none  [exchange_upper(): lax.all_to_all(values, 'lon', split_axis=0, concat_axis=0, axis_index_gro...]
    all_to_all x4 -> x0, waiting for transfers between devices: 14.8 us -> none  [exchange_upper(): lax.all_to_all(values, 'lon', split_axis=0, concat_axis=0, axis_index_gro...]
    pallas_call x1, Pallas kernels: 15.5 us -> 9.8 us  [on_device(): pl.pallas_call(functools.partial(slots_kernel, peers), grid=(tiles,), in_...]
    pallas_call x2, Pallas kernels: 9.33 us -> 14.9 us  [the longest x1 7.81 us: on_device(): pl.pallas_call(out_kernel, grid=(tiles,), in_specs=[smem, smem, index_til...]
    reduce_sum x4 -> x0, other arithmetic: 3.62 us -> none  [total_of(): return jnp.sum(blocks[:, start:stop].astype(F32), axis=0)]
    pallas_call x1, Pallas kernels: 17.6 us -> 14.8 us  [on_device(): pl.pallas_call(functools.partial(forward_kernel, peers), grid=(tiles,), i...]
    add x0 -> x4, other arithmetic: none -> 2.68 us  [total_of(): total = total + term[start:stop].astype(F32)]
  transfers between devices with their start and end apart: 25 -> 32, of which waited for: 6 -> 7; matrix products, arithmetic and copies ran while one was open for 4% -> 3% of each run, Pallas kernels for 29% -> 32%
where the time goes in v4:
time: 119 us; the launch traced here: 118 us
  Pallas kernels  56.3 us (47%)
  starting transfers between devices  36.3 us (31%)
  waiting for transfers between devices  17 us (14%)
  other arithmetic  4.37 us (4%)
  local copies, waits for them, and re-layouts  2.07 us (2%)
  between operations  1.78 us (1%)
    ppermute x32, starting transfers between devices, send(): return lax.ppermute(values, 'lon', perm)  36.3 us
    ppermute x32, waiting for transfers between devices, send(): return lax.ppermute(values, 'lon', perm)  17 us
    pallas_call x1, Pallas kernels, on_device(): pl.pallas_call(functools.partial(forward_kernel, peers), grid=(tiles,), i...  14.8 us
    pallas_call x1, Pallas kernels, on_device(): pl.pallas_call(functools.partial(slots_kernel, peers), grid=(tiles,), in_...  9.8 us
    pallas_call x1, Pallas kernels, on_device(): pl.pallas_call(functools.partial(edges_kernel, peers), grid=(tiles,), in_...  9.47 us
    pallas_call x1, Pallas kernels, on_device(): pl.pallas_call(out_kernel, grid=(tiles,), in_specs=[smem, smem, index_til...  7.81 us
    pallas_call x1, Pallas kernels, on_device(): pl.pallas_call(local_kernel, grid=(tiles,), in_specs=[index_tile, tile_of...  7.07 us
    pallas_call x1, Pallas kernels, on_device(): pl.pallas_call(functools.partial(scatter_kernel, out_rows), grid=(2,), in...  3.97 us
  transfers between devices with their start and end apart: 32, of which 7 were waited for; matrix products, arithmetic and copies ran while one was open for 3% of the time, Pallas kernels for 32%

profile of v4, /device:TPU:0, one launch (start us, length us, event | category | flops | bytes accessed | tf_op | source)
XLA Modules:
  0.0 117.8 jit_solution(4546263386574449067)
XLA Ops:
  0.6 3.4 %gather_lists.1 = (bf16[48,512]{1,0:T(8,128)(2,1)}, bf16[48,512]{1,0:T(8,128)(2,1)}, bf16[96,512]{1,0:T(8,128)(2,1)}, bf16[96,512]{1,0:T(8,128)(2,1)}, bf16[48,512]{1,0:T(8,128)(2,1)}, /*index=5*/bf16[48,512]{1,0:T(8,128)(2,1)}) custom-call(s32[1]{0:T(128)} %bitcast.me_ref, s32[16,48]{1,0:T(8,128)} %bitcast.30, bf16[2048,512]{1,0:T(8,128)(2,1)} %grid_ref.1), custom_call_target="tpu_custom_call" | custom-call | tf_op jit(solution)/shard_map/gather_lists/pallas_call | solution.py:501
  4.0 5.1 %collective-permute-start.2 = (bf16[48,512]{1,0:T(8,128)(2,1)}, bf16[48,512]{1,0:T(8,128)(2,1)S(1)}, u32[]{:S(2)}, u32[]{:S(2)}) collective-permute-start(bf16[48,512]{1,0:T(8,128)(2,1)} %get-tuple-element.70), channel_id=1, source_target_pairs={{0,12},{1,13},{2,14},{3,15},{4,8},{5,9},{6,10},{7,11},{8,4},{9,5},... | collective-permute-start | bytes 147464 | tf_op jit(solution)/shard_map/ppermute | solution.py:371
  9.7 2.3 %collective-permute-start.7 = (bf16[48,512]{1,0:T(8,128)(2,1)}, bf16[48,512]{1,0:T(8,128)(2,1)S(1)}, u32[]{:S(2)}, u32[]{:S(2)}) collective-permute-start(bf16[48,512]{1,0:T(8,128)(2,1)} %get-tuple-element.76), channel_id=1, source_target_pairs={{0,13},{1,4},{2,15},{3,6},{4,1},{5,8},{6,3},{7,10},{8,5},{9,12},{1... | collective-permute-start | bytes 147464 | tf_op jit(solution)/shard_map/ppermute | solution.py:371
  12.0 1.5 %collective-permute-start.5 = (bf16[96,512]{1,0:T(8,128)(2,1)}, bf16[96,512]{1,0:T(8,128)(2,1)S(1)}, u32[]{:S(2)}, u32[]{:S(2)}) collective-permute-start(bf16[96,512]{1,0:T(8,128)(2,1)} %get-tuple-element.74), channel_id=1, source_target_pairs={{0,2},{1,3},{2,4},{3,5},{4,6},{5,7},{6,8},{7,9},{8,10},{9,11},{10,... | collective-permute-start | bytes 294920 | tf_op jit(solution)/shard_map/ppermute | solution.py:371
  13.6 3.2 %collective-permute-start.6 = (bf16[96,512]{1,0:T(8,128)(2,1)}, bf16[96,512]{1,0:T(8,128)(2,1)S(1)}, u32[]{:S(2)}, u32[]{:S(2)}) collective-permute-start(bf16[96,512]{1,0:T(8,128)(2,1)} %get-tuple-element.75), channel_id=1, source_target_pairs={{0,14},{1,15},{2,0},{3,1},{4,2},{5,3},{6,4},{7,5},{8,6},{9,7},{10,... | collective-permute-start | bytes 294920 | tf_op jit(solution)/shard_map/ppermute | solution.py:371
  17.8 7.1 %edge_local.1.local_ref = bf16[3072,512]{1,0:T(8,128)(2,1)} custom-call(s32[3,1,1024]{2,1,0:T(1,128)} %bitcast.26, bf16[3072,512]{1,0:T(8,128)(2,1)} %refs_0_.1, bf16[256,512]{1,0:T(8,128)(2,1)} %refs_4_.3, bf16[1536,512]{1,0:T(8,128)(2,1)} %refs_7_.1, bf16[1536,512]{1,0:T(8,128)(2,1)} %refs_7_.1), custom_call_target="tpu_custom_call" | custom-call | flops 2415919104 | bytes 6291456 | tf_op jit(solution)/shard_map/edge_local/pallas_call | solution.py:518
  27.9 14.8 %forward.1 = (bf16[768,512]{1,0:T(8,128)(2,1)}, bf16[3072,512]{1,0:T(8,128)(2,1)}, bf16[3072,512]{1,0:T(8,128)(2,1)}, bf16[3072,512]{1,0:T(8,128)(2,1)}, f32[307...) custom-call(s32[1]{0:T(128)} %bitcast.me_ref, ...), custom_call_target="tpu_custom_call" | custom-call | tf_op jit(solution)/shard_map/forward/pallas_call | solution.py:538
  42.7 3.0 %collective-permute-start.12 = (bf16[2,384,512]{2,1,0:T(8,128)(2,1)}, bf16[2,384,512]{2,1,0:T(8,128)(2,1)S(1)}, u32[]{:S(2)}, u32[]{:S(2)}) collective-permute-start(bf16[2,384,512]{2,1,0:T(8,128)(2,1)} %get-tuple-element.87), channel_id=1, source_target_pairs={{0,1},{1,0},{2,3},{3,2},{4,5},{5,4},{6,7},{7,6},{8,9},{9,8},{10,11... | collective-permute-start | bytes 2359304 | tf_op jit(solution)/shard_map/ppermute | solution.py:371
  45.7 7.8 %backward_out.1 = (bf16[3072,512]{1,0:T(8,128)(2,1)}, f32[512,512]{1,0:T(8,128)}) custom-call(s32[1]{0:T(128)} %bitcast.me_ref, s32[1]{0:T(128)S(6)} %copy.19.count_ref, s32[3,1,1024]{2,1,0:T(1,128)} %bitcast.28, bf16[3072,512]{1,0:T(8,128)(2,1)} %get-tuple-element.88.refs_0_, bf16[3072,512]{1,0:T(8,128)(2,1)} %get-tuple-element.89.refs_1_, ...), custom_call_target="tpu_custom_call" | custom-call | flops 2415919104 | bytes 9437184 | tf_op jit(solution)/shard_map/backward_out/pallas_call | solution.py:585
  53.8 3.1 %collective-permute-start.13 = (bf16[384,512]{1,0:T(8,128)(2,1)S(1)}, bf16[384,512]{1,0:T(8,128)(2,1)S(1)}, u32[]{:S(2)}, u32[]{:S(2)}) collective-permute-start(bf16[384,512]{1,0:T(8,128)(2,1)S(1)} %get-tuple-element.95), channel_id=1, source_target_pairs={{0,2},{1,3},{2,0},{3,1},{4,6},{5,7},{6,4},{7,5},{8,10},{9,11},{10,... | collective-permute-start | bytes 1179656 | tf_op jit(solution)/shard_map/ppermute | solution.py:371
  56.9 9.8 %backward_slots.1 = (bf16[3072,512]{1,0:T(8,128)(2,1)}, f32[512,512]{1,0:T(8,128)}, bf16[2,320,512]{2,1,0:T(8,128)(2,1)}, bf16[2,320,512]{2,1,0:T(8,128)(2,1)}, ...) custom-call(s32[1]{0:T(128)} %bitcast.me_ref, ...), custom_call_target="tpu_custom_call" | custom-call | flops 4026531840 | bytes 9437184 | tf_op jit(solution)/shard_map/backward_slots/pallas_call | solution.py:605
  68.2 3.5 %collective-permute-start.17 = (bf16[96,512]{1,0:T(8,128)(2,1)}, bf16[96,512]{1,0:T(8,128)(2,1)S(1)}, u32[]{:S(2)}, u32[]{:S(2)}) collective-permute-start(bf16[96,512]{1,0:T(8,128)(2,1)} %get-tuple-element.114), channel_id=1, source_target_pairs={{0,14},{1,15},{2,0},{3,1},{4,2},{5,3},{6,4},{7,5},{8,6},{9,7},{10,... | collective-permute-start | bytes 294920 | tf_op jit(solution)/shard_map/ppermute | solution.py:371
  71.7 9.5 %backward_edges.1 = (bf16[3072,512]{1,0:T(8,128)(2,1)}, bf16[256,512]{1,0:T(8,128)(2,1)}, bf16[2,384,512]{2,1,0:T(8,128)(2,1)}, bf16[2,384,512]{2,1,0:T(8,128)(2,1)}) custom-call(s32[1]{0:T(128)} %bitcast.me_ref, s32[1]{0:T(128)S(6)} %copy.19.count_ref, s32[3,1,1024]{2,1,0:T(1,128)} %bitcast.29, bf16[3072,512]{1,0:T(8,128)(2,1)} %refs_0_.1, ...), custom_call_target="tpu_custom_call" | custom-call | flops 4831838208 | bytes 9437184 | tf_op jit(solution)/shard_map/backward_edges/pallas_call | solution.py:632
  81.5 2.0 %collective-permute-start.26 = (bf16[2,384,512]{2,1,0:T(8,128)(2,1)}, bf16[2,384,512]{2,1,0:T(8,128)(2,1)S(1)}, u32[]{:S(2)}, u32[]{:S(2)}) collective-permute-start(bf16[2,384,512]{2,1,0:T(8,128)(2,1)} %get-tuple-element.131), channel_id=1, source_target_pairs={{0,1},{1,0},{2,3},{3,2},{4,5},{5,4},{6,7},{7,6},{8,9},{9,8},{10,11... | collective-permute-start | bytes 2359304 | tf_op jit(solution)/shard_map/ppermute | solution.py:371
  83.6 1.4 %collective-permute-start.31 = (bf16[96,512]{1,0:T(8,128)(2,1)S(1)}, bf16[96,512]{1,0:T(8,128)(2,1)S(1)}, u32[]{:S(2)}, u32[]{:S(2)}) collective-permute-start(bf16[96,512]{1,0:T(8,128)(2,1)S(1)} %slice.124), channel_id=1, source_target_pairs={{0,8},{1,9},{2,10},{3,11},{4,12},{5,13},{6,14},{7,15},{8,0},{9,1},... | collective-permute-start | bytes 294920 | tf_op jit(solution)/shard_map/ppermute | solution.py:371
  85.8 5.2 %collective-permute-done.31 = bf16[96,512]{1,0:T(8,128)(2,1)S(1)} collective-permute-done((bf16[96,512]{1,0:T(8,128)(2,1)S(1)}, bf16[96,512]{1,0:T(8,128)(2,1)S(1)}, u32[]{:S(2)}, u32[]{:S(2)}) %collective-permute-start.31) | collective-permute-done | bytes 98336 | tf_op jit(solution)/shard_map/ppermute | solution.py:371
  92.5 2.8 %collective-permute-done.22 = bf16[320,512]{1,0:T(8,128)(2,1)S(1)} collective-permute-done((bf16[320,512]{1,0:T(8,128)(2,1)S(1)}, bf16[320,512]{1,0:T(8,128)(2,1)S(1)}, u32[]{:S(2)}, u32[]{:S(2)}) %collective-permute-start.22) | collective-permute-done | bytes 327712 | tf_op jit(solution)/shard_map/ppermute | solution.py:371
  97.1 1.4 %collective-permute-start.24 = (bf16[80,512]{1,0:T(8,128)(2,1)S(1)}, bf16[80,512]{1,0:T(8,128)(2,1)S(1)}, u32[]{:S(2)}, u32[]{:S(2)}) collective-permute-start(bf16[80,512]{1,0:T(8,128)(2,1)S(1)} %get-tuple-element.143), channel_id=1, source_target_pairs={{0,8},{1,9},{2,10},{3,11},{4,12},{5,13},{6,14},{7,15},{8,0},{9,1},... | collective-permute-start | bytes 245768 | tf_op jit(solution)/shard_map/ppermute | solution.py:371
  98.5 5.2 %collective-permute-done.27 = bf16[384,512]{1,0:T(8,128)(2,1)S(1)} collective-permute-done((bf16[384,512]{1,0:T(8,128)(2,1)S(1)}, bf16[384,512]{1,0:T(8,128)(2,1)S(1)}, u32[]{:S(2)}, u32[]{:S(2)}) %collective-permute-start.27) | collective-permute-done | bytes 393248 | tf_op jit(solution)/shard_map/ppermute | solution.py:371
  104.3 1.8 %collective-permute-start.28 = (bf16[96,512]{1,0:T(8,128)(2,1)S(1)}, bf16[96,512]{1,0:T(8,128)(2,1)S(1)}, u32[]{:S(2)}, u32[]{:S(2)}) collective-permute-start(bf16[96,512]{1,0:T(8,128)(2,1)S(1)} %get-tuple-element.137), channel_id=1, source_target_pairs={{0,4},{1,5},{2,6},{3,7},{4,0},{5,1},{6,2},{7,3},{8,12},{9,13},{10,... | collective-permute-start | bytes 294920 | tf_op jit(solution)/shard_map/ppermute | solution.py:371
  106.1 1.3 %collective-permute-start.30 = (bf16[96,512]{1,0:T(8,128)(2,1)S(1)}, bf16[96,512]{1,0:T(8,128)(2,1)S(1)}, u32[]{:S(2)}, u32[]{:S(2)}) collective-permute-start(bf16[96,512]{1,0:T(8,128)(2,1)S(1)} %get-tuple-element.138), channel_id=1, source_target_pairs={{0,12},{1,13},{2,14},{3,15},{4,8},{5,9},{6,10},{7,11},{8,4},{9,5},... | collective-permute-start | bytes 294920 | tf_op jit(solution)/shard_map/ppermute | solution.py:371
  107.5 1.5 %collective-permute-done.23.refs_8_ = bf16[80,512]{1,0:T(8,128)(2,1)S(1)} collective-permute-done((bf16[80,512]{1,0:T(8,128)(2,1)S(1)}, bf16[80,512]{1,0:T(8,128)(2,1)S(1)}, u32[]{:S(2)}, u32[]{:S(2)}) %collective-permute-start.23) | collective-permute-done | bytes 81952 | tf_op jit(solution)/shard_map/ppermute | solution.py:371
  111.4 4.0 %scatter_lists.1 = bf16[2048,512]{1,0:T(8,128)(2,1)} custom-call(s32[1]{0:T(128)} %bitcast.me_ref, s32[16,48]{1,0:T(8,128)} %bitcast.31, bf16[48,512]{1,0:T(8,128)(2,1)} %get-tuple-element.121.refs_0_, bf16[48,512]{1,0:T(8,128)(2,1)} %copy-done.21, bf16[96,512]{1,0:T(8,128)(2,1)} %copy-done.14, bf16[96,512]{1,0:T(8,128)(2,1)} %copy-done.15, ...), custom_call_target="tpu_custom_call" | custom-call | tf_op jit(solution)/shard_map/scatter_lists/pallas_call | solution.py:678
  115.4 1.7 %collective-permute-done.29 = bf16[96,512]{1,0:T(8,128)(2,1)S(1)} collective-permute-done((bf16[96,512]{1,0:T(8,128)(2,1)S(1)}, bf16[96,512]{1,0:T(8,128)(2,1)S(1)}, u32[]{:S(2)}, u32[]{:S(2)}) %collective-permute-start.29) | collective-permute-done | bytes 98336 | tf_op jit(solution)/shard_map/ppermute | solution.py:371
  (111 shorter events, 13.7 us)
Async XLA Ops:
  4.0 9.6 %collective-permute-start.2 = (bf16[48,512]{1,0:T(8,128)(2,1)}, bf16[48,512]{1,0:T(8,128)(2,1)S(1)}, u32[]{:S(2)}, u32[]{:S(2)}) collective-permute-start(bf16[48,512]{1,0:T(8,128)(2,1)} %get-tuple-element.70), channel_id=1, source_target_pairs={{0,12},{1,13},{2,14},{3,15},{4,8},{5,9},{6,10},{7,11},{8,4},{9,5},... | collective-permute-start | bytes 147464 | tf_op jit(solution)/shard_map/ppermute | solution.py:371
  9.1 7.7 %collective-permute-start.1 = (bf16[48,512]{1,0:T(8,128)(2,1)}, bf16[48,512]{1,0:T(8,128)(2,1)S(1)}, u32[]{:S(2)}, u32[]{:S(2)}) collective-permute-start(bf16[48,512]{1,0:T(8,128)(2,1)} %get-tuple-element.70), channel_id=1, source_target_pairs={{0,8},{1,9},{2,10},{3,11},{4,12},{5,13},{6,14},{7,15},{8,0},{9,1},... | collective-permute-start | bytes 147464 | tf_op jit(solution)/shard_map/ppermute | solution.py:371
  9.1 7.7 %collective-permute-start = (bf16[48,512]{1,0:T(8,128)(2,1)}, bf16[48,512]{1,0:T(8,128)(2,1)S(1)}, u32[]{:S(2)}, u32[]{:S(2)}) collective-permute-start(bf16[48,512]{1,0:T(8,128)(2,1)} %get-tuple-element.70), channel_id=1, source_target_pairs={{0,4},{1,5},{2,6},{3,7},{4,0},{5,1},{6,2},{7,3},{8,12},{9,13},{10,... | collective-permute-start | bytes 147464 | tf_op jit(solution)/shard_map/ppermute | solution.py:371
  9.7 15.1 %collective-permute-start.7 = (bf16[48,512]{1,0:T(8,128)(2,1)}, bf16[48,512]{1,0:T(8,128)(2,1)S(1)}, u32[]{:S(2)}, u32[]{:S(2)}) collective-permute-start(bf16[48,512]{1,0:T(8,128)(2,1)} %get-tuple-element.76), channel_id=1, source_target_pairs={{0,13},{1,4},{2,15},{3,6},{4,1},{5,8},{6,3},{7,10},{8,5},{9,12},{1... | collective-permute-start | bytes 147464 | tf_op jit(solution)/shard_map/ppermute | solution.py:371
  12.0 12.8 %collective-permute-start.5 = (bf16[96,512]{1,0:T(8,128)(2,1)}, bf16[96,512]{1,0:T(8,128)(2,1)S(1)}, u32[]{:S(2)}, u32[]{:S(2)}) collective-permute-start(bf16[96,512]{1,0:T(8,128)(2,1)} %get-tuple-element.74), channel_id=1, source_target_pairs={{0,2},{1,3},{2,4},{3,5},{4,6},{5,7},{6,8},{7,9},{8,10},{9,11},{10,... | collective-permute-start | bytes 294920 | tf_op jit(solution)/shard_map/ppermute | solution.py:371
  13.6 11.3 %collective-permute-start.6 = (bf16[96,512]{1,0:T(8,128)(2,1)}, bf16[96,512]{1,0:T(8,128)(2,1)S(1)}, u32[]{:S(2)}, u32[]{:S(2)}) collective-permute-start(bf16[96,512]{1,0:T(8,128)(2,1)} %get-tuple-element.75), channel_id=1, source_target_pairs={{0,14},{1,15},{2,0},{3,1},{4,2},{5,3},{6,4},{7,5},{8,6},{9,7},{10,... | collective-permute-start | bytes 294920 | tf_op jit(solution)/shard_map/ppermute | solution.py:371
  42.7 10.8 %collective-permute-start.12 = (bf16[2,384,512]{2,1,0:T(8,128)(2,1)}, bf16[2,384,512]{2,1,0:T(8,128)(2,1)S(1)}, u32[]{:S(2)}, u32[]{:S(2)}) collective-permute-start(bf16[2,384,512]{2,1,0:T(8,128)(2,1)} %get-tuple-element.87), channel_id=1, source_target_pairs={{0,1},{1,0},{2,3},{3,2},{4,5},{5,4},{6,7},{7,6},{8,9},{9,8},{10,11... | collective-permute-start | bytes 2359304 | tf_op jit(solution)/shard_map/ppermute | solution.py:371
  53.8 12.9 %collective-permute-start.13 = (bf16[384,512]{1,0:T(8,128)(2,1)S(1)}, bf16[384,512]{1,0:T(8,128)(2,1)S(1)}, u32[]{:S(2)}, u32[]{:S(2)}) collective-permute-start(bf16[384,512]{1,0:T(8,128)(2,1)S(1)} %get-tuple-element.95), channel_id=1, source_target_pairs={{0,2},{1,3},{2,0},{3,1},{4,6},{5,7},{6,4},{7,5},{8,10},{9,11},{10,... | collective-permute-start | bytes 1179656 | tf_op jit(solution)/shard_map/ppermute | solution.py:371
  66.8 14.6 %collective-permute-start.18 = (bf16[48,512]{1,0:T(8,128)(2,1)}, bf16[48,512]{1,0:T(8,128)(2,1)S(1)}, u32[]{:S(2)}, u32[]{:S(2)}) collective-permute-start(bf16[48,512]{1,0:T(8,128)(2,1)} %get-tuple-element.115), channel_id=1, source_target_pairs={{0,13},{1,4},{2,15},{3,6},{4,1},{5,8},{6,3},{7,10},{8,5},{9,12},{1... | collective-permute-start | bytes 147464 | tf_op jit(solution)/shard_map/ppermute | solution.py:371
  66.9 14.6 %collective-permute-start.16 = (bf16[96,512]{1,0:T(8,128)(2,1)}, bf16[96,512]{1,0:T(8,128)(2,1)S(1)}, u32[]{:S(2)}, u32[]{:S(2)}) collective-permute-start(bf16[96,512]{1,0:T(8,128)(2,1)} %get-tuple-element.113), channel_id=1, source_target_pairs={{0,2},{1,3},{2,4},{3,5},{4,6},{5,7},{6,8},{7,9},{8,10},{9,11},{10,... | collective-permute-start | bytes 294920 | tf_op jit(solution)/shard_map/ppermute | solution.py:371
  68.2 13.3 %collective-permute-start.17 = (bf16[96,512]{1,0:T(8,128)(2,1)}, bf16[96,512]{1,0:T(8,128)(2,1)S(1)}, u32[]{:S(2)}, u32[]{:S(2)}) collective-permute-start(bf16[96,512]{1,0:T(8,128)(2,1)} %get-tuple-element.114), channel_id=1, source_target_pairs={{0,14},{1,15},{2,0},{3,1},{4,2},{5,3},{6,4},{7,5},{8,6},{9,7},{10,... | collective-permute-start | bytes 294920 | tf_op jit(solution)/shard_map/ppermute | solution.py:371
  71.7 9.5 %collective-permute-start.14 = (bf16[192,512]{1,0:T(8,128)(2,1)S(1)}, bf16[192,512]{1,0:T(8,128)(2,1)S(1)}, u32[]{:S(2)}, u32[]{:S(2)}) collective-permute-start(bf16[192,512]{1,0:T(8,128)(2,1)S(1)} %bitcast.25), channel_id=1, source_target_pairs={{0,4},{1,5},{2,6},{3,7},{4,0},{5,1},{6,2},{7,3},{8,12},{9,13},{10,... | collective-permute-start | bytes 589832 | tf_op jit(solution)/shard_map/ppermute | solution.py:371
  71.7 9.6 %collective-permute-start.15 = (bf16[2,320,512]{2,1,0:T(8,128)(2,1)}, bf16[2,320,512]{2,1,0:T(8,128)(2,1)S(1)}, u32[]{:S(2)}, u32[]{:S(2)}) collective-permute-start(bf16[2,320,512]{2,1,0:T(8,128)(2,1)} %get-tuple-element.110), channel_id=1, source_target_pairs={{0,1},{1,0},{2,3},{3,2},{4,5},{5,4},{6,7},{7,6},{8,9},{9,8},{10,11... | collective-permute-start | bytes 1966088 | tf_op jit(solution)/shard_map/ppermute | solution.py:371
  81.5 10.8 %collective-permute-start.26 = (bf16[2,384,512]{2,1,0:T(8,128)(2,1)}, bf16[2,384,512]{2,1,0:T(8,128)(2,1)S(1)}, u32[]{:S(2)}, u32[]{:S(2)}) collective-permute-start(bf16[2,384,512]{2,1,0:T(8,128)(2,1)} %get-tuple-element.131), channel_id=1, source_target_pairs={{0,1},{1,0},{2,3},{3,2},{4,5},{5,4},{6,7},{7,6},{8,9},{9,8},{10,11... | collective-permute-start | bytes 2359304 | tf_op jit(solution)/shard_map/ppermute | solution.py:371
  83.6 7.5 %collective-permute-start.31 = (bf16[96,512]{1,0:T(8,128)(2,1)S(1)}, bf16[96,512]{1,0:T(8,128)(2,1)S(1)}, u32[]{:S(2)}, u32[]{:S(2)}) collective-permute-start(bf16[96,512]{1,0:T(8,128)(2,1)S(1)} %slice.124), channel_id=1, source_target_pairs={{0,8},{1,9},{2,10},{3,11},{4,12},{5,13},{6,14},{7,15},{8,0},{9,1},... | collective-permute-start | bytes 294920 | tf_op jit(solution)/shard_map/ppermute | solution.py:371
  85.0 19.2 %collective-permute-start.19 = (bf16[48,512]{1,0:T(8,128)(2,1)S(1)}, bf16[48,512]{1,0:T(8,128)(2,1)S(1)}, u32[]{:S(2)}, u32[]{:S(2)}) collective-permute-start(bf16[48,512]{1,0:T(8,128)(2,1)S(1)} %copy-done.22), channel_id=1, source_target_pairs={{0,1},{1,0},{2,3},{3,2},{4,5},{5,4},{6,7},{7,6},{8,9},{9,8},{10,11... | collective-permute-start | bytes 147464 | tf_op jit(solution)/shard_map/ppermute | solution.py:371
  85.2 25.6 %collective-permute-start.20 = (bf16[96,512]{1,0:T(8,128)(2,1)S(1)}, bf16[96,512]{1,0:T(8,128)(2,1)S(1)}, u32[]{:S(2)}, u32[]{:S(2)}) collective-permute-start(bf16[96,512]{1,0:T(8,128)(2,1)S(1)} %collective-permute-done.16.refs_2_), channel_id=1, source_target_pairs={{0,1},{1,0},{2,3},{3,2},{4,5},{5,4},{6,7},{7,6},{8,9},{9,8},{10,11... | collective-permute-start | bytes 294920 | tf_op jit(solution)/shard_map/ppermute | solution.py:371
  85.5 9.9 %collective-permute-start.22 = (bf16[320,512]{1,0:T(8,128)(2,1)S(1)}, bf16[320,512]{1,0:T(8,128)(2,1)S(1)}, u32[]{:S(2)}, u32[]{:S(2)}) collective-permute-start(bf16[320,512]{1,0:T(8,128)(2,1)S(1)} %get-tuple-element.127), channel_id=1, source_target_pairs={{0,2},{1,3},{2,0},{3,1},{4,6},{5,7},{6,4},{7,5},{8,10},{9,11},{10,... | collective-permute-start | bytes 983048 | tf_op jit(solution)/shard_map/ppermute | solution.py:371
  92.4 11.3 %collective-permute-start.27 = (bf16[384,512]{1,0:T(8,128)(2,1)S(1)}, bf16[384,512]{1,0:T(8,128)(2,1)S(1)}, u32[]{:S(2)}, u32[]{:S(2)}) collective-permute-start(bf16[384,512]{1,0:T(8,128)(2,1)S(1)} %fusion.4), channel_id=1, source_target_pairs={{0,2},{1,3},{2,0},{3,1},{4,6},{5,7},{6,4},{7,5},{8,10},{9,11},{10,... | collective-permute-start | bytes 1179656 | tf_op jit(solution)/shard_map/ppermute | solution.py:371
  96.1 8.2 %collective-permute-start.25 = (bf16[80,512]{1,0:T(8,128)(2,1)S(1)}, bf16[80,512]{1,0:T(8,128)(2,1)S(1)}, u32[]{:S(2)}, u32[]{:S(2)}) collective-permute-start(bf16[80,512]{1,0:T(8,128)(2,1)S(1)} %get-tuple-element.142), channel_id=1, source_target_pairs={{0,12},{1,13},{2,14},{3,15},{4,8},{5,9},{6,10},{7,11},{8,4},{9,5},... | collective-permute-start | bytes 245768 | tf_op jit(solution)/shard_map/ppermute | solution.py:371
  97.1 9.0 %collective-permute-start.24 = (bf16[80,512]{1,0:T(8,128)(2,1)S(1)}, bf16[80,512]{1,0:T(8,128)(2,1)S(1)}, u32[]{:S(2)}, u32[]{:S(2)}) collective-permute-start(bf16[80,512]{1,0:T(8,128)(2,1)S(1)} %get-tuple-element.143), channel_id=1, source_target_pairs={{0,8},{1,9},{2,10},{3,11},{4,12},{5,13},{6,14},{7,15},{8,0},{9,1},... | collective-permute-start | bytes 245768 | tf_op jit(solution)/shard_map/ppermute | solution.py:371
  104.3 11.1 %collective-permute-start.28 = (bf16[96,512]{1,0:T(8,128)(2,1)S(1)}, bf16[96,512]{1,0:T(8,128)(2,1)S(1)}, u32[]{:S(2)}, u32[]{:S(2)}) collective-permute-start(bf16[96,512]{1,0:T(8,128)(2,1)S(1)} %get-tuple-element.137), channel_id=1, source_target_pairs={{0,4},{1,5},{2,6},{3,7},{4,0},{5,1},{6,2},{7,3},{8,12},{9,13},{10,... | collective-permute-start | bytes 294920 | tf_op jit(solution)/shard_map/ppermute | solution.py:371
  106.1 9.3 %collective-permute-start.30 = (bf16[96,512]{1,0:T(8,128)(2,1)S(1)}, bf16[96,512]{1,0:T(8,128)(2,1)S(1)}, u32[]{:S(2)}, u32[]{:S(2)}) collective-permute-start(bf16[96,512]{1,0:T(8,128)(2,1)S(1)} %get-tuple-element.138), channel_id=1, source_target_pairs={{0,12},{1,13},{2,14},{3,15},{4,8},{5,9},{6,10},{7,11},{8,4},{9,5},... | collective-permute-start | bytes 294920 | tf_op jit(solution)/shard_map/ppermute | solution.py:371
  108.9 8.2 %collective-permute-start.29 = (bf16[96,512]{1,0:T(8,128)(2,1)S(1)}, bf16[96,512]{1,0:T(8,128)(2,1)S(1)}, u32[]{:S(2)}, u32[]{:S(2)}) collective-permute-start(bf16[96,512]{1,0:T(8,128)(2,1)S(1)} %get-tuple-element.139), channel_id=1, source_target_pairs={{0,8},{1,9},{2,10},{3,11},{4,12},{5,13},{6,14},{7,15},{8,0},{9,1},... | collective-permute-start | bytes 294920 | tf_op jit(solution)/shard_map/ppermute | solution.py:371
  (32 other events, 213.9 us)

commit v5 on v4

--- a/solution.py
+++ b/solution.py
@@ -57,11 +57,23 @@
         piece = row[:, start : start + block].astype(F32)
         picked = jnp.where(down == along, piece, 0.0)
         columns.append(jnp.sum(picked, axis=1, keepdims=True))
-    return jnp.concatenate(columns, axis=0).astype(jnp.int32)
+    return jnp.concatenate(columns, axis=0)
+
+
+def as_row(column):
+    count = column.shape[0]
+    block = min(count, LANES)
+    down = lax.broadcasted_iota(jnp.int32, (block, block), 0)
+    along = lax.broadcasted_iota(jnp.int32, (block, block), 1)
+    rows = []
+    for start in range(0, count, block):
+        picked = jnp.where(down == along, column[start : start + block], 0.0)
+        rows.append(jnp.sum(picked, axis=0, keepdims=True))
+    return jnp.concatenate(rows, axis=1)
 
 
 def hot_rows(row, width, first=0):
-    column = as_column(row) - first
+    column = as_column(row).astype(jnp.int32) - first
     along = lax.broadcasted_iota(jnp.int32, (row.shape[1], width), 1)
     return (column == along).astype(F32).astype(BF16)
 
@@ -170,9 +182,10 @@
         ).astype(BF16)
 
 
-def split_out(me, peers, send_ref, keep_ref, parts):
+def split_out(me, peers, first, send_ref, keep_ref, parts):
     for low in range(4):
-        target = send_ref if low % 2 else keep_ref
+        target = send_ref if low & first else keep_ref
+        half = 1 if low & (3 - first) else 0
         at = 0
         for upper in range(peers // 4):
             owner = me ^ (4 * upper + low)
@@ -182,7 +195,7 @@
                     ahead = lax.rem(owner - me + peers, peers)
                     apart = jnp.minimum(ahead, peers - ahead)
                     piece = jnp.where(apart > NEAR, piece.astype(F32), 0.0)
-                target[low // 2, at : at + share, :] = piece.astype(BF16)
+                target[half, at : at + share, :] = piece.astype(BF16)
                 at += share
 
 
@@ -237,7 +250,7 @@
         for (start, part), proj in zip(parts, projs):
             normed, inverse = layer_norm(proj)
             norm_ref[part, :] = normed.astype(BF16)
-            inverse_ref[part, :] = inverse
+            inverse_ref[0, :, part] = as_row(inverse)
             edge_new = (edge_ref[part, :].astype(F32) + normed).astype(BF16)
             receivers = live_only(dst_ref[0, :, part], step * STEP + start, count_ref[0] * TILE)
             aggregate[...] += dot(hot_columns(receivers, aggregate.shape[0]), edge_new)
@@ -261,110 +274,94 @@
         split_out(
             me,
             peers,
+            2,
             send_ref,
             keep_ref,
             ((grad_in, grad_in.shape[0] // peers, False), (grad_out, grad_out.shape[0] // peers, False)),
         )
 
 
-def out_kernel(me_ref, count_ref, dst_ref, *refs):
-    (hidden_ref, norm_ref, inverse_ref, d_aggregate_ref, d_proj_ref, grad_ref) = refs
+def backward_kernel(peers, me_ref, count_ref, src_ref, dst_ref, inverse_ref, *refs):
+    (hidden_ref, slope_ref, norm_ref, edge_ref) = refs[:4]
+    (d_aggregate_ref, received_ref, mesh_ref, d_mesh_ref) = refs[4:8]
+    (w_sender_ref, w_receiver_ref, w_out_ref) = refs[8:11]
+    (d_pre_ref, mesh_grad_ref, slot_send_ref, slot_keep_ref, edge_send_ref, edge_keep_ref) = refs[11:17]
+    near_refs = refs[17:22]
+    (end_sum, grad_in, grad_out, d_slots) = refs[22:]
     step = pl.program_id(0)
+    me = me_ref[0]
+    slots, width = received_ref.shape
+    mesh_count = mesh_ref.shape[0]
 
     @pl.when(step == 0)
     def _():
-        grad_ref[...] = jnp.zeros_like(grad_ref)
+        end_sum[...] = jnp.zeros_like(end_sum)
+        grad_in[:width, :] = jnp.zeros((width, width), F32)
+        grad_out[...] = jnp.zeros_like(grad_out)
 
     @pl.when(step * STEP < count_ref[0] * TILE)
     def _():
         parts = halves_of(hidden_ref)
         upstreams = []
+        columns = []
         for start, part in parts:
-            receivers = live_only(dst_ref[0, :, part], step * STEP + start, count_ref[0] * TILE)
-            onehot = hot_rows(receivers, d_aggregate_ref.shape[0])
-            upstreams.append(dot(onehot, d_aggregate_ref[...]))
+            first = step * STEP + start
+            live = count_ref[0] * TILE
+            receivers = live_only(dst_ref[0, :, part], first, live)
+            upstreams.append(dot(hot_rows(receivers, mesh_count), d_aggregate_ref[...]))
+            senders = live_only(src_ref[0, :, part], first, live)
+            columns.append(
+                jnp.concatenate([hot_columns(senders, slots), hot_columns(receivers, mesh_count)], axis=0)
+            )
+        d_projs = []
+        d_hiddens = []
         for (start, part), upstream in zip(parts, upstreams):
-            d_proj = norm_back(norm_ref[part, :].astype(F32), inverse_ref[part, :], upstream).astype(BF16)
-            d_proj_ref[part, :] = d_proj
-            grad_ref[...] += contract_rows(hidden_ref[part, :], d_proj)
-
-
-def slots_kernel(peers, me_ref, count_ref, src_ref, *refs):
-    (d_proj_ref, slope_ref, received_ref, w_sender_ref, w_out_ref, grad_out_ref) = refs[:6]
-    (d_pre_ref, grad_sender_ref, send_ref, keep_ref) = refs[6:10]
-    near_refs = refs[10:15]
-    (slot_sum, d_slots) = refs[15:]
-    step = pl.program_id(0)
-    me = me_ref[0]
-
-    @pl.when(step == 0)
-    def _():
-        slot_sum[...] = jnp.zeros_like(slot_sum)
-
-    @pl.when(step * STEP < count_ref[0] * TILE)
-    def _():
-        parts = halves_of(d_proj_ref)
-        d_hiddens = [contract_cols(d_proj_ref[part, :], w_out_ref[...]) for start, part in parts]
-        for (start, part), d_hidden in zip(parts, d_hiddens):
+            inverse = as_column(inverse_ref[0, :, part])
+            d_proj = norm_back(norm_ref[part, :].astype(F32), inverse, upstream).astype(BF16)
+            d_projs.append(d_proj)
+            d_hiddens.append(contract_cols(d_proj, w_out_ref[...]))
+        for (start, part), d_proj, d_hidden, column in zip(parts, d_projs, d_hiddens, columns):
+            grad_out[...] += contract_rows(hidden_ref[part, :], d_proj)
             d_pre = (d_hidden * slope_ref[part, :].astype(F32)).astype(BF16)
             d_pre_ref[part, :] = d_pre
-            senders = live_only(src_ref[0, :, part], step * STEP + start, count_ref[0] * TILE)
-            slot_sum[...] += dot(hot_columns(senders, slot_sum.shape[0]), d_pre)
+            end_sum[...] += dot(column, d_pre)
+            grad_in[:width, :] += contract_rows(edge_ref[part, :], d_pre)
 
     @pl.when(step == pl.num_programs(0) - 1)
     def _():
-        summed = slot_sum[...].astype(BF16)
-        grad_sender_ref[...] = contract_rows(received_ref[...], summed)
+        summed = end_sum[:slots, :].astype(BF16)
+        mesh_summed = end_sum[slots:, :].astype(BF16)
         d_slots[...] = contract_cols(summed, w_sender_ref[...]).astype(BF16)
+        grad_in[width : 2 * width, :] = contract_rows(received_ref[...], summed)
+        grad_in[2 * width :, :] = contract_rows(mesh_ref[...], mesh_summed)
+        mesh_grad_ref[...] = (d_mesh_ref[...] + contract_cols(mesh_summed, w_receiver_ref[...])).astype(BF16)
         cap = near_refs[0].shape[0]
         owners = near_peers(me, peers)
         write_near(
             near_refs, cap, [d_slots[pl.ds(pl.multiple_of(owner * cap, 16), cap), :] for owner in owners]
         )
+        out_share = grad_out.shape[0] // peers
         split_out(
-            me,
-            peers,
-            send_ref,
-            keep_ref,
-            ((grad_out_ref, grad_out_ref.shape[0] // peers, False), (d_slots, cap, True)),
+            me, peers, 1, slot_send_ref, slot_keep_ref, ((grad_out, out_share, False), (d_slots, cap, True))
         )
-
-
-def edges_kernel(peers, me_ref, count_ref, dst_ref, *refs):
-    (edge_ref, d_pre_ref, d_aggregate_ref, d_mesh_ref, mesh_ref, grad_sender_ref) = refs[:6]
-    (w_edge_ref, w_receiver_ref) = refs[6:8]
-    (edge_grad_ref, mesh_grad_ref, send_ref, keep_ref) = refs[8:12]
-    (grad_in, mesh_sum) = refs[12:]
+        split_out(
+            me, peers, 1, edge_send_ref, edge_keep_ref, ((grad_in, grad_in.shape[0] // peers, False),)
+        )
+
+
+def edges_kernel(count_ref, dst_ref, d_pre_ref, d_aggregate_ref, w_edge_ref, edge_grad_ref):
     step = pl.program_id(0)
-    width = edge_ref.shape[1]
-
-    @pl.when(step == 0)
-    def _():
-        grad_in[:width, :] = jnp.zeros((width, grad_in.shape[1]), F32)
-        mesh_sum[...] = jnp.zeros_like(mesh_sum)
 
     @pl.when(step * STEP < count_ref[0] * TILE)
     def _():
-        for start, part in halves_of(edge_ref):
-            d_pre = d_pre_ref[part, :]
+        for start, part in halves_of(d_pre_ref):
             receivers = live_only(dst_ref[0, :, part], step * STEP + start, count_ref[0] * TILE)
-            onehot = hot_rows(receivers, d_aggregate_ref.shape[0])
-            upstream = dot(onehot, d_aggregate_ref[...])
-            edge_grad_ref[part, :] = (upstream + contract_cols(d_pre, w_edge_ref[...])).astype(BF16)
-            grad_in[:width, :] += contract_rows(edge_ref[part, :], d_pre)
-            mesh_sum[...] += dot(hot_columns(receivers, mesh_sum.shape[0]), d_pre)
+            upstream = dot(hot_rows(receivers, d_aggregate_ref.shape[0]), d_aggregate_ref[...])
+            edge_grad_ref[part, :] = (upstream + contract_cols(d_pre_ref[part, :], w_edge_ref[...])).astype(BF16)
 
     @pl.when(step * STEP >= count_ref[0] * TILE)
     def _():
         edge_grad_ref[...] = jnp.zeros_like(edge_grad_ref)
-
-    @pl.when(step == pl.num_programs(0) - 1)
-    def _():
-        summed = mesh_sum[...].astype(BF16)
-        mesh_grad_ref[...] = (d_mesh_ref[...] + contract_cols(summed, w_receiver_ref[...])).astype(BF16)
-        grad_in[width : 2 * width, :] = grad_sender_ref[...]
-        grad_in[2 * width :, :] = contract_rows(mesh_ref[...], summed)
-        split_out(me_ref[0], peers, send_ref, keep_ref, ((grad_in, grad_in.shape[0] // peers, False),))
 
 
 def send(values, perm):
@@ -404,13 +401,13 @@
     return (left.astype(F32) + right.astype(F32)).astype(BF16)
 
 
-def core_sum(peers, outgoing, kept):
-    arrived = send(outgoing, by_xor(peers, 1))
+def first_sum(peers, bit, outgoing, kept):
+    arrived = send(outgoing, by_xor(peers, bit))
     return add(kept[1], arrived[1]), add(kept[0], arrived[0])
 
 
-def next_sum(peers, outgoing, kept):
-    return add(kept, send(outgoing, by_xor(peers, 2)))
+def next_sum(peers, bit, outgoing, kept):
+    return add(kept, send(outgoing, by_xor(peers, bit)))
 
 
 def last_terms(peers, pieces):
@@ -545,12 +542,12 @@
         + [whole(w.shape) for w in (w_edge_out, w_node_in, w_node_out, mesh_latent, mesh_cotangent)],
         out_specs=[whole((slots, width))]
         + [tile_of(width)] * 3
-        + [tile_of(1)]
+        + [index_tile]
         + node_spec
         + [whole((mesh_count, width))] * 2,
         out_shape=[jax.ShapeDtypeStruct((slots, width), BF16)]
         + [jax.ShapeDtypeStruct((edges, width), BF16)] * 3
-        + [jax.ShapeDtypeStruct((edges, 1), F32)]
+        + [jax.ShapeDtypeStruct((tiles, 1, STEP), F32)]
         + node_shape
         + [jax.ShapeDtypeStruct((mesh_count, width), BF16), jax.ShapeDtypeStruct((mesh_count, width), F32)],
         scratch_shapes=[
@@ -581,98 +578,89 @@
         mesh_cotangent,
     )
 
-    node_next, node_kept = core_sum(peers, node_send, node_keep)
-    d_proj, grad_out = pl.pallas_call(
-        out_kernel,
+    node_next, node_kept = first_sum(peers, 2, node_send, node_keep)
+    slot_shape, slot_spec = halves(w_edge_out.shape[0] // peers + cap)
+    edge_shape, edge_spec = halves(w_edge_in.shape[0] // peers)
+    results = pl.pallas_call(
+        functools.partial(backward_kernel, peers),
         grid=(tiles,),
-        in_specs=[smem, smem, index_tile]
-        + [tile_of(width)] * 2
-        + [tile_of(1), whole((mesh_count, width))],
-        out_specs=[tile_of(width), whole(square)],
-        out_shape=[jax.ShapeDtypeStruct((edges, width), BF16), jax.ShapeDtypeStruct(square, F32)],
-        compiler_params=params,
-        cost_estimate=pl.CostEstimate(
-            flops=2 * edges * width * (mesh_count + width), bytes_accessed=6 * edges * width, transcendentals=0
-        ),
-        name="backward_out",
-    )(me, tile_count, dst, hidden, norm, inverse, d_aggregate)
-    node_next, node_kept, d_proj, grad_out = lax.optimization_barrier(
-        (node_next, node_kept, d_proj, grad_out)
-    )
-    node_pieces = next_sum(peers, node_next, node_kept)
-
-    slot_shape, slot_spec = halves(w_edge_out.shape[0] // peers + cap)
-    results = pl.pallas_call(
-        functools.partial(slots_kernel, peers),
-        grid=(tiles,),
-        in_specs=[smem, smem, index_tile]
-        + [tile_of(width)] * 2
-        + [whole((slots, width)), weight(1), whole(square), whole(square)],
-        out_specs=[tile_of(width), whole(square)] + slot_spec + near_specs,
-        out_shape=[jax.ShapeDtypeStruct((edges, width), BF16), jax.ShapeDtypeStruct(square, F32)]
-        + slot_shape
-        + near_shapes,
-        scratch_shapes=[pltpu.VMEM((slots, width), F32), pltpu.VMEM((slots, width), BF16)],
-        compiler_params=params,
-        cost_estimate=pl.CostEstimate(
-            flops=2 * edges * width * (width + slots), bytes_accessed=6 * edges * width, transcendentals=0
-        ),
-        name="backward_slots",
-    )(me, tile_count, src, d_proj, slope, received, w_edge_in, w_edge_out, grad_out)
-    (d_pre, grad_sender, slot_send, slot_keep), returns = results[:4], results[4:]
-    (node_pieces, d_pre, slot_send, slot_keep, returns) = lax.optimization_barrier(
-        (node_pieces, d_pre, slot_send, slot_keep, returns)
-    )
-    slot_next, slot_kept = core_sum(peers, slot_send, slot_keep)
-    returned = exchange_near(peers, returns)
-    node_kept, node_next = halve_first(peers, node_pieces)
-    node_pieces = add(node_kept, send(node_next, by_xor(peers, 4)))
-
-    edge_shape, edge_spec = halves(w_edge_in.shape[0] // peers)
-    edge_grad, mesh_grad, edge_send, edge_keep = pl.pallas_call(
-        functools.partial(edges_kernel, peers),
-        grid=(tiles,),
-        in_specs=[smem, smem, index_tile, tile_of(width), tile_of(width)]
-        + [whole((mesh_count, width))] * 3
-        + [whole(square), weight(0), weight(2)],
-        out_specs=[tile_of(width), whole((mesh_count, width))] + edge_spec,
+        in_specs=[smem, smem, index_tile, index_tile, index_tile]
+        + [tile_of(width)] * 4
+        + [whole((mesh_count, width)), whole((slots, width))]
+        + [whole((mesh_count, width))] * 2
+        + [weight(1), weight(2), whole(square)],
+        out_specs=[tile_of(width), whole((mesh_count, width))] + slot_spec + edge_spec + near_specs,
         out_shape=[
             jax.ShapeDtypeStruct((edges, width), BF16),
             jax.ShapeDtypeStruct((mesh_count, width), BF16),
         ]
-        + edge_shape,
-        scratch_shapes=[pltpu.VMEM(w_edge_in.shape, F32), pltpu.VMEM((mesh_count, width), F32)],
+        + slot_shape
+        + edge_shape
+        + near_shapes,
+        scratch_shapes=[
+            pltpu.VMEM((slots + mesh_count, width), F32),
+            pltpu.VMEM(w_edge_in.shape, F32),
+            pltpu.VMEM(square, F32),
+            pltpu.VMEM((slots, width), BF16),
+        ],
         compiler_params=params,
         cost_estimate=pl.CostEstimate(
-            flops=2 * edges * width * (2 * mesh_count + 2 * width),
-            bytes_accessed=6 * edges * width,
+            flops=2 * edges * width * (2 * mesh_count + 3 * width + slots),
+            bytes_accessed=10 * edges * width,
             transcendentals=0,
         ),
-        name="backward_edges",
+        name="backward",
     )(
         me,
         tile_count,
+        src,
         dst,
+        inverse,
+        hidden,
+        slope,
+        norm,
         edge_latent,
-        d_pre,
         d_aggregate,
+        received,
+        mesh_latent,
         d_mesh,
-        mesh_latent,
-        grad_sender,
         w_edge_in,
         w_edge_in,
+        w_edge_out,
     )
-
-    (node_pieces, slot_next, slot_kept, returned, edge_send, edge_keep) = lax.optimization_barrier(
-        (node_pieces, slot_next, slot_kept, returned, edge_send, edge_keep)
+    (d_pre, mesh_grad, slot_send, slot_keep, edge_send, edge_keep), returns = results[:6], results[6:]
+    (node_next, node_kept, d_pre, slot_send, slot_keep, edge_send, edge_keep, returns) = lax.optimization_barrier(
+        (node_next, node_kept, d_pre, slot_send, slot_keep, edge_send, edge_keep, returns)
     )
-    slot_pieces = next_sum(peers, slot_next, slot_kept)
-    edge_next, edge_kept = core_sum(peers, edge_send, edge_keep)
+    slot_next, slot_kept = first_sum(peers, 1, slot_send, slot_keep)
+    edge_next, edge_kept = first_sum(peers, 1, edge_send, edge_keep)
+    node_pieces = next_sum(peers, 1, node_next, node_kept)
+    returned = exchange_near(peers, returns)
+    (slot_next, slot_kept, edge_next, edge_kept, node_pieces, returned, d_pre) = lax.optimization_barrier(
+        (slot_next, slot_kept, edge_next, edge_kept, node_pieces, returned, d_pre)
+    )
+    slot_pieces = next_sum(peers, 2, slot_next, slot_kept)
+    edge_pieces = next_sum(peers, 2, edge_next, edge_kept)
+    node_kept, node_next = halve_first(peers, node_pieces)
+    node_pieces = add(node_kept, send(node_next, by_xor(peers, 4)))
+    edge_grad = pl.pallas_call(
+        edges_kernel,
+        grid=(tiles,),
+        in_specs=[smem, index_tile, tile_of(width), whole((mesh_count, width)), weight(0)],
+        out_specs=tile_of(width),
+        out_shape=jax.ShapeDtypeStruct((edges, width), BF16),
+        compiler_params=params,
+        cost_estimate=pl.CostEstimate(
+            flops=2 * edges * width * (mesh_count + width), bytes_accessed=4 * edges * width, transcendentals=0
+        ),
+        name="edge_grad",
+    )(tile_count, dst, d_pre, d_aggregate, w_edge_in)
+    node_pieces, slot_pieces, edge_grad = lax.optimization_barrier((node_pieces, slot_pieces, edge_grad))
+    returned = core_near(peers, returned)
+    slot_terms = last_terms(peers, slot_pieces)
     node_terms = node_last(peers, node_pieces)
-    returned = core_near(peers, returned)
-    edge_pieces = next_sum(peers, edge_next, edge_kept)
-    slot_terms = last_terms(peers, slot_pieces)
     edge_terms = last_terms(peers, edge_pieces)
+    node_terms, edge_terms[0] = lax.optimization_barrier((node_terms, edge_terms[0]))
     node_rows = w_node_in.shape[0] // peers
     out_rows = w_edge_out.shape[0] // peers
     grid_grad = pl.pallas_call(

time: 119 us -> 115 us (0.966)
  starting transfers between devices: 36.3 us -> 29.5 us
  Pallas kernels: 56.3 us -> 58 us
  waiting for transfers between devices: 17 us -> 18.2 us
    ppermute x32, starting transfers between devices: 36.3 us -> 29.5 us  [send(): return lax.ppermute(values, 'lon', perm)]
    pallas_call x1, Pallas kernels: 14.8 us -> 17.5 us  [on_device(): pl.pallas_call(functools.partial(forward_kernel, peers), grid=(tiles,), i...]
    pallas_call x3 -> x2, Pallas kernels: 27.1 us -> 26.2 us  [the longest x1 19.9 us: on_device(): pl.pallas_call(functools.partial(backward_kernel, peers), grid=(tiles,),...]
  transfers between devices with their start and end apart: 32 -> 32, of which waited for: 7 -> 11; matrix products, arithmetic and copies ran while one was open for 3% -> 4% of each run, Pallas kernels for 32% -> 33%
where the time goes in v5:
time: 115 us; the launch traced here: 114 us
  Pallas kernels  58 us (50%)
  starting transfers between devices  29.5 us (26%)
  waiting for transfers between devices  18.2 us (16%)
  other arithmetic  4.43 us (4%)
  local copies, waits for them, and re-layouts  2.07 us (2%)
  between operations  1.72 us (1%)
    ppermute x32, starting transfers between devices, send(): return lax.ppermute(values, 'lon', perm)  29.5 us
    pallas_call x1, Pallas kernels, on_device(): pl.pallas_call(functools.partial(backward_kernel, peers), grid=(tiles,),...  19.9 us
    ppermute x32, waiting for transfers between devices, send(): return lax.ppermute(values, 'lon', perm)  18.2 us
    pallas_call x1, Pallas kernels, on_device(): pl.pallas_call(functools.partial(forward_kernel, peers), grid=(tiles,), i...  17.5 us
    pallas_call x1, Pallas kernels, on_device(): pl.pallas_call(local_kernel, grid=(tiles,), in_specs=[index_tile, tile_of...  7.07 us
    pallas_call x1, Pallas kernels, on_device(): pl.pallas_call(edges_kernel, grid=(tiles,), in_specs=[smem, index_tile, t...  6.21 us
    pallas_call x1, Pallas kernels, on_device(): pl.pallas_call(functools.partial(scatter_kernel, out_rows), grid=(2,), in...  3.96 us
    pallas_call x1, Pallas kernels, on_device(): pl.pallas_call(gather_kernel, grid=(2,), in_specs=[smem, whole(rows.shape...  3.36 us
  transfers between devices with their start and end apart: 32, of which 11 were waited for; matrix products, arithmetic and copies ran while one was open for 4% of the time, Pallas kernels for 33%

profile of v5, /device:TPU:0, one launch (start us, length us, event | category | flops | bytes accessed | tf_op | source)
XLA Modules:
  0.0 113.9 jit_solution(5002267474052183191)
XLA Ops:
  0.6 3.4 %gather_lists.1 = (bf16[48,512]{1,0:T(8,128)(2,1)}, bf16[48,512]{1,0:T(8,128)(2,1)}, bf16[96,512]{1,0:T(8,128)(2,1)}, bf16[96,512]{1,0:T(8,128)(2,1)}, bf16[48,512]{1,0:T(8,128)(2,1)}, /*index=5*/bf16[48,512]{1,0:T(8,128)(2,1)}) custom-call(s32[1]{0:T(128)} %bitcast.me_ref, s32[16,48]{1,0:T(8,128)} %bitcast.27, bf16[2048,512]{1,0:T(8,128)(2,1)} %grid_ref.1), custom_call_target="tpu_custom_call" | custom-call | tf_op jit(solution)/shard_map/gather_lists/pallas_call | solution.py:498
  4.0 5.1 %collective-permute-start.2 = (bf16[48,512]{1,0:T(8,128)(2,1)}, bf16[48,512]{1,0:T(8,128)(2,1)S(1)}, u32[]{:S(2)}, u32[]{:S(2)}) collective-permute-start(bf16[48,512]{1,0:T(8,128)(2,1)} %get-tuple-element.72), channel_id=1, source_target_pairs={{0,12},{1,13},{2,14},{3,15},{4,8},{5,9},{6,10},{7,11},{8,4},{9,5},... | collective-permute-start | bytes 147464 | tf_op jit(solution)/shard_map/ppermute | solution.py:368
  9.7 2.3 %collective-permute-start.7 = (bf16[48,512]{1,0:T(8,128)(2,1)}, bf16[48,512]{1,0:T(8,128)(2,1)S(1)}, u32[]{:S(2)}, u32[]{:S(2)}) collective-permute-start(bf16[48,512]{1,0:T(8,128)(2,1)} %get-tuple-element.78), channel_id=1, source_target_pairs={{0,13},{1,4},{2,15},{3,6},{4,1},{5,8},{6,3},{7,10},{8,5},{9,12},{1... | collective-permute-start | bytes 147464 | tf_op jit(solution)/shard_map/ppermute | solution.py:368
  12.0 1.5 %collective-permute-start.5 = (bf16[96,512]{1,0:T(8,128)(2,1)}, bf16[96,512]{1,0:T(8,128)(2,1)S(1)}, u32[]{:S(2)}, u32[]{:S(2)}) collective-permute-start(bf16[96,512]{1,0:T(8,128)(2,1)} %get-tuple-element.76), channel_id=1, source_target_pairs={{0,2},{1,3},{2,4},{3,5},{4,6},{5,7},{6,8},{7,9},{8,10},{9,11},{10,... | collective-permute-start | bytes 294920 | tf_op jit(solution)/shard_map/ppermute | solution.py:368
  13.6 3.2 %collective-permute-start.6 = (bf16[96,512]{1,0:T(8,128)(2,1)}, bf16[96,512]{1,0:T(8,128)(2,1)S(1)}, u32[]{:S(2)}, u32[]{:S(2)}) collective-permute-start(bf16[96,512]{1,0:T(8,128)(2,1)} %get-tuple-element.77), channel_id=1, source_target_pairs={{0,14},{1,15},{2,0},{3,1},{4,2},{5,3},{6,4},{7,5},{8,6},{9,7},{10,... | collective-permute-start | bytes 294920 | tf_op jit(solution)/shard_map/ppermute | solution.py:368
  17.8 7.1 %edge_local.1.local_ref = bf16[3072,512]{1,0:T(8,128)(2,1)} custom-call(s32[3,1,1024]{2,1,0:T(1,128)} %bitcast.23, bf16[3072,512]{1,0:T(8,128)(2,1)} %refs_3_.1, bf16[256,512]{1,0:T(8,128)(2,1)} %refs_6_.1, bf16[1536,512]{1,0:T(8,128)(2,1)} %w_edge_ref.3, bf16[1536,512]{1,0:T(8,128)(2,1)} %w_edge_ref.3), custom_call_target="tpu_custom_call" | custom-call | flops 2415919104 | bytes 6291456 | tf_op jit(solution)/shard_map/edge_local/pallas_call | solution.py:515
  27.9 17.5 %forward.1 = (bf16[768,512]{1,0:T(8,128)(2,1)}, bf16[3072,512]{1,0:T(8,128)(2,1)}, bf16[3072,512]{1,0:T(8,128)(2,1)}, bf16[3072,512]{1,0:T(8,128)(2,1)}, f32[3,1...) custom-call(s32[1]{0:T(128)} %bitcast.me_ref, ...), custom_call_target="tpu_custom_call" | custom-call | tf_op jit(solution)/shard_map/forward/pallas_call | solution.py:535
  45.5 19.9 %backward.1 = (bf16[3072,512]{1,0:T(8,128)(2,1)}, bf16[256,512]{1,0:T(8,128)(2,1)}, bf16[2,320,512]{2,1,0:T(8,128)(2,1)}, bf16[2,320,512]{2,1,0:T(8,128)(2,1)}, ...) custom-call(s32[1]{0:T(128)} %bitcast.me_ref, ...), custom_call_target="tpu_custom_call" | custom-call | flops 8858370048 | bytes 15728640 | tf_op jit(solution)/shard_map/backward/pallas_call | solution.py:584
  65.7 1.8 %collective-permute-start.13 = (bf16[2,320,512]{2,1,0:T(8,128)(2,1)}, bf16[2,320,512]{2,1,0:T(8,128)(2,1)S(1)}, u32[]{:S(2)}, u32[]{:S(2)}) collective-permute-start(bf16[2,320,512]{2,1,0:T(8,128)(2,1)} %get-tuple-element.108), channel_id=1, source_target_pairs={{0,1},{1,0},{2,3},{3,2},{4,5},{5,4},{6,7},{7,6},{8,9},{9,8},{10,11... | collective-permute-start | bytes 1966088 | tf_op jit(solution)/shard_map/ppermute | solution.py:368
  68.0 1.1 collective-permute-start.16
  69.2 1.1 collective-permute-done.15
  70.2 2.5 %collective-permute-start.17 = (bf16[96,512]{1,0:T(8,128)(2,1)}, bf16[96,512]{1,0:T(8,128)(2,1)S(1)}, u32[]{:S(2)}, u32[]{:S(2)}) collective-permute-start(bf16[96,512]{1,0:T(8,128)(2,1)} %get-tuple-element.116), channel_id=1, source_target_pairs={{0,14},{1,15},{2,0},{3,1},{4,2},{5,3},{6,4},{7,5},{8,6},{9,7},{10,... | collective-permute-start | bytes 294920 | tf_op jit(solution)/shard_map/ppermute | solution.py:368
  73.7 2.1 %collective-permute-done.16.refs_2_ = bf16[96,512]{1,0:T(8,128)(2,1)S(1)} collective-permute-done((bf16[96,512]{1,0:T(8,128)(2,1)}, bf16[96,512]{1,0:T(8,128)(2,1)S(1)}, u32[]{:S(2)}, u32[]{:S(2)}) %collective-permute-start.16) | collective-permute-done | bytes 98336 | tf_op jit(solution)/shard_map/ppermute | solution.py:368
  75.8 1.8 %collective-permute-done.17.refs_3_ = bf16[96,512]{1,0:T(8,128)(2,1)S(1)} collective-permute-done((bf16[96,512]{1,0:T(8,128)(2,1)}, bf16[96,512]{1,0:T(8,128)(2,1)S(1)}, u32[]{:S(2)}, u32[]{:S(2)}) %collective-permute-start.17) | collective-permute-done | bytes 98336 | tf_op jit(solution)/shard_map/ppermute | solution.py:368
  78.2 2.1 %collective-permute-start.28 = (bf16[384,512]{1,0:T(8,128)(2,1)S(1)}, bf16[384,512]{1,0:T(8,128)(2,1)S(1)}, u32[]{:S(2)}, u32[]{:S(2)}) collective-permute-start(bf16[384,512]{1,0:T(8,128)(2,1)S(1)} %get-tuple-element.133), channel_id=1, source_target_pairs={{0,2},{1,3},{2,0},{3,1},{4,6},{5,7},{6,4},{7,5},{8,10},{9,11},{10,... | collective-permute-start | bytes 1179656 | tf_op jit(solution)/shard_map/ppermute | solution.py:368
  80.3 6.2 %edge_grad.1 = bf16[3072,512]{1,0:T(8,128)(2,1)} custom-call(s32[1]{0:T(128)S(6)} %copy.19.count_ref, s32[3,1,1024]{2,1,0:T(1,128)} %bitcast.26, bf16[3072,512]{1,0:T(8,128)(2,1)} %get-tuple-element.127.d_pre_ref, bf16[256,512]{1,0:T(8,128)(2,1)} %get-tuple-element.94.refs_4_.d_aggregate_ref, bf16[1536,512]{1,0:T(8,128)(2,1)} %w_edge_ref.3), custom_call_target="tpu_custom_call" | custom-call | flops 2415919104 | bytes 6291456 | tf_op jit(solution)/shard_map/edge_grad/pallas_call | solution.py:646
  86.6 2.1 %collective-permute-done.23 = bf16[320,512]{1,0:T(8,128)(2,1)S(1)} collective-permute-done((bf16[320,512]{1,0:T(8,128)(2,1)S(1)}, bf16[320,512]{1,0:T(8,128)(2,1)S(1)}, u32[]{:S(2)}, u32[]{:S(2)}) %collective-permute-start.23) | collective-permute-done | bytes 327712 | tf_op jit(solution)/shard_map/ppermute | solution.py:368
  89.4 1.2 %collective-permute-start.26 = (bf16[80,512]{1,0:T(8,128)(2,1)S(1)}, bf16[80,512]{1,0:T(8,128)(2,1)S(1)}, u32[]{:S(2)}, u32[]{:S(2)}) collective-permute-start(bf16[80,512]{1,0:T(8,128)(2,1)S(1)} %get-tuple-element.149), channel_id=1, source_target_pairs={{0,12},{1,13},{2,14},{3,15},{4,8},{5,9},{6,10},{7,11},{8,4},{9,5},... | collective-permute-start | bytes 245768 | tf_op jit(solution)/shard_map/ppermute | solution.py:368
  90.6 5.6 %collective-permute-done.28 = bf16[384,512]{1,0:T(8,128)(2,1)S(1)} collective-permute-done((bf16[384,512]{1,0:T(8,128)(2,1)S(1)}, bf16[384,512]{1,0:T(8,128)(2,1)S(1)}, u32[]{:S(2)}, u32[]{:S(2)}) %collective-permute-start.28) | collective-permute-done | bytes 393248 | tf_op jit(solution)/shard_map/ppermute | solution.py:368
  96.5 1.0 collective-permute-done.25.refs_9_
  97.5 1.2 %collective-permute-start.27 = (bf16[96,512]{1,0:T(8,128)(2,1)S(1)}, bf16[96,512]{1,0:T(8,128)(2,1)S(1)}, u32[]{:S(2)}, u32[]{:S(2)}) collective-permute-start(bf16[96,512]{1,0:T(8,128)(2,1)S(1)} %get-tuple-element.153), channel_id=1, source_target_pairs={{0,8},{1,9},{2,10},{3,11},{4,12},{5,13},{6,14},{7,15},{8,0},{9,1},... | collective-permute-start | bytes 294920 | tf_op jit(solution)/shard_map/ppermute | solution.py:368
  98.6 3.1 %collective-permute-done.24.refs_8_ = bf16[80,512]{1,0:T(8,128)(2,1)S(1)} collective-permute-done((bf16[80,512]{1,0:T(8,128)(2,1)S(1)}, bf16[80,512]{1,0:T(8,128)(2,1)S(1)}, u32[]{:S(2)}, u32[]{:S(2)}) %collective-permute-start.24) | collective-permute-done | bytes 81952 | tf_op jit(solution)/shard_map/ppermute | solution.py:368
  102.9 3.9 %collective-permute-start.29 = (bf16[96,512]{1,0:T(8,128)(2,1)S(1)}, bf16[96,512]{1,0:T(8,128)(2,1)S(1)}, u32[]{:S(2)}, u32[]{:S(2)}) collective-permute-start(bf16[96,512]{1,0:T(8,128)(2,1)S(1)} %get-tuple-element.146), channel_id=1, source_target_pairs={{0,4},{1,5},{2,6},{3,7},{4,0},{5,1},{6,2},{7,3},{8,12},{9,13},{10,... | collective-permute-start | bytes 294920 | tf_op jit(solution)/shard_map/ppermute | solution.py:368
  107.4 4.0 %scatter_lists.1 = bf16[2048,512]{1,0:T(8,128)(2,1)} custom-call(s32[1]{0:T(128)} %bitcast.me_ref, s32[16,48]{1,0:T(8,128)} %bitcast.28, bf16[48,512]{1,0:T(8,128)(2,1)} %get-tuple-element.119.refs_0_, bf16[48,512]{1,0:T(8,128)(2,1)} %copy-done.21, bf16[96,512]{1,0:T(8,128)(2,1)} %copy-done.14, bf16[96,512]{1,0:T(8,128)(2,1)} %copy-done.15, ...), custom_call_target="tpu_custom_call" | custom-call | tf_op jit(solution)/shard_map/scatter_lists/pallas_call | solution.py:666
  (110 shorter events, 11.5 us)
Async XLA Ops:
  4.0 9.6 %collective-permute-start.2 = (bf16[48,512]{1,0:T(8,128)(2,1)}, bf16[48,512]{1,0:T(8,128)(2,1)S(1)}, u32[]{:S(2)}, u32[]{:S(2)}) collective-permute-start(bf16[48,512]{1,0:T(8,128)(2,1)} %get-tuple-element.72), channel_id=1, source_target_pairs={{0,12},{1,13},{2,14},{3,15},{4,8},{5,9},{6,10},{7,11},{8,4},{9,5},... | collective-permute-start | bytes 147464 | tf_op jit(solution)/shard_map/ppermute | solution.py:368
  9.1 7.7 %collective-permute-start.1 = (bf16[48,512]{1,0:T(8,128)(2,1)}, bf16[48,512]{1,0:T(8,128)(2,1)S(1)}, u32[]{:S(2)}, u32[]{:S(2)}) collective-permute-start(bf16[48,512]{1,0:T(8,128)(2,1)} %get-tuple-element.72), channel_id=1, source_target_pairs={{0,8},{1,9},{2,10},{3,11},{4,12},{5,13},{6,14},{7,15},{8,0},{9,1},... | collective-permute-start | bytes 147464 | tf_op jit(solution)/shard_map/ppermute | solution.py:368
  9.1 7.7 %collective-permute-start = (bf16[48,512]{1,0:T(8,128)(2,1)}, bf16[48,512]{1,0:T(8,128)(2,1)S(1)}, u32[]{:S(2)}, u32[]{:S(2)}) collective-permute-start(bf16[48,512]{1,0:T(8,128)(2,1)} %get-tuple-element.72), channel_id=1, source_target_pairs={{0,4},{1,5},{2,6},{3,7},{4,0},{5,1},{6,2},{7,3},{8,12},{9,13},{10,... | collective-permute-start | bytes 147464 | tf_op jit(solution)/shard_map/ppermute | solution.py:368
  9.7 15.1 %collective-permute-start.7 = (bf16[48,512]{1,0:T(8,128)(2,1)}, bf16[48,512]{1,0:T(8,128)(2,1)S(1)}, u32[]{:S(2)}, u32[]{:S(2)}) collective-permute-start(bf16[48,512]{1,0:T(8,128)(2,1)} %get-tuple-element.78), channel_id=1, source_target_pairs={{0,13},{1,4},{2,15},{3,6},{4,1},{5,8},{6,3},{7,10},{8,5},{9,12},{1... | collective-permute-start | bytes 147464 | tf_op jit(solution)/shard_map/ppermute | solution.py:368
  12.0 12.8 %collective-permute-start.5 = (bf16[96,512]{1,0:T(8,128)(2,1)}, bf16[96,512]{1,0:T(8,128)(2,1)S(1)}, u32[]{:S(2)}, u32[]{:S(2)}) collective-permute-start(bf16[96,512]{1,0:T(8,128)(2,1)} %get-tuple-element.76), channel_id=1, source_target_pairs={{0,2},{1,3},{2,4},{3,5},{4,6},{5,7},{6,8},{7,9},{8,10},{9,11},{10,... | collective-permute-start | bytes 294920 | tf_op jit(solution)/shard_map/ppermute | solution.py:368
  13.6 11.3 %collective-permute-start.6 = (bf16[96,512]{1,0:T(8,128)(2,1)}, bf16[96,512]{1,0:T(8,128)(2,1)S(1)}, u32[]{:S(2)}, u32[]{:S(2)}) collective-permute-start(bf16[96,512]{1,0:T(8,128)(2,1)} %get-tuple-element.77), channel_id=1, source_target_pairs={{0,14},{1,15},{2,0},{3,1},{4,2},{5,3},{6,4},{7,5},{8,6},{9,7},{10,... | collective-permute-start | bytes 294920 | tf_op jit(solution)/shard_map/ppermute | solution.py:368
  17.6 7.3 %collective-permute-start.4 = (bf16[192,512]{1,0:T(8,128)(2,1)S(1)}, bf16[192,512]{1,0:T(8,128)(2,1)S(1)}, u32[]{:S(2)}, u32[]{:S(2)}) collective-permute-start(bf16[192,512]{1,0:T(8,128)(2,1)S(1)} %pad_maximum_fusion.refs_7_), channel_id=1, source_target_pairs={{0,1},{1,0},{2,3},{3,2},{4,5},{5,4},{6,7},{7,6},{8,9},{9,8},{10,11... | collective-permute-start | bytes 589832 | tf_op jit(solution)/shard_map/ppermute | solution.py:368
  17.7 7.3 %collective-permute-start.3 = (bf16[192,512]{1,0:T(8,128)(2,1)S(1)}, bf16[192,512]{1,0:T(8,128)(2,1)S(1)}, u32[]{:S(2)}, u32[]{:S(2)}) collective-permute-start(bf16[192,512]{1,0:T(8,128)(2,1)S(1)} %pad_maximum_fusion.refs_7_), channel_id=1, source_target_pairs={{0,2},{1,3},{2,0},{3,1},{4,6},{5,7},{6,4},{7,5},{8,10},{9,11},{10,... | collective-permute-start | bytes 589832 | tf_op jit(solution)/shard_map/ppermute | solution.py:368
  45.4 20.1 %collective-permute-start.12 = (bf16[2,384,512]{2,1,0:T(8,128)(2,1)}, bf16[2,384,512]{2,1,0:T(8,128)(2,1)S(1)}, u32[]{:S(2)}, u32[]{:S(2)}) collective-permute-start(bf16[2,384,512]{2,1,0:T(8,128)(2,1)} %get-tuple-element.89), channel_id=1, source_target_pairs={{0,2},{1,3},{2,0},{3,1},{4,6},{5,7},{6,4},{7,5},{8,10},{9,11},{10,... | collective-permute-start | bytes 2359304 | tf_op jit(solution)/shard_map/ppermute | solution.py:368
  65.7 7.2 %collective-permute-start.13 = (bf16[2,320,512]{2,1,0:T(8,128)(2,1)}, bf16[2,320,512]{2,1,0:T(8,128)(2,1)S(1)}, u32[]{:S(2)}, u32[]{:S(2)}) collective-permute-start(bf16[2,320,512]{2,1,0:T(8,128)(2,1)} %get-tuple-element.108), channel_id=1, source_target_pairs={{0,1},{1,0},{2,3},{3,2},{4,5},{5,4},{6,7},{7,6},{8,9},{9,8},{10,11... | collective-permute-start | bytes 1966088 | tf_op jit(solution)/shard_map/ppermute | solution.py:368
  68.0 7.8 %collective-permute-start.16 = (bf16[96,512]{1,0:T(8,128)(2,1)}, bf16[96,512]{1,0:T(8,128)(2,1)S(1)}, u32[]{:S(2)}, u32[]{:S(2)}) collective-permute-start(bf16[96,512]{1,0:T(8,128)(2,1)} %get-tuple-element.115), channel_id=1, source_target_pairs={{0,2},{1,3},{2,4},{3,5},{4,6},{5,7},{6,8},{7,9},{8,10},{9,11},{10,... | collective-permute-start | bytes 294920 | tf_op jit(solution)/shard_map/ppermute | solution.py:368
  70.2 7.4 %collective-permute-start.17 = (bf16[96,512]{1,0:T(8,128)(2,1)}, bf16[96,512]{1,0:T(8,128)(2,1)S(1)}, u32[]{:S(2)}, u32[]{:S(2)}) collective-permute-start(bf16[96,512]{1,0:T(8,128)(2,1)} %get-tuple-element.116), channel_id=1, source_target_pairs={{0,14},{1,15},{2,0},{3,1},{4,2},{5,3},{6,4},{7,5},{8,6},{9,7},{10,... | collective-permute-start | bytes 294920 | tf_op jit(solution)/shard_map/ppermute | solution.py:368
  77.6 25.2 %collective-permute-start.19 = (bf16[48,512]{1,0:T(8,128)(2,1)S(1)}, bf16[48,512]{1,0:T(8,128)(2,1)S(1)}, u32[]{:S(2)}, u32[]{:S(2)}) collective-permute-start(bf16[48,512]{1,0:T(8,128)(2,1)S(1)} %copy-done.22), channel_id=1, source_target_pairs={{0,1},{1,0},{2,3},{3,2},{4,5},{5,4},{6,7},{7,6},{8,9},{9,8},{10,11... | collective-permute-start | bytes 147464 | tf_op jit(solution)/shard_map/ppermute | solution.py:368
  77.6 25.2 %collective-permute-start.20 = (bf16[96,512]{1,0:T(8,128)(2,1)S(1)}, bf16[96,512]{1,0:T(8,128)(2,1)S(1)}, u32[]{:S(2)}, u32[]{:S(2)}) collective-permute-start(bf16[96,512]{1,0:T(8,128)(2,1)S(1)} %collective-permute-done.16.refs_2_), channel_id=1, source_target_pairs={{0,1},{1,0},{2,3},{3,2},{4,5},{5,4},{6,7},{7,6},{8,9},{9,8},{10,11... | collective-permute-start | bytes 294920 | tf_op jit(solution)/shard_map/ppermute | solution.py:368
  78.1 10.6 %collective-permute-start.23 = (bf16[320,512]{1,0:T(8,128)(2,1)S(1)}, bf16[320,512]{1,0:T(8,128)(2,1)S(1)}, u32[]{:S(2)}, u32[]{:S(2)}) collective-permute-start(bf16[320,512]{1,0:T(8,128)(2,1)S(1)} %get-tuple-element.126), channel_id=1, source_target_pairs={{0,2},{1,3},{2,0},{3,1},{4,6},{5,7},{6,4},{7,5},{8,10},{9,11},{10,... | collective-permute-start | bytes 983048 | tf_op jit(solution)/shard_map/ppermute | solution.py:368
  78.2 8.4 %collective-permute-start.22 = (bf16[192,512]{1,0:T(8,128)(2,1)S(1)}, bf16[192,512]{1,0:T(8,128)(2,1)S(1)}, u32[]{:S(2)}, u32[]{:S(2)}) collective-permute-start(bf16[192,512]{1,0:T(8,128)(2,1)S(1)} %bitcast.22), channel_id=1, source_target_pairs={{0,4},{1,5},{2,6},{3,7},{4,0},{5,1},{6,2},{7,3},{8,12},{9,13},{10,... | collective-permute-start | bytes 589832 | tf_op jit(solution)/shard_map/ppermute | solution.py:368
  78.2 18.0 %collective-permute-start.28 = (bf16[384,512]{1,0:T(8,128)(2,1)S(1)}, bf16[384,512]{1,0:T(8,128)(2,1)S(1)}, u32[]{:S(2)}, u32[]{:S(2)}) collective-permute-start(bf16[384,512]{1,0:T(8,128)(2,1)S(1)} %get-tuple-element.133), channel_id=1, source_target_pairs={{0,2},{1,3},{2,0},{3,1},{4,6},{5,7},{6,4},{7,5},{8,10},{9,11},{10,... | collective-permute-start | bytes 1179656 | tf_op jit(solution)/shard_map/ppermute | solution.py:368
  89.4 6.9 %collective-permute-start.26 = (bf16[80,512]{1,0:T(8,128)(2,1)S(1)}, bf16[80,512]{1,0:T(8,128)(2,1)S(1)}, u32[]{:S(2)}, u32[]{:S(2)}) collective-permute-start(bf16[80,512]{1,0:T(8,128)(2,1)S(1)} %get-tuple-element.149), channel_id=1, source_target_pairs={{0,12},{1,13},{2,14},{3,15},{4,8},{5,9},{6,10},{7,11},{8,4},{9,5},... | collective-permute-start | bytes 245768 | tf_op jit(solution)/shard_map/ppermute | solution.py:368
  90.6 6.8 %collective-permute-start.25 = (bf16[80,512]{1,0:T(8,128)(2,1)S(1)}, bf16[80,512]{1,0:T(8,128)(2,1)S(1)}, u32[]{:S(2)}, u32[]{:S(2)}) collective-permute-start(bf16[80,512]{1,0:T(8,128)(2,1)S(1)} %get-tuple-element.150), channel_id=1, source_target_pairs={{0,8},{1,9},{2,10},{3,11},{4,12},{5,13},{6,14},{7,15},{8,0},{9,1},... | collective-permute-start | bytes 245768 | tf_op jit(solution)/shard_map/ppermute | solution.py:368
  96.4 10.4 %collective-permute-start.21 = (bf16[96,512]{1,0:T(8,128)(2,1)S(1)}, bf16[96,512]{1,0:T(8,128)(2,1)S(1)}, u32[]{:S(2)}, u32[]{:S(2)}) collective-permute-start(bf16[96,512]{1,0:T(8,128)(2,1)S(1)} %collective-permute-done.17.refs_3_), channel_id=1, source_target_pairs={{0,1},{1,0},{2,3},{3,2},{4,5},{5,4},{6,7},{7,6},{8,9},{9,8},{10,11... | collective-permute-start | bytes 294920 | tf_op jit(solution)/shard_map/ppermute | solution.py:368
  97.5 13.9 %collective-permute-start.27 = (bf16[96,512]{1,0:T(8,128)(2,1)S(1)}, bf16[96,512]{1,0:T(8,128)(2,1)S(1)}, u32[]{:S(2)}, u32[]{:S(2)}) collective-permute-start(bf16[96,512]{1,0:T(8,128)(2,1)S(1)} %get-tuple-element.153), channel_id=1, source_target_pairs={{0,8},{1,9},{2,10},{3,11},{4,12},{5,13},{6,14},{7,15},{8,0},{9,1},... | collective-permute-start | bytes 294920 | tf_op jit(solution)/shard_map/ppermute | solution.py:368
  101.7 11.0 %collective-permute-start.31 = (bf16[96,512]{1,0:T(8,128)(2,1)S(1)}, bf16[96,512]{1,0:T(8,128)(2,1)S(1)}, u32[]{:S(2)}, u32[]{:S(2)}) collective-permute-start(bf16[96,512]{1,0:T(8,128)(2,1)S(1)} %get-tuple-element.144), channel_id=1, source_target_pairs={{0,12},{1,13},{2,14},{3,15},{4,8},{5,9},{6,10},{7,11},{8,4},{9,5},... | collective-permute-start | bytes 294920 | tf_op jit(solution)/shard_map/ppermute | solution.py:368
  102.8 10.3 %collective-permute-start.30 = (bf16[96,512]{1,0:T(8,128)(2,1)S(1)}, bf16[96,512]{1,0:T(8,128)(2,1)S(1)}, u32[]{:S(2)}, u32[]{:S(2)}) collective-permute-start(bf16[96,512]{1,0:T(8,128)(2,1)S(1)} %get-tuple-element.145), channel_id=1, source_target_pairs={{0,8},{1,9},{2,10},{3,11},{4,12},{5,13},{6,14},{7,15},{8,0},{9,1},... | collective-permute-start | bytes 294920 | tf_op jit(solution)/shard_map/ppermute | solution.py:368
  102.9 10.3 %collective-permute-start.29 = (bf16[96,512]{1,0:T(8,128)(2,1)S(1)}, bf16[96,512]{1,0:T(8,128)(2,1)S(1)}, u32[]{:S(2)}, u32[]{:S(2)}) collective-permute-start(bf16[96,512]{1,0:T(8,128)(2,1)S(1)} %get-tuple-element.146), channel_id=1, source_target_pairs={{0,4},{1,5},{2,6},{3,7},{4,0},{5,1},{6,2},{7,3},{8,12},{9,13},{10,... | collective-permute-start | bytes 294920 | tf_op jit(solution)/shard_map/ppermute | solution.py:368
  (32 other events, 178.8 us)

commit v6 on v5

--- a/solution.py
+++ b/solution.py
@@ -119,6 +119,29 @@
     ]
 
 
+def write_back(refs, cap, lists):
+    mine, swapped, after, before, across = refs
+    mine[...] = lists[0]
+    for place, index in enumerate((1, 3, 5)):
+        swapped[place * cap : (place + 1) * cap, :] = lists[index]
+    after[...] = lists[2]
+    before[...] = lists[4]
+    across[...] = lists[6]
+
+
+def read_back(refs, cap):
+    mine, swapped, from_before, from_after, across = refs
+    return [
+        mine[...],
+        swapped[:cap, :],
+        from_after[:cap, :],
+        from_after[cap:, :],
+        from_before[:cap, :],
+        from_before[cap:, :],
+        across[...],
+    ]
+
+
 def list_hots(me, rows_ref, grid_count, first):
     peers, cap = rows_ref.shape
     pieces = []
@@ -152,14 +175,14 @@
 
 
 def scatter_kernel(skip, me_ref, rows_ref, *refs):
-    near_refs, far_refs, out_ref = refs[:7], refs[7:-1], refs[-1]
+    near_refs, far_refs, out_ref = refs[:5], refs[5:-1], refs[-1]
     part = out_ref.shape[0]
     cap = rows_ref.shape[1]
     hots = list_hots(me_ref[0], rows_ref, part, pl.program_id(0) * part)
     far = far_refs[0][skip:, :].astype(F32)
     for ref in far_refs[1:]:
         far = far + ref[skip:, :].astype(F32)
-    values = jnp.concatenate(read_near(near_refs, cap) + [far.astype(BF16)], axis=0)
+    values = jnp.concatenate(read_back(near_refs, cap) + [far.astype(BF16)], axis=0)
     out_ref[...] = contract_rows(hots, values).astype(BF16)
 
 
@@ -168,18 +191,18 @@
     return [(start, slice(start, start + SUB)) for start in range(0, rows, SUB)]
 
 
-def local_kernel(dst_ref, edge_ref, mesh_ref, w_edge_ref, w_receiver_ref, *refs):
-    out_ref, mesh_proj = refs[-2:]
+def local_kernel(dst_ref, edge_ref, mesh_ref, w_edge_ref, w_receiver_ref, out_ref, weights):
+    width = edge_ref.shape[1]
 
     @pl.when(pl.program_id(0) == 0)
     def _():
-        mesh_proj[...] = dot(mesh_ref[...], w_receiver_ref[...]).astype(BF16)
+        weights[:width, :] = w_edge_ref[...]
+        weights[width:, :] = dot(mesh_ref[...], w_receiver_ref[...]).astype(BF16)
 
     for start, part in halves_of(edge_ref):
         onehot = hot_rows(dst_ref[0, :, part], mesh_ref.shape[0])
-        out_ref[part, :] = (
-            dot(edge_ref[part, :], w_edge_ref[...]) + dot(onehot, mesh_proj[...])
-        ).astype(BF16)
+        joined = jnp.concatenate([edge_ref[part, :], onehot], axis=1)
+        out_ref[part, :] = dot(joined, weights[...]).astype(BF16)
 
 
 def split_out(me, peers, first, send_ref, keep_ref, parts):
@@ -337,7 +360,7 @@
         mesh_grad_ref[...] = (d_mesh_ref[...] + contract_cols(mesh_summed, w_receiver_ref[...])).astype(BF16)
         cap = near_refs[0].shape[0]
         owners = near_peers(me, peers)
-        write_near(
+        write_back(
             near_refs, cap, [d_slots[pl.ds(pl.multiple_of(owner * cap, 16), cap), :] for owner in owners]
         )
         out_share = grad_out.shape[0] // peers
@@ -420,14 +443,14 @@
     return terms
 
 
-def halve_first(peers, pieces):
+def halve_sum(peers, pieces):
     count = peers // 4
-    share = pieces.shape[0] // count
-    blocks = pieces.reshape(count // 2, 2, share, -1)
-    return blocks[:, 0].reshape(-1, pieces.shape[1]), blocks[:, 1].reshape(-1, pieces.shape[1])
-
-
-def node_last(peers, pieces):
+    blocks = pieces.reshape(count // 2, 2, -1, pieces.shape[1])
+    kept, outgoing = [blocks[:, place].reshape(-1, pieces.shape[1]) for place in range(2)]
+    return add(kept, send(outgoing, by_xor(peers, 4)))
+
+
+def rest_terms(peers, pieces):
     count = peers // 8
     share = pieces.shape[0] // count
     terms = [pieces[:share]]
@@ -495,6 +518,10 @@
     near_specs = [whole((count, width)) for count in near_rows]
     near_shapes = [jax.ShapeDtypeStruct((count, width), BF16) for count in near_rows]
     core_specs = near_specs + [whole((2 * cap, width))] * 2
+    back_rows = (cap, 3 * cap, cap, cap, cap)
+    back_specs = [whole((count, width)) for count in back_rows]
+    back_shapes = [jax.ShapeDtypeStruct((count, width), BF16) for count in back_rows]
+    return_specs = [whole((count, width)) for count in (cap, 3 * cap, 2 * cap, 2 * cap, cap)]
     lists = pl.pallas_call(
         gather_kernel,
         grid=(2,),
@@ -518,7 +545,7 @@
         in_specs=[index_tile, tile_of(width), whole(mesh_latent.shape), weight(0), weight(2)],
         out_specs=tile_of(width),
         out_shape=jax.ShapeDtypeStruct((edges, width), BF16),
-        scratch_shapes=[pltpu.VMEM((mesh_count, width), BF16)],
+        scratch_shapes=[pltpu.VMEM((width + mesh_count, width), BF16)],
         compiler_params=params,
         cost_estimate=pl.CostEstimate(
             flops=2 * edges * width * (width + mesh_count),
@@ -589,14 +616,14 @@
         + [whole((mesh_count, width)), whole((slots, width))]
         + [whole((mesh_count, width))] * 2
         + [weight(1), weight(2), whole(square)],
-        out_specs=[tile_of(width), whole((mesh_count, width))] + slot_spec + edge_spec + near_specs,
+        out_specs=[tile_of(width), whole((mesh_count, width))] + slot_spec + edge_spec + back_specs,
         out_shape=[
             jax.ShapeDtypeStruct((edges, width), BF16),
             jax.ShapeDtypeStruct((mesh_count, width), BF16),
         ]
         + slot_shape
         + edge_shape
-        + near_shapes,
+        + back_shapes,
         scratch_shapes=[
             pltpu.VMEM((slots + mesh_count, width), F32),
             pltpu.VMEM(w_edge_in.shape, F32),
@@ -635,14 +662,16 @@
     slot_next, slot_kept = first_sum(peers, 1, slot_send, slot_keep)
     edge_next, edge_kept = first_sum(peers, 1, edge_send, edge_keep)
     node_pieces = next_sum(peers, 1, node_next, node_kept)
-    returned = exchange_near(peers, returns)
-    (slot_next, slot_kept, edge_next, edge_kept, node_pieces, returned, d_pre) = lax.optimization_barrier(
-        (slot_next, slot_kept, edge_next, edge_kept, node_pieces, returned, d_pre)
+    swapped = send(returns[1], by_xor(peers, 1))
+    (slot_next, slot_kept, edge_next, edge_kept, swapped) = lax.optimization_barrier(
+        (slot_next, slot_kept, edge_next, edge_kept, swapped)
     )
     slot_pieces = next_sum(peers, 2, slot_next, slot_kept)
     edge_pieces = next_sum(peers, 2, edge_next, edge_kept)
-    node_kept, node_next = halve_first(peers, node_pieces)
-    node_pieces = add(node_kept, send(node_next, by_xor(peers, 4)))
+    to_after = jnp.concatenate([returns[2], swapped[cap : 2 * cap]], axis=0)
+    to_before = jnp.concatenate([returns[3], swapped[2 * cap :]], axis=0)
+    node_pieces, d_pre, to_after, to_before = lax.optimization_barrier((node_pieces, d_pre, to_after, to_before))
+    node_pieces = halve_sum(peers, node_pieces)
     edge_grad = pl.pallas_call(
         edges_kernel,
         grid=(tiles,),
@@ -655,20 +684,29 @@
         ),
         name="edge_grad",
     )(tile_count, dst, d_pre, d_aggregate, w_edge_in)
-    node_pieces, slot_pieces, edge_grad = lax.optimization_barrier((node_pieces, slot_pieces, edge_grad))
-    returned = core_near(peers, returned)
-    slot_terms = last_terms(peers, slot_pieces)
-    node_terms = node_last(peers, node_pieces)
+    (node_pieces, slot_pieces, edge_grad, to_after, to_before, across) = lax.optimization_barrier(
+        (node_pieces, slot_pieces, edge_grad, to_after, to_before, returns[4])
+    )
+    slot_half = halve_sum(peers, slot_pieces)
+    node_terms = rest_terms(peers, node_pieces)
+    near = [
+        send(to_after, by_shift(peers, 2)),
+        send(to_before, by_shift(peers, -2)),
+        send(across, across_chips(peers)),
+    ]
+    slot_half, edge_pieces, near = lax.optimization_barrier((slot_half, edge_pieces, near))
+    slot_terms = rest_terms(peers, slot_half)
     edge_terms = last_terms(peers, edge_pieces)
-    node_terms, edge_terms[0] = lax.optimization_barrier((node_terms, edge_terms[0]))
+    node_terms, slot_terms = lax.optimization_barrier((node_terms, slot_terms))
+    returned = [returns[0], swapped, *near]
     node_rows = w_node_in.shape[0] // peers
     out_rows = w_edge_out.shape[0] // peers
     grid_grad = pl.pallas_call(
         functools.partial(scatter_kernel, out_rows),
         grid=(2,),
         in_specs=[smem, whole(rows.shape)]
-        + core_specs
-        + [whole((out_rows + cap, width))] * upper,
+        + return_specs
+        + [whole((out_rows + cap, width))] * (upper // 2),
         out_specs=pl.BlockSpec((grid_part, width), lambda step: (step, 0)),
         out_shape=jax.ShapeDtypeStruct((grid_count, width), BF16),
         compiler_params=params,

time: 115 us -> 113 us (0.983); the launches traced: 114 us -> 111 us
  Pallas kernels: 58 us -> 49.6 us
  starting transfers between devices: 29.5 us -> 36.7 us
  local copies, waits for them, and re-layouts: 2.07 us -> 0.87 us
    ppermute x32 -> x29, starting transfers between devices: 29.5 us -> 36.7 us  [send(): return lax.ppermute(values, 'lon', perm)]
    pallas_call x1, Pallas kernels: 19.9 us -> 15.9 us  [on_device(): pl.pallas_call(functools.partial(backward_kernel, peers), grid=(tiles,),...]
    pallas_call x1, Pallas kernels: 17.5 us -> 14.5 us  [on_device(): pl.pallas_call(functools.partial(forward_kernel, peers), grid=(tiles,), i...]
    ppermute x32 -> x29, waiting for transfers between devices: 18.2 us -> 17.2 us  [send(): return lax.ppermute(values, 'lon', perm)]
  transfers between devices with their start and end apart: 32 -> 29, of which waited for: 11 -> 10; matrix products, arithmetic and copies ran while one was open for 4% -> 3% of each run, Pallas kernels for 33% -> 29%
where the time goes in v6:
time: 113 us; the launch traced here: 111 us
  Pallas kernels  49.6 us (44%)
  starting transfers between devices  36.7 us (32%)
  waiting for transfers between devices  17.2 us (15%)
  other arithmetic  4.5 us (4%)
  between operations  1.77 us (2%)
    ppermute x29, starting transfers between devices, send(): return lax.ppermute(values, 'lon', perm)  36.7 us
    ppermute x29, waiting for transfers between devices, send(): return lax.ppermute(values, 'lon', perm)  17.2 us
    pallas_call x1, Pallas kernels, on_device(): pl.pallas_call(functools.partial(backward_kernel, peers), grid=(tiles,),...  15.9 us
    pallas_call x1, Pallas kernels, on_device(): pl.pallas_call(functools.partial(forward_kernel, peers), grid=(tiles,), i...  14.5 us
    pallas_call x1, Pallas kernels, on_device(): pl.pallas_call(local_kernel, grid=(tiles,), in_specs=[index_tile, tile_of...  6.62 us
    pallas_call x1, Pallas kernels, on_device(): pl.pallas_call(edges_kernel, grid=(tiles,), in_specs=[smem, index_tile, t...  5.21 us
    pallas_call x1, Pallas kernels, on_device(): pl.pallas_call(functools.partial(scatter_kernel, out_rows), grid=(2,), in...  3.91 us
    pallas_call x1, Pallas kernels, on_device(): pl.pallas_call(gather_kernel, grid=(2,), in_specs=[smem, whole(rows.shape...  3.36 us
  transfers between devices with their start and end apart: 29, of which 10 were waited for; matrix products, arithmetic and copies ran while one was open for 3% of the time, Pallas kernels for 29%

profile of v6, /device:TPU:0, one launch (start us, length us, event | category | flops | bytes accessed | tf_op | source)
XLA Modules:
  0.0 110.6 jit_solution(6063690034298993391)
XLA Ops:
  0.6 3.4 %gather_lists.1 = (bf16[48,512]{1,0:T(8,128)(2,1)}, bf16[48,512]{1,0:T(8,128)(2,1)}, bf16[96,512]{1,0:T(8,128)(2,1)}, bf16[96,512]{1,0:T(8,128)(2,1)}, bf16[48,512]{1,0:T(8,128)(2,1)}, /*index=5*/bf16[48,512]{1,0:T(8,128)(2,1)}) custom-call(s32[1]{0:T(128)} %bitcast.me_ref, s32[16,48]{1,0:T(8,128)} %bitcast.38, bf16[2048,512]{1,0:T(8,128)(2,1)} %grid_ref.1), custom_call_target="tpu_custom_call" | custom-call | tf_op jit(solution)/shard_map/gather_lists/pallas_call | solution.py:525
  4.0 5.1 %collective-permute-start.2 = (bf16[48,512]{1,0:T(8,128)(2,1)}, bf16[48,512]{1,0:T(8,128)(2,1)S(1)}, u32[]{:S(2)}, u32[]{:S(2)}) collective-permute-start(bf16[48,512]{1,0:T(8,128)(2,1)} %get-tuple-element.79), channel_id=1, source_target_pairs={{0,12},{1,13},{2,14},{3,15},{4,8},{5,9},{6,10},{7,11},{8,4},{9,5},... | collective-permute-start | bytes 147464 | tf_op jit(solution)/shard_map/ppermute | solution.py:391
  9.7 2.3 %collective-permute-start.7 = (bf16[48,512]{1,0:T(8,128)(2,1)}, bf16[48,512]{1,0:T(8,128)(2,1)S(1)}, u32[]{:S(2)}, u32[]{:S(2)}) collective-permute-start(bf16[48,512]{1,0:T(8,128)(2,1)} %get-tuple-element.85), channel_id=1, source_target_pairs={{0,13},{1,4},{2,15},{3,6},{4,1},{5,8},{6,3},{7,10},{8,5},{9,12},{1... | collective-permute-start | bytes 147464 | tf_op jit(solution)/shard_map/ppermute | solution.py:391
  12.0 1.5 %collective-permute-start.5 = (bf16[96,512]{1,0:T(8,128)(2,1)}, bf16[96,512]{1,0:T(8,128)(2,1)S(1)}, u32[]{:S(2)}, u32[]{:S(2)}) collective-permute-start(bf16[96,512]{1,0:T(8,128)(2,1)} %get-tuple-element.83), channel_id=1, source_target_pairs={{0,2},{1,3},{2,4},{3,5},{4,6},{5,7},{6,8},{7,9},{8,10},{9,11},{10,... | collective-permute-start | bytes 294920 | tf_op jit(solution)/shard_map/ppermute | solution.py:391
  13.6 3.2 %collective-permute-start.6 = (bf16[96,512]{1,0:T(8,128)(2,1)}, bf16[96,512]{1,0:T(8,128)(2,1)S(1)}, u32[]{:S(2)}, u32[]{:S(2)}) collective-permute-start(bf16[96,512]{1,0:T(8,128)(2,1)} %get-tuple-element.84), channel_id=1, source_target_pairs={{0,14},{1,15},{2,0},{3,1},{4,2},{5,3},{6,4},{7,5},{8,6},{9,7},{10,... | collective-permute-start | bytes 294920 | tf_op jit(solution)/shard_map/ppermute | solution.py:391
  17.8 6.6 %edge_local.1.local_ref = bf16[3072,512]{1,0:T(8,128)(2,1)} custom-call(s32[3,1,1024]{2,1,0:T(1,128)} %bitcast.34, bf16[3072,512]{1,0:T(8,128)(2,1)} %refs_3_.1, bf16[256,512]{1,0:T(8,128)(2,1)} %refs_6_.1, bf16[1536,512]{1,0:T(8,128)(2,1)} %w_edge_ref.3, bf16[1536,512]{1,0:T(8,128)(2,1)} %w_edge_ref.3), custom_call_target="tpu_custom_call" | custom-call | flops 2415919104 | bytes 6291456 | tf_op jit(solution)/shard_map/edge_local/pallas_call | solution.py:542
  27.7 14.5 %forward.1 = (bf16[768,512]{1,0:T(8,128)(2,1)}, bf16[3072,512]{1,0:T(8,128)(2,1)}, bf16[3072,512]{1,0:T(8,128)(2,1)}, bf16[3072,512]{1,0:T(8,128)(2,1)}, f32[3,1...) custom-call(s32[1]{0:T(128)} %bitcast.me_ref, ...), custom_call_target="tpu_custom_call" | custom-call | tf_op jit(solution)/shard_map/forward/pallas_call | solution.py:562
  42.2 1.7 %collective-permute-start.12 = (bf16[2,384,512]{2,1,0:T(8,128)(2,1)}, bf16[2,384,512]{2,1,0:T(8,128)(2,1)S(1)}, u32[]{:S(2)}, u32[]{:S(2)}) collective-permute-start(bf16[2,384,512]{2,1,0:T(8,128)(2,1)} %get-tuple-element.96), channel_id=1, source_target_pairs={{0,2},{1,3},{2,0},{3,1},{4,6},{5,7},{6,4},{7,5},{8,10},{9,11},{10,... | collective-permute-start | bytes 2359304 | tf_op jit(solution)/shard_map/ppermute | solution.py:391
  43.9 15.9 %backward.1 = (bf16[3072,512]{1,0:T(8,128)(2,1)}, bf16[256,512]{1,0:T(8,128)(2,1)}, bf16[2,320,512]{2,1,0:T(8,128)(2,1)}, bf16[2,320,512]{2,1,0:T(8,128)(2,1)}, ...) custom-call(s32[1]{0:T(128)} %bitcast.me_ref, ...), custom_call_target="tpu_custom_call" | custom-call | flops 8858370048 | bytes 15728640 | tf_op jit(solution)/shard_map/backward/pallas_call | solution.py:611
  59.9 1.3 %collective-permute-done.12 = bf16[2,384,512]{2,1,0:T(8,128)(2,1)S(1)} collective-permute-done((bf16[2,384,512]{2,1,0:T(8,128)(2,1)}, bf16[2,384,512]{2,1,0:T(8,128)(2,1)S(1)}, u32[]{:S(2)}, u32[]{:S(2)}) %collective-permute-start.12) | collective-permute-done | bytes 786464 | tf_op jit(solution)/shard_map/ppermute | solution.py:391
  61.5 4.4 %collective-permute-start.13 = (bf16[2,320,512]{2,1,0:T(8,128)(2,1)}, bf16[2,320,512]{2,1,0:T(8,128)(2,1)S(1)}, u32[]{:S(2)}, u32[]{:S(2)}) collective-permute-start(bf16[2,320,512]{2,1,0:T(8,128)(2,1)} %get-tuple-element.116), channel_id=1, source_target_pairs={{0,1},{1,0},{2,3},{3,2},{4,5},{5,4},{6,7},{7,6},{8,9},{9,8},{10,11... | collective-permute-start | bytes 1966088 | tf_op jit(solution)/shard_map/ppermute | solution.py:391
  66.5 2.1 %collective-permute-done.16 = bf16[384,512]{1,0:T(8,128)(2,1)S(1)} collective-permute-done((bf16[384,512]{1,0:T(8,128)(2,1)S(1)}, bf16[384,512]{1,0:T(8,128)(2,1)S(1)}, u32[]{:S(2)}, u32[]{:S(2)}) %collective-permute-start.16) | collective-permute-done | bytes 393248 | tf_op jit(solution)/shard_map/ppermute | solution.py:391
  70.1 1.9 %collective-permute-start.20 = (bf16[384,512]{1,0:T(8,128)(2,1)S(1)}, bf16[384,512]{1,0:T(8,128)(2,1)S(1)}, u32[]{:S(2)}, u32[]{:S(2)}) collective-permute-start(bf16[384,512]{1,0:T(8,128)(2,1)S(1)} %get-tuple-element.135), channel_id=1, source_target_pairs={{0,2},{1,3},{2,0},{3,1},{4,6},{5,7},{6,4},{7,5},{8,10},{9,11},{10,... | collective-permute-start | bytes 1179656 | tf_op jit(solution)/shard_map/ppermute | solution.py:391
  72.1 5.2 %edge_grad.1 = bf16[3072,512]{1,0:T(8,128)(2,1)} custom-call(s32[1]{0:T(128)S(6)} %copy.23.count_ref, s32[3,1,1024]{2,1,0:T(1,128)} %bitcast.37, bf16[3072,512]{1,0:T(8,128)(2,1)} %get-tuple-element.129.d_pre_ref, bf16[256,512]{1,0:T(8,128)(2,1)} %get-tuple-element.101.refs_4_.d_aggregate_ref, bf16[1536,512]{1,0:T(8,128)(2,1)} %w_edge_ref.3), custom_call_target="tpu_custom_call" | custom-call | flops 2415919104 | bytes 6291456 | tf_op jit(solution)/shard_map/edge_grad/pallas_call | solution.py:675
  77.3 3.2 %collective-permute-done.18 = bf16[320,512]{1,0:T(8,128)(2,1)S(1)} collective-permute-done((bf16[320,512]{1,0:T(8,128)(2,1)S(1)}, bf16[320,512]{1,0:T(8,128)(2,1)S(1)}, u32[]{:S(2)}, u32[]{:S(2)}) %collective-permute-start.18) | collective-permute-done | bytes 327712 | tf_op jit(solution)/shard_map/ppermute | solution.py:391
  80.6 1.2 %collective-permute-start.23 = (bf16[48,512]{1,0:T(8,128)(2,1)S(1)}, bf16[48,512]{1,0:T(8,128)(2,1)S(1)}, u32[]{:S(2)}, u32[]{:S(2)}) collective-permute-start(bf16[48,512]{1,0:T(8,128)(2,1)S(1)} %copy-done.21), channel_id=1, source_target_pairs={{0,13},{1,4},{2,15},{3,6},{4,1},{5,8},{6,3},{7,10},{8,5},{9,12},{1... | collective-permute-start | bytes 147464 | tf_op jit(solution)/shard_map/ppermute | solution.py:391
  82.6 4.0 %collective-permute-start.22 = (bf16[96,512]{1,0:T(8,128)(2,1)S(1)}, bf16[96,512]{1,0:T(8,128)(2,1)S(1)}, u32[]{:S(2)}, u32[]{:S(2)}) collective-permute-start(bf16[96,512]{1,0:T(8,128)(2,1)S(1)} %get-tuple-element.137), channel_id=1, source_target_pairs={{0,14},{1,15},{2,0},{3,1},{4,2},{5,3},{6,4},{7,5},{8,6},{9,7},{10,... | collective-permute-start | bytes 294920 | tf_op jit(solution)/shard_map/ppermute | solution.py:391
  86.7 4.3 %collective-permute-done.20 = bf16[384,512]{1,0:T(8,128)(2,1)S(1)} collective-permute-done((bf16[384,512]{1,0:T(8,128)(2,1)S(1)}, bf16[384,512]{1,0:T(8,128)(2,1)S(1)}, u32[]{:S(2)}, u32[]{:S(2)}) %collective-permute-start.20) | collective-permute-done | bytes 393248 | tf_op jit(solution)/shard_map/ppermute | solution.py:391
  91.1 3.2 %collective-permute-start.24 = (bf16[96,512]{1,0:T(8,128)(2,1)S(1)}, bf16[96,512]{1,0:T(8,128)(2,1)S(1)}, u32[]{:S(2)}, u32[]{:S(2)}) collective-permute-start(bf16[96,512]{1,0:T(8,128)(2,1)S(1)} %get-tuple-element.164), channel_id=1, source_target_pairs={{0,8},{1,9},{2,10},{3,11},{4,12},{5,13},{6,14},{7,15},{8,0},{9,1},... | collective-permute-start | bytes 294920 | tf_op jit(solution)/shard_map/ppermute | solution.py:391
  94.6 1.1 collective-permute-start.25
  96.4 2.7 %collective-permute-start.28 = (bf16[96,512]{1,0:T(8,128)(2,1)S(1)}, bf16[96,512]{1,0:T(8,128)(2,1)S(1)}, u32[]{:S(2)}, u32[]{:S(2)}) collective-permute-start(bf16[96,512]{1,0:T(8,128)(2,1)S(1)} %get-tuple-element.158), channel_id=1, source_target_pairs={{0,12},{1,13},{2,14},{3,15},{4,8},{5,9},{6,10},{7,11},{8,4},{9,5},... | collective-permute-start | bytes 294920 | tf_op jit(solution)/shard_map/ppermute | solution.py:391
  99.3 3.7 %collective-permute-done.25.refs_6_ = bf16[80,512]{1,0:T(8,128)(2,1)S(1)} collective-permute-done((bf16[80,512]{1,0:T(8,128)(2,1)S(1)}, bf16[80,512]{1,0:T(8,128)(2,1)S(1)}, u32[]{:S(2)}, u32[]{:S(2)}) %collective-permute-start.25) | collective-permute-done | bytes 81952 | tf_op jit(solution)/shard_map/ppermute | solution.py:391
  105.0 3.9 %scatter_lists.1 = bf16[2048,512]{1,0:T(8,128)(2,1)} custom-call(s32[1]{0:T(128)} %bitcast.me_ref, s32[16,48]{1,0:T(8,128)} %bitcast.39, bf16[48,512]{1,0:T(8,128)(2,1)} %get-tuple-element.114.refs_0_, bf16[144,512]{1,0:T(8,128)(2,1)} %copy-done.5, bf16[96,512]{1,0:T(8,128)(2,1)} %copy-done.14, bf16[96,512]{1,0:T(8,128)(2,1)} %copy-done.15, ...), custom_call_target="tpu_custom_call" | custom-call | tf_op jit(solution)/shard_map/scatter_lists/pallas_call | solution.py:704
  108.9 1.0 collective-permute-done.27
  (106 shorter events, 11.1 us)
Async XLA Ops:
  4.0 9.6 %collective-permute-start.2 = (bf16[48,512]{1,0:T(8,128)(2,1)}, bf16[48,512]{1,0:T(8,128)(2,1)S(1)}, u32[]{:S(2)}, u32[]{:S(2)}) collective-permute-start(bf16[48,512]{1,0:T(8,128)(2,1)} %get-tuple-element.79), channel_id=1, source_target_pairs={{0,12},{1,13},{2,14},{3,15},{4,8},{5,9},{6,10},{7,11},{8,4},{9,5},... | collective-permute-start | bytes 147464 | tf_op jit(solution)/shard_map/ppermute | solution.py:391
  9.1 7.7 %collective-permute-start.1 = (bf16[48,512]{1,0:T(8,128)(2,1)}, bf16[48,512]{1,0:T(8,128)(2,1)S(1)}, u32[]{:S(2)}, u32[]{:S(2)}) collective-permute-start(bf16[48,512]{1,0:T(8,128)(2,1)} %get-tuple-element.79), channel_id=1, source_target_pairs={{0,8},{1,9},{2,10},{3,11},{4,12},{5,13},{6,14},{7,15},{8,0},{9,1},... | collective-permute-start | bytes 147464 | tf_op jit(solution)/shard_map/ppermute | solution.py:391
  9.1 7.7 %collective-permute-start = (bf16[48,512]{1,0:T(8,128)(2,1)}, bf16[48,512]{1,0:T(8,128)(2,1)S(1)}, u32[]{:S(2)}, u32[]{:S(2)}) collective-permute-start(bf16[48,512]{1,0:T(8,128)(2,1)} %get-tuple-element.79), channel_id=1, source_target_pairs={{0,4},{1,5},{2,6},{3,7},{4,0},{5,1},{6,2},{7,3},{8,12},{9,13},{10,... | collective-permute-start | bytes 147464 | tf_op jit(solution)/shard_map/ppermute | solution.py:391
  9.7 14.7 %collective-permute-start.7 = (bf16[48,512]{1,0:T(8,128)(2,1)}, bf16[48,512]{1,0:T(8,128)(2,1)S(1)}, u32[]{:S(2)}, u32[]{:S(2)}) collective-permute-start(bf16[48,512]{1,0:T(8,128)(2,1)} %get-tuple-element.85), channel_id=1, source_target_pairs={{0,13},{1,4},{2,15},{3,6},{4,1},{5,8},{6,3},{7,10},{8,5},{9,12},{1... | collective-permute-start | bytes 147464 | tf_op jit(solution)/shard_map/ppermute | solution.py:391
  12.0 12.4 %collective-permute-start.5 = (bf16[96,512]{1,0:T(8,128)(2,1)}, bf16[96,512]{1,0:T(8,128)(2,1)S(1)}, u32[]{:S(2)}, u32[]{:S(2)}) collective-permute-start(bf16[96,512]{1,0:T(8,128)(2,1)} %get-tuple-element.83), channel_id=1, source_target_pairs={{0,2},{1,3},{2,4},{3,5},{4,6},{5,7},{6,8},{7,9},{8,10},{9,11},{10,... | collective-permute-start | bytes 294920 | tf_op jit(solution)/shard_map/ppermute | solution.py:391
  13.6 10.9 %collective-permute-start.6 = (bf16[96,512]{1,0:T(8,128)(2,1)}, bf16[96,512]{1,0:T(8,128)(2,1)S(1)}, u32[]{:S(2)}, u32[]{:S(2)}) collective-permute-start(bf16[96,512]{1,0:T(8,128)(2,1)} %get-tuple-element.84), channel_id=1, source_target_pairs={{0,14},{1,15},{2,0},{3,1},{4,2},{5,3},{6,4},{7,5},{8,6},{9,7},{10,... | collective-permute-start | bytes 294920 | tf_op jit(solution)/shard_map/ppermute | solution.py:391
  17.6 6.8 %collective-permute-start.4 = (bf16[192,512]{1,0:T(8,128)(2,1)S(1)}, bf16[192,512]{1,0:T(8,128)(2,1)S(1)}, u32[]{:S(2)}, u32[]{:S(2)}) collective-permute-start(bf16[192,512]{1,0:T(8,128)(2,1)S(1)} %pad_maximum_fusion.refs_7_), channel_id=1, source_target_pairs={{0,1},{1,0},{2,3},{3,2},{4,5},{5,4},{6,7},{7,6},{8,9},{9,8},{10,11... | collective-permute-start | bytes 589832 | tf_op jit(solution)/shard_map/ppermute | solution.py:391
  17.7 7.3 %collective-permute-start.3 = (bf16[192,512]{1,0:T(8,128)(2,1)S(1)}, bf16[192,512]{1,0:T(8,128)(2,1)S(1)}, u32[]{:S(2)}, u32[]{:S(2)}) collective-permute-start(bf16[192,512]{1,0:T(8,128)(2,1)S(1)} %pad_maximum_fusion.refs_7_), channel_id=1, source_target_pairs={{0,2},{1,3},{2,0},{3,1},{4,6},{5,7},{6,4},{7,5},{8,10},{9,11},{10,... | collective-permute-start | bytes 589832 | tf_op jit(solution)/shard_map/ppermute | solution.py:391
  42.2 19.0 %collective-permute-start.12 = (bf16[2,384,512]{2,1,0:T(8,128)(2,1)}, bf16[2,384,512]{2,1,0:T(8,128)(2,1)S(1)}, u32[]{:S(2)}, u32[]{:S(2)}) collective-permute-start(bf16[2,384,512]{2,1,0:T(8,128)(2,1)} %get-tuple-element.96), channel_id=1, source_target_pairs={{0,2},{1,3},{2,0},{3,1},{4,6},{5,7},{6,4},{7,5},{8,10},{9,11},{10,... | collective-permute-start | bytes 2359304 | tf_op jit(solution)/shard_map/ppermute | solution.py:391
  61.5 7.3 %collective-permute-start.13 = (bf16[2,320,512]{2,1,0:T(8,128)(2,1)}, bf16[2,320,512]{2,1,0:T(8,128)(2,1)S(1)}, u32[]{:S(2)}, u32[]{:S(2)}) collective-permute-start(bf16[2,320,512]{2,1,0:T(8,128)(2,1)} %get-tuple-element.116), channel_id=1, source_target_pairs={{0,1},{1,0},{2,3},{3,2},{4,5},{5,4},{6,7},{7,6},{8,9},{9,8},{10,11... | collective-permute-start | bytes 1966088 | tf_op jit(solution)/shard_map/ppermute | solution.py:391
  66.0 3.5 %collective-permute-start.14 = (bf16[2,384,512]{2,1,0:T(8,128)(2,1)}, bf16[2,384,512]{2,1,0:T(8,128)(2,1)S(1)}, u32[]{:S(2)}, u32[]{:S(2)}) collective-permute-start(bf16[2,384,512]{2,1,0:T(8,128)(2,1)} %get-tuple-element.118), channel_id=1, source_target_pairs={{0,1},{1,0},{2,3},{3,2},{4,5},{5,4},{6,7},{7,6},{8,9},{9,8},{10,11... | collective-permute-start | bytes 2359304 | tf_op jit(solution)/shard_map/ppermute | solution.py:391
  66.4 3.3 %collective-permute-start.15 = (bf16[144,512]{1,0:T(8,128)(2,1)}, bf16[144,512]{1,0:T(8,128)(2,1)S(1)}, u32[]{:S(2)}, u32[]{:S(2)}) collective-permute-start(bf16[144,512]{1,0:T(8,128)(2,1)} %get-tuple-element.119), channel_id=1, source_target_pairs={{0,1},{1,0},{2,3},{3,2},{4,5},{5,4},{6,7},{7,6},{8,9},{9,8},{10,11... | collective-permute-start | bytes 442376 | tf_op jit(solution)/shard_map/ppermute | solution.py:391
  69.9 7.4 %collective-permute-start.17 = (bf16[192,512]{1,0:T(8,128)(2,1)S(1)}, bf16[192,512]{1,0:T(8,128)(2,1)S(1)}, u32[]{:S(2)}, u32[]{:S(2)}) collective-permute-start(bf16[192,512]{1,0:T(8,128)(2,1)S(1)} %bitcast.32), channel_id=1, source_target_pairs={{0,4},{1,5},{2,6},{3,7},{4,0},{5,1},{6,2},{7,3},{8,12},{9,13},{10,... | collective-permute-start | bytes 589832 | tf_op jit(solution)/shard_map/ppermute | solution.py:391
  69.9 10.6 %collective-permute-start.18 = (bf16[320,512]{1,0:T(8,128)(2,1)S(1)}, bf16[320,512]{1,0:T(8,128)(2,1)S(1)}, u32[]{:S(2)}, u32[]{:S(2)}) collective-permute-start(bf16[320,512]{1,0:T(8,128)(2,1)S(1)} %get-tuple-element.128), channel_id=1, source_target_pairs={{0,2},{1,3},{2,0},{3,1},{4,6},{5,7},{6,4},{7,5},{8,10},{9,11},{10,... | collective-permute-start | bytes 983048 | tf_op jit(solution)/shard_map/ppermute | solution.py:391
  70.1 21.0 %collective-permute-start.20 = (bf16[384,512]{1,0:T(8,128)(2,1)S(1)}, bf16[384,512]{1,0:T(8,128)(2,1)S(1)}, u32[]{:S(2)}, u32[]{:S(2)}) collective-permute-start(bf16[384,512]{1,0:T(8,128)(2,1)S(1)} %get-tuple-element.135), channel_id=1, source_target_pairs={{0,2},{1,3},{2,0},{3,1},{4,6},{5,7},{6,4},{7,5},{8,10},{9,11},{10,... | collective-permute-start | bytes 1179656 | tf_op jit(solution)/shard_map/ppermute | solution.py:391
  80.6 13.8 %collective-permute-start.23 = (bf16[48,512]{1,0:T(8,128)(2,1)S(1)}, bf16[48,512]{1,0:T(8,128)(2,1)S(1)}, u32[]{:S(2)}, u32[]{:S(2)}) collective-permute-start(bf16[48,512]{1,0:T(8,128)(2,1)S(1)} %copy-done.21), channel_id=1, source_target_pairs={{0,13},{1,4},{2,15},{3,6},{4,1},{5,8},{6,3},{7,10},{8,5},{9,12},{1... | collective-permute-start | bytes 147464 | tf_op jit(solution)/shard_map/ppermute | solution.py:391
  81.9 12.6 %collective-permute-start.21 = (bf16[96,512]{1,0:T(8,128)(2,1)S(1)}, bf16[96,512]{1,0:T(8,128)(2,1)S(1)}, u32[]{:S(2)}, u32[]{:S(2)}) collective-permute-start(bf16[96,512]{1,0:T(8,128)(2,1)S(1)} %get-tuple-element.136), channel_id=1, source_target_pairs={{0,2},{1,3},{2,4},{3,5},{4,6},{5,7},{6,8},{7,9},{8,10},{9,11},{10,... | collective-permute-start | bytes 294920 | tf_op jit(solution)/shard_map/ppermute | solution.py:391
  82.6 11.9 %collective-permute-start.22 = (bf16[96,512]{1,0:T(8,128)(2,1)S(1)}, bf16[96,512]{1,0:T(8,128)(2,1)S(1)}, u32[]{:S(2)}, u32[]{:S(2)}) collective-permute-start(bf16[96,512]{1,0:T(8,128)(2,1)S(1)} %get-tuple-element.137), channel_id=1, source_target_pairs={{0,14},{1,15},{2,0},{3,1},{4,2},{5,3},{6,4},{7,5},{8,6},{9,7},{10,... | collective-permute-start | bytes 294920 | tf_op jit(solution)/shard_map/ppermute | solution.py:391
  86.6 7.8 %collective-permute-start.19 = (bf16[160,512]{1,0:T(8,128)(2,1)S(1)}, bf16[160,512]{1,0:T(8,128)(2,1)S(1)}, u32[]{:S(2)}, u32[]{:S(2)}) collective-permute-start(bf16[160,512]{1,0:T(8,128)(2,1)S(1)} %bitcast.33), channel_id=1, source_target_pairs={{0,4},{1,5},{2,6},{3,7},{4,0},{5,1},{6,2},{7,3},{8,12},{9,13},{10,... | collective-permute-start | bytes 491528 | tf_op jit(solution)/shard_map/ppermute | solution.py:391
  91.1 8.2 %collective-permute-start.24 = (bf16[96,512]{1,0:T(8,128)(2,1)S(1)}, bf16[96,512]{1,0:T(8,128)(2,1)S(1)}, u32[]{:S(2)}, u32[]{:S(2)}) collective-permute-start(bf16[96,512]{1,0:T(8,128)(2,1)S(1)} %get-tuple-element.164), channel_id=1, source_target_pairs={{0,8},{1,9},{2,10},{3,11},{4,12},{5,13},{6,14},{7,15},{8,0},{9,1},... | collective-permute-start | bytes 294920 | tf_op jit(solution)/shard_map/ppermute | solution.py:391
  94.6 8.4 %collective-permute-start.25 = (bf16[80,512]{1,0:T(8,128)(2,1)S(1)}, bf16[80,512]{1,0:T(8,128)(2,1)S(1)}, u32[]{:S(2)}, u32[]{:S(2)}) collective-permute-start(bf16[80,512]{1,0:T(8,128)(2,1)S(1)} %get-tuple-element.166), channel_id=1, source_target_pairs={{0,8},{1,9},{2,10},{3,11},{4,12},{5,13},{6,14},{7,15},{8,0},{9,1},... | collective-permute-start | bytes 245768 | tf_op jit(solution)/shard_map/ppermute | solution.py:391
  95.6 13.2 %collective-permute-start.26 = (bf16[96,512]{1,0:T(8,128)(2,1)S(1)}, bf16[96,512]{1,0:T(8,128)(2,1)S(1)}, u32[]{:S(2)}, u32[]{:S(2)}) collective-permute-start(bf16[96,512]{1,0:T(8,128)(2,1)S(1)} %get-tuple-element.157), channel_id=1, source_target_pairs={{0,4},{1,5},{2,6},{3,7},{4,0},{5,1},{6,2},{7,3},{8,12},{9,13},{10,... | collective-permute-start | bytes 294920 | tf_op jit(solution)/shard_map/ppermute | solution.py:391
  96.4 12.5 %collective-permute-start.28 = (bf16[96,512]{1,0:T(8,128)(2,1)S(1)}, bf16[96,512]{1,0:T(8,128)(2,1)S(1)}, u32[]{:S(2)}, u32[]{:S(2)}) collective-permute-start(bf16[96,512]{1,0:T(8,128)(2,1)S(1)} %get-tuple-element.158), channel_id=1, source_target_pairs={{0,12},{1,13},{2,14},{3,15},{4,8},{5,9},{6,10},{7,11},{8,4},{9,5},... | collective-permute-start | bytes 294920 | tf_op jit(solution)/shard_map/ppermute | solution.py:391
  99.1 10.8 %collective-permute-start.27 = (bf16[96,512]{1,0:T(8,128)(2,1)S(1)}, bf16[96,512]{1,0:T(8,128)(2,1)S(1)}, u32[]{:S(2)}, u32[]{:S(2)}) collective-permute-start(bf16[96,512]{1,0:T(8,128)(2,1)S(1)} %get-tuple-element.159), channel_id=1, source_target_pairs={{0,8},{1,9},{2,10},{3,11},{4,12},{5,13},{6,14},{7,15},{8,0},{9,1},... | collective-permute-start | bytes 294920 | tf_op jit(solution)/shard_map/ppermute | solution.py:391
  (28 other events, 153.4 us)

commit v7 on v6

--- a/solution.py
+++ b/solution.py
@@ -307,10 +307,10 @@
 def backward_kernel(peers, me_ref, count_ref, src_ref, dst_ref, inverse_ref, *refs):
     (hidden_ref, slope_ref, norm_ref, edge_ref) = refs[:4]
     (d_aggregate_ref, received_ref, mesh_ref, d_mesh_ref) = refs[4:8]
-    (w_sender_ref, w_receiver_ref, w_out_ref) = refs[8:11]
-    (d_pre_ref, mesh_grad_ref, slot_send_ref, slot_keep_ref, edge_send_ref, edge_keep_ref) = refs[11:17]
-    near_refs = refs[17:22]
-    (end_sum, grad_in, grad_out, d_slots) = refs[22:]
+    (w_sender_ref, w_receiver_ref, w_edge_ref, w_out_ref) = refs[8:12]
+    (edge_grad_ref, mesh_grad_ref, slot_send_ref, slot_keep_ref, edge_send_ref, edge_keep_ref) = refs[12:18]
+    near_refs = refs[18:23]
+    (end_sum, grad_in, grad_out, d_slots) = refs[23:]
     step = pl.program_id(0)
     me = me_ref[0]
     slots, width = received_ref.shape
@@ -343,12 +343,18 @@
             d_proj = norm_back(norm_ref[part, :].astype(F32), inverse, upstream).astype(BF16)
             d_projs.append(d_proj)
             d_hiddens.append(contract_cols(d_proj, w_out_ref[...]))
-        for (start, part), d_proj, d_hidden, column in zip(parts, d_projs, d_hiddens, columns):
+        for (start, part), d_proj, d_hidden, column, upstream in zip(
+            parts, d_projs, d_hiddens, columns, upstreams
+        ):
             grad_out[...] += contract_rows(hidden_ref[part, :], d_proj)
             d_pre = (d_hidden * slope_ref[part, :].astype(F32)).astype(BF16)
-            d_pre_ref[part, :] = d_pre
+            edge_grad_ref[part, :] = (upstream + contract_cols(d_pre, w_edge_ref[...])).astype(BF16)
             end_sum[...] += dot(column, d_pre)
             grad_in[:width, :] += contract_rows(edge_ref[part, :], d_pre)
+
+    @pl.when(step * STEP >= count_ref[0] * TILE)
+    def _():
+        edge_grad_ref[...] = jnp.zeros_like(edge_grad_ref)
 
     @pl.when(step == pl.num_programs(0) - 1)
     def _():
@@ -372,21 +378,6 @@
         )
 
 
-def edges_kernel(count_ref, dst_ref, d_pre_ref, d_aggregate_ref, w_edge_ref, edge_grad_ref):
-    step = pl.program_id(0)
-
-    @pl.when(step * STEP < count_ref[0] * TILE)
-    def _():
-        for start, part in halves_of(d_pre_ref):
-            receivers = live_only(dst_ref[0, :, part], step * STEP + start, count_ref[0] * TILE)
-            upstream = dot(hot_rows(receivers, d_aggregate_ref.shape[0]), d_aggregate_ref[...])
-            edge_grad_ref[part, :] = (upstream + contract_cols(d_pre_ref[part, :], w_edge_ref[...])).astype(BF16)
-
-    @pl.when(step * STEP >= count_ref[0] * TILE)
-    def _():
-        edge_grad_ref[...] = jnp.zeros_like(edge_grad_ref)
-
-
 def send(values, perm):
     return lax.ppermute(values, "lon", perm)
 
@@ -440,23 +431,6 @@
     for place in range(1, count):
         piece = pieces[place * share : (place + 1) * share]
         terms.append(send(piece, by_xor(peers, 4 * place)))
-    return terms
-
-
-def halve_sum(peers, pieces):
-    count = peers // 4
-    blocks = pieces.reshape(count // 2, 2, -1, pieces.shape[1])
-    kept, outgoing = [blocks[:, place].reshape(-1, pieces.shape[1]) for place in range(2)]
-    return add(kept, send(outgoing, by_xor(peers, 4)))
-
-
-def rest_terms(peers, pieces):
-    count = peers // 8
-    share = pieces.shape[0] // count
-    terms = [pieces[:share]]
-    for place in range(1, count):
-        piece = pieces[place * share : (place + 1) * share]
-        terms.append(send(piece, by_xor(peers, 8 * place)))
     return terms
 
 
@@ -615,7 +589,7 @@
         + [tile_of(width)] * 4
         + [whole((mesh_count, width)), whole((slots, width))]
         + [whole((mesh_count, width))] * 2
-        + [weight(1), weight(2), whole(square)],
+        + [weight(1), weight(2), weight(0), whole(square)],
         out_specs=[tile_of(width), whole((mesh_count, width))] + slot_spec + edge_spec + back_specs,
         out_shape=[
             jax.ShapeDtypeStruct((edges, width), BF16),
@@ -632,7 +606,7 @@
         ],
         compiler_params=params,
         cost_estimate=pl.CostEstimate(
-            flops=2 * edges * width * (2 * mesh_count + 3 * width + slots),
+            flops=2 * edges * width * (2 * mesh_count + 4 * width + slots),
             bytes_accessed=10 * edges * width,
             transcendentals=0,
         ),
@@ -653,49 +627,33 @@
         d_mesh,
         w_edge_in,
         w_edge_in,
+        w_edge_in,
         w_edge_out,
     )
-    (d_pre, mesh_grad, slot_send, slot_keep, edge_send, edge_keep), returns = results[:6], results[6:]
-    (node_next, node_kept, d_pre, slot_send, slot_keep, edge_send, edge_keep, returns) = lax.optimization_barrier(
-        (node_next, node_kept, d_pre, slot_send, slot_keep, edge_send, edge_keep, returns)
+    (edge_grad, mesh_grad, slot_send, slot_keep, edge_send, edge_keep), returns = results[:6], results[6:]
+    (node_next, node_kept, slot_send, slot_keep, edge_send, edge_keep, returns) = lax.optimization_barrier(
+        (node_next, node_kept, slot_send, slot_keep, edge_send, edge_keep, returns)
     )
     slot_next, slot_kept = first_sum(peers, 1, slot_send, slot_keep)
     edge_next, edge_kept = first_sum(peers, 1, edge_send, edge_keep)
     node_pieces = next_sum(peers, 1, node_next, node_kept)
     swapped = send(returns[1], by_xor(peers, 1))
-    (slot_next, slot_kept, edge_next, edge_kept, swapped) = lax.optimization_barrier(
-        (slot_next, slot_kept, edge_next, edge_kept, swapped)
+    slot_pieces = next_sum(peers, 2, slot_next, slot_kept)
+    node_pieces, edge_next, edge_kept, swapped, slot_next = lax.optimization_barrier(
+        (node_pieces, edge_next, edge_kept, swapped, slot_next)
     )
-    slot_pieces = next_sum(peers, 2, slot_next, slot_kept)
-    edge_pieces = next_sum(peers, 2, edge_next, edge_kept)
+    node_terms = last_terms(peers, node_pieces)
     to_after = jnp.concatenate([returns[2], swapped[cap : 2 * cap]], axis=0)
     to_before = jnp.concatenate([returns[3], swapped[2 * cap :]], axis=0)
-    node_pieces, d_pre, to_after, to_before = lax.optimization_barrier((node_pieces, d_pre, to_after, to_before))
-    node_pieces = halve_sum(peers, node_pieces)
-    edge_grad = pl.pallas_call(
-        edges_kernel,
-        grid=(tiles,),
-        in_specs=[smem, index_tile, tile_of(width), whole((mesh_count, width)), weight(0)],
-        out_specs=tile_of(width),
-        out_shape=jax.ShapeDtypeStruct((edges, width), BF16),
-        compiler_params=params,
-        cost_estimate=pl.CostEstimate(
-            flops=2 * edges * width * (mesh_count + width), bytes_accessed=4 * edges * width, transcendentals=0
-        ),
-        name="edge_grad",
-    )(tile_count, dst, d_pre, d_aggregate, w_edge_in)
-    (node_pieces, slot_pieces, edge_grad, to_after, to_before, across) = lax.optimization_barrier(
-        (node_pieces, slot_pieces, edge_grad, to_after, to_before, returns[4])
-    )
-    slot_half = halve_sum(peers, slot_pieces)
-    node_terms = rest_terms(peers, node_pieces)
     near = [
         send(to_after, by_shift(peers, 2)),
         send(to_before, by_shift(peers, -2)),
-        send(across, across_chips(peers)),
+        send(returns[4], across_chips(peers)),
     ]
-    slot_half, edge_pieces, near = lax.optimization_barrier((slot_half, edge_pieces, near))
-    slot_terms = rest_terms(peers, slot_half)
+    slot_pieces, edge_next, edge_kept = lax.optimization_barrier((slot_pieces, edge_next, edge_kept))
+    edge_pieces = next_sum(peers, 2, edge_next, edge_kept)
+    slot_terms = last_terms(peers, slot_pieces)
+    edge_pieces, near = lax.optimization_barrier((edge_pieces, near))
     edge_terms = last_terms(peers, edge_pieces)
     node_terms, slot_terms = lax.optimization_barrier((node_terms, slot_terms))
     returned = [returns[0], swapped, *near]
@@ -706,7 +664,7 @@
         grid=(2,),
         in_specs=[smem, whole(rows.shape)]
         + return_specs
-        + [whole((out_rows + cap, width))] * (upper // 2),
+        + [whole((out_rows + cap, width))] * upper,
         out_specs=pl.BlockSpec((grid_part, width), lambda step: (step, 0)),
         out_shape=jax.ShapeDtypeStruct((grid_count, width), BF16),
         compiler_params=params,

time: 113 us -> 110 us (0.973); the launches traced: 111 us -> 109 us
  Pallas kernels: 49.6 us -> 53 us
  waiting for transfers between devices: 17.2 us -> 15 us
  starting transfers between devices: 36.7 us -> 34.8 us
    pallas_call x1, Pallas kernels: 15.9 us -> 21.6 us  [on_device(): pl.pallas_call(functools.partial(backward_kernel, peers), grid=(tiles,),...]
    pallas_call x1 -> x0, Pallas kernels: 5.21 us -> none  [on_device(): pl.pallas_call(edges_kernel, grid=(tiles,), in_specs=[smem, index_tile, t...]
    pallas_call x1, Pallas kernels: 14.5 us -> 17.5 us  [on_device(): pl.pallas_call(functools.partial(forward_kernel, peers), grid=(tiles,), i...]
    ppermute x29 -> x31, waiting for transfers between devices: 17.2 us -> 15 us  [send(): return lax.ppermute(values, 'lon', perm)]
    ppermute x29 -> x31, starting transfers between devices: 36.7 us -> 34.8 us  [send(): return lax.ppermute(values, 'lon', perm)]
    add x4 -> x3, other arithmetic: 2.69 us -> 2.1 us  [total_of(): total = total + term[start:stop].astype(F32)]
  transfers between devices with their start and end apart: 29 -> 31, of which waited for: 10 -> 10; matrix products, arithmetic and copies ran while one was open for 3% -> 3% of each run, Pallas kernels for 29% -> 29%
where the time goes in v7:
time: 110 us; the launch traced here: 109 us
  Pallas kernels  53 us (48%)
  starting transfers between devices  34.8 us (32%)
  waiting for transfers between devices  15 us (14%)
  other arithmetic  3.75 us (3%)
  between operations  1.77 us (2%)
    ppermute x31, starting transfers between devices, send(): return lax.ppermute(values, 'lon', perm)  34.8 us
    pallas_call x1, Pallas kernels, on_device(): pl.pallas_call(functools.partial(backward_kernel, peers), grid=(tiles,),...  21.6 us
    pallas_call x1, Pallas kernels, on_device(): pl.pallas_call(functools.partial(forward_kernel, peers), grid=(tiles,), i...  17.5 us
    ppermute x31, waiting for transfers between devices, send(): return lax.ppermute(values, 'lon', perm)  15 us
    pallas_call x1, Pallas kernels, on_device(): pl.pallas_call(local_kernel, grid=(tiles,), in_specs=[index_tile, tile_of...  6.62 us
    pallas_call x1, Pallas kernels, on_device(): pl.pallas_call(functools.partial(scatter_kernel, out_rows), grid=(2,), in...  3.97 us
    pallas_call x1, Pallas kernels, on_device(): pl.pallas_call(gather_kernel, grid=(2,), in_specs=[smem, whole(rows.shape...  3.36 us
  transfers between devices with their start and end apart: 31, of which 10 were waited for; matrix products, arithmetic and copies ran while one was open for 3% of the time, Pallas kernels for 29%

profile of v7, /device:TPU:0, one launch (start us, length us, event | category | flops | bytes accessed | tf_op | source)
XLA Modules:
  0.0 109.2 jit_solution(15330639990960937431)
XLA Ops:
  0.6 3.4 %gather_lists.1 = (bf16[48,512]{1,0:T(8,128)(2,1)}, bf16[48,512]{1,0:T(8,128)(2,1)}, bf16[96,512]{1,0:T(8,128)(2,1)}, bf16[96,512]{1,0:T(8,128)(2,1)}, bf16[48,512]{1,0:T(8,128)(2,1)}, /*index=5*/bf16[48,512]{1,0:T(8,128)(2,1)}) custom-call(s32[1]{0:T(128)} %bitcast.me_ref, s32[16,48]{1,0:T(8,128)} %bitcast.22, bf16[2048,512]{1,0:T(8,128)(2,1)} %grid_ref.1), custom_call_target="tpu_custom_call" | custom-call | tf_op jit(solution)/shard_map/gather_lists/pallas_call | solution.py:499
  4.0 5.1 %collective-permute-start.2 = (bf16[48,512]{1,0:T(8,128)(2,1)}, bf16[48,512]{1,0:T(8,128)(2,1)S(1)}, u32[]{:S(2)}, u32[]{:S(2)}) collective-permute-start(bf16[48,512]{1,0:T(8,128)(2,1)} %get-tuple-element.73), channel_id=1, source_target_pairs={{0,12},{1,13},{2,14},{3,15},{4,8},{5,9},{6,10},{7,11},{8,4},{9,5},... | collective-permute-start | bytes 147464 | tf_op jit(solution)/shard_map/ppermute | solution.py:382
  9.7 2.3 %collective-permute-start.7 = (bf16[48,512]{1,0:T(8,128)(2,1)}, bf16[48,512]{1,0:T(8,128)(2,1)S(1)}, u32[]{:S(2)}, u32[]{:S(2)}) collective-permute-start(bf16[48,512]{1,0:T(8,128)(2,1)} %get-tuple-element.79), channel_id=1, source_target_pairs={{0,13},{1,4},{2,15},{3,6},{4,1},{5,8},{6,3},{7,10},{8,5},{9,12},{1... | collective-permute-start | bytes 147464 | tf_op jit(solution)/shard_map/ppermute | solution.py:382
  12.0 1.5 %collective-permute-start.5 = (bf16[96,512]{1,0:T(8,128)(2,1)}, bf16[96,512]{1,0:T(8,128)(2,1)S(1)}, u32[]{:S(2)}, u32[]{:S(2)}) collective-permute-start(bf16[96,512]{1,0:T(8,128)(2,1)} %get-tuple-element.77), channel_id=1, source_target_pairs={{0,2},{1,3},{2,4},{3,5},{4,6},{5,7},{6,8},{7,9},{8,10},{9,11},{10,... | collective-permute-start | bytes 294920 | tf_op jit(solution)/shard_map/ppermute | solution.py:382
  13.6 3.2 %collective-permute-start.6 = (bf16[96,512]{1,0:T(8,128)(2,1)}, bf16[96,512]{1,0:T(8,128)(2,1)S(1)}, u32[]{:S(2)}, u32[]{:S(2)}) collective-permute-start(bf16[96,512]{1,0:T(8,128)(2,1)} %get-tuple-element.78), channel_id=1, source_target_pairs={{0,14},{1,15},{2,0},{3,1},{4,2},{5,3},{6,4},{7,5},{8,6},{9,7},{10,... | collective-permute-start | bytes 294920 | tf_op jit(solution)/shard_map/ppermute | solution.py:382
  16.8 0.8 pad_maximum_fusion.refs_7_
  17.8 6.6 %edge_local.1.local_ref = bf16[3072,512]{1,0:T(8,128)(2,1)} custom-call(s32[3,1,1024]{2,1,0:T(1,128)} %bitcast.19, bf16[3072,512]{1,0:T(8,128)(2,1)} %refs_3_.1, bf16[256,512]{1,0:T(8,128)(2,1)} %refs_6_.1, bf16[1536,512]{1,0:T(8,128)(2,1)} %refs_10_.1, bf16[1536,512]{1,0:T(8,128)(2,1)} %refs_10_.1), custom_call_target="tpu_custom_call" | custom-call | flops 2415919104 | bytes 6291456 | tf_op jit(solution)/shard_map/edge_local/pallas_call | solution.py:516
  27.7 17.5 %forward.1 = (bf16[768,512]{1,0:T(8,128)(2,1)}, bf16[3072,512]{1,0:T(8,128)(2,1)}, bf16[3072,512]{1,0:T(8,128)(2,1)}, bf16[3072,512]{1,0:T(8,128)(2,1)}, f32[3,1...) custom-call(s32[1]{0:T(128)} %bitcast.me_ref, ...), custom_call_target="tpu_custom_call" | custom-call | tf_op jit(solution)/shard_map/forward/pallas_call | solution.py:536
  45.1 1.6 %collective-permute-start.12 = (bf16[2,384,512]{2,1,0:T(8,128)(2,1)}, bf16[2,384,512]{2,1,0:T(8,128)(2,1)S(1)}, u32[]{:S(2)}, u32[]{:S(2)}) collective-permute-start(bf16[2,384,512]{2,1,0:T(8,128)(2,1)} %get-tuple-element.90), channel_id=1, source_target_pairs={{0,2},{1,3},{2,0},{3,1},{4,6},{5,7},{6,4},{7,5},{8,10},{9,11},{10,... | collective-permute-start | bytes 2359304 | tf_op jit(solution)/shard_map/ppermute | solution.py:382
  46.8 21.6 %backward.1 = (bf16[3072,512]{1,0:T(8,128)(2,1)}, bf16[256,512]{1,0:T(8,128)(2,1)}, bf16[2,320,512]{2,1,0:T(8,128)(2,1)}, bf16[2,320,512]{2,1,0:T(8,128)(2,1)}, ...) custom-call(s32[1]{0:T(128)} %bitcast.me_ref, ...), custom_call_target="tpu_custom_call" | custom-call | flops 10468982784 | bytes 15728640 | tf_op jit(solution)/shard_map/backward/pallas_call | solution.py:585
  69.7 2.0 %collective-permute-done.13 = bf16[384,512]{1,0:T(8,128)(2,1)S(1)} collective-permute-done((bf16[384,512]{1,0:T(8,128)(2,1)S(1)}, bf16[384,512]{1,0:T(8,128)(2,1)S(1)}, u32[]{:S(2)}, u32[]{:S(2)}) %collective-permute-start.13) | collective-permute-done | bytes 393248 | tf_op jit(solution)/shard_map/ppermute | solution.py:382
  73.8 3.7 %collective-permute-start.22 = (bf16[96,512]{1,0:T(8,128)(2,1)S(1)}, bf16[96,512]{1,0:T(8,128)(2,1)S(1)}, u32[]{:S(2)}, u32[]{:S(2)}) collective-permute-start(bf16[96,512]{1,0:T(8,128)(2,1)S(1)} %get-tuple-element.148), channel_id=1, source_target_pairs={{0,4},{1,5},{2,6},{3,7},{4,0},{5,1},{6,2},{7,3},{8,12},{9,13},{10,... | collective-permute-start | bytes 294920 | tf_op jit(solution)/shard_map/ppermute | solution.py:382
  77.5 4.4 %collective-permute-done.17 = bf16[320,512]{1,0:T(8,128)(2,1)S(1)} collective-permute-done((bf16[320,512]{1,0:T(8,128)(2,1)S(1)}, bf16[320,512]{1,0:T(8,128)(2,1)S(1)}, u32[]{:S(2)}, u32[]{:S(2)}) %collective-permute-start.17) | collective-permute-done | bytes 327712 | tf_op jit(solution)/shard_map/ppermute | solution.py:382
  82.7 1.0 collective-permute-start.26
  83.7 3.4 %collective-permute-start.25 = (bf16[80,512]{1,0:T(8,128)(2,1)S(1)}, bf16[80,512]{1,0:T(8,128)(2,1)S(1)}, u32[]{:S(2)}, u32[]{:S(2)}) collective-permute-start(bf16[80,512]{1,0:T(8,128)(2,1)S(1)} %get-tuple-element.152), channel_id=1, source_target_pairs={{0,4},{1,5},{2,6},{3,7},{4,0},{5,1},{6,2},{7,3},{8,12},{9,13},{10,... | collective-permute-start | bytes 245768 | tf_op jit(solution)/shard_map/ppermute | solution.py:382
  87.2 2.6 %collective-permute-done.27.refs_8_ = bf16[80,512]{1,0:T(8,128)(2,1)S(1)} collective-permute-done((bf16[80,512]{1,0:T(8,128)(2,1)S(1)}, bf16[80,512]{1,0:T(8,128)(2,1)S(1)}, u32[]{:S(2)}, u32[]{:S(2)}) %collective-permute-start.27) | collective-permute-done | bytes 81952 | tf_op jit(solution)/shard_map/ppermute | solution.py:382
  89.8 1.5 %collective-permute-start.19 = (bf16[96,512]{1,0:T(8,128)(2,1)S(1)}, bf16[96,512]{1,0:T(8,128)(2,1)S(1)}, u32[]{:S(2)}, u32[]{:S(2)}) collective-permute-start(bf16[96,512]{1,0:T(8,128)(2,1)S(1)} %pad_maximum_fusion.1), channel_id=1, source_target_pairs={{0,2},{1,3},{2,4},{3,5},{4,6},{5,7},{6,8},{7,9},{8,10},{9,11},{10,... | collective-permute-start | bytes 294920 | tf_op jit(solution)/shard_map/ppermute | solution.py:382
  91.5 3.1 %collective-permute-start.20 = (bf16[96,512]{1,0:T(8,128)(2,1)S(1)}, bf16[96,512]{1,0:T(8,128)(2,1)S(1)}, u32[]{:S(2)}, u32[]{:S(2)}) collective-permute-start(bf16[96,512]{1,0:T(8,128)(2,1)S(1)} %pad_maximum_fusion.2), channel_id=1, source_target_pairs={{0,14},{1,15},{2,0},{3,1},{4,2},{5,3},{6,4},{7,5},{8,6},{9,7},{10,... | collective-permute-start | bytes 294920 | tf_op jit(solution)/shard_map/ppermute | solution.py:382
  95.4 1.9 %collective-permute-done.19.refs_2_ = bf16[96,512]{1,0:T(8,128)(2,1)S(1)} collective-permute-done((bf16[96,512]{1,0:T(8,128)(2,1)S(1)}, bf16[96,512]{1,0:T(8,128)(2,1)S(1)}, u32[]{:S(2)}, u32[]{:S(2)}) %collective-permute-start.19) | collective-permute-done | bytes 98336 | tf_op jit(solution)/shard_map/ppermute | solution.py:382
  97.7 1.3 %collective-permute-start.30 = (bf16[96,512]{1,0:T(8,128)(2,1)S(1)}, bf16[96,512]{1,0:T(8,128)(2,1)S(1)}, u32[]{:S(2)}, u32[]{:S(2)}) collective-permute-start(bf16[96,512]{1,0:T(8,128)(2,1)S(1)} %get-tuple-element.144), channel_id=1, source_target_pairs={{0,12},{1,13},{2,14},{3,15},{4,8},{5,9},{6,10},{7,11},{8,4},{9,5},... | collective-permute-start | bytes 294920 | tf_op jit(solution)/shard_map/ppermute | solution.py:382
  99.0 2.1 %collective-permute-start.29 = (bf16[96,512]{1,0:T(8,128)(2,1)S(1)}, bf16[96,512]{1,0:T(8,128)(2,1)S(1)}, u32[]{:S(2)}, u32[]{:S(2)}) collective-permute-start(bf16[96,512]{1,0:T(8,128)(2,1)S(1)} %get-tuple-element.145), channel_id=1, source_target_pairs={{0,8},{1,9},{2,10},{3,11},{4,12},{5,13},{6,14},{7,15},{8,0},{9,1},... | collective-permute-start | bytes 294920 | tf_op jit(solution)/shard_map/ppermute | solution.py:382
  101.9 4.0 %scatter_lists.1 = bf16[2048,512]{1,0:T(8,128)(2,1)} custom-call(s32[1]{0:T(128)} %bitcast.me_ref, s32[16,48]{1,0:T(8,128)} %bitcast.23, bf16[48,512]{1,0:T(8,128)(2,1)} %get-tuple-element.107.refs_0_, bf16[144,512]{1,0:T(8,128)(2,1)} %copy-done.5, bf16[96,512]{1,0:T(8,128)(2,1)} %copy-done.16, bf16[96,512]{1,0:T(8,128)(2,1)} %copy-done.17, ...), custom_call_target="tpu_custom_call" | custom-call | tf_op jit(solution)/shard_map/scatter_lists/pallas_call | solution.py:662
  105.9 2.6 %collective-permute-done.29 = bf16[96,512]{1,0:T(8,128)(2,1)S(1)} collective-permute-done((bf16[96,512]{1,0:T(8,128)(2,1)S(1)}, bf16[96,512]{1,0:T(8,128)(2,1)S(1)}, u32[]{:S(2)}, u32[]{:S(2)}) %collective-permute-start.29) | collective-permute-done | bytes 98336 | tf_op jit(solution)/shard_map/ppermute | solution.py:382
  108.4 0.7 convert_add_fusion.1
  (109 shorter events, 9.5 us)
Async XLA Ops:
  4.0 9.6 %collective-permute-start.2 = (bf16[48,512]{1,0:T(8,128)(2,1)}, bf16[48,512]{1,0:T(8,128)(2,1)S(1)}, u32[]{:S(2)}, u32[]{:S(2)}) collective-permute-start(bf16[48,512]{1,0:T(8,128)(2,1)} %get-tuple-element.73), channel_id=1, source_target_pairs={{0,12},{1,13},{2,14},{3,15},{4,8},{5,9},{6,10},{7,11},{8,4},{9,5},... | collective-permute-start | bytes 147464 | tf_op jit(solution)/shard_map/ppermute | solution.py:382
  9.1 7.7 %collective-permute-start.1 = (bf16[48,512]{1,0:T(8,128)(2,1)}, bf16[48,512]{1,0:T(8,128)(2,1)S(1)}, u32[]{:S(2)}, u32[]{:S(2)}) collective-permute-start(bf16[48,512]{1,0:T(8,128)(2,1)} %get-tuple-element.73), channel_id=1, source_target_pairs={{0,8},{1,9},{2,10},{3,11},{4,12},{5,13},{6,14},{7,15},{8,0},{9,1},... | collective-permute-start | bytes 147464 | tf_op jit(solution)/shard_map/ppermute | solution.py:382
  9.1 7.7 %collective-permute-start = (bf16[48,512]{1,0:T(8,128)(2,1)}, bf16[48,512]{1,0:T(8,128)(2,1)S(1)}, u32[]{:S(2)}, u32[]{:S(2)}) collective-permute-start(bf16[48,512]{1,0:T(8,128)(2,1)} %get-tuple-element.73), channel_id=1, source_target_pairs={{0,4},{1,5},{2,6},{3,7},{4,0},{5,1},{6,2},{7,3},{8,12},{9,13},{10,... | collective-permute-start | bytes 147464 | tf_op jit(solution)/shard_map/ppermute | solution.py:382
  9.7 14.7 %collective-permute-start.7 = (bf16[48,512]{1,0:T(8,128)(2,1)}, bf16[48,512]{1,0:T(8,128)(2,1)S(1)}, u32[]{:S(2)}, u32[]{:S(2)}) collective-permute-start(bf16[48,512]{1,0:T(8,128)(2,1)} %get-tuple-element.79), channel_id=1, source_target_pairs={{0,13},{1,4},{2,15},{3,6},{4,1},{5,8},{6,3},{7,10},{8,5},{9,12},{1... | collective-permute-start | bytes 147464 | tf_op jit(solution)/shard_map/ppermute | solution.py:382
  12.0 12.4 %collective-permute-start.5 = (bf16[96,512]{1,0:T(8,128)(2,1)}, bf16[96,512]{1,0:T(8,128)(2,1)S(1)}, u32[]{:S(2)}, u32[]{:S(2)}) collective-permute-start(bf16[96,512]{1,0:T(8,128)(2,1)} %get-tuple-element.77), channel_id=1, source_target_pairs={{0,2},{1,3},{2,4},{3,5},{4,6},{5,7},{6,8},{7,9},{8,10},{9,11},{10,... | collective-permute-start | bytes 294920 | tf_op jit(solution)/shard_map/ppermute | solution.py:382
  13.6 10.9 %collective-permute-start.6 = (bf16[96,512]{1,0:T(8,128)(2,1)}, bf16[96,512]{1,0:T(8,128)(2,1)S(1)}, u32[]{:S(2)}, u32[]{:S(2)}) collective-permute-start(bf16[96,512]{1,0:T(8,128)(2,1)} %get-tuple-element.78), channel_id=1, source_target_pairs={{0,14},{1,15},{2,0},{3,1},{4,2},{5,3},{6,4},{7,5},{8,6},{9,7},{10,... | collective-permute-start | bytes 294920 | tf_op jit(solution)/shard_map/ppermute | solution.py:382
  17.6 6.8 %collective-permute-start.4 = (bf16[192,512]{1,0:T(8,128)(2,1)S(1)}, bf16[192,512]{1,0:T(8,128)(2,1)S(1)}, u32[]{:S(2)}, u32[]{:S(2)}) collective-permute-start(bf16[192,512]{1,0:T(8,128)(2,1)S(1)} %pad_maximum_fusion.refs_7_), channel_id=1, source_target_pairs={{0,1},{1,0},{2,3},{3,2},{4,5},{5,4},{6,7},{7,6},{8,9},{9,8},{10,11... | collective-permute-start | bytes 589832 | tf_op jit(solution)/shard_map/ppermute | solution.py:382
  17.7 7.3 %collective-permute-start.3 = (bf16[192,512]{1,0:T(8,128)(2,1)S(1)}, bf16[192,512]{1,0:T(8,128)(2,1)S(1)}, u32[]{:S(2)}, u32[]{:S(2)}) collective-permute-start(bf16[192,512]{1,0:T(8,128)(2,1)S(1)} %pad_maximum_fusion.refs_7_), channel_id=1, source_target_pairs={{0,2},{1,3},{2,0},{3,1},{4,6},{5,7},{6,4},{7,5},{8,10},{9,11},{10,... | collective-permute-start | bytes 589832 | tf_op jit(solution)/shard_map/ppermute | solution.py:382
  45.1 23.2 %collective-permute-start.12 = (bf16[2,384,512]{2,1,0:T(8,128)(2,1)}, bf16[2,384,512]{2,1,0:T(8,128)(2,1)S(1)}, u32[]{:S(2)}, u32[]{:S(2)}) collective-permute-start(bf16[2,384,512]{2,1,0:T(8,128)(2,1)} %get-tuple-element.90), channel_id=1, source_target_pairs={{0,2},{1,3},{2,0},{3,1},{4,6},{5,7},{6,4},{7,5},{8,10},{9,11},{10,... | collective-permute-start | bytes 2359304 | tf_op jit(solution)/shard_map/ppermute | solution.py:382
  69.3 3.6 %collective-permute-start.15 = (bf16[144,512]{1,0:T(8,128)(2,1)}, bf16[144,512]{1,0:T(8,128)(2,1)S(1)}, u32[]{:S(2)}, u32[]{:S(2)}) collective-permute-start(bf16[144,512]{1,0:T(8,128)(2,1)} %get-tuple-element.112), channel_id=1, source_target_pairs={{0,1},{1,0},{2,3},{3,2},{4,5},{5,4},{6,7},{7,6},{8,9},{9,8},{10,11... | collective-permute-start | bytes 442376 | tf_op jit(solution)/shard_map/ppermute | solution.py:382
  72.0 9.9 %collective-permute-start.17 = (bf16[320,512]{1,0:T(8,128)(2,1)S(1)}, bf16[320,512]{1,0:T(8,128)(2,1)S(1)}, u32[]{:S(2)}, u32[]{:S(2)}) collective-permute-start(bf16[320,512]{1,0:T(8,128)(2,1)S(1)} %fusion.5), channel_id=1, source_target_pairs={{0,2},{1,3},{2,0},{3,1},{4,6},{5,7},{6,4},{7,5},{8,10},{9,11},{10,... | collective-permute-start | bytes 983048 | tf_op jit(solution)/shard_map/ppermute | solution.py:382
  73.0 9.7 %collective-permute-start.24 = (bf16[96,512]{1,0:T(8,128)(2,1)S(1)}, bf16[96,512]{1,0:T(8,128)(2,1)S(1)}, u32[]{:S(2)}, u32[]{:S(2)}) collective-permute-start(bf16[96,512]{1,0:T(8,128)(2,1)S(1)} %get-tuple-element.146), channel_id=1, source_target_pairs={{0,12},{1,13},{2,14},{3,15},{4,8},{5,9},{6,10},{7,11},{8,4},{9,5},... | collective-permute-start | bytes 294920 | tf_op jit(solution)/shard_map/ppermute | solution.py:382
  73.1 10.6 %collective-permute-start.23 = (bf16[96,512]{1,0:T(8,128)(2,1)S(1)}, bf16[96,512]{1,0:T(8,128)(2,1)S(1)}, u32[]{:S(2)}, u32[]{:S(2)}) collective-permute-start(bf16[96,512]{1,0:T(8,128)(2,1)S(1)} %get-tuple-element.147), channel_id=1, source_target_pairs={{0,8},{1,9},{2,10},{3,11},{4,12},{5,13},{6,14},{7,15},{8,0},{9,1},... | collective-permute-start | bytes 294920 | tf_op jit(solution)/shard_map/ppermute | solution.py:382
  73.8 13.3 %collective-permute-start.22 = (bf16[96,512]{1,0:T(8,128)(2,1)S(1)}, bf16[96,512]{1,0:T(8,128)(2,1)S(1)}, u32[]{:S(2)}, u32[]{:S(2)}) collective-permute-start(bf16[96,512]{1,0:T(8,128)(2,1)S(1)} %get-tuple-element.148), channel_id=1, source_target_pairs={{0,4},{1,5},{2,6},{3,7},{4,0},{5,1},{6,2},{7,3},{8,12},{9,13},{10,... | collective-permute-start | bytes 294920 | tf_op jit(solution)/shard_map/ppermute | solution.py:382
  82.0 13.2 %collective-permute-start.18 = (bf16[384,512]{1,0:T(8,128)(2,1)S(1)}, bf16[384,512]{1,0:T(8,128)(2,1)S(1)}, u32[]{:S(2)}, u32[]{:S(2)}) collective-permute-start(bf16[384,512]{1,0:T(8,128)(2,1)S(1)} %get-tuple-element.119), channel_id=1, source_target_pairs={{0,2},{1,3},{2,0},{3,1},{4,6},{5,7},{6,4},{7,5},{8,10},{9,11},{10,... | collective-permute-start | bytes 1179656 | tf_op jit(solution)/shard_map/ppermute | solution.py:382
  82.6 7.2 %collective-permute-start.27 = (bf16[80,512]{1,0:T(8,128)(2,1)S(1)}, bf16[80,512]{1,0:T(8,128)(2,1)S(1)}, u32[]{:S(2)}, u32[]{:S(2)}) collective-permute-start(bf16[80,512]{1,0:T(8,128)(2,1)S(1)} %get-tuple-element.150), channel_id=1, source_target_pairs={{0,12},{1,13},{2,14},{3,15},{4,8},{5,9},{6,10},{7,11},{8,4},{9,5},... | collective-permute-start | bytes 245768 | tf_op jit(solution)/shard_map/ppermute | solution.py:382
  82.7 8.8 %collective-permute-start.26 = (bf16[80,512]{1,0:T(8,128)(2,1)S(1)}, bf16[80,512]{1,0:T(8,128)(2,1)S(1)}, u32[]{:S(2)}, u32[]{:S(2)}) collective-permute-start(bf16[80,512]{1,0:T(8,128)(2,1)S(1)} %get-tuple-element.151), channel_id=1, source_target_pairs={{0,8},{1,9},{2,10},{3,11},{4,12},{5,13},{6,14},{7,15},{8,0},{9,1},... | collective-permute-start | bytes 245768 | tf_op jit(solution)/shard_map/ppermute | solution.py:382
  83.7 10.8 %collective-permute-start.25 = (bf16[80,512]{1,0:T(8,128)(2,1)S(1)}, bf16[80,512]{1,0:T(8,128)(2,1)S(1)}, u32[]{:S(2)}, u32[]{:S(2)}) collective-permute-start(bf16[80,512]{1,0:T(8,128)(2,1)S(1)} %get-tuple-element.152), channel_id=1, source_target_pairs={{0,4},{1,5},{2,6},{3,7},{4,0},{5,1},{6,2},{7,3},{8,12},{9,13},{10,... | collective-permute-start | bytes 245768 | tf_op jit(solution)/shard_map/ppermute | solution.py:382
  87.1 8.2 %collective-permute-start.21 = (bf16[48,512]{1,0:T(8,128)(2,1)S(1)}, bf16[48,512]{1,0:T(8,128)(2,1)S(1)}, u32[]{:S(2)}, u32[]{:S(2)}) collective-permute-start(bf16[48,512]{1,0:T(8,128)(2,1)S(1)} %copy-done.23), channel_id=1, source_target_pairs={{0,13},{1,4},{2,15},{3,6},{4,1},{5,8},{6,3},{7,10},{8,5},{9,12},{1... | collective-permute-start | bytes 147464 | tf_op jit(solution)/shard_map/ppermute | solution.py:382
  89.8 7.4 %collective-permute-start.19 = (bf16[96,512]{1,0:T(8,128)(2,1)S(1)}, bf16[96,512]{1,0:T(8,128)(2,1)S(1)}, u32[]{:S(2)}, u32[]{:S(2)}) collective-permute-start(bf16[96,512]{1,0:T(8,128)(2,1)S(1)} %pad_maximum_fusion.1), channel_id=1, source_target_pairs={{0,2},{1,3},{2,4},{3,5},{4,6},{5,7},{6,8},{7,9},{8,10},{9,11},{10,... | collective-permute-start | bytes 294920 | tf_op jit(solution)/shard_map/ppermute | solution.py:382
  91.5 6.1 %collective-permute-start.20 = (bf16[96,512]{1,0:T(8,128)(2,1)S(1)}, bf16[96,512]{1,0:T(8,128)(2,1)S(1)}, u32[]{:S(2)}, u32[]{:S(2)}) collective-permute-start(bf16[96,512]{1,0:T(8,128)(2,1)S(1)} %pad_maximum_fusion.2), channel_id=1, source_target_pairs={{0,14},{1,15},{2,0},{3,1},{4,2},{5,3},{6,4},{7,5},{8,6},{9,7},{10,... | collective-permute-start | bytes 294920 | tf_op jit(solution)/shard_map/ppermute | solution.py:382
  97.6 8.3 %collective-permute-start.28 = (bf16[96,512]{1,0:T(8,128)(2,1)S(1)}, bf16[96,512]{1,0:T(8,128)(2,1)S(1)}, u32[]{:S(2)}, u32[]{:S(2)}) collective-permute-start(bf16[96,512]{1,0:T(8,128)(2,1)S(1)} %get-tuple-element.143), channel_id=1, source_target_pairs={{0,4},{1,5},{2,6},{3,7},{4,0},{5,1},{6,2},{7,3},{8,12},{9,13},{10,... | collective-permute-start | bytes 294920 | tf_op jit(solution)/shard_map/ppermute | solution.py:382
  97.7 8.2 %collective-permute-start.30 = (bf16[96,512]{1,0:T(8,128)(2,1)S(1)}, bf16[96,512]{1,0:T(8,128)(2,1)S(1)}, u32[]{:S(2)}, u32[]{:S(2)}) collective-permute-start(bf16[96,512]{1,0:T(8,128)(2,1)S(1)} %get-tuple-element.144), channel_id=1, source_target_pairs={{0,12},{1,13},{2,14},{3,15},{4,8},{5,9},{6,10},{7,11},{8,4},{9,5},... | collective-permute-start | bytes 294920 | tf_op jit(solution)/shard_map/ppermute | solution.py:382
  99.0 9.4 %collective-permute-start.29 = (bf16[96,512]{1,0:T(8,128)(2,1)S(1)}, bf16[96,512]{1,0:T(8,128)(2,1)S(1)}, u32[]{:S(2)}, u32[]{:S(2)}) collective-permute-start(bf16[96,512]{1,0:T(8,128)(2,1)S(1)} %get-tuple-element.145), channel_id=1, source_target_pairs={{0,8},{1,9},{2,10},{3,11},{4,12},{5,13},{6,14},{7,15},{8,0},{9,1},... | collective-permute-start | bytes 294920 | tf_op jit(solution)/shard_map/ppermute | solution.py:382
  (32 other events, 208.0 us)

commit v8 on v7

--- a/solution.py
+++ b/solution.py
@@ -14,7 +14,7 @@
 NEAR = 3
 BF16 = jnp.bfloat16
 F32 = jnp.float32
-VMEM_BYTES = 56 * 1024 * 1024
+VMEM_BYTES = 24 * 1024 * 1024
 
 
 def dot(left, right):
@@ -431,6 +431,23 @@
     for place in range(1, count):
         piece = pieces[place * share : (place + 1) * share]
         terms.append(send(piece, by_xor(peers, 4 * place)))
+    return terms
+
+
+def halve_sum(peers, pieces):
+    count = peers // 4
+    blocks = pieces.reshape(count // 2, 2, -1, pieces.shape[1])
+    kept, outgoing = [blocks[:, place].reshape(-1, pieces.shape[1]) for place in range(2)]
+    return add(kept, send(outgoing, by_xor(peers, 4)))
+
+
+def rest_terms(peers, pieces):
+    count = peers // 8
+    share = pieces.shape[0] // count
+    terms = [pieces[:share]]
+    for place in range(1, count):
+        piece = pieces[place * share : (place + 1) * share]
+        terms.append(send(piece, by_xor(peers, 8 * place)))
     return terms
 
 
@@ -642,7 +659,7 @@
     node_pieces, edge_next, edge_kept, swapped, slot_next = lax.optimization_barrier(
         (node_pieces, edge_next, edge_kept, swapped, slot_next)
     )
-    node_terms = last_terms(peers, node_pieces)
+    node_pieces = halve_sum(peers, node_pieces)
     to_after = jnp.concatenate([returns[2], swapped[cap : 2 * cap]], axis=0)
     to_before = jnp.concatenate([returns[3], swapped[2 * cap :]], axis=0)
     near = [
@@ -650,10 +667,12 @@
         send(to_before, by_shift(peers, -2)),
         send(returns[4], across_chips(peers)),
     ]
-    slot_pieces, edge_next, edge_kept = lax.optimization_barrier((slot_pieces, edge_next, edge_kept))
+    (slot_pieces, edge_next, edge_kept, near, node_pieces) = lax.optimization_barrier(
+        (slot_pieces, edge_next, edge_kept, near, node_pieces)
+    )
+    node_terms = rest_terms(peers, node_pieces)
     edge_pieces = next_sum(peers, 2, edge_next, edge_kept)
     slot_terms = last_terms(peers, slot_pieces)
-    edge_pieces, near = lax.optimization_barrier((edge_pieces, near))
     edge_terms = last_terms(peers, edge_pieces)
     node_terms, slot_terms = lax.optimization_barrier((node_terms, slot_terms))
     returned = [returns[0], swapped, *near]

time: 110 us -> 104 us (0.945)
  Pallas kernels: 53 us -> 22.1 us
  waiting for transfers between devices: 15 us -> 31.1 us
  local copies, waits for them, and re-layouts: 0.84 us -> 6.06 us
  starting transfers between devices: 34.8 us -> 39.4 us
    ppermute x31 -> x30, waiting for transfers between devices: 15 us -> 31.1 us  [send(): return lax.ppermute(values, 'lon', perm)]
    pallas_call x1, Pallas kernels: 21.6 us -> 8.51 us  [on_device(): pl.pallas_call(functools.partial(backward_kernel, peers), grid=(tiles,),...]
    pallas_call x1, Pallas kernels: 17.5 us -> 6.05 us  [on_device(): pl.pallas_call(functools.partial(forward_kernel, peers), grid=(tiles,), i...]
    unnamed x50 -> x24, local copies, waits for them, and re-layouts: 0.76 us -> 5.97 us
    ppermute x31 -> x30, starting transfers between devices: 34.8 us -> 39.4 us  [send(): return lax.ppermute(values, 'lon', perm)]
    pallas_call x1, Pallas kernels: 6.62 us -> 3.46 us  [on_device(): pl.pallas_call(local_kernel, grid=(tiles,), in_specs=[index_tile, tile_of...]
    pallas_call x1, Pallas kernels: 3.36 us -> 1.37 us  [on_device(): pl.pallas_call(gather_kernel, grid=(2,), in_specs=[smem, whole(rows.shape...]
    pallas_call x1, Pallas kernels: 3.97 us -> 2.69 us  [on_device(): pl.pallas_call(functools.partial(scatter_kernel, out_rows), grid=(2,), in...]
  transfers between devices with their start and end apart: 31 -> 30, of which waited for: 10 -> 12; matrix products, arithmetic and copies ran while one was open for 3% -> 2% of each run, Pallas kernels for 29% -> 14%
where the time goes in v8:
time: 104 us; the launch traced here: 103 us
  starting transfers between devices  39.4 us (38%)
  waiting for transfers between devices  31.1 us (30%)
  Pallas kernels  22.1 us (21%)
  local copies, waits for them, and re-layouts  6.06 us (6%)
  other arithmetic  3.01 us (3%)
  between operations  1.6 us (2%)
    ppermute x30, starting transfers between devices, send(): return lax.ppermute(values, 'lon', perm)  39.4 us
    ppermute x30, waiting for transfers between devices, send(): return lax.ppermute(values, 'lon', perm)  31.1 us
    pallas_call x1, Pallas kernels, on_device(): pl.pallas_call(functools.partial(backward_kernel, peers), grid=(tiles,),...  8.51 us
    pallas_call x1, Pallas kernels, on_device(): pl.pallas_call(functools.partial(forward_kernel, peers), grid=(tiles,), i...  6.05 us
    unnamed x24, local copies, waits for them, and re-layouts  5.97 us
    pallas_call x1, Pallas kernels, on_device(): pl.pallas_call(local_kernel, grid=(tiles,), in_specs=[index_tile, tile_of...  3.46 us
    pallas_call x1, Pallas kernels, on_device(): pl.pallas_call(functools.partial(scatter_kernel, out_rows), grid=(2,), in...  2.69 us
  transfers between devices with their start and end apart: 30, of which 12 were waited for; matrix products, arithmetic and copies ran while one was open for 2% of the time, Pallas kernels for 14%

profile of v8, /device:TPU:0, one launch (start us, length us, event | category | flops | bytes accessed | tf_op | source)
XLA Modules:
  0.0 103.2 jit_solution(4395517529300219639)
XLA Ops:
  0.7 1.7 %copy-done.2 = bf16[2048,512]{1,0:T(8,128)(2,1)S(1)} copy-done((bf16[2048,512]{1,0:T(8,128)(2,1)S(1)}, bf16[2048,512]{1,0:T(8,128)(2,1)}, u32[]{:S(2)}) %copy-start.2) | copy-done | bytes 2097176
  3.1 1.4 %gather_lists.1 = (bf16[48,512]{1,0:T(8,128)(2,1)S(1)}, bf16[48,512]{1,0:T(8,128)(2,1)S(1)}, bf16[96,512]{1,0:T(8,128)(2,1)S(1)}, bf16[96,512]{1,0:T(8,128)(2,1)...) custom-call(s32[1]{0:T(128)} %bitcast.me_ref, s32[16,48]{1,0:T(8,128)S(1)} %bitcast.27, ...), custom_call_target="tpu_custom_call" | custom-call | tf_op jit(solution)/shard_map/gather_lists/pallas_call | solution.py:516
  4.4 5.1 %collective-permute-start.2 = (bf16[48,512]{1,0:T(8,128)(2,1)S(1)}, bf16[48,512]{1,0:T(8,128)(2,1)S(1)}, u32[]{:S(2)}, u32[]{:S(2)}) collective-permute-start(bf16[48,512]{1,0:T(8,128)(2,1)S(1)} %get-tuple-element.71), channel_id=1, source_target_pairs={{0,12},{1,13},{2,14},{3,15},{4,8},{5,9},{6,10},{7,11},{8,4},{9,5},... | collective-permute-start | bytes 147464 | tf_op jit(solution)/shard_map/ppermute | solution.py:382
  10.2 2.3 %collective-permute-start.7 = (bf16[48,512]{1,0:T(8,128)(2,1)S(1)}, bf16[48,512]{1,0:T(8,128)(2,1)S(1)}, u32[]{:S(2)}, u32[]{:S(2)}) collective-permute-start(bf16[48,512]{1,0:T(8,128)(2,1)S(1)} %get-tuple-element.77), channel_id=1, source_target_pairs={{0,13},{1,4},{2,15},{3,6},{4,1},{5,8},{6,3},{7,10},{8,5},{9,12},{1... | collective-permute-start | bytes 147464 | tf_op jit(solution)/shard_map/ppermute | solution.py:382
  12.5 1.5 %collective-permute-start.5 = (bf16[96,512]{1,0:T(8,128)(2,1)S(1)}, bf16[96,512]{1,0:T(8,128)(2,1)S(1)}, u32[]{:S(2)}, u32[]{:S(2)}) collective-permute-start(bf16[96,512]{1,0:T(8,128)(2,1)S(1)} %get-tuple-element.75), channel_id=1, source_target_pairs={{0,2},{1,3},{2,4},{3,5},{4,6},{5,7},{6,8},{7,9},{8,10},{9,11},{10,... | collective-permute-start | bytes 294920 | tf_op jit(solution)/shard_map/ppermute | solution.py:382
  14.1 3.2 %collective-permute-start.6 = (bf16[96,512]{1,0:T(8,128)(2,1)S(1)}, bf16[96,512]{1,0:T(8,128)(2,1)S(1)}, u32[]{:S(2)}, u32[]{:S(2)}) collective-permute-start(bf16[96,512]{1,0:T(8,128)(2,1)S(1)} %get-tuple-element.76), channel_id=1, source_target_pairs={{0,14},{1,15},{2,0},{3,1},{4,2},{5,3},{6,4},{7,5},{8,6},{9,7},{10,... | collective-permute-start | bytes 294920 | tf_op jit(solution)/shard_map/ppermute | solution.py:382
  17.5 1.9 %copy-done.1 = bf16[3072,512]{1,0:T(8,128)(2,1)S(1)} copy-done((bf16[3072,512]{1,0:T(8,128)(2,1)S(1)}, bf16[3072,512]{1,0:T(8,128)(2,1)}, u32[]{:S(2)}) %copy-start.1) | copy-done | bytes 3145752
  21.0 3.5 %edge_local.1.local_ref = bf16[3072,512]{1,0:T(8,128)(2,1)S(1)} custom-call(s32[3,1,1024]{2,1,0:T(1,128)S(1)} %bitcast.24, bf16[3072,512]{1,0:T(8,128)(2,1)S(1)} %copy-done.1, bf16[256,512]{1,0:T(8,128)(2,1)S(1)} %copy-done.3, bf16[1536,512]{1,0:T(8,128)(2,1)S(1)} %copy-done, bf16[1536,512]{1,0:T(8,128)(2,1)S(1)} %copy-done), custom_call_target="tpu_custom_call" | custom-call | flops 2415919104 | bytes 6291456 | tf_op jit(solution)/shard_map/edge_local/pallas_call | solution.py:533
  26.8 6.0 %forward.1 = (bf16[768,512]{1,0:T(8,128)(2,1)S(1)}, bf16[3072,512]{1,0:T(8,128)(2,1)S(1)}, bf16[3072,512]{1,0:T(8,128)(2,1)S(1)}, bf16[3072,512]{1,0:T(8,128)(2,...) custom-call(s32[1]{0:T(128)} %bitcast.me_ref, ...), custom_call_target="tpu_custom_call" | custom-call | tf_op jit(solution)/shard_map/forward/pallas_call | solution.py:553
  32.9 7.7 %collective-permute-start.12 = (bf16[2,384,512]{2,1,0:T(8,128)(2,1)S(1)}, bf16[2,384,512]{2,1,0:T(8,128)(2,1)S(1)}, u32[]{:S(2)}, u32[]{:S(2)}) collective-permute-start(bf16[2,384,512]{2,1,0:T(8,128)(2,1)S(1)} %get-tuple-element.88), channel_id=1, source_target_pairs={{0,2},{1,3},{2,0},{3,1},{4,6},{5,7},{6,4},{7,5},{8,10},{9,11},{10,... | collective-permute-start | bytes 2359304 | tf_op jit(solution)/shard_map/ppermute | solution.py:382
  40.6 8.5 %backward.1 = (bf16[3072,512]{1,0:T(8,128)(2,1)}, bf16[256,512]{1,0:T(8,128)(2,1)}, bf16[2,320,512]{2,1,0:T(8,128)(2,1)S(1)}, bf16[2,320,512]{2,1,0:T(8,128)(2,1...) custom-call(s32[1]{0:T(128)} %bitcast.me_ref, ...), custom_call_target="tpu_custom_call" | custom-call | flops 10468982784 | bytes 15728640 | tf_op jit(solution)/shard_map/backward/pallas_call | solution.py:602
  49.1 9.5 %collective-permute-done.12 = bf16[2,384,512]{2,1,0:T(8,128)(2,1)S(1)} collective-permute-done((bf16[2,384,512]{2,1,0:T(8,128)(2,1)S(1)}, bf16[2,384,512]{2,1,0:T(8,128)(2,1)S(1)}, u32[]{:S(2)}, u32[]{:S(2)}) %collective-permute-start.12) | collective-permute-done | bytes 786464 | tf_op jit(solution)/shard_map/ppermute | solution.py:382
  60.0 1.6 %collective-permute-done.13 = bf16[384,512]{1,0:T(8,128)(2,1)S(1)} collective-permute-done((bf16[384,512]{1,0:T(8,128)(2,1)S(1)}, bf16[384,512]{1,0:T(8,128)(2,1)S(1)}, u32[]{:S(2)}, u32[]{:S(2)}) %collective-permute-start.13) | collective-permute-done | bytes 393248 | tf_op jit(solution)/shard_map/ppermute | solution.py:382
  61.8 1.8 %collective-permute-start.17 = (bf16[320,512]{1,0:T(8,128)(2,1)S(1)}, bf16[320,512]{1,0:T(8,128)(2,1)S(1)}, u32[]{:S(2)}, u32[]{:S(2)}) collective-permute-start(bf16[320,512]{1,0:T(8,128)(2,1)S(1)} %fusion.6), channel_id=1, source_target_pairs={{0,2},{1,3},{2,0},{3,1},{4,6},{5,7},{6,4},{7,5},{8,10},{9,11},{10,... | collective-permute-start | bytes 983048 | tf_op jit(solution)/shard_map/ppermute | solution.py:382
  64.8 3.9 %collective-permute-start.19 = (bf16[96,512]{1,0:T(8,128)(2,1)S(1)}, bf16[96,512]{1,0:T(8,128)(2,1)S(1)}, u32[]{:S(2)}, u32[]{:S(2)}) collective-permute-start(bf16[96,512]{1,0:T(8,128)(2,1)S(1)} %pad_maximum_fusion.2), channel_id=1, source_target_pairs={{0,14},{1,15},{2,0},{3,1},{4,2},{5,3},{6,4},{7,5},{8,6},{9,7},{10,... | collective-permute-start | bytes 294920 | tf_op jit(solution)/shard_map/ppermute | solution.py:382
  68.8 5.7 %collective-permute-done.17 = bf16[320,512]{1,0:T(8,128)(2,1)S(1)} collective-permute-done((bf16[320,512]{1,0:T(8,128)(2,1)S(1)}, bf16[320,512]{1,0:T(8,128)(2,1)S(1)}, u32[]{:S(2)}, u32[]{:S(2)}) %collective-permute-start.17) | collective-permute-done | bytes 327712 | tf_op jit(solution)/shard_map/ppermute | solution.py:382
  75.9 1.8 %collective-permute-start.26 = (bf16[384,512]{1,0:T(8,128)(2,1)S(1)}, bf16[384,512]{1,0:T(8,128)(2,1)S(1)}, u32[]{:S(2)}, u32[]{:S(2)}) collective-permute-start(bf16[384,512]{1,0:T(8,128)(2,1)S(1)} %get-tuple-element.132), channel_id=1, source_target_pairs={{0,2},{1,3},{2,0},{3,1},{4,6},{5,7},{6,4},{7,5},{8,10},{9,11},{10,... | collective-permute-start | bytes 1179656 | tf_op jit(solution)/shard_map/ppermute | solution.py:382
  77.8 2.7 %collective-permute-start.25 = (bf16[80,512]{1,0:T(8,128)(2,1)S(1)}, bf16[80,512]{1,0:T(8,128)(2,1)S(1)}, u32[]{:S(2)}, u32[]{:S(2)}) collective-permute-start(bf16[80,512]{1,0:T(8,128)(2,1)S(1)} %get-tuple-element.144), channel_id=1, source_target_pairs={{0,12},{1,13},{2,14},{3,15},{4,8},{5,9},{6,10},{7,11},{8,4},{9,5},... | collective-permute-start | bytes 245768 | tf_op jit(solution)/shard_map/ppermute | solution.py:382
  82.2 3.0 %collective-permute-done.25.refs_8_ = bf16[80,512]{1,0:T(8,128)(2,1)S(1)} collective-permute-done((bf16[80,512]{1,0:T(8,128)(2,1)S(1)}, bf16[80,512]{1,0:T(8,128)(2,1)S(1)}, u32[]{:S(2)}, u32[]{:S(2)}) %collective-permute-start.25) | collective-permute-done | bytes 81952 | tf_op jit(solution)/shard_map/ppermute | solution.py:382
  85.2 4.8 %collective-permute-done.24.refs_7_ = bf16[80,512]{1,0:T(8,128)(2,1)S(1)} collective-permute-done((bf16[80,512]{1,0:T(8,128)(2,1)S(1)}, bf16[80,512]{1,0:T(8,128)(2,1)S(1)}, u32[]{:S(2)}, u32[]{:S(2)}) %collective-permute-start.24) | collective-permute-done | bytes 81952 | tf_op jit(solution)/shard_map/ppermute | solution.py:382
  90.9 1.2 %collective-permute-start.29 = (bf16[96,512]{1,0:T(8,128)(2,1)S(1)}, bf16[96,512]{1,0:T(8,128)(2,1)S(1)}, u32[]{:S(2)}, u32[]{:S(2)}) collective-permute-start(bf16[96,512]{1,0:T(8,128)(2,1)S(1)} %get-tuple-element.140), channel_id=1, source_target_pairs={{0,12},{1,13},{2,14},{3,15},{4,8},{5,9},{6,10},{7,11},{8,4},{9,5},... | collective-permute-start | bytes 294920 | tf_op jit(solution)/shard_map/ppermute | solution.py:382
  92.1 2.2 %collective-permute-start.28 = (bf16[96,512]{1,0:T(8,128)(2,1)S(1)}, bf16[96,512]{1,0:T(8,128)(2,1)S(1)}, u32[]{:S(2)}, u32[]{:S(2)}) collective-permute-start(bf16[96,512]{1,0:T(8,128)(2,1)S(1)} %get-tuple-element.141), channel_id=1, source_target_pairs={{0,8},{1,9},{2,10},{3,11},{4,12},{5,13},{6,14},{7,15},{8,0},{9,1},... | collective-permute-start | bytes 294920 | tf_op jit(solution)/shard_map/ppermute | solution.py:382
  95.0 2.7 %scatter_lists.1 = bf16[2048,512]{1,0:T(8,128)(2,1)} custom-call(s32[1]{0:T(128)} %bitcast.me_ref, s32[16,48]{1,0:T(8,128)S(1)} %bitcast.28, bf16[48,512]{1,0:T(8,128)(2,1)S(1)} %get-tuple-element.105.refs_0_, bf16[144,512]{1,0:T(8,128)(2,1)S(1)} %collective-permute-done.15.refs_1_, bf16[96,512]{1,0:T(8,128)(2,1)S(1)} %collective-permute-done.18.refs_2_, ...), custom_call_target="tpu_custom_call" | custom-call | tf_op jit(solution)/shard_map/scatter_lists/pallas_call | solution.py:681
  98.0 4.4 %collective-permute-done.28 = bf16[96,512]{1,0:T(8,128)(2,1)S(1)} collective-permute-done((bf16[96,512]{1,0:T(8,128)(2,1)S(1)}, bf16[96,512]{1,0:T(8,128)(2,1)S(1)}, u32[]{:S(2)}, u32[]{:S(2)}) %collective-permute-start.28) | collective-permute-done | bytes 98336 | tf_op jit(solution)/shard_map/ppermute | solution.py:382
  (83 shorter events, 13.3 us)
Async XLA Ops:
  4.4 9.6 %collective-permute-start.2 = (bf16[48,512]{1,0:T(8,128)(2,1)S(1)}, bf16[48,512]{1,0:T(8,128)(2,1)S(1)}, u32[]{:S(2)}, u32[]{:S(2)}) collective-permute-start(bf16[48,512]{1,0:T(8,128)(2,1)S(1)} %get-tuple-element.71), channel_id=1, source_target_pairs={{0,12},{1,13},{2,14},{3,15},{4,8},{5,9},{6,10},{7,11},{8,4},{9,5},... | collective-permute-start | bytes 147464 | tf_op jit(solution)/shard_map/ppermute | solution.py:382
  9.5 7.7 %collective-permute-start.1 = (bf16[48,512]{1,0:T(8,128)(2,1)S(1)}, bf16[48,512]{1,0:T(8,128)(2,1)S(1)}, u32[]{:S(2)}, u32[]{:S(2)}) collective-permute-start(bf16[48,512]{1,0:T(8,128)(2,1)S(1)} %get-tuple-element.71), channel_id=1, source_target_pairs={{0,8},{1,9},{2,10},{3,11},{4,12},{5,13},{6,14},{7,15},{8,0},{9,1},... | collective-permute-start | bytes 147464 | tf_op jit(solution)/shard_map/ppermute | solution.py:382
  9.5 7.7 %collective-permute-start = (bf16[48,512]{1,0:T(8,128)(2,1)S(1)}, bf16[48,512]{1,0:T(8,128)(2,1)S(1)}, u32[]{:S(2)}, u32[]{:S(2)}) collective-permute-start(bf16[48,512]{1,0:T(8,128)(2,1)S(1)} %get-tuple-element.71), channel_id=1, source_target_pairs={{0,4},{1,5},{2,6},{3,7},{4,0},{5,1},{6,2},{7,3},{8,12},{9,13},{10,... | collective-permute-start | bytes 147464 | tf_op jit(solution)/shard_map/ppermute | solution.py:382
  10.2 14.3 %collective-permute-start.7 = (bf16[48,512]{1,0:T(8,128)(2,1)S(1)}, bf16[48,512]{1,0:T(8,128)(2,1)S(1)}, u32[]{:S(2)}, u32[]{:S(2)}) collective-permute-start(bf16[48,512]{1,0:T(8,128)(2,1)S(1)} %get-tuple-element.77), channel_id=1, source_target_pairs={{0,13},{1,4},{2,15},{3,6},{4,1},{5,8},{6,3},{7,10},{8,5},{9,12},{1... | collective-permute-start | bytes 147464 | tf_op jit(solution)/shard_map/ppermute | solution.py:382
  12.5 12.0 %collective-permute-start.5 = (bf16[96,512]{1,0:T(8,128)(2,1)S(1)}, bf16[96,512]{1,0:T(8,128)(2,1)S(1)}, u32[]{:S(2)}, u32[]{:S(2)}) collective-permute-start(bf16[96,512]{1,0:T(8,128)(2,1)S(1)} %get-tuple-element.75), channel_id=1, source_target_pairs={{0,2},{1,3},{2,4},{3,5},{4,6},{5,7},{6,8},{7,9},{8,10},{9,11},{10,... | collective-permute-start | bytes 294920 | tf_op jit(solution)/shard_map/ppermute | solution.py:382
  14.1 10.5 %collective-permute-start.6 = (bf16[96,512]{1,0:T(8,128)(2,1)S(1)}, bf16[96,512]{1,0:T(8,128)(2,1)S(1)}, u32[]{:S(2)}, u32[]{:S(2)}) collective-permute-start(bf16[96,512]{1,0:T(8,128)(2,1)S(1)} %get-tuple-element.76), channel_id=1, source_target_pairs={{0,14},{1,15},{2,0},{3,1},{4,2},{5,3},{6,4},{7,5},{8,6},{9,7},{10,... | collective-permute-start | bytes 294920 | tf_op jit(solution)/shard_map/ppermute | solution.py:382
  17.3 7.2 %collective-permute-start.4 = (bf16[192,512]{1,0:T(8,128)(2,1)S(1)}, bf16[192,512]{1,0:T(8,128)(2,1)S(1)}, u32[]{:S(2)}, u32[]{:S(2)}) collective-permute-start(bf16[192,512]{1,0:T(8,128)(2,1)S(1)} %pad_maximum_fusion.refs_7_), channel_id=1, source_target_pairs={{0,1},{1,0},{2,3},{3,2},{4,5},{5,4},{6,7},{7,6},{8,9},{9,8},{10,11... | collective-permute-start | bytes 589832 | tf_op jit(solution)/shard_map/ppermute | solution.py:382
  17.4 7.3 %collective-permute-start.3 = (bf16[192,512]{1,0:T(8,128)(2,1)S(1)}, bf16[192,512]{1,0:T(8,128)(2,1)S(1)}, u32[]{:S(2)}, u32[]{:S(2)}) collective-permute-start(bf16[192,512]{1,0:T(8,128)(2,1)S(1)} %pad_maximum_fusion.refs_7_), channel_id=1, source_target_pairs={{0,2},{1,3},{2,0},{3,1},{4,6},{5,7},{6,4},{7,5},{8,10},{9,11},{10,... | collective-permute-start | bytes 589832 | tf_op jit(solution)/shard_map/ppermute | solution.py:382
  32.9 25.8 %collective-permute-start.12 = (bf16[2,384,512]{2,1,0:T(8,128)(2,1)S(1)}, bf16[2,384,512]{2,1,0:T(8,128)(2,1)S(1)}, u32[]{:S(2)}, u32[]{:S(2)}) collective-permute-start(bf16[2,384,512]{2,1,0:T(8,128)(2,1)S(1)} %get-tuple-element.88), channel_id=1, source_target_pairs={{0,2},{1,3},{2,0},{3,1},{4,6},{5,7},{6,4},{7,5},{8,10},{9,11},{10,... | collective-permute-start | bytes 2359304 | tf_op jit(solution)/shard_map/ppermute | solution.py:382
  59.5 4.2 %collective-permute-start.14 = (bf16[2,384,512]{2,1,0:T(8,128)(2,1)S(1)}, bf16[2,384,512]{2,1,0:T(8,128)(2,1)S(1)}, u32[]{:S(2)}, u32[]{:S(2)}) collective-permute-start(bf16[2,384,512]{2,1,0:T(8,128)(2,1)S(1)} %get-tuple-element.109), channel_id=1, source_target_pairs={{0,1},{1,0},{2,3},{3,2},{4,5},{5,4},{6,7},{7,6},{8,9},{9,8},{10,11... | collective-permute-start | bytes 2359304 | tf_op jit(solution)/shard_map/ppermute | solution.py:382
  59.5 15.5 %collective-permute-start.20 = (bf16[48,512]{1,0:T(8,128)(2,1)S(1)}, bf16[48,512]{1,0:T(8,128)(2,1)S(1)}, u32[]{:S(2)}, u32[]{:S(2)}) collective-permute-start(bf16[48,512]{1,0:T(8,128)(2,1)S(1)} %get-tuple-element.118), channel_id=1, source_target_pairs={{0,13},{1,4},{2,15},{3,6},{4,1},{5,8},{6,3},{7,10},{8,5},{9,12},{1... | collective-permute-start | bytes 147464 | tf_op jit(solution)/shard_map/ppermute | solution.py:382
  59.5 4.3 %collective-permute-start.15 = (bf16[144,512]{1,0:T(8,128)(2,1)S(1)}, bf16[144,512]{1,0:T(8,128)(2,1)S(1)}, u32[]{:S(2)}, u32[]{:S(2)}) collective-permute-start(bf16[144,512]{1,0:T(8,128)(2,1)S(1)} %get-tuple-element.110), channel_id=1, source_target_pairs={{0,1},{1,0},{2,3},{3,2},{4,5},{5,4},{6,7},{7,6},{8,9},{9,8},{10,11... | collective-permute-start | bytes 442376 | tf_op jit(solution)/shard_map/ppermute | solution.py:382
  61.8 12.7 %collective-permute-start.17 = (bf16[320,512]{1,0:T(8,128)(2,1)S(1)}, bf16[320,512]{1,0:T(8,128)(2,1)S(1)}, u32[]{:S(2)}, u32[]{:S(2)}) collective-permute-start(bf16[320,512]{1,0:T(8,128)(2,1)S(1)} %fusion.6), channel_id=1, source_target_pairs={{0,2},{1,3},{2,0},{3,1},{4,6},{5,7},{6,4},{7,5},{8,10},{9,11},{10,... | collective-permute-start | bytes 983048 | tf_op jit(solution)/shard_map/ppermute | solution.py:382
  63.9 11.2 %collective-permute-start.18 = (bf16[96,512]{1,0:T(8,128)(2,1)S(1)}, bf16[96,512]{1,0:T(8,128)(2,1)S(1)}, u32[]{:S(2)}, u32[]{:S(2)}) collective-permute-start(bf16[96,512]{1,0:T(8,128)(2,1)S(1)} %pad_maximum_fusion.1), channel_id=1, source_target_pairs={{0,2},{1,3},{2,4},{3,5},{4,6},{5,7},{6,8},{7,9},{8,10},{9,11},{10,... | collective-permute-start | bytes 294920 | tf_op jit(solution)/shard_map/ppermute | solution.py:382
  64.8 11.0 %collective-permute-start.19 = (bf16[96,512]{1,0:T(8,128)(2,1)S(1)}, bf16[96,512]{1,0:T(8,128)(2,1)S(1)}, u32[]{:S(2)}, u32[]{:S(2)}) collective-permute-start(bf16[96,512]{1,0:T(8,128)(2,1)S(1)} %pad_maximum_fusion.2), channel_id=1, source_target_pairs={{0,14},{1,15},{2,0},{3,1},{4,2},{5,3},{6,4},{7,5},{8,6},{9,7},{10,... | collective-permute-start | bytes 294920 | tf_op jit(solution)/shard_map/ppermute | solution.py:382
  68.8 6.2 %collective-permute-start.21 = (bf16[192,512]{1,0:T(8,128)(2,1)S(1)}, bf16[192,512]{1,0:T(8,128)(2,1)S(1)}, u32[]{:S(2)}, u32[]{:S(2)}) collective-permute-start(bf16[192,512]{1,0:T(8,128)(2,1)S(1)} %bitcast.32), channel_id=1, source_target_pairs={{0,4},{1,5},{2,6},{3,7},{4,0},{5,1},{6,2},{7,3},{8,12},{9,13},{10,... | collective-permute-start | bytes 589832 | tf_op jit(solution)/shard_map/ppermute | solution.py:382
  75.9 14.1 %collective-permute-start.22 = (bf16[96,512]{1,0:T(8,128)(2,1)S(1)}, bf16[96,512]{1,0:T(8,128)(2,1)S(1)}, u32[]{:S(2)}, u32[]{:S(2)}) collective-permute-start(bf16[96,512]{1,0:T(8,128)(2,1)S(1)} %get-tuple-element.148), channel_id=1, source_target_pairs={{0,8},{1,9},{2,10},{3,11},{4,12},{5,13},{6,14},{7,15},{8,0},{9,1},... | collective-permute-start | bytes 294920 | tf_op jit(solution)/shard_map/ppermute | solution.py:382
  75.9 14.7 %collective-permute-start.26 = (bf16[384,512]{1,0:T(8,128)(2,1)S(1)}, bf16[384,512]{1,0:T(8,128)(2,1)S(1)}, u32[]{:S(2)}, u32[]{:S(2)}) collective-permute-start(bf16[384,512]{1,0:T(8,128)(2,1)S(1)} %get-tuple-element.132), channel_id=1, source_target_pairs={{0,2},{1,3},{2,0},{3,1},{4,6},{5,7},{6,4},{7,5},{8,10},{9,11},{10,... | collective-permute-start | bytes 1179656 | tf_op jit(solution)/shard_map/ppermute | solution.py:382
  77.8 7.4 %collective-permute-start.25 = (bf16[80,512]{1,0:T(8,128)(2,1)S(1)}, bf16[80,512]{1,0:T(8,128)(2,1)S(1)}, u32[]{:S(2)}, u32[]{:S(2)}) collective-permute-start(bf16[80,512]{1,0:T(8,128)(2,1)S(1)} %get-tuple-element.144), channel_id=1, source_target_pairs={{0,12},{1,13},{2,14},{3,15},{4,8},{5,9},{6,10},{7,11},{8,4},{9,5},... | collective-permute-start | bytes 245768 | tf_op jit(solution)/shard_map/ppermute | solution.py:382
  80.5 9.5 %collective-permute-start.24 = (bf16[80,512]{1,0:T(8,128)(2,1)S(1)}, bf16[80,512]{1,0:T(8,128)(2,1)S(1)}, u32[]{:S(2)}, u32[]{:S(2)}) collective-permute-start(bf16[80,512]{1,0:T(8,128)(2,1)S(1)} %get-tuple-element.145), channel_id=1, source_target_pairs={{0,8},{1,9},{2,10},{3,11},{4,12},{5,13},{6,14},{7,15},{8,0},{9,1},... | collective-permute-start | bytes 245768 | tf_op jit(solution)/shard_map/ppermute | solution.py:382
  81.5 8.4 %collective-permute-start.23 = (bf16[80,512]{1,0:T(8,128)(2,1)S(1)}, bf16[80,512]{1,0:T(8,128)(2,1)S(1)}, u32[]{:S(2)}, u32[]{:S(2)}) collective-permute-start(bf16[80,512]{1,0:T(8,128)(2,1)S(1)} %get-tuple-element.146), channel_id=1, source_target_pairs={{0,4},{1,5},{2,6},{3,7},{4,0},{5,1},{6,2},{7,3},{8,12},{9,13},{10,... | collective-permute-start | bytes 245768 | tf_op jit(solution)/shard_map/ppermute | solution.py:382
  90.8 6.9 %collective-permute-start.27 = (bf16[96,512]{1,0:T(8,128)(2,1)S(1)}, bf16[96,512]{1,0:T(8,128)(2,1)S(1)}, u32[]{:S(2)}, u32[]{:S(2)}) collective-permute-start(bf16[96,512]{1,0:T(8,128)(2,1)S(1)} %get-tuple-element.139), channel_id=1, source_target_pairs={{0,4},{1,5},{2,6},{3,7},{4,0},{5,1},{6,2},{7,3},{8,12},{9,13},{10,... | collective-permute-start | bytes 294920 | tf_op jit(solution)/shard_map/ppermute | solution.py:382
  90.9 7.2 %collective-permute-start.29 = (bf16[96,512]{1,0:T(8,128)(2,1)S(1)}, bf16[96,512]{1,0:T(8,128)(2,1)S(1)}, u32[]{:S(2)}, u32[]{:S(2)}) collective-permute-start(bf16[96,512]{1,0:T(8,128)(2,1)S(1)} %get-tuple-element.140), channel_id=1, source_target_pairs={{0,12},{1,13},{2,14},{3,15},{4,8},{5,9},{6,10},{7,11},{8,4},{9,5},... | collective-permute-start | bytes 294920 | tf_op jit(solution)/shard_map/ppermute | solution.py:382
  92.1 10.4 %collective-permute-start.28 = (bf16[96,512]{1,0:T(8,128)(2,1)S(1)}, bf16[96,512]{1,0:T(8,128)(2,1)S(1)}, u32[]{:S(2)}, u32[]{:S(2)}) collective-permute-start(bf16[96,512]{1,0:T(8,128)(2,1)S(1)} %get-tuple-element.141), channel_id=1, source_target_pairs={{0,8},{1,9},{2,10},{3,11},{4,12},{5,13},{6,14},{7,15},{8,0},{9,1},... | collective-permute-start | bytes 294920 | tf_op jit(solution)/shard_map/ppermute | solution.py:382
  (18 other events, 94.1 us)

commit v9 on v8

--- a/solution.py
+++ b/solution.py
@@ -11,10 +11,12 @@
 STEP = 1024
 SUB = 512
 LANES = 128
+GRID_PARTS = 4
 NEAR = 3
 BF16 = jnp.bfloat16
 F32 = jnp.float32
 VMEM_BYTES = 24 * 1024 * 1024
+GATHER_BYTES = 56 * 1024 * 1024
 
 
 def dot(left, right):
@@ -155,23 +157,32 @@
     return jnp.concatenate(pieces, axis=0)
 
 
-def gather_kernel(me_ref, rows_ref, grid_ref, *refs):
-    near_refs, far_ref, total = refs[:5], refs[5], refs[6]
+def gather_kernel(me_ref, rows_hbm, grid_hbm, *refs):
+    near_refs, far_ref = refs[:5], refs[5]
+    rows_ref, grid_ref, rows_done, grid_done = refs[6:]
     cap = rows_ref.shape[1]
-    step = pl.program_id(0)
-    part = grid_ref.shape[0]
-    found = dot(list_hots(me_ref[0], rows_ref, part, step * part), grid_ref[...])
-
-    @pl.when(step == 0)
-    def _():
-        total[...] = found
-
-    @pl.when(step == pl.num_programs(0) - 1)
-    def _():
-        rows = (total[...] + found).astype(BF16)
-        lists = [rows[at : at + cap] for at in range(0, 8 * cap, cap)]
-        write_near(near_refs, cap, lists)
-        far_ref[...] = lists[7]
+    part = grid_ref.shape[0] // GRID_PARTS
+    copies = [
+        pltpu.make_async_copy(
+            grid_hbm.at[pl.ds(at * part, part)], grid_ref.at[pl.ds(at * part, part)], grid_done.at[at]
+        )
+        for at in range(GRID_PARTS)
+    ]
+    rows_copy = pltpu.make_async_copy(rows_hbm, rows_ref, rows_done)
+    rows_copy.start()
+    for copy in copies:
+        copy.start()
+    rows_copy.wait()
+    found = None
+    for at, copy in enumerate(copies):
+        hots = list_hots(me_ref[0], rows_ref, part, at * part)
+        copy.wait()
+        piece = dot(hots, grid_ref[at * part : (at + 1) * part, :])
+        found = piece if found is None else found + piece
+    rows = found.astype(BF16)
+    lists = [rows[at : at + cap] for at in range(0, 8 * cap, cap)]
+    write_near(near_refs, cap, lists)
+    far_ref[...] = lists[7]
 
 
 def scatter_kernel(skip, me_ref, rows_ref, *refs):
@@ -489,6 +500,7 @@
     src = edge_src.reshape(tiles, 1, STEP)
     dst = edge_dst.reshape(tiles, 1, STEP)
     smem = pl.BlockSpec(memory_space=pltpu.SMEM)
+    hbm = pl.BlockSpec(memory_space=pltpu.HBM)
     params = pltpu.CompilerParams(vmem_limit_bytes=VMEM_BYTES)
     square = (width, width)
 
@@ -515,12 +527,21 @@
     return_specs = [whole((count, width)) for count in (cap, 3 * cap, 2 * cap, 2 * cap, cap)]
     lists = pl.pallas_call(
         gather_kernel,
-        grid=(2,),
-        in_specs=[smem, whole(rows.shape), pl.BlockSpec((grid_part, width), lambda step: (step, 0))],
+        in_specs=[smem, hbm, hbm],
         out_specs=near_specs + [whole((cap, width))],
         out_shape=near_shapes + [jax.ShapeDtypeStruct((cap, width), BF16)],
-        scratch_shapes=[pltpu.VMEM((8 * cap, width), F32)],
-        compiler_params=params,
+        scratch_shapes=[
+            pltpu.VMEM(rows.shape, jnp.int32),
+            pltpu.VMEM(grid_latent.shape, BF16),
+            pltpu.SemaphoreType.DMA,
+            pltpu.SemaphoreType.DMA((GRID_PARTS,)),
+        ],
+        compiler_params=pltpu.CompilerParams(vmem_limit_bytes=GATHER_BYTES),
+        cost_estimate=pl.CostEstimate(
+            flops=40 * 16 * cap * grid_count * width,
+            bytes_accessed=2 * grid_count * width,
+            transcendentals=0,
+        ),
         name="gather_lists",
     )(me, rows, grid_latent)
 
@@ -656,26 +677,27 @@
     node_pieces = next_sum(peers, 1, node_next, node_kept)
     swapped = send(returns[1], by_xor(peers, 1))
     slot_pieces = next_sum(peers, 2, slot_next, slot_kept)
-    node_pieces, edge_next, edge_kept, swapped, slot_next = lax.optimization_barrier(
-        (node_pieces, edge_next, edge_kept, swapped, slot_next)
+    node_pieces, edge_next, edge_kept, swapped, across = lax.optimization_barrier(
+        (node_pieces, edge_next, edge_kept, swapped, returns[4])
     )
     node_pieces = halve_sum(peers, node_pieces)
+    across = send(across, across_chips(peers))
     to_after = jnp.concatenate([returns[2], swapped[cap : 2 * cap]], axis=0)
     to_before = jnp.concatenate([returns[3], swapped[2 * cap :]], axis=0)
-    near = [
-        send(to_after, by_shift(peers, 2)),
-        send(to_before, by_shift(peers, -2)),
-        send(returns[4], across_chips(peers)),
-    ]
-    (slot_pieces, edge_next, edge_kept, near, node_pieces) = lax.optimization_barrier(
-        (slot_pieces, edge_next, edge_kept, near, node_pieces)
+    (slot_pieces, edge_next, edge_kept, across, node_pieces, to_after, to_before) = lax.optimization_barrier(
+        (slot_pieces, edge_next, edge_kept, across, node_pieces, to_after, to_before)
     )
+    edge_pieces = next_sum(peers, 2, edge_next, edge_kept)
+    slot_half = halve_sum(peers, slot_pieces)
     node_terms = rest_terms(peers, node_pieces)
-    edge_pieces = next_sum(peers, 2, edge_next, edge_kept)
-    slot_terms = last_terms(peers, slot_pieces)
+    (slot_half, edge_pieces, node_terms, to_after, to_before) = lax.optimization_barrier(
+        (slot_half, edge_pieces, node_terms, to_after, to_before)
+    )
+    slot_terms = rest_terms(peers, slot_half)
     edge_terms = last_terms(peers, edge_pieces)
+    bundles = [send(to_after, by_shift(peers, 2)), send(to_before, by_shift(peers, -2))]
     node_terms, slot_terms = lax.optimization_barrier((node_terms, slot_terms))
-    returned = [returns[0], swapped, *near]
+    returned = [returns[0], swapped, *bundles, across]
     node_rows = w_node_in.shape[0] // peers
     out_rows = w_edge_out.shape[0] // peers
     grid_grad = pl.pallas_call(
@@ -683,12 +705,13 @@
         grid=(2,),
         in_specs=[smem, whole(rows.shape)]
         + return_specs
-        + [whole((out_rows + cap, width))] * upper,
+        + [whole((out_rows + cap, width))] * (upper // 2),
         out_specs=pl.BlockSpec((grid_part, width), lambda step: (step, 0)),
         out_shape=jax.ShapeDtypeStruct((grid_count, width), BF16),
         compiler_params=params,
         name="scatter_lists",
     )(me, rows, *returned, *slot_terms)
+    edge_terms, grid_grad = lax.optimization_barrier((edge_terms, grid_grad))
     return (
         grid_grad,
         edge_grad,

time: 104 us -> 102 us (0.981); the launches traced: 103 us -> 102 us
  Pallas kernels: 22.1 us -> 38.4 us
  waiting for transfers between devices: 31.1 us -> 21.8 us
  local copies, waits for them, and re-layouts: 6.06 us -> 0.18 us
  starting transfers between devices: 39.4 us -> 35.9 us
  other arithmetic: 3.01 us -> 4.49 us
    ppermute x30 -> x29, waiting for transfers between devices: 31.1 us -> 21.8 us  [send(): return lax.ppermute(values, 'lon', perm)]
    pallas_call x1, Pallas kernels: 8.51 us -> 16.7 us  [on_device(): pl.pallas_call(functools.partial(backward_kernel, peers), grid=(tiles,),...]
    unnamed x24, local copies, waits for them, and re-layouts: 5.97 us -> 0.07 us
    pallas_call x1, Pallas kernels: 6.05 us -> 11.9 us  [on_device(): pl.pallas_call(functools.partial(forward_kernel, peers), grid=(tiles,), i...]
    ppermute x30 -> x29, starting transfers between devices: 39.4 us -> 35.9 us  [send(): return lax.ppermute(values, 'lon', perm)]
    pallas_call x1, Pallas kernels: 1.37 us -> 3.6 us  [on_device(): pl.pallas_call(gather_kernel, in_specs=[smem, hbm, hbm], out_specs=near_s...]
    add x3 -> x4, other arithmetic: 2.07 us -> 2.67 us  [total_of(): total = total + term[start:stop].astype(F32)]
  transfers between devices with their start and end apart: 30 -> 29, of which waited for: 12 -> 9; matrix products, arithmetic and copies ran while one was open for 2% -> 4% of each run, Pallas kernels for 14% -> 22%
where the time goes in v9:
time: 102 us
  Pallas kernels  38.4 us (38%)
  starting transfers between devices  35.9 us (35%)
  waiting for transfers between devices  21.8 us (21%)
  other arithmetic  4.49 us (4%)
  between operations  1.7 us (2%)
    ppermute x29, starting transfers between devices, send(): return lax.ppermute(values, 'lon', perm)  35.9 us
    ppermute x29, waiting for transfers between devices, send(): return lax.ppermute(values, 'lon', perm)  21.8 us
    pallas_call x1, Pallas kernels, on_device(): pl.pallas_call(functools.partial(backward_kernel, peers), grid=(tiles,),...  16.7 us
    pallas_call x1, Pallas kernels, on_device(): pl.pallas_call(functools.partial(forward_kernel, peers), grid=(tiles,), i...  11.9 us
    pallas_call x1, Pallas kernels, on_device(): pl.pallas_call(gather_kernel, in_specs=[smem, hbm, hbm], out_specs=near_s...  3.6 us
    pallas_call x1, Pallas kernels, on_device(): pl.pallas_call(local_kernel, grid=(tiles,), in_specs=[index_tile, tile_of...  3.44 us
    pallas_call x1, Pallas kernels, on_device(): pl.pallas_call(functools.partial(scatter_kernel, out_rows), grid=(2,), in...  2.69 us
    add x4, other arithmetic, total_of(): total = total + term[start:stop].astype(F32)  2.67 us
  transfers between devices with their start and end apart: 29, of which 9 were waited for; matrix products, arithmetic and copies ran while one was open for 4% of the time, Pallas kernels for 22%

profile of v9, /device:TPU:0, one launch (start us, length us, event | category | flops | bytes accessed | tf_op | source)
XLA Modules:
  0.0 102.4 jit_solution(17494923691293966438)
XLA Ops:
  0.7 3.6 %gather_lists.1 = (bf16[48,512]{1,0:T(8,128)(2,1)}, bf16[48,512]{1,0:T(8,128)(2,1)}, bf16[96,512]{1,0:T(8,128)(2,1)}, bf16[96,512]{1,0:T(8,128)(2,1)}, bf16[48,512]{1,0:T(8,128)(2,1)}, /*index=5*/bf16[48,512]{1,0:T(8,128)(2,1)}) custom-call(s32[1]{0:T(128)} %bitcast.me_ref, s32[16,48]{1,0:T(8,128)} %bitcast.38, bf16[2048,512]{1,0:T(8,128)(2,1)} %grid_hbm.1), custom_call_target="tpu_custom_call" | custom-call | flops 32212254720 | bytes 2097152 | tf_op jit(solution)/shard_map/gather_lists/pallas_call | solution.py:528
  4.3 5.1 %collective-permute-start.2 = (bf16[48,512]{1,0:T(8,128)(2,1)}, bf16[48,512]{1,0:T(8,128)(2,1)S(1)}, u32[]{:S(2)}, u32[]{:S(2)}) collective-permute-start(bf16[48,512]{1,0:T(8,128)(2,1)} %get-tuple-element.81), channel_id=1, source_target_pairs={{0,12},{1,13},{2,14},{3,15},{4,8},{5,9},{6,10},{7,11},{8,4},{9,5},... | collective-permute-start | bytes 147464 | tf_op jit(solution)/shard_map/ppermute | solution.py:393
  10.0 2.3 %collective-permute-start.7 = (bf16[48,512]{1,0:T(8,128)(2,1)}, bf16[48,512]{1,0:T(8,128)(2,1)S(1)}, u32[]{:S(2)}, u32[]{:S(2)}) collective-permute-start(bf16[48,512]{1,0:T(8,128)(2,1)} %get-tuple-element.87), channel_id=1, source_target_pairs={{0,13},{1,4},{2,15},{3,6},{4,1},{5,8},{6,3},{7,10},{8,5},{9,12},{1... | collective-permute-start | bytes 147464 | tf_op jit(solution)/shard_map/ppermute | solution.py:393
  12.4 1.5 %collective-permute-start.5 = (bf16[96,512]{1,0:T(8,128)(2,1)}, bf16[96,512]{1,0:T(8,128)(2,1)S(1)}, u32[]{:S(2)}, u32[]{:S(2)}) collective-permute-start(bf16[96,512]{1,0:T(8,128)(2,1)} %get-tuple-element.85), channel_id=1, source_target_pairs={{0,2},{1,3},{2,4},{3,5},{4,6},{5,7},{6,8},{7,9},{8,10},{9,11},{10,... | collective-permute-start | bytes 294920 | tf_op jit(solution)/shard_map/ppermute | solution.py:393
  13.9 3.2 %collective-permute-start.6 = (bf16[96,512]{1,0:T(8,128)(2,1)}, bf16[96,512]{1,0:T(8,128)(2,1)S(1)}, u32[]{:S(2)}, u32[]{:S(2)}) collective-permute-start(bf16[96,512]{1,0:T(8,128)(2,1)} %get-tuple-element.86), channel_id=1, source_target_pairs={{0,14},{1,15},{2,0},{3,1},{4,2},{5,3},{6,4},{7,5},{8,6},{9,7},{10,... | collective-permute-start | bytes 294920 | tf_op jit(solution)/shard_map/ppermute | solution.py:393
  18.2 3.4 %edge_local.1.local_ref = bf16[3072,512]{1,0:T(8,128)(2,1)S(1)} custom-call(s32[3,1,1024]{2,1,0:T(1,128)S(1)} %bitcast.33, bf16[3072,512]{1,0:T(8,128)(2,1)S(1)} %copy-done.1, bf16[256,512]{1,0:T(8,128)(2,1)S(1)} %copy-done.2, bf16[1536,512]{1,0:T(8,128)(2,1)S(1)} %copy-done, bf16[1536,512]{1,0:T(8,128)(2,1)S(1)} %copy-done), custom_call_target="tpu_custom_call" | custom-call | flops 2415919104 | bytes 6291456 | tf_op jit(solution)/shard_map/edge_local/pallas_call | solution.py:554
  21.7 3.7 %collective-permute-done.3.refs_9_ = bf16[192,512]{1,0:T(8,128)(2,1)S(1)} collective-permute-done((bf16[192,512]{1,0:T(8,128)(2,1)S(1)}, bf16[192,512]{1,0:T(8,128)(2,1)S(1)}, u32[]{:S(2)}, u32[]{:S(2)}) %collective-permute-start.3) | collective-permute-done | bytes 196640 | tf_op jit(solution)/shard_map/ppermute | solution.py:393
  27.4 11.9 %forward.1 = (bf16[768,512]{1,0:T(8,128)(2,1)S(1)}, bf16[3072,512]{1,0:T(8,128)(2,1)S(1)}, bf16[3072,512]{1,0:T(8,128)(2,1)S(1)}, bf16[3072,512]{1,0:T(8,128)(2,...) custom-call(s32[1]{0:T(128)} %bitcast.me_ref, ...), custom_call_target="tpu_custom_call" | custom-call | tf_op jit(solution)/shard_map/forward/pallas_call | solution.py:574
  39.7 16.7 %backward.1 = (bf16[3072,512]{1,0:T(8,128)(2,1)}, bf16[256,512]{1,0:T(8,128)(2,1)}, bf16[2,320,512]{2,1,0:T(8,128)(2,1)S(1)}, bf16[2,320,512]{2,1,0:T(8,128)(2,1...) custom-call(s32[1]{0:T(128)} %bitcast.me_ref, ...), custom_call_target="tpu_custom_call" | custom-call | flops 10468982784 | bytes 15728640 | tf_op jit(solution)/shard_map/backward/pallas_call | solution.py:623
  56.4 1.3 %collective-permute-done.12 = bf16[2,384,512]{2,1,0:T(8,128)(2,1)S(1)} collective-permute-done((bf16[2,384,512]{2,1,0:T(8,128)(2,1)S(1)}, bf16[2,384,512]{2,1,0:T(8,128)(2,1)S(1)}, u32[]{:S(2)}, u32[]{:S(2)}) %collective-permute-start.12) | collective-permute-done | bytes 786464 | tf_op jit(solution)/shard_map/ppermute | solution.py:393
  59.0 1.6 %collective-permute-done.15 = bf16[384,512]{1,0:T(8,128)(2,1)S(1)} collective-permute-done((bf16[384,512]{1,0:T(8,128)(2,1)S(1)}, bf16[384,512]{1,0:T(8,128)(2,1)S(1)}, u32[]{:S(2)}, u32[]{:S(2)}) %collective-permute-start.15) | collective-permute-done | bytes 393248 | tf_op jit(solution)/shard_map/ppermute | solution.py:393
  60.9 1.8 %collective-permute-start.14 = (bf16[320,512]{1,0:T(8,128)(2,1)S(1)}, bf16[320,512]{1,0:T(8,128)(2,1)S(1)}, u32[]{:S(2)}, u32[]{:S(2)}) collective-permute-start(bf16[320,512]{1,0:T(8,128)(2,1)S(1)} %fusion.7), channel_id=1, source_target_pairs={{0,2},{1,3},{2,0},{3,1},{4,6},{5,7},{6,4},{7,5},{8,10},{9,11},{10,... | collective-permute-start | bytes 983048 | tf_op jit(solution)/shard_map/ppermute | solution.py:393
  62.9 1.6 %collective-permute-start.18 = (bf16[48,512]{1,0:T(8,128)(2,1)S(1)}, bf16[48,512]{1,0:T(8,128)(2,1)S(1)}, u32[]{:S(2)}, u32[]{:S(2)}) collective-permute-start(bf16[48,512]{1,0:T(8,128)(2,1)S(1)} %get-tuple-element.125), channel_id=1, source_target_pairs={{0,13},{1,4},{2,15},{3,6},{4,1},{5,8},{6,3},{7,10},{8,5},{9,12},{1... | collective-permute-start | bytes 147464 | tf_op jit(solution)/shard_map/ppermute | solution.py:393
  64.6 6.1 %collective-permute-done.14 = bf16[320,512]{1,0:T(8,128)(2,1)S(1)} collective-permute-done((bf16[320,512]{1,0:T(8,128)(2,1)S(1)}, bf16[320,512]{1,0:T(8,128)(2,1)S(1)}, u32[]{:S(2)}, u32[]{:S(2)}) %collective-permute-start.14) | collective-permute-done | bytes 327712 | tf_op jit(solution)/shard_map/ppermute | solution.py:393
  71.2 1.7 %collective-permute-start.21 = (bf16[384,512]{1,0:T(8,128)(2,1)S(1)}, bf16[384,512]{1,0:T(8,128)(2,1)S(1)}, u32[]{:S(2)}, u32[]{:S(2)}) collective-permute-start(bf16[384,512]{1,0:T(8,128)(2,1)S(1)} %get-tuple-element.132), channel_id=1, source_target_pairs={{0,2},{1,3},{2,0},{3,1},{4,6},{5,7},{6,4},{7,5},{8,10},{9,11},{10,... | collective-permute-start | bytes 1179656 | tf_op jit(solution)/shard_map/ppermute | solution.py:393
  72.9 1.8 %collective-permute-start.22 = (bf16[96,512]{1,0:T(8,128)(2,1)S(1)}, bf16[96,512]{1,0:T(8,128)(2,1)S(1)}, u32[]{:S(2)}, u32[]{:S(2)}) collective-permute-start(bf16[96,512]{1,0:T(8,128)(2,1)S(1)} %get-tuple-element.167), channel_id=1, source_target_pairs={{0,8},{1,9},{2,10},{3,11},{4,12},{5,13},{6,14},{7,15},{8,0},{9,1},... | collective-permute-start | bytes 294920 | tf_op jit(solution)/shard_map/ppermute | solution.py:393
  74.6 3.0 %collective-permute-done.20 = bf16[160,512]{1,0:T(8,128)(2,1)S(1)} collective-permute-done((bf16[160,512]{1,0:T(8,128)(2,1)S(1)}, bf16[160,512]{1,0:T(8,128)(2,1)S(1)}, u32[]{:S(2)}, u32[]{:S(2)}) %collective-permute-start.20) | collective-permute-done | bytes 163872 | tf_op jit(solution)/shard_map/ppermute | solution.py:393
  77.7 3.8 %collective-permute-done.21 = bf16[384,512]{1,0:T(8,128)(2,1)S(1)} collective-permute-done((bf16[384,512]{1,0:T(8,128)(2,1)S(1)}, bf16[384,512]{1,0:T(8,128)(2,1)S(1)}, u32[]{:S(2)}, u32[]{:S(2)}) %collective-permute-start.21) | collective-permute-done | bytes 393248 | tf_op jit(solution)/shard_map/ppermute | solution.py:393
  81.6 3.4 %collective-permute-start.28 = (bf16[80,512]{1,0:T(8,128)(2,1)S(1)}, bf16[80,512]{1,0:T(8,128)(2,1)S(1)}, u32[]{:S(2)}, u32[]{:S(2)}) collective-permute-start(bf16[80,512]{1,0:T(8,128)(2,1)S(1)} %get-tuple-element.169), channel_id=1, source_target_pairs={{0,8},{1,9},{2,10},{3,11},{4,12},{5,13},{6,14},{7,15},{8,0},{9,1},... | collective-permute-start | bytes 245768 | tf_op jit(solution)/shard_map/ppermute | solution.py:393
  85.8 1.1 %collective-permute-start.24 = (bf16[96,512]{1,0:T(8,128)(2,1)S(1)}, bf16[96,512]{1,0:T(8,128)(2,1)S(1)}, u32[]{:S(2)}, u32[]{:S(2)}) collective-permute-start(bf16[96,512]{1,0:T(8,128)(2,1)S(1)} %get-tuple-element.160), channel_id=1, source_target_pairs={{0,8},{1,9},{2,10},{3,11},{4,12},{5,13},{6,14},{7,15},{8,0},{9,1},... | collective-permute-start | bytes 294920 | tf_op jit(solution)/shard_map/ppermute | solution.py:393
  86.9 2.6 %collective-permute-start.23 = (bf16[96,512]{1,0:T(8,128)(2,1)S(1)}, bf16[96,512]{1,0:T(8,128)(2,1)S(1)}, u32[]{:S(2)}, u32[]{:S(2)}) collective-permute-start(bf16[96,512]{1,0:T(8,128)(2,1)S(1)} %get-tuple-element.161), channel_id=1, source_target_pairs={{0,4},{1,5},{2,6},{3,7},{4,0},{5,1},{6,2},{7,3},{8,12},{9,13},{10,... | collective-permute-start | bytes 294920 | tf_op jit(solution)/shard_map/ppermute | solution.py:393
  90.3 1.8 %collective-permute-done.28.refs_6_ = bf16[80,512]{1,0:T(8,128)(2,1)S(1)} collective-permute-done((bf16[80,512]{1,0:T(8,128)(2,1)S(1)}, bf16[80,512]{1,0:T(8,128)(2,1)S(1)}, u32[]{:S(2)}, u32[]{:S(2)}) %collective-permute-start.28) | collective-permute-done | bytes 81952 | tf_op jit(solution)/shard_map/ppermute | solution.py:393
  92.1 4.6 %collective-permute-start.27 = (bf16[96,512]{1,0:T(8,128)(2,1)S(1)}, bf16[96,512]{1,0:T(8,128)(2,1)S(1)}, u32[]{:S(2)}, u32[]{:S(2)}) collective-permute-start(bf16[96,512]{1,0:T(8,128)(2,1)S(1)} %get-tuple-element.139), channel_id=1, source_target_pairs={{0,14},{1,15},{2,0},{3,1},{4,2},{5,3},{6,4},{7,5},{8,6},{9,7},{10,... | collective-permute-start | bytes 294920 | tf_op jit(solution)/shard_map/ppermute | solution.py:393
  99.0 2.7 %scatter_lists.1 = bf16[2048,512]{1,0:T(8,128)(2,1)} custom-call(s32[1]{0:T(128)} %bitcast.me_ref, s32[16,48]{1,0:T(8,128)S(1)} %bitcast.39, bf16[48,512]{1,0:T(8,128)(2,1)S(1)} %get-tuple-element.137.refs_0_, bf16[144,512]{1,0:T(8,128)(2,1)S(1)} %collective-permute-done.17.refs_1_, bf16[96,512]{1,0:T(8,128)(2,1)S(1)} %collective-permute-done.26.refs_2_, ...), custom_call_target="tpu_custom_call" | custom-call | tf_op jit(solution)/shard_map/scatter_lists/pallas_call | solution.py:703
  (83 shorter events, 10.4 us)
Async XLA Ops:
  4.3 9.6 %collective-permute-start.2 = (bf16[48,512]{1,0:T(8,128)(2,1)}, bf16[48,512]{1,0:T(8,128)(2,1)S(1)}, u32[]{:S(2)}, u32[]{:S(2)}) collective-permute-start(bf16[48,512]{1,0:T(8,128)(2,1)} %get-tuple-element.81), channel_id=1, source_target_pairs={{0,12},{1,13},{2,14},{3,15},{4,8},{5,9},{6,10},{7,11},{8,4},{9,5},... | collective-permute-start | bytes 147464 | tf_op jit(solution)/shard_map/ppermute | solution.py:393
  9.4 7.7 %collective-permute-start.1 = (bf16[48,512]{1,0:T(8,128)(2,1)}, bf16[48,512]{1,0:T(8,128)(2,1)S(1)}, u32[]{:S(2)}, u32[]{:S(2)}) collective-permute-start(bf16[48,512]{1,0:T(8,128)(2,1)} %get-tuple-element.81), channel_id=1, source_target_pairs={{0,8},{1,9},{2,10},{3,11},{4,12},{5,13},{6,14},{7,15},{8,0},{9,1},... | collective-permute-start | bytes 147464 | tf_op jit(solution)/shard_map/ppermute | solution.py:393
  9.4 7.7 %collective-permute-start = (bf16[48,512]{1,0:T(8,128)(2,1)}, bf16[48,512]{1,0:T(8,128)(2,1)S(1)}, u32[]{:S(2)}, u32[]{:S(2)}) collective-permute-start(bf16[48,512]{1,0:T(8,128)(2,1)} %get-tuple-element.81), channel_id=1, source_target_pairs={{0,4},{1,5},{2,6},{3,7},{4,0},{5,1},{6,2},{7,3},{8,12},{9,13},{10,... | collective-permute-start | bytes 147464 | tf_op jit(solution)/shard_map/ppermute | solution.py:393
  10.0 11.6 %collective-permute-start.7 = (bf16[48,512]{1,0:T(8,128)(2,1)}, bf16[48,512]{1,0:T(8,128)(2,1)S(1)}, u32[]{:S(2)}, u32[]{:S(2)}) collective-permute-start(bf16[48,512]{1,0:T(8,128)(2,1)} %get-tuple-element.87), channel_id=1, source_target_pairs={{0,13},{1,4},{2,15},{3,6},{4,1},{5,8},{6,3},{7,10},{8,5},{9,12},{1... | collective-permute-start | bytes 147464 | tf_op jit(solution)/shard_map/ppermute | solution.py:393
  12.4 9.3 %collective-permute-start.5 = (bf16[96,512]{1,0:T(8,128)(2,1)}, bf16[96,512]{1,0:T(8,128)(2,1)S(1)}, u32[]{:S(2)}, u32[]{:S(2)}) collective-permute-start(bf16[96,512]{1,0:T(8,128)(2,1)} %get-tuple-element.85), channel_id=1, source_target_pairs={{0,2},{1,3},{2,4},{3,5},{4,6},{5,7},{6,8},{7,9},{8,10},{9,11},{10,... | collective-permute-start | bytes 294920 | tf_op jit(solution)/shard_map/ppermute | solution.py:393
  13.9 7.8 %collective-permute-start.6 = (bf16[96,512]{1,0:T(8,128)(2,1)}, bf16[96,512]{1,0:T(8,128)(2,1)S(1)}, u32[]{:S(2)}, u32[]{:S(2)}) collective-permute-start(bf16[96,512]{1,0:T(8,128)(2,1)} %get-tuple-element.86), channel_id=1, source_target_pairs={{0,14},{1,15},{2,0},{3,1},{4,2},{5,3},{6,4},{7,5},{8,6},{9,7},{10,... | collective-permute-start | bytes 294920 | tf_op jit(solution)/shard_map/ppermute | solution.py:393
  18.0 3.7 %collective-permute-start.4 = (bf16[192,512]{1,0:T(8,128)(2,1)S(1)}, bf16[192,512]{1,0:T(8,128)(2,1)S(1)}, u32[]{:S(2)}, u32[]{:S(2)}) collective-permute-start(bf16[192,512]{1,0:T(8,128)(2,1)S(1)} %pad_maximum_fusion.refs_7_), channel_id=1, source_target_pairs={{0,1},{1,0},{2,3},{3,2},{4,5},{5,4},{6,7},{7,6},{8,9},{9,8},{10,11... | collective-permute-start | bytes 589832 | tf_op jit(solution)/shard_map/ppermute | solution.py:393
  18.1 7.3 %collective-permute-start.3 = (bf16[192,512]{1,0:T(8,128)(2,1)S(1)}, bf16[192,512]{1,0:T(8,128)(2,1)S(1)}, u32[]{:S(2)}, u32[]{:S(2)}) collective-permute-start(bf16[192,512]{1,0:T(8,128)(2,1)S(1)} %pad_maximum_fusion.refs_7_), channel_id=1, source_target_pairs={{0,2},{1,3},{2,0},{3,1},{4,6},{5,7},{6,4},{7,5},{8,10},{9,11},{10,... | collective-permute-start | bytes 589832 | tf_op jit(solution)/shard_map/ppermute | solution.py:393
  39.3 18.4 %collective-permute-start.12 = (bf16[2,384,512]{2,1,0:T(8,128)(2,1)S(1)}, bf16[2,384,512]{2,1,0:T(8,128)(2,1)S(1)}, u32[]{:S(2)}, u32[]{:S(2)}) collective-permute-start(bf16[2,384,512]{2,1,0:T(8,128)(2,1)S(1)} %get-tuple-element.98), channel_id=1, source_target_pairs={{0,2},{1,3},{2,0},{3,1},{4,6},{5,7},{6,4},{7,5},{8,10},{9,11},{10,... | collective-permute-start | bytes 2359304 | tf_op jit(solution)/shard_map/ppermute | solution.py:393
  57.9 2.8 %collective-permute-start.13 = (bf16[2,320,512]{2,1,0:T(8,128)(2,1)S(1)}, bf16[2,320,512]{2,1,0:T(8,128)(2,1)S(1)}, u32[]{:S(2)}, u32[]{:S(2)}) collective-permute-start(bf16[2,320,512]{2,1,0:T(8,128)(2,1)S(1)} %get-tuple-element.116), channel_id=1, source_target_pairs={{0,1},{1,0},{2,3},{3,2},{4,5},{5,4},{6,7},{7,6},{8,9},{9,8},{10,11... | collective-permute-start | bytes 1966088 | tf_op jit(solution)/shard_map/ppermute | solution.py:393
  58.5 4.2 %collective-permute-start.16 = (bf16[2,384,512]{2,1,0:T(8,128)(2,1)S(1)}, bf16[2,384,512]{2,1,0:T(8,128)(2,1)S(1)}, u32[]{:S(2)}, u32[]{:S(2)}) collective-permute-start(bf16[2,384,512]{2,1,0:T(8,128)(2,1)S(1)} %get-tuple-element.120), channel_id=1, source_target_pairs={{0,1},{1,0},{2,3},{3,2},{4,5},{5,4},{6,7},{7,6},{8,9},{9,8},{10,11... | collective-permute-start | bytes 2359304 | tf_op jit(solution)/shard_map/ppermute | solution.py:393
  58.6 4.3 %collective-permute-start.17 = (bf16[144,512]{1,0:T(8,128)(2,1)S(1)}, bf16[144,512]{1,0:T(8,128)(2,1)S(1)}, u32[]{:S(2)}, u32[]{:S(2)}) collective-permute-start(bf16[144,512]{1,0:T(8,128)(2,1)S(1)} %get-tuple-element.121), channel_id=1, source_target_pairs={{0,1},{1,0},{2,3},{3,2},{4,5},{5,4},{6,7},{7,6},{8,9},{9,8},{10,11... | collective-permute-start | bytes 442376 | tf_op jit(solution)/shard_map/ppermute | solution.py:393
  60.9 9.8 %collective-permute-start.14 = (bf16[320,512]{1,0:T(8,128)(2,1)S(1)}, bf16[320,512]{1,0:T(8,128)(2,1)S(1)}, u32[]{:S(2)}, u32[]{:S(2)}) collective-permute-start(bf16[320,512]{1,0:T(8,128)(2,1)S(1)} %fusion.7), channel_id=1, source_target_pairs={{0,2},{1,3},{2,0},{3,1},{4,6},{5,7},{6,4},{7,5},{8,10},{9,11},{10,... | collective-permute-start | bytes 983048 | tf_op jit(solution)/shard_map/ppermute | solution.py:393
  62.9 8.0 %collective-permute-start.18 = (bf16[48,512]{1,0:T(8,128)(2,1)S(1)}, bf16[48,512]{1,0:T(8,128)(2,1)S(1)}, u32[]{:S(2)}, u32[]{:S(2)}) collective-permute-start(bf16[48,512]{1,0:T(8,128)(2,1)S(1)} %get-tuple-element.125), channel_id=1, source_target_pairs={{0,13},{1,4},{2,15},{3,6},{4,1},{5,8},{6,3},{7,10},{8,5},{9,12},{1... | collective-permute-start | bytes 147464 | tf_op jit(solution)/shard_map/ppermute | solution.py:393
  64.5 6.3 %collective-permute-start.19 = (bf16[192,512]{1,0:T(8,128)(2,1)S(1)}, bf16[192,512]{1,0:T(8,128)(2,1)S(1)}, u32[]{:S(2)}, u32[]{:S(2)}) collective-permute-start(bf16[192,512]{1,0:T(8,128)(2,1)S(1)} %bitcast.42), channel_id=1, source_target_pairs={{0,4},{1,5},{2,6},{3,7},{4,0},{5,1},{6,2},{7,3},{8,12},{9,13},{10,... | collective-permute-start | bytes 589832 | tf_op jit(solution)/shard_map/ppermute | solution.py:393
  71.0 6.6 %collective-permute-start.20 = (bf16[160,512]{1,0:T(8,128)(2,1)S(1)}, bf16[160,512]{1,0:T(8,128)(2,1)S(1)}, u32[]{:S(2)}, u32[]{:S(2)}) collective-permute-start(bf16[160,512]{1,0:T(8,128)(2,1)S(1)} %bitcast.43), channel_id=1, source_target_pairs={{0,4},{1,5},{2,6},{3,7},{4,0},{5,1},{6,2},{7,3},{8,12},{9,13},{10,... | collective-permute-start | bytes 491528 | tf_op jit(solution)/shard_map/ppermute | solution.py:393
  71.2 10.3 %collective-permute-start.21 = (bf16[384,512]{1,0:T(8,128)(2,1)S(1)}, bf16[384,512]{1,0:T(8,128)(2,1)S(1)}, u32[]{:S(2)}, u32[]{:S(2)}) collective-permute-start(bf16[384,512]{1,0:T(8,128)(2,1)S(1)} %get-tuple-element.132), channel_id=1, source_target_pairs={{0,2},{1,3},{2,0},{3,1},{4,6},{5,7},{6,4},{7,5},{8,10},{9,11},{10,... | collective-permute-start | bytes 1179656 | tf_op jit(solution)/shard_map/ppermute | solution.py:393
  72.9 8.7 %collective-permute-start.22 = (bf16[96,512]{1,0:T(8,128)(2,1)S(1)}, bf16[96,512]{1,0:T(8,128)(2,1)S(1)}, u32[]{:S(2)}, u32[]{:S(2)}) collective-permute-start(bf16[96,512]{1,0:T(8,128)(2,1)S(1)} %get-tuple-element.167), channel_id=1, source_target_pairs={{0,8},{1,9},{2,10},{3,11},{4,12},{5,13},{6,14},{7,15},{8,0},{9,1},... | collective-permute-start | bytes 294920 | tf_op jit(solution)/shard_map/ppermute | solution.py:393
  81.6 10.6 %collective-permute-start.28 = (bf16[80,512]{1,0:T(8,128)(2,1)S(1)}, bf16[80,512]{1,0:T(8,128)(2,1)S(1)}, u32[]{:S(2)}, u32[]{:S(2)}) collective-permute-start(bf16[80,512]{1,0:T(8,128)(2,1)S(1)} %get-tuple-element.169), channel_id=1, source_target_pairs={{0,8},{1,9},{2,10},{3,11},{4,12},{5,13},{6,14},{7,15},{8,0},{9,1},... | collective-permute-start | bytes 245768 | tf_op jit(solution)/shard_map/ppermute | solution.py:393
  85.0 16.7 %collective-permute-start.25 = (bf16[96,512]{1,0:T(8,128)(2,1)S(1)}, bf16[96,512]{1,0:T(8,128)(2,1)S(1)}, u32[]{:S(2)}, u32[]{:S(2)}) collective-permute-start(bf16[96,512]{1,0:T(8,128)(2,1)S(1)} %get-tuple-element.159), channel_id=1, source_target_pairs={{0,12},{1,13},{2,14},{3,15},{4,8},{5,9},{6,10},{7,11},{8,4},{9,5},... | collective-permute-start | bytes 294920 | tf_op jit(solution)/shard_map/ppermute | solution.py:393
  85.8 15.9 %collective-permute-start.24 = (bf16[96,512]{1,0:T(8,128)(2,1)S(1)}, bf16[96,512]{1,0:T(8,128)(2,1)S(1)}, u32[]{:S(2)}, u32[]{:S(2)}) collective-permute-start(bf16[96,512]{1,0:T(8,128)(2,1)S(1)} %get-tuple-element.160), channel_id=1, source_target_pairs={{0,8},{1,9},{2,10},{3,11},{4,12},{5,13},{6,14},{7,15},{8,0},{9,1},... | collective-permute-start | bytes 294920 | tf_op jit(solution)/shard_map/ppermute | solution.py:393
  86.9 14.8 %collective-permute-start.23 = (bf16[96,512]{1,0:T(8,128)(2,1)S(1)}, bf16[96,512]{1,0:T(8,128)(2,1)S(1)}, u32[]{:S(2)}, u32[]{:S(2)}) collective-permute-start(bf16[96,512]{1,0:T(8,128)(2,1)S(1)} %get-tuple-element.161), channel_id=1, source_target_pairs={{0,4},{1,5},{2,6},{3,7},{4,0},{5,1},{6,2},{7,3},{8,12},{9,13},{10,... | collective-permute-start | bytes 294920 | tf_op jit(solution)/shard_map/ppermute | solution.py:393
  89.4 9.3 %collective-permute-start.26 = (bf16[96,512]{1,0:T(8,128)(2,1)S(1)}, bf16[96,512]{1,0:T(8,128)(2,1)S(1)}, u32[]{:S(2)}, u32[]{:S(2)}) collective-permute-start(bf16[96,512]{1,0:T(8,128)(2,1)S(1)} %get-tuple-element.138), channel_id=1, source_target_pairs={{0,2},{1,3},{2,4},{3,5},{4,6},{5,7},{6,8},{7,9},{8,10},{9,11},{10,... | collective-permute-start | bytes 294920 | tf_op jit(solution)/shard_map/ppermute | solution.py:393
  92.1 6.9 %collective-permute-start.27 = (bf16[96,512]{1,0:T(8,128)(2,1)S(1)}, bf16[96,512]{1,0:T(8,128)(2,1)S(1)}, u32[]{:S(2)}, u32[]{:S(2)}) collective-permute-start(bf16[96,512]{1,0:T(8,128)(2,1)S(1)} %get-tuple-element.139), channel_id=1, source_target_pairs={{0,14},{1,15},{2,0},{3,1},{4,2},{5,3},{6,4},{7,5},{8,6},{9,7},{10,... | collective-permute-start | bytes 294920 | tf_op jit(solution)/shard_map/ppermute | solution.py:393
  (17 other events, 178.1 us)

commit v10 on v9

--- a/solution.py
+++ b/solution.py
@@ -117,29 +117,6 @@
         core_after[cap:, :],
         from_before[:cap, :],
         core_before[cap:, :],
-        across[...],
-    ]
-
-
-def write_back(refs, cap, lists):
-    mine, swapped, after, before, across = refs
-    mine[...] = lists[0]
-    for place, index in enumerate((1, 3, 5)):
-        swapped[place * cap : (place + 1) * cap, :] = lists[index]
-    after[...] = lists[2]
-    before[...] = lists[4]
-    across[...] = lists[6]
-
-
-def read_back(refs, cap):
-    mine, swapped, from_before, from_after, across = refs
-    return [
-        mine[...],
-        swapped[:cap, :],
-        from_after[:cap, :],
-        from_after[cap:, :],
-        from_before[:cap, :],
-        from_before[cap:, :],
         across[...],
     ]
 
@@ -186,14 +163,14 @@
 
 
 def scatter_kernel(skip, me_ref, rows_ref, *refs):
-    near_refs, far_refs, out_ref = refs[:5], refs[5:-1], refs[-1]
+    near_refs, far_refs, out_ref = refs[:7], refs[7:-1], refs[-1]
     part = out_ref.shape[0]
     cap = rows_ref.shape[1]
     hots = list_hots(me_ref[0], rows_ref, part, pl.program_id(0) * part)
     far = far_refs[0][skip:, :].astype(F32)
     for ref in far_refs[1:]:
         far = far + ref[skip:, :].astype(F32)
-    values = jnp.concatenate(read_back(near_refs, cap) + [far.astype(BF16)], axis=0)
+    values = jnp.concatenate(read_near(near_refs, cap) + [far.astype(BF16)], axis=0)
     out_ref[...] = contract_rows(hots, values).astype(BF16)
 
 
@@ -318,10 +295,10 @@
 def backward_kernel(peers, me_ref, count_ref, src_ref, dst_ref, inverse_ref, *refs):
     (hidden_ref, slope_ref, norm_ref, edge_ref) = refs[:4]
     (d_aggregate_ref, received_ref, mesh_ref, d_mesh_ref) = refs[4:8]
-    (w_sender_ref, w_receiver_ref, w_edge_ref, w_out_ref) = refs[8:12]
-    (edge_grad_ref, mesh_grad_ref, slot_send_ref, slot_keep_ref, edge_send_ref, edge_keep_ref) = refs[12:18]
-    near_refs = refs[18:23]
-    (end_sum, grad_in, grad_out, d_slots) = refs[23:]
+    (w_sender_ref, w_receiver_ref, w_out_ref) = refs[8:11]
+    (d_pre_ref, mesh_grad_ref, slot_send_ref, slot_keep_ref, edge_send_ref, edge_keep_ref) = refs[11:17]
+    near_refs = refs[17:22]
+    (end_sum, grad_in, grad_out, d_slots) = refs[22:]
     step = pl.program_id(0)
     me = me_ref[0]
     slots, width = received_ref.shape
@@ -354,18 +331,12 @@
             d_proj = norm_back(norm_ref[part, :].astype(F32), inverse, upstream).astype(BF16)
             d_projs.append(d_proj)
             d_hiddens.append(contract_cols(d_proj, w_out_ref[...]))
-        for (start, part), d_proj, d_hidden, column, upstream in zip(
-            parts, d_projs, d_hiddens, columns, upstreams
-        ):
+        for (start, part), d_proj, d_hidden, column in zip(parts, d_projs, d_hiddens, columns):
             grad_out[...] += contract_rows(hidden_ref[part, :], d_proj)
             d_pre = (d_hidden * slope_ref[part, :].astype(F32)).astype(BF16)
-            edge_grad_ref[part, :] = (upstream + contract_cols(d_pre, w_edge_ref[...])).astype(BF16)
+            d_pre_ref[part, :] = d_pre
             end_sum[...] += dot(column, d_pre)
             grad_in[:width, :] += contract_rows(edge_ref[part, :], d_pre)
-
-    @pl.when(step * STEP >= count_ref[0] * TILE)
-    def _():
-        edge_grad_ref[...] = jnp.zeros_like(edge_grad_ref)
 
     @pl.when(step == pl.num_programs(0) - 1)
     def _():
@@ -377,7 +348,7 @@
         mesh_grad_ref[...] = (d_mesh_ref[...] + contract_cols(mesh_summed, w_receiver_ref[...])).astype(BF16)
         cap = near_refs[0].shape[0]
         owners = near_peers(me, peers)
-        write_back(
+        write_near(
             near_refs, cap, [d_slots[pl.ds(pl.multiple_of(owner * cap, 16), cap), :] for owner in owners]
         )
         out_share = grad_out.shape[0] // peers
@@ -389,6 +360,21 @@
         )
 
 
+def edges_kernel(count_ref, dst_ref, d_pre_ref, d_aggregate_ref, w_edge_ref, edge_grad_ref):
+    step = pl.program_id(0)
+
+    @pl.when(step * STEP < count_ref[0] * TILE)
+    def _():
+        for start, part in halves_of(d_pre_ref):
+            receivers = live_only(dst_ref[0, :, part], step * STEP + start, count_ref[0] * TILE)
+            upstream = dot(hot_rows(receivers, d_aggregate_ref.shape[0]), d_aggregate_ref[...])
+            edge_grad_ref[part, :] = (upstream + contract_cols(d_pre_ref[part, :], w_edge_ref[...])).astype(BF16)
+
+    @pl.when(step * STEP >= count_ref[0] * TILE)
+    def _():
+        edge_grad_ref[...] = jnp.zeros_like(edge_grad_ref)
+
+
 def send(values, perm):
     return lax.ppermute(values, "lon", perm)
 
@@ -416,10 +402,8 @@
     ]
 
 
-def core_near(peers, near):
-    mine, other, after, before, across = near
-    swap = by_xor(peers, 1)
-    return [mine, send(other, swap), after, before, across, send(after, swap), send(before, swap)]
+def core_bundles(peers, bundles):
+    return [send(bundle, by_xor(peers, 1)) for bundle in bundles]
 
 
 def add(left, right):
@@ -521,10 +505,6 @@
     near_specs = [whole((count, width)) for count in near_rows]
     near_shapes = [jax.ShapeDtypeStruct((count, width), BF16) for count in near_rows]
     core_specs = near_specs + [whole((2 * cap, width))] * 2
-    back_rows = (cap, 3 * cap, cap, cap, cap)
-    back_specs = [whole((count, width)) for count in back_rows]
-    back_shapes = [jax.ShapeDtypeStruct((count, width), BF16) for count in back_rows]
-    return_specs = [whole((count, width)) for count in (cap, 3 * cap, 2 * cap, 2 * cap, cap)]
     lists = pl.pallas_call(
         gather_kernel,
         in_specs=[smem, hbm, hbm],
@@ -567,7 +547,7 @@
         name="edge_local",
     )(receivers, edge_latent, mesh_latent, w_edge_in, w_edge_in)
     far_next, far_core, near, local = lax.optimization_barrier((far_next, far_core, near, local))
-    near = core_near(peers, near)
+    near = [near[0], send(near[1], by_xor(peers, 1)), *near[2:]] + core_bundles(peers, near[2:4])
     far_both = send(far_next, by_xor(peers, 1))
 
     node_shape, node_spec = halves(w_node_in.shape[0] // peers + w_node_out.shape[0] // peers)
@@ -627,15 +607,15 @@
         + [tile_of(width)] * 4
         + [whole((mesh_count, width)), whole((slots, width))]
         + [whole((mesh_count, width))] * 2
-        + [weight(1), weight(2), weight(0), whole(square)],
-        out_specs=[tile_of(width), whole((mesh_count, width))] + slot_spec + edge_spec + back_specs,
+        + [weight(1), weight(2), whole(square)],
+        out_specs=[tile_of(width), whole((mesh_count, width))] + slot_spec + edge_spec + near_specs,
         out_shape=[
             jax.ShapeDtypeStruct((edges, width), BF16),
             jax.ShapeDtypeStruct((mesh_count, width), BF16),
         ]
         + slot_shape
         + edge_shape
-        + back_shapes,
+        + near_shapes,
         scratch_shapes=[
             pltpu.VMEM((slots + mesh_count, width), F32),
             pltpu.VMEM(w_edge_in.shape, F32),
@@ -644,7 +624,7 @@
         ],
         compiler_params=params,
         cost_estimate=pl.CostEstimate(
-            flops=2 * edges * width * (2 * mesh_count + 4 * width + slots),
+            flops=2 * edges * width * (2 * mesh_count + 3 * width + slots),
             bytes_accessed=10 * edges * width,
             transcendentals=0,
         ),
@@ -665,46 +645,51 @@
         d_mesh,
         w_edge_in,
         w_edge_in,
-        w_edge_in,
         w_edge_out,
     )
-    (edge_grad, mesh_grad, slot_send, slot_keep, edge_send, edge_keep), returns = results[:6], results[6:]
-    (node_next, node_kept, slot_send, slot_keep, edge_send, edge_keep, returns) = lax.optimization_barrier(
-        (node_next, node_kept, slot_send, slot_keep, edge_send, edge_keep, returns)
+    (d_pre, mesh_grad, slot_send, slot_keep, edge_send, edge_keep), returns = results[:6], results[6:]
+    (node_next, node_kept, slot_send, slot_keep, edge_send, edge_keep, returns, d_pre) = lax.optimization_barrier(
+        (node_next, node_kept, slot_send, slot_keep, edge_send, edge_keep, returns, d_pre)
     )
     slot_next, slot_kept = first_sum(peers, 1, slot_send, slot_keep)
     edge_next, edge_kept = first_sum(peers, 1, edge_send, edge_keep)
     node_pieces = next_sum(peers, 1, node_next, node_kept)
-    swapped = send(returns[1], by_xor(peers, 1))
+    bundles = [send(returns[2], by_shift(peers, 2)), send(returns[3], by_shift(peers, -2))]
+    other = send(returns[1], by_xor(peers, 1))
+    (slot_next, slot_kept, edge_next, edge_kept, node_pieces, bundles, other, d_pre) = lax.optimization_barrier(
+        (slot_next, slot_kept, edge_next, edge_kept, node_pieces, bundles, other, d_pre)
+    )
     slot_pieces = next_sum(peers, 2, slot_next, slot_kept)
-    node_pieces, edge_next, edge_kept, swapped, across = lax.optimization_barrier(
-        (node_pieces, edge_next, edge_kept, swapped, returns[4])
+    edge_pieces = next_sum(peers, 2, edge_next, edge_kept)
+    node_terms = last_terms(peers, node_pieces)
+    edge_grad = pl.pallas_call(
+        edges_kernel,
+        grid=(tiles,),
+        in_specs=[smem, index_tile, tile_of(width), whole((mesh_count, width)), weight(0)],
+        out_specs=tile_of(width),
+        out_shape=jax.ShapeDtypeStruct((edges, width), BF16),
+        compiler_params=params,
+        cost_estimate=pl.CostEstimate(
+            flops=2 * edges * width * (mesh_count + width), bytes_accessed=4 * edges * width, transcendentals=0
+        ),
+        name="edge_grad",
+    )(tile_count, dst, d_pre, d_aggregate, w_edge_in)
+    (slot_pieces, node_terms, across, bundles, edge_grad) = lax.optimization_barrier(
+        (slot_pieces, node_terms, returns[4], bundles, edge_grad)
     )
-    node_pieces = halve_sum(peers, node_pieces)
-    across = send(across, across_chips(peers))
-    to_after = jnp.concatenate([returns[2], swapped[cap : 2 * cap]], axis=0)
-    to_before = jnp.concatenate([returns[3], swapped[2 * cap :]], axis=0)
-    (slot_pieces, edge_next, edge_kept, across, node_pieces, to_after, to_before) = lax.optimization_barrier(
-        (slot_pieces, edge_next, edge_kept, across, node_pieces, to_after, to_before)
-    )
-    edge_pieces = next_sum(peers, 2, edge_next, edge_kept)
+    returned = [returns[0], other, *bundles, send(across, across_chips(peers))] + core_bundles(peers, bundles)
     slot_half = halve_sum(peers, slot_pieces)
-    node_terms = rest_terms(peers, node_pieces)
-    (slot_half, edge_pieces, node_terms, to_after, to_before) = lax.optimization_barrier(
-        (slot_half, edge_pieces, node_terms, to_after, to_before)
-    )
+    slot_half, edge_pieces, returned = lax.optimization_barrier((slot_half, edge_pieces, returned))
     slot_terms = rest_terms(peers, slot_half)
     edge_terms = last_terms(peers, edge_pieces)
-    bundles = [send(to_after, by_shift(peers, 2)), send(to_before, by_shift(peers, -2))]
     node_terms, slot_terms = lax.optimization_barrier((node_terms, slot_terms))
-    returned = [returns[0], swapped, *bundles, across]
     node_rows = w_node_in.shape[0] // peers
     out_rows = w_edge_out.shape[0] // peers
     grid_grad = pl.pallas_call(
         functools.partial(scatter_kernel, out_rows),
         grid=(2,),
         in_specs=[smem, whole(rows.shape)]
-        + return_specs
+        + core_specs
         + [whole((out_rows + cap, width))] * (upper // 2),
         out_specs=pl.BlockSpec((grid_part, width), lambda step: (step, 0)),
         out_shape=jax.ShapeDtypeStruct((grid_count, width), BF16),

time: 102 us -> 104 us (1.020); the launches traced: 102 us -> 103 us
  Pallas kernels: 38.4 us -> 40.6 us
  starting transfers between devices: 35.9 us -> 33.9 us
  waiting for transfers between devices: 21.8 us -> 23 us
    pallas_call x0 -> x1, Pallas kernels: none -> 4.23 us  [on_device(): pl.pallas_call(edges_kernel, grid=(tiles,), in_specs=[smem, index_tile, t...]
    pallas_call x1, Pallas kernels: 16.7 us -> 14.8 us  [on_device(): pl.pallas_call(functools.partial(backward_kernel, peers), grid=(tiles,),...]
    ppermute x29 -> x32, starting transfers between devices: 35.9 us -> 33.9 us  [send(): return lax.ppermute(values, 'lon', perm)]
    ppermute x29 -> x32, waiting for transfers between devices: 21.8 us -> 23 us  [send(): return lax.ppermute(values, 'lon', perm)]
    add x4 -> x3, other arithmetic: 2.67 us -> 2.09 us  [total_of(): total = total + term[start:stop].astype(F32)]
  transfers between devices with their start and end apart: 29 -> 32, of which waited for: 9 -> 9; matrix products, arithmetic and copies ran while one was open for 4% -> 3% of each run, Pallas kernels for 22% -> 24%
where the time goes in v10:
time: 104 us; the launch traced here: 103 us
  Pallas kernels  40.6 us (39%)
  starting transfers between devices  33.9 us (33%)
  waiting for transfers between devices  23 us (22%)
  other arithmetic  3.86 us (4%)
  between operations  1.69 us (2%)
    ppermute x32, starting transfers between devices, send(): return lax.ppermute(values, 'lon', perm)  33.9 us
    ppermute x32, waiting for transfers between devices, send(): return lax.ppermute(values, 'lon', perm)  23 us
    pallas_call x1, Pallas kernels, on_device(): pl.pallas_call(functools.partial(backward_kernel, peers), grid=(tiles,),...  14.8 us
    pallas_call x1, Pallas kernels, on_device(): pl.pallas_call(functools.partial(forward_kernel, peers), grid=(tiles,), i...  11.9 us
    pallas_call x1, Pallas kernels, on_device(): pl.pallas_call(edges_kernel, grid=(tiles,), in_specs=[smem, index_tile, t...  4.23 us
    pallas_call x1, Pallas kernels, on_device(): pl.pallas_call(gather_kernel, in_specs=[smem, hbm, hbm], out_specs=near_s...  3.6 us
    pallas_call x1, Pallas kernels, on_device(): pl.pallas_call(local_kernel, grid=(tiles,), in_specs=[index_tile, tile_of...  3.44 us
    pallas_call x1, Pallas kernels, on_device(): pl.pallas_call(functools.partial(scatter_kernel, out_rows), grid=(2,), in...  2.69 us
  transfers between devices with their start and end apart: 32, of which 9 were waited for; matrix products, arithmetic and copies ran while one was open for 3% of the time, Pallas kernels for 24%

profile of v10, /device:TPU:0, one launch (start us, length us, event | category | flops | bytes accessed | tf_op | source)
XLA Modules:
  0.0 103.3 jit_solution(10629203368289103293)
XLA Ops:
  0.7 3.6 %gather_lists.1 = (bf16[48,512]{1,0:T(8,128)(2,1)}, bf16[48,512]{1,0:T(8,128)(2,1)}, bf16[96,512]{1,0:T(8,128)(2,1)}, bf16[96,512]{1,0:T(8,128)(2,1)}, bf16[48,512]{1,0:T(8,128)(2,1)}, /*index=5*/bf16[48,512]{1,0:T(8,128)(2,1)}) custom-call(s32[1]{0:T(128)} %bitcast.me_ref, s32[16,48]{1,0:T(8,128)} %bitcast.31, bf16[2048,512]{1,0:T(8,128)(2,1)} %grid_hbm.1), custom_call_target="tpu_custom_call" | custom-call | flops 32212254720 | bytes 2097152 | tf_op jit(solution)/shard_map/gather_lists/pallas_call | solution.py:508
  4.3 5.1 %collective-permute-start.2 = (bf16[48,512]{1,0:T(8,128)(2,1)}, bf16[48,512]{1,0:T(8,128)(2,1)S(1)}, u32[]{:S(2)}, u32[]{:S(2)}) collective-permute-start(bf16[48,512]{1,0:T(8,128)(2,1)} %get-tuple-element.93), channel_id=1, source_target_pairs={{0,12},{1,13},{2,14},{3,15},{4,8},{5,9},{6,10},{7,11},{8,4},{9,5},... | collective-permute-start | bytes 147464 | tf_op jit(solution)/shard_map/ppermute | solution.py:379
  10.0 2.3 %collective-permute-start.7 = (bf16[48,512]{1,0:T(8,128)(2,1)}, bf16[48,512]{1,0:T(8,128)(2,1)S(1)}, u32[]{:S(2)}, u32[]{:S(2)}) collective-permute-start(bf16[48,512]{1,0:T(8,128)(2,1)} %get-tuple-element.99), channel_id=1, source_target_pairs={{0,13},{1,4},{2,15},{3,6},{4,1},{5,8},{6,3},{7,10},{8,5},{9,12},{1... | collective-permute-start | bytes 147464 | tf_op jit(solution)/shard_map/ppermute | solution.py:379
  12.4 1.5 %collective-permute-start.5 = (bf16[96,512]{1,0:T(8,128)(2,1)}, bf16[96,512]{1,0:T(8,128)(2,1)S(1)}, u32[]{:S(2)}, u32[]{:S(2)}) collective-permute-start(bf16[96,512]{1,0:T(8,128)(2,1)} %get-tuple-element.97), channel_id=1, source_target_pairs={{0,2},{1,3},{2,4},{3,5},{4,6},{5,7},{6,8},{7,9},{8,10},{9,11},{10,... | collective-permute-start | bytes 294920 | tf_op jit(solution)/shard_map/ppermute | solution.py:379
  13.9 3.2 %collective-permute-start.6 = (bf16[96,512]{1,0:T(8,128)(2,1)}, bf16[96,512]{1,0:T(8,128)(2,1)S(1)}, u32[]{:S(2)}, u32[]{:S(2)}) collective-permute-start(bf16[96,512]{1,0:T(8,128)(2,1)} %get-tuple-element.98), channel_id=1, source_target_pairs={{0,14},{1,15},{2,0},{3,1},{4,2},{5,3},{6,4},{7,5},{8,6},{9,7},{10,... | collective-permute-start | bytes 294920 | tf_op jit(solution)/shard_map/ppermute | solution.py:379
  18.2 3.4 %edge_local.1.local_ref = bf16[3072,512]{1,0:T(8,128)(2,1)S(1)} custom-call(s32[3,1,1024]{2,1,0:T(1,128)S(1)} %bitcast.25, bf16[3072,512]{1,0:T(8,128)(2,1)S(1)} %copy-done.1, bf16[256,512]{1,0:T(8,128)(2,1)S(1)} %copy-done.2, bf16[1536,512]{1,0:T(8,128)(2,1)S(1)} %copy-done, bf16[1536,512]{1,0:T(8,128)(2,1)S(1)} %copy-done), custom_call_target="tpu_custom_call" | custom-call | flops 2415919104 | bytes 6291456 | tf_op jit(solution)/shard_map/edge_local/pallas_call | solution.py:534
  21.7 3.7 %collective-permute-done.3.refs_9_ = bf16[192,512]{1,0:T(8,128)(2,1)S(1)} collective-permute-done((bf16[192,512]{1,0:T(8,128)(2,1)S(1)}, bf16[192,512]{1,0:T(8,128)(2,1)S(1)}, u32[]{:S(2)}, u32[]{:S(2)}) %collective-permute-start.3) | collective-permute-done | bytes 196640 | tf_op jit(solution)/shard_map/ppermute | solution.py:379
  27.4 11.9 %forward.1 = (bf16[768,512]{1,0:T(8,128)(2,1)S(1)}, bf16[3072,512]{1,0:T(8,128)(2,1)S(1)}, bf16[3072,512]{1,0:T(8,128)(2,1)S(1)}, bf16[3072,512]{1,0:T(8,128)(2,...) custom-call(s32[1]{0:T(128)} %bitcast.me_ref, ...), custom_call_target="tpu_custom_call" | custom-call | tf_op jit(solution)/shard_map/forward/pallas_call | solution.py:554
  39.6 14.8 %backward.1 = (bf16[3072,512]{1,0:T(8,128)(2,1)S(1)}, bf16[256,512]{1,0:T(8,128)(2,1)}, bf16[2,320,512]{2,1,0:T(8,128)(2,1)S(1)}, bf16[2,320,512]{2,1,0:T(8,128)...) custom-call(s32[1]{0:T(128)} %bitcast.me_ref, ...), custom_call_target="tpu_custom_call" | custom-call | flops 8858370048 | bytes 15728640 | tf_op jit(solution)/shard_map/backward/pallas_call | solution.py:603
  54.4 3.3 %collective-permute-done.12 = bf16[2,384,512]{2,1,0:T(8,128)(2,1)S(1)} collective-permute-done((bf16[2,384,512]{2,1,0:T(8,128)(2,1)S(1)}, bf16[2,384,512]{2,1,0:T(8,128)(2,1)S(1)}, u32[]{:S(2)}, u32[]{:S(2)}) %collective-permute-start.12) | collective-permute-done | bytes 786464 | tf_op jit(solution)/shard_map/ppermute | solution.py:379
  59.0 1.7 %collective-permute-start.16 = (bf16[96,512]{1,0:T(8,128)(2,1)S(1)}, bf16[96,512]{1,0:T(8,128)(2,1)S(1)}, u32[]{:S(2)}, u32[]{:S(2)}) collective-permute-start(bf16[96,512]{1,0:T(8,128)(2,1)S(1)} %get-tuple-element.134), channel_id=1, source_target_pairs={{0,2},{1,3},{2,4},{3,5},{4,6},{5,7},{6,8},{7,9},{8,10},{9,11},{10,... | collective-permute-start | bytes 294920 | tf_op jit(solution)/shard_map/ppermute | solution.py:379
  60.7 3.0 %collective-permute-start.17 = (bf16[96,512]{1,0:T(8,128)(2,1)S(1)}, bf16[96,512]{1,0:T(8,128)(2,1)S(1)}, u32[]{:S(2)}, u32[]{:S(2)}) collective-permute-start(bf16[96,512]{1,0:T(8,128)(2,1)S(1)} %get-tuple-element.135), channel_id=1, source_target_pairs={{0,14},{1,15},{2,0},{3,1},{4,2},{5,3},{6,4},{7,5},{8,6},{9,7},{10,... | collective-permute-start | bytes 294920 | tf_op jit(solution)/shard_map/ppermute | solution.py:379
  64.3 2.3 %collective-permute-done.16.refs_2_ = bf16[96,512]{1,0:T(8,128)(2,1)S(1)} collective-permute-done((bf16[96,512]{1,0:T(8,128)(2,1)S(1)}, bf16[96,512]{1,0:T(8,128)(2,1)S(1)}, u32[]{:S(2)}, u32[]{:S(2)}) %collective-permute-start.16) | collective-permute-done | bytes 98336 | tf_op jit(solution)/shard_map/ppermute | solution.py:379
  66.6 1.0 collective-permute-done.17.refs_3_
  68.2 3.6 %collective-permute-start.22 = (bf16[96,512]{1,0:T(8,128)(2,1)S(1)}, bf16[96,512]{1,0:T(8,128)(2,1)S(1)}, u32[]{:S(2)}, u32[]{:S(2)}) collective-permute-start(bf16[96,512]{1,0:T(8,128)(2,1)S(1)} %get-tuple-element.189), channel_id=1, source_target_pairs={{0,12},{1,13},{2,14},{3,15},{4,8},{5,9},{6,10},{7,11},{8,4},{9,5},... | collective-permute-start | bytes 294920 | tf_op jit(solution)/shard_map/ppermute | solution.py:379
  72.6 1.5 %collective-permute-start.24 = (bf16[384,512]{1,0:T(8,128)(2,1)S(1)}, bf16[384,512]{1,0:T(8,128)(2,1)S(1)}, u32[]{:S(2)}, u32[]{:S(2)}) collective-permute-start(bf16[384,512]{1,0:T(8,128)(2,1)S(1)} %get-tuple-element.147), channel_id=1, source_target_pairs={{0,2},{1,3},{2,0},{3,1},{4,6},{5,7},{6,4},{7,5},{8,10},{9,11},{10,... | collective-permute-start | bytes 1179656 | tf_op jit(solution)/shard_map/ppermute | solution.py:379
  74.1 4.2 %edge_grad.1 = bf16[3072,512]{1,0:T(8,128)(2,1)} custom-call(s32[1]{0:T(128)S(6)} %copy.23.count_ref, s32[3,1,1024]{2,1,0:T(1,128)S(1)} %bitcast.28, bf16[3072,512]{1,0:T(8,128)(2,1)S(1)} %get-tuple-element.144.d_pre_ref, bf16[256,512]{1,0:T(8,128)(2,1)S(1)} %get-tuple-element.115.refs_4_.d_aggregate_ref, bf16[1536,512]{1,0:T(8,128)(2,1)S(1)} %copy-done), custom_call_target="tpu_custom_call" | custom-call | flops 2415919104 | bytes 6291456 | tf_op jit(solution)/shard_map/edge_grad/pallas_call | solution.py:665
  78.7 1.3 %collective-permute-start.25 = (bf16[48,512]{1,0:T(8,128)(2,1)S(1)}, bf16[48,512]{1,0:T(8,128)(2,1)S(1)}, u32[]{:S(2)}, u32[]{:S(2)}) collective-permute-start(bf16[48,512]{1,0:T(8,128)(2,1)S(1)} %get-tuple-element.152), channel_id=1, source_target_pairs={{0,13},{1,4},{2,15},{3,6},{4,1},{5,8},{6,3},{7,10},{8,5},{9,12},{1... | collective-permute-start | bytes 147464 | tf_op jit(solution)/shard_map/ppermute | solution.py:379
  80.7 4.2 %collective-permute-done.24 = bf16[384,512]{1,0:T(8,128)(2,1)S(1)} collective-permute-done((bf16[384,512]{1,0:T(8,128)(2,1)S(1)}, bf16[384,512]{1,0:T(8,128)(2,1)S(1)}, u32[]{:S(2)}, u32[]{:S(2)}) %collective-permute-start.24) | collective-permute-done | bytes 393248 | tf_op jit(solution)/shard_map/ppermute | solution.py:379
  84.9 2.4 %collective-permute-done.23 = bf16[160,512]{1,0:T(8,128)(2,1)S(1)} collective-permute-done((bf16[160,512]{1,0:T(8,128)(2,1)S(1)}, bf16[160,512]{1,0:T(8,128)(2,1)S(1)}, u32[]{:S(2)}, u32[]{:S(2)}) %collective-permute-start.23) | collective-permute-done | bytes 163872 | tf_op jit(solution)/shard_map/ppermute | solution.py:379
  88.4 1.8 %collective-permute-start.30 = (bf16[96,512]{1,0:T(8,128)(2,1)S(1)}, bf16[96,512]{1,0:T(8,128)(2,1)S(1)}, u32[]{:S(2)}, u32[]{:S(2)}) collective-permute-start(bf16[96,512]{1,0:T(8,128)(2,1)S(1)} %get-tuple-element.185), channel_id=1, source_target_pairs={{0,12},{1,13},{2,14},{3,15},{4,8},{5,9},{6,10},{7,11},{8,4},{9,5},... | collective-permute-start | bytes 294920 | tf_op jit(solution)/shard_map/ppermute | solution.py:379
  90.2 1.8 %collective-permute-start.29 = (bf16[96,512]{1,0:T(8,128)(2,1)S(1)}, bf16[96,512]{1,0:T(8,128)(2,1)S(1)}, u32[]{:S(2)}, u32[]{:S(2)}) collective-permute-start(bf16[96,512]{1,0:T(8,128)(2,1)S(1)} %get-tuple-element.186), channel_id=1, source_target_pairs={{0,8},{1,9},{2,10},{3,11},{4,12},{5,13},{6,14},{7,15},{8,0},{9,1},... | collective-permute-start | bytes 294920 | tf_op jit(solution)/shard_map/ppermute | solution.py:379
  92.9 5.6 %collective-permute-done.31.refs_8_ = bf16[80,512]{1,0:T(8,128)(2,1)S(1)} collective-permute-done((bf16[80,512]{1,0:T(8,128)(2,1)S(1)}, bf16[80,512]{1,0:T(8,128)(2,1)S(1)}, u32[]{:S(2)}, u32[]{:S(2)}) %collective-permute-start.31) | collective-permute-done | bytes 81952 | tf_op jit(solution)/shard_map/ppermute | solution.py:379
  99.9 2.7 %scatter_lists.1 = bf16[2048,512]{1,0:T(8,128)(2,1)} custom-call(s32[1]{0:T(128)} %bitcast.me_ref, s32[16,48]{1,0:T(8,128)S(1)} %bitcast.32, bf16[48,512]{1,0:T(8,128)(2,1)S(1)} %get-tuple-element.154.refs_0_, bf16[48,512]{1,0:T(8,128)(2,1)S(1)} %collective-permute-done.18.refs_1_, bf16[96,512]{1,0:T(8,128)(2,1)S(1)} %collective-permute-done.16.refs_2_, ...), custom_call_target="tpu_custom_call" | custom-call | tf_op jit(solution)/shard_map/scatter_lists/pallas_call | solution.py:688
  (85 shorter events, 11.7 us)
Async XLA Ops:
  4.3 9.6 %collective-permute-start.2 = (bf16[48,512]{1,0:T(8,128)(2,1)}, bf16[48,512]{1,0:T(8,128)(2,1)S(1)}, u32[]{:S(2)}, u32[]{:S(2)}) collective-permute-start(bf16[48,512]{1,0:T(8,128)(2,1)} %get-tuple-element.93), channel_id=1, source_target_pairs={{0,12},{1,13},{2,14},{3,15},{4,8},{5,9},{6,10},{7,11},{8,4},{9,5},... | collective-permute-start | bytes 147464 | tf_op jit(solution)/shard_map/ppermute | solution.py:379
  9.4 7.7 %collective-permute-start.1 = (bf16[48,512]{1,0:T(8,128)(2,1)}, bf16[48,512]{1,0:T(8,128)(2,1)S(1)}, u32[]{:S(2)}, u32[]{:S(2)}) collective-permute-start(bf16[48,512]{1,0:T(8,128)(2,1)} %get-tuple-element.93), channel_id=1, source_target_pairs={{0,8},{1,9},{2,10},{3,11},{4,12},{5,13},{6,14},{7,15},{8,0},{9,1},... | collective-permute-start | bytes 147464 | tf_op jit(solution)/shard_map/ppermute | solution.py:379
  9.4 7.7 %collective-permute-start = (bf16[48,512]{1,0:T(8,128)(2,1)}, bf16[48,512]{1,0:T(8,128)(2,1)S(1)}, u32[]{:S(2)}, u32[]{:S(2)}) collective-permute-start(bf16[48,512]{1,0:T(8,128)(2,1)} %get-tuple-element.93), channel_id=1, source_target_pairs={{0,4},{1,5},{2,6},{3,7},{4,0},{5,1},{6,2},{7,3},{8,12},{9,13},{10,... | collective-permute-start | bytes 147464 | tf_op jit(solution)/shard_map/ppermute | solution.py:379
  10.0 11.6 %collective-permute-start.7 = (bf16[48,512]{1,0:T(8,128)(2,1)}, bf16[48,512]{1,0:T(8,128)(2,1)S(1)}, u32[]{:S(2)}, u32[]{:S(2)}) collective-permute-start(bf16[48,512]{1,0:T(8,128)(2,1)} %get-tuple-element.99), channel_id=1, source_target_pairs={{0,13},{1,4},{2,15},{3,6},{4,1},{5,8},{6,3},{7,10},{8,5},{9,12},{1... | collective-permute-start | bytes 147464 | tf_op jit(solution)/shard_map/ppermute | solution.py:379
  12.4 9.3 %collective-permute-start.5 = (bf16[96,512]{1,0:T(8,128)(2,1)}, bf16[96,512]{1,0:T(8,128)(2,1)S(1)}, u32[]{:S(2)}, u32[]{:S(2)}) collective-permute-start(bf16[96,512]{1,0:T(8,128)(2,1)} %get-tuple-element.97), channel_id=1, source_target_pairs={{0,2},{1,3},{2,4},{3,5},{4,6},{5,7},{6,8},{7,9},{8,10},{9,11},{10,... | collective-permute-start | bytes 294920 | tf_op jit(solution)/shard_map/ppermute | solution.py:379
  13.9 7.8 %collective-permute-start.6 = (bf16[96,512]{1,0:T(8,128)(2,1)}, bf16[96,512]{1,0:T(8,128)(2,1)S(1)}, u32[]{:S(2)}, u32[]{:S(2)}) collective-permute-start(bf16[96,512]{1,0:T(8,128)(2,1)} %get-tuple-element.98), channel_id=1, source_target_pairs={{0,14},{1,15},{2,0},{3,1},{4,2},{5,3},{6,4},{7,5},{8,6},{9,7},{10,... | collective-permute-start | bytes 294920 | tf_op jit(solution)/shard_map/ppermute | solution.py:379
  18.1 7.3 %collective-permute-start.3 = (bf16[192,512]{1,0:T(8,128)(2,1)S(1)}, bf16[192,512]{1,0:T(8,128)(2,1)S(1)}, u32[]{:S(2)}, u32[]{:S(2)}) collective-permute-start(bf16[192,512]{1,0:T(8,128)(2,1)S(1)} %pad_maximum_fusion.refs_7_), channel_id=1, source_target_pairs={{0,2},{1,3},{2,0},{3,1},{4,6},{5,7},{6,4},{7,5},{8,10},{9,11},{10,... | collective-permute-start | bytes 589832 | tf_op jit(solution)/shard_map/ppermute | solution.py:379
  39.3 18.4 %collective-permute-start.12 = (bf16[2,384,512]{2,1,0:T(8,128)(2,1)S(1)}, bf16[2,384,512]{2,1,0:T(8,128)(2,1)S(1)}, u32[]{:S(2)}, u32[]{:S(2)}) collective-permute-start(bf16[2,384,512]{2,1,0:T(8,128)(2,1)S(1)} %get-tuple-element.110), channel_id=1, source_target_pairs={{0,2},{1,3},{2,0},{3,1},{4,6},{5,7},{6,4},{7,5},{8,10},{9,11},{10,... | collective-permute-start | bytes 2359304 | tf_op jit(solution)/shard_map/ppermute | solution.py:379
  57.9 5.9 %collective-permute-start.13 = (bf16[2,320,512]{2,1,0:T(8,128)(2,1)S(1)}, bf16[2,320,512]{2,1,0:T(8,128)(2,1)S(1)}, u32[]{:S(2)}, u32[]{:S(2)}) collective-permute-start(bf16[2,320,512]{2,1,0:T(8,128)(2,1)S(1)} %get-tuple-element.129), channel_id=1, source_target_pairs={{0,1},{1,0},{2,3},{3,2},{4,5},{5,4},{6,7},{7,6},{8,9},{9,8},{10,11... | collective-permute-start | bytes 1966088 | tf_op jit(solution)/shard_map/ppermute | solution.py:379
  59.0 7.6 %collective-permute-start.16 = (bf16[96,512]{1,0:T(8,128)(2,1)S(1)}, bf16[96,512]{1,0:T(8,128)(2,1)S(1)}, u32[]{:S(2)}, u32[]{:S(2)}) collective-permute-start(bf16[96,512]{1,0:T(8,128)(2,1)S(1)} %get-tuple-element.134), channel_id=1, source_target_pairs={{0,2},{1,3},{2,4},{3,5},{4,6},{5,7},{6,8},{7,9},{8,10},{9,11},{10,... | collective-permute-start | bytes 294920 | tf_op jit(solution)/shard_map/ppermute | solution.py:379
  60.7 6.8 %collective-permute-start.17 = (bf16[96,512]{1,0:T(8,128)(2,1)S(1)}, bf16[96,512]{1,0:T(8,128)(2,1)S(1)}, u32[]{:S(2)}, u32[]{:S(2)}) collective-permute-start(bf16[96,512]{1,0:T(8,128)(2,1)S(1)} %get-tuple-element.135), channel_id=1, source_target_pairs={{0,14},{1,15},{2,0},{3,1},{4,2},{5,3},{6,4},{7,5},{8,6},{9,7},{10,... | collective-permute-start | bytes 294920 | tf_op jit(solution)/shard_map/ppermute | solution.py:379
  67.6 10.8 %collective-permute-start.19 = (bf16[320,512]{1,0:T(8,128)(2,1)S(1)}, bf16[320,512]{1,0:T(8,128)(2,1)S(1)}, u32[]{:S(2)}, u32[]{:S(2)}) collective-permute-start(bf16[320,512]{1,0:T(8,128)(2,1)S(1)} %get-tuple-element.139), channel_id=1, source_target_pairs={{0,2},{1,3},{2,0},{3,1},{4,6},{5,7},{6,4},{7,5},{8,10},{9,11},{10,... | collective-permute-start | bytes 983048 | tf_op jit(solution)/shard_map/ppermute | solution.py:379
  68.2 10.3 %collective-permute-start.22 = (bf16[96,512]{1,0:T(8,128)(2,1)S(1)}, bf16[96,512]{1,0:T(8,128)(2,1)S(1)}, u32[]{:S(2)}, u32[]{:S(2)}) collective-permute-start(bf16[96,512]{1,0:T(8,128)(2,1)S(1)} %get-tuple-element.189), channel_id=1, source_target_pairs={{0,12},{1,13},{2,14},{3,15},{4,8},{5,9},{6,10},{7,11},{8,4},{9,5},... | collective-permute-start | bytes 294920 | tf_op jit(solution)/shard_map/ppermute | solution.py:379
  71.7 7.0 %collective-permute-start.21 = (bf16[96,512]{1,0:T(8,128)(2,1)S(1)}, bf16[96,512]{1,0:T(8,128)(2,1)S(1)}, u32[]{:S(2)}, u32[]{:S(2)}) collective-permute-start(bf16[96,512]{1,0:T(8,128)(2,1)S(1)} %get-tuple-element.190), channel_id=1, source_target_pairs={{0,8},{1,9},{2,10},{3,11},{4,12},{5,13},{6,14},{7,15},{8,0},{9,1},... | collective-permute-start | bytes 294920 | tf_op jit(solution)/shard_map/ppermute | solution.py:379
  71.7 7.0 %collective-permute-start.20 = (bf16[96,512]{1,0:T(8,128)(2,1)S(1)}, bf16[96,512]{1,0:T(8,128)(2,1)S(1)}, u32[]{:S(2)}, u32[]{:S(2)}) collective-permute-start(bf16[96,512]{1,0:T(8,128)(2,1)S(1)} %get-tuple-element.191), channel_id=1, source_target_pairs={{0,4},{1,5},{2,6},{3,7},{4,0},{5,1},{6,2},{7,3},{8,12},{9,13},{10,... | collective-permute-start | bytes 294920 | tf_op jit(solution)/shard_map/ppermute | solution.py:379
  72.6 12.2 %collective-permute-start.24 = (bf16[384,512]{1,0:T(8,128)(2,1)S(1)}, bf16[384,512]{1,0:T(8,128)(2,1)S(1)}, u32[]{:S(2)}, u32[]{:S(2)}) collective-permute-start(bf16[384,512]{1,0:T(8,128)(2,1)S(1)} %get-tuple-element.147), channel_id=1, source_target_pairs={{0,2},{1,3},{2,0},{3,1},{4,6},{5,7},{6,4},{7,5},{8,10},{9,11},{10,... | collective-permute-start | bytes 1179656 | tf_op jit(solution)/shard_map/ppermute | solution.py:379
  78.7 8.6 %collective-permute-start.25 = (bf16[48,512]{1,0:T(8,128)(2,1)S(1)}, bf16[48,512]{1,0:T(8,128)(2,1)S(1)}, u32[]{:S(2)}, u32[]{:S(2)}) collective-permute-start(bf16[48,512]{1,0:T(8,128)(2,1)S(1)} %get-tuple-element.152), channel_id=1, source_target_pairs={{0,13},{1,4},{2,15},{3,6},{4,1},{5,8},{6,3},{7,10},{8,5},{9,12},{1... | collective-permute-start | bytes 147464 | tf_op jit(solution)/shard_map/ppermute | solution.py:379
  80.0 7.3 %collective-permute-start.26 = (bf16[96,512]{1,0:T(8,128)(2,1)S(1)}, bf16[96,512]{1,0:T(8,128)(2,1)S(1)}, u32[]{:S(2)}, u32[]{:S(2)}) collective-permute-start(bf16[96,512]{1,0:T(8,128)(2,1)S(1)} %collective-permute-done.16.refs_2_), channel_id=1, source_target_pairs={{0,1},{1,0},{2,3},{3,2},{4,5},{5,4},{6,7},{7,6},{8,9},{9,8},{10,11... | collective-permute-start | bytes 294920 | tf_op jit(solution)/shard_map/ppermute | solution.py:379
  80.0 7.3 %collective-permute-start.27 = (bf16[96,512]{1,0:T(8,128)(2,1)S(1)}, bf16[96,512]{1,0:T(8,128)(2,1)S(1)}, u32[]{:S(2)}, u32[]{:S(2)}) collective-permute-start(bf16[96,512]{1,0:T(8,128)(2,1)S(1)} %collective-permute-done.17.refs_3_), channel_id=1, source_target_pairs={{0,1},{1,0},{2,3},{3,2},{4,5},{5,4},{6,7},{7,6},{8,9},{9,8},{10,11... | collective-permute-start | bytes 294920 | tf_op jit(solution)/shard_map/ppermute | solution.py:379
  80.6 6.7 %collective-permute-start.23 = (bf16[160,512]{1,0:T(8,128)(2,1)S(1)}, bf16[160,512]{1,0:T(8,128)(2,1)S(1)}, u32[]{:S(2)}, u32[]{:S(2)}) collective-permute-start(bf16[160,512]{1,0:T(8,128)(2,1)S(1)} %bitcast.34), channel_id=1, source_target_pairs={{0,4},{1,5},{2,6},{3,7},{4,0},{5,1},{6,2},{7,3},{8,12},{9,13},{10,... | collective-permute-start | bytes 491528 | tf_op jit(solution)/shard_map/ppermute | solution.py:379
  87.4 11.1 %collective-permute-start.31 = (bf16[80,512]{1,0:T(8,128)(2,1)S(1)}, bf16[80,512]{1,0:T(8,128)(2,1)S(1)}, u32[]{:S(2)}, u32[]{:S(2)}) collective-permute-start(bf16[80,512]{1,0:T(8,128)(2,1)S(1)} %get-tuple-element.195), channel_id=1, source_target_pairs={{0,8},{1,9},{2,10},{3,11},{4,12},{5,13},{6,14},{7,15},{8,0},{9,1},... | collective-permute-start | bytes 245768 | tf_op jit(solution)/shard_map/ppermute | solution.py:379
  88.4 14.1 %collective-permute-start.30 = (bf16[96,512]{1,0:T(8,128)(2,1)S(1)}, bf16[96,512]{1,0:T(8,128)(2,1)S(1)}, u32[]{:S(2)}, u32[]{:S(2)}) collective-permute-start(bf16[96,512]{1,0:T(8,128)(2,1)S(1)} %get-tuple-element.185), channel_id=1, source_target_pairs={{0,12},{1,13},{2,14},{3,15},{4,8},{5,9},{6,10},{7,11},{8,4},{9,5},... | collective-permute-start | bytes 294920 | tf_op jit(solution)/shard_map/ppermute | solution.py:379
  90.2 12.3 %collective-permute-start.29 = (bf16[96,512]{1,0:T(8,128)(2,1)S(1)}, bf16[96,512]{1,0:T(8,128)(2,1)S(1)}, u32[]{:S(2)}, u32[]{:S(2)}) collective-permute-start(bf16[96,512]{1,0:T(8,128)(2,1)S(1)} %get-tuple-element.186), channel_id=1, source_target_pairs={{0,8},{1,9},{2,10},{3,11},{4,12},{5,13},{6,14},{7,15},{8,0},{9,1},... | collective-permute-start | bytes 294920 | tf_op jit(solution)/shard_map/ppermute | solution.py:379
  92.0 10.6 %collective-permute-start.28 = (bf16[96,512]{1,0:T(8,128)(2,1)S(1)}, bf16[96,512]{1,0:T(8,128)(2,1)S(1)}, u32[]{:S(2)}, u32[]{:S(2)}) collective-permute-start(bf16[96,512]{1,0:T(8,128)(2,1)S(1)} %get-tuple-element.187), channel_id=1, source_target_pairs={{0,4},{1,5},{2,6},{3,7},{4,0},{5,1},{6,2},{7,3},{8,12},{9,13},{10,... | collective-permute-start | bytes 294920 | tf_op jit(solution)/shard_map/ppermute | solution.py:379
  (20 other events, 180.3 us)

commit v11 on v10

--- a/solution.py
+++ b/solution.py
@@ -654,14 +654,14 @@
     slot_next, slot_kept = first_sum(peers, 1, slot_send, slot_keep)
     edge_next, edge_kept = first_sum(peers, 1, edge_send, edge_keep)
     node_pieces = next_sum(peers, 1, node_next, node_kept)
-    bundles = [send(returns[2], by_shift(peers, 2)), send(returns[3], by_shift(peers, -2))]
     other = send(returns[1], by_xor(peers, 1))
-    (slot_next, slot_kept, edge_next, edge_kept, node_pieces, bundles, other, d_pre) = lax.optimization_barrier(
-        (slot_next, slot_kept, edge_next, edge_kept, node_pieces, bundles, other, d_pre)
+    (slot_next, slot_kept, edge_next, edge_kept, node_pieces, other, d_pre, returns) = lax.optimization_barrier(
+        (slot_next, slot_kept, edge_next, edge_kept, node_pieces, other, d_pre, returns)
     )
     slot_pieces = next_sum(peers, 2, slot_next, slot_kept)
     edge_pieces = next_sum(peers, 2, edge_next, edge_kept)
-    node_terms = last_terms(peers, node_pieces)
+    node_pieces = halve_sum(peers, node_pieces)
+    across = send(returns[4], across_chips(peers))
     edge_grad = pl.pallas_call(
         edges_kernel,
         grid=(tiles,),
@@ -674,14 +674,18 @@
         ),
         name="edge_grad",
     )(tile_count, dst, d_pre, d_aggregate, w_edge_in)
-    (slot_pieces, node_terms, across, bundles, edge_grad) = lax.optimization_barrier(
-        (slot_pieces, node_terms, returns[4], bundles, edge_grad)
+    (slot_pieces, node_pieces, across, edge_grad) = lax.optimization_barrier(
+        (slot_pieces, node_pieces, across, edge_grad)
     )
-    returned = [returns[0], other, *bundles, send(across, across_chips(peers))] + core_bundles(peers, bundles)
     slot_half = halve_sum(peers, slot_pieces)
-    slot_half, edge_pieces, returned = lax.optimization_barrier((slot_half, edge_pieces, returned))
+    node_terms = rest_terms(peers, node_pieces)
+    (slot_half, edge_pieces, node_terms, to_after, to_before) = lax.optimization_barrier(
+        (slot_half, edge_pieces, node_terms, returns[2], returns[3])
+    )
     slot_terms = rest_terms(peers, slot_half)
     edge_terms = last_terms(peers, edge_pieces)
+    bundles = [send(to_after, by_shift(peers, 2)), send(to_before, by_shift(peers, -2))]
+    returned = [returns[0], other, *bundles, across] + core_bundles(peers, bundles)
     node_terms, slot_terms = lax.optimization_barrier((node_terms, slot_terms))
     node_rows = w_node_in.shape[0] // peers
     out_rows = w_edge_out.shape[0] // peers

time: 104 us -> 103 us (level); the launches traced: 103 us -> 101 us
  waiting for transfers between devices: 23 us -> 32.6 us
  Pallas kernels: 40.6 us -> 32.9 us
  starting transfers between devices: 33.9 us -> 29.5 us
    ppermute x32 -> x31, waiting for transfers between devices: 23 us -> 32.6 us  [send(): return lax.ppermute(values, 'lon', perm)]
    ppermute x32 -> x31, starting transfers between devices: 33.9 us -> 29.5 us  [send(): return lax.ppermute(values, 'lon', perm)]
    pallas_call x1, Pallas kernels: 14.8 us -> 10.8 us  [on_device(): pl.pallas_call(functools.partial(backward_kernel, peers), grid=(tiles,),...]
    pallas_call x1, Pallas kernels: 11.9 us -> 8.96 us  [on_device(): pl.pallas_call(functools.partial(forward_kernel, peers), grid=(tiles,), i...]
  transfers between devices with their start and end apart: 32 -> 31, of which waited for: 9 -> 13; matrix products, arithmetic and copies ran while one was open for 3% -> 3% of each run, Pallas kernels for 24% -> 20%
where the time goes in v11:
time: 103 us; the launch traced here: 101 us
  Pallas kernels  32.9 us (32%)
  waiting for transfers between devices  32.6 us (32%)
  starting transfers between devices  29.5 us (29%)
  other arithmetic  3.89 us (4%)
  between operations  1.68 us (2%)
    ppermute x31, waiting for transfers between devices, send(): return lax.ppermute(values, 'lon', perm)  32.6 us
    ppermute x31, starting transfers between devices, send(): return lax.ppermute(values, 'lon', perm)  29.5 us
    pallas_call x1, Pallas kernels, on_device(): pl.pallas_call(functools.partial(backward_kernel, peers), grid=(tiles,),...  10.8 us
    pallas_call x1, Pallas kernels, on_device(): pl.pallas_call(functools.partial(forward_kernel, peers), grid=(tiles,), i...  8.96 us
    pallas_call x1, Pallas kernels, on_device(): pl.pallas_call(gather_kernel, in_specs=[smem, hbm, hbm], out_specs=near_s...  3.6 us
    pallas_call x1, Pallas kernels, on_device(): pl.pallas_call(edges_kernel, grid=(tiles,), in_specs=[smem, index_tile, t...  3.49 us
    pallas_call x1, Pallas kernels, on_device(): pl.pallas_call(local_kernel, grid=(tiles,), in_specs=[index_tile, tile_of...  3.44 us
    pallas_call x1, Pallas kernels, on_device(): pl.pallas_call(functools.partial(scatter_kernel, out_rows), grid=(2,), in...  2.69 us
  transfers between devices with their start and end apart: 31, of which 13 were waited for; matrix products, arithmetic and copies ran while one was open for 3% of the time, Pallas kernels for 20%

profile of v11, /device:TPU:0, one launch (start us, length us, event | category | flops | bytes accessed | tf_op | source)
XLA Modules:
  0.0 100.8 jit_solution(17277764174215351819)
XLA Ops:
  0.7 3.6 %gather_lists.1 = (bf16[48,512]{1,0:T(8,128)(2,1)}, bf16[48,512]{1,0:T(8,128)(2,1)}, bf16[96,512]{1,0:T(8,128)(2,1)}, bf16[96,512]{1,0:T(8,128)(2,1)}, bf16[48,512]{1,0:T(8,128)(2,1)}, /*index=5*/bf16[48,512]{1,0:T(8,128)(2,1)}) custom-call(s32[1]{0:T(128)} %bitcast.me_ref, s32[16,48]{1,0:T(8,128)} %bitcast.36, bf16[2048,512]{1,0:T(8,128)(2,1)} %grid_hbm.1), custom_call_target="tpu_custom_call" | custom-call | flops 32212254720 | bytes 2097152 | tf_op jit(solution)/shard_map/gather_lists/pallas_call | solution.py:508
  4.3 5.1 %collective-permute-start.2 = (bf16[48,512]{1,0:T(8,128)(2,1)}, bf16[48,512]{1,0:T(8,128)(2,1)S(1)}, u32[]{:S(2)}, u32[]{:S(2)}) collective-permute-start(bf16[48,512]{1,0:T(8,128)(2,1)} %get-tuple-element.85), channel_id=1, source_target_pairs={{0,12},{1,13},{2,14},{3,15},{4,8},{5,9},{6,10},{7,11},{8,4},{9,5},... | collective-permute-start | bytes 147464 | tf_op jit(solution)/shard_map/ppermute | solution.py:379
  10.0 2.3 %collective-permute-start.7 = (bf16[48,512]{1,0:T(8,128)(2,1)}, bf16[48,512]{1,0:T(8,128)(2,1)S(1)}, u32[]{:S(2)}, u32[]{:S(2)}) collective-permute-start(bf16[48,512]{1,0:T(8,128)(2,1)} %get-tuple-element.91), channel_id=1, source_target_pairs={{0,13},{1,4},{2,15},{3,6},{4,1},{5,8},{6,3},{7,10},{8,5},{9,12},{1... | collective-permute-start | bytes 147464 | tf_op jit(solution)/shard_map/ppermute | solution.py:379
  12.4 1.5 %collective-permute-start.5 = (bf16[96,512]{1,0:T(8,128)(2,1)}, bf16[96,512]{1,0:T(8,128)(2,1)S(1)}, u32[]{:S(2)}, u32[]{:S(2)}) collective-permute-start(bf16[96,512]{1,0:T(8,128)(2,1)} %get-tuple-element.89), channel_id=1, source_target_pairs={{0,2},{1,3},{2,4},{3,5},{4,6},{5,7},{6,8},{7,9},{8,10},{9,11},{10,... | collective-permute-start | bytes 294920 | tf_op jit(solution)/shard_map/ppermute | solution.py:379
  13.9 3.2 %collective-permute-start.6 = (bf16[96,512]{1,0:T(8,128)(2,1)}, bf16[96,512]{1,0:T(8,128)(2,1)S(1)}, u32[]{:S(2)}, u32[]{:S(2)}) collective-permute-start(bf16[96,512]{1,0:T(8,128)(2,1)} %get-tuple-element.90), channel_id=1, source_target_pairs={{0,14},{1,15},{2,0},{3,1},{4,2},{5,3},{6,4},{7,5},{8,6},{9,7},{10,... | collective-permute-start | bytes 294920 | tf_op jit(solution)/shard_map/ppermute | solution.py:379
  18.2 3.4 %edge_local.1.local_ref = bf16[3072,512]{1,0:T(8,128)(2,1)S(1)} custom-call(s32[3,1,1024]{2,1,0:T(1,128)S(1)} %bitcast.30, bf16[3072,512]{1,0:T(8,128)(2,1)S(1)} %copy-done.1, bf16[256,512]{1,0:T(8,128)(2,1)S(1)} %copy-done.2, bf16[1536,512]{1,0:T(8,128)(2,1)S(1)} %copy-done, bf16[1536,512]{1,0:T(8,128)(2,1)S(1)} %copy-done), custom_call_target="tpu_custom_call" | custom-call | flops 2415919104 | bytes 6291456 | tf_op jit(solution)/shard_map/edge_local/pallas_call | solution.py:534
  21.7 3.7 %collective-permute-done.3.refs_9_ = bf16[192,512]{1,0:T(8,128)(2,1)S(1)} collective-permute-done((bf16[192,512]{1,0:T(8,128)(2,1)S(1)}, bf16[192,512]{1,0:T(8,128)(2,1)S(1)}, u32[]{:S(2)}, u32[]{:S(2)}) %collective-permute-start.3) | collective-permute-done | bytes 196640 | tf_op jit(solution)/shard_map/ppermute | solution.py:379
  27.4 9.0 %forward.1 = (bf16[768,512]{1,0:T(8,128)(2,1)S(1)}, bf16[3072,512]{1,0:T(8,128)(2,1)S(1)}, bf16[3072,512]{1,0:T(8,128)(2,1)S(1)}, bf16[3072,512]{1,0:T(8,128)(2,...) custom-call(s32[1]{0:T(128)} %bitcast.me_ref, ...), custom_call_target="tpu_custom_call" | custom-call | tf_op jit(solution)/shard_map/forward/pallas_call | solution.py:554
  36.4 10.8 %backward.1 = (bf16[3072,512]{1,0:T(8,128)(2,1)S(1)}, bf16[256,512]{1,0:T(8,128)(2,1)}, bf16[2,320,512]{2,1,0:T(8,128)(2,1)S(1)}, bf16[2,320,512]{2,1,0:T(8,128)...) custom-call(s32[1]{0:T(128)} %bitcast.me_ref, ...), custom_call_target="tpu_custom_call" | custom-call | flops 8858370048 | bytes 15728640 | tf_op jit(solution)/shard_map/backward/pallas_call | solution.py:603
  47.2 8.8 %collective-permute-done.12 = bf16[2,384,512]{2,1,0:T(8,128)(2,1)S(1)} collective-permute-done((bf16[2,384,512]{2,1,0:T(8,128)(2,1)S(1)}, bf16[2,384,512]{2,1,0:T(8,128)(2,1)S(1)}, u32[]{:S(2)}, u32[]{:S(2)}) %collective-permute-start.12) | collective-permute-done | bytes 786464 | tf_op jit(solution)/shard_map/ppermute | solution.py:379
  57.5 1.7 %collective-permute-done.15 = bf16[384,512]{1,0:T(8,128)(2,1)S(1)} collective-permute-done((bf16[384,512]{1,0:T(8,128)(2,1)S(1)}, bf16[384,512]{1,0:T(8,128)(2,1)S(1)}, u32[]{:S(2)}, u32[]{:S(2)}) %collective-permute-start.15) | collective-permute-done | bytes 393248 | tf_op jit(solution)/shard_map/ppermute | solution.py:379
  60.6 3.9 %collective-permute-start.19 = (bf16[48,512]{1,0:T(8,128)(2,1)S(1)}, bf16[48,512]{1,0:T(8,128)(2,1)S(1)}, u32[]{:S(2)}, u32[]{:S(2)}) collective-permute-start(bf16[48,512]{1,0:T(8,128)(2,1)S(1)} %get-tuple-element.135), channel_id=1, source_target_pairs={{0,13},{1,4},{2,15},{3,6},{4,1},{5,8},{6,3},{7,10},{8,5},{9,12},{1... | collective-permute-start | bytes 147464 | tf_op jit(solution)/shard_map/ppermute | solution.py:379
  64.8 1.8 %collective-permute-start.21 = (bf16[384,512]{1,0:T(8,128)(2,1)S(1)}, bf16[384,512]{1,0:T(8,128)(2,1)S(1)}, u32[]{:S(2)}, u32[]{:S(2)}) collective-permute-start(bf16[384,512]{1,0:T(8,128)(2,1)S(1)} %get-tuple-element.139), channel_id=1, source_target_pairs={{0,2},{1,3},{2,0},{3,1},{4,6},{5,7},{6,4},{7,5},{8,10},{9,11},{10,... | collective-permute-start | bytes 1179656 | tf_op jit(solution)/shard_map/ppermute | solution.py:379
  66.6 3.5 %edge_grad.1 = bf16[3072,512]{1,0:T(8,128)(2,1)} custom-call(s32[1]{0:T(128)S(6)} %copy.23.count_ref, s32[3,1,1024]{2,1,0:T(1,128)S(1)} %bitcast.33, bf16[3072,512]{1,0:T(8,128)(2,1)S(1)} %get-tuple-element.136.d_pre_ref, bf16[256,512]{1,0:T(8,128)(2,1)S(1)} %get-tuple-element.107.refs_4_.d_aggregate_ref, bf16[1536,512]{1,0:T(8,128)(2,1)S(1)} %copy-done), custom_call_target="tpu_custom_call" | custom-call | flops 2415919104 | bytes 6291456 | tf_op jit(solution)/shard_map/edge_grad/pallas_call | solution.py:665
  71.2 3.8 %collective-permute-done.17 = bf16[320,512]{1,0:T(8,128)(2,1)S(1)} collective-permute-done((bf16[320,512]{1,0:T(8,128)(2,1)S(1)}, bf16[320,512]{1,0:T(8,128)(2,1)S(1)}, u32[]{:S(2)}, u32[]{:S(2)}) %collective-permute-start.17) | collective-permute-done | bytes 327712 | tf_op jit(solution)/shard_map/ppermute | solution.py:379
  75.2 1.0 collective-permute-start.22
  76.2 3.0 %collective-permute-done.21 = bf16[384,512]{1,0:T(8,128)(2,1)S(1)} collective-permute-done((bf16[384,512]{1,0:T(8,128)(2,1)S(1)}, bf16[384,512]{1,0:T(8,128)(2,1)S(1)}, u32[]{:S(2)}, u32[]{:S(2)}) %collective-permute-start.21) | collective-permute-done | bytes 393248 | tf_op jit(solution)/shard_map/ppermute | solution.py:379
  79.2 2.3 %collective-permute-done.20 = bf16[160,512]{1,0:T(8,128)(2,1)S(1)} collective-permute-done((bf16[160,512]{1,0:T(8,128)(2,1)S(1)}, bf16[160,512]{1,0:T(8,128)(2,1)S(1)}, u32[]{:S(2)}, u32[]{:S(2)}) %collective-permute-start.20) | collective-permute-done | bytes 163872 | tf_op jit(solution)/shard_map/ppermute | solution.py:379
  82.5 2.9 %collective-permute-start.25 = (bf16[96,512]{1,0:T(8,128)(2,1)S(1)}, bf16[96,512]{1,0:T(8,128)(2,1)S(1)}, u32[]{:S(2)}, u32[]{:S(2)}) collective-permute-start(bf16[96,512]{1,0:T(8,128)(2,1)S(1)} %get-tuple-element.169), channel_id=1, source_target_pairs={{0,12},{1,13},{2,14},{3,15},{4,8},{5,9},{6,10},{7,11},{8,4},{9,5},... | collective-permute-start | bytes 294920 | tf_op jit(solution)/shard_map/ppermute | solution.py:379
  85.4 1.6 %collective-permute-start.23 = (bf16[96,512]{1,0:T(8,128)(2,1)S(1)}, bf16[96,512]{1,0:T(8,128)(2,1)S(1)}, u32[]{:S(2)}, u32[]{:S(2)}) collective-permute-start(bf16[96,512]{1,0:T(8,128)(2,1)S(1)} %get-tuple-element.171), channel_id=1, source_target_pairs={{0,4},{1,5},{2,6},{3,7},{4,0},{5,1},{6,2},{7,3},{8,12},{9,13},{10,... | collective-permute-start | bytes 294920 | tf_op jit(solution)/shard_map/ppermute | solution.py:379
  87.3 4.1 %collective-permute-done.30.refs_8_ = bf16[80,512]{1,0:T(8,128)(2,1)S(1)} collective-permute-done((bf16[80,512]{1,0:T(8,128)(2,1)S(1)}, bf16[80,512]{1,0:T(8,128)(2,1)S(1)}, u32[]{:S(2)}, u32[]{:S(2)}) %collective-permute-start.30) | collective-permute-done | bytes 81952 | tf_op jit(solution)/shard_map/ppermute | solution.py:379
  91.4 1.4 %collective-permute-start.27 = (bf16[96,512]{1,0:T(8,128)(2,1)S(1)}, bf16[96,512]{1,0:T(8,128)(2,1)S(1)}, u32[]{:S(2)}, u32[]{:S(2)}) collective-permute-start(bf16[96,512]{1,0:T(8,128)(2,1)S(1)} %get-tuple-element.147), channel_id=1, source_target_pairs={{0,14},{1,15},{2,0},{3,1},{4,2},{5,3},{6,4},{7,5},{8,6},{9,7},{10,... | collective-permute-start | bytes 294920 | tf_op jit(solution)/shard_map/ppermute | solution.py:379
  94.4 1.6 %collective-permute-done.27.refs_3_ = bf16[96,512]{1,0:T(8,128)(2,1)S(1)} collective-permute-done((bf16[96,512]{1,0:T(8,128)(2,1)S(1)}, bf16[96,512]{1,0:T(8,128)(2,1)S(1)}, u32[]{:S(2)}, u32[]{:S(2)}) %collective-permute-start.27) | collective-permute-done | bytes 98336 | tf_op jit(solution)/shard_map/ppermute | solution.py:379
  97.3 2.7 %scatter_lists.1 = bf16[2048,512]{1,0:T(8,128)(2,1)} custom-call(s32[1]{0:T(128)} %bitcast.me_ref, s32[16,48]{1,0:T(8,128)S(1)} %bitcast.37, bf16[48,512]{1,0:T(8,128)(2,1)S(1)} %get-tuple-element.144.refs_0_, bf16[48,512]{1,0:T(8,128)(2,1)S(1)} %collective-permute-done.16.refs_1_, bf16[96,512]{1,0:T(8,128)(2,1)S(1)} %collective-permute-done.26.refs_2_, ...), custom_call_target="tpu_custom_call" | custom-call | tf_op jit(solution)/shard_map/scatter_lists/pallas_call | solution.py:692
  (85 shorter events, 12.4 us)
Async XLA Ops:
  4.3 9.6 %collective-permute-start.2 = (bf16[48,512]{1,0:T(8,128)(2,1)}, bf16[48,512]{1,0:T(8,128)(2,1)S(1)}, u32[]{:S(2)}, u32[]{:S(2)}) collective-permute-start(bf16[48,512]{1,0:T(8,128)(2,1)} %get-tuple-element.85), channel_id=1, source_target_pairs={{0,12},{1,13},{2,14},{3,15},{4,8},{5,9},{6,10},{7,11},{8,4},{9,5},... | collective-permute-start | bytes 147464 | tf_op jit(solution)/shard_map/ppermute | solution.py:379
  9.4 7.7 %collective-permute-start.1 = (bf16[48,512]{1,0:T(8,128)(2,1)}, bf16[48,512]{1,0:T(8,128)(2,1)S(1)}, u32[]{:S(2)}, u32[]{:S(2)}) collective-permute-start(bf16[48,512]{1,0:T(8,128)(2,1)} %get-tuple-element.85), channel_id=1, source_target_pairs={{0,8},{1,9},{2,10},{3,11},{4,12},{5,13},{6,14},{7,15},{8,0},{9,1},... | collective-permute-start | bytes 147464 | tf_op jit(solution)/shard_map/ppermute | solution.py:379
  9.4 7.7 %collective-permute-start = (bf16[48,512]{1,0:T(8,128)(2,1)}, bf16[48,512]{1,0:T(8,128)(2,1)S(1)}, u32[]{:S(2)}, u32[]{:S(2)}) collective-permute-start(bf16[48,512]{1,0:T(8,128)(2,1)} %get-tuple-element.85), channel_id=1, source_target_pairs={{0,4},{1,5},{2,6},{3,7},{4,0},{5,1},{6,2},{7,3},{8,12},{9,13},{10,... | collective-permute-start | bytes 147464 | tf_op jit(solution)/shard_map/ppermute | solution.py:379
  10.0 11.6 %collective-permute-start.7 = (bf16[48,512]{1,0:T(8,128)(2,1)}, bf16[48,512]{1,0:T(8,128)(2,1)S(1)}, u32[]{:S(2)}, u32[]{:S(2)}) collective-permute-start(bf16[48,512]{1,0:T(8,128)(2,1)} %get-tuple-element.91), channel_id=1, source_target_pairs={{0,13},{1,4},{2,15},{3,6},{4,1},{5,8},{6,3},{7,10},{8,5},{9,12},{1... | collective-permute-start | bytes 147464 | tf_op jit(solution)/shard_map/ppermute | solution.py:379
  12.4 9.3 %collective-permute-start.5 = (bf16[96,512]{1,0:T(8,128)(2,1)}, bf16[96,512]{1,0:T(8,128)(2,1)S(1)}, u32[]{:S(2)}, u32[]{:S(2)}) collective-permute-start(bf16[96,512]{1,0:T(8,128)(2,1)} %get-tuple-element.89), channel_id=1, source_target_pairs={{0,2},{1,3},{2,4},{3,5},{4,6},{5,7},{6,8},{7,9},{8,10},{9,11},{10,... | collective-permute-start | bytes 294920 | tf_op jit(solution)/shard_map/ppermute | solution.py:379
  13.9 7.8 %collective-permute-start.6 = (bf16[96,512]{1,0:T(8,128)(2,1)}, bf16[96,512]{1,0:T(8,128)(2,1)S(1)}, u32[]{:S(2)}, u32[]{:S(2)}) collective-permute-start(bf16[96,512]{1,0:T(8,128)(2,1)} %get-tuple-element.90), channel_id=1, source_target_pairs={{0,14},{1,15},{2,0},{3,1},{4,2},{5,3},{6,4},{7,5},{8,6},{9,7},{10,... | collective-permute-start | bytes 294920 | tf_op jit(solution)/shard_map/ppermute | solution.py:379
  18.0 3.7 %collective-permute-start.4 = (bf16[192,512]{1,0:T(8,128)(2,1)S(1)}, bf16[192,512]{1,0:T(8,128)(2,1)S(1)}, u32[]{:S(2)}, u32[]{:S(2)}) collective-permute-start(bf16[192,512]{1,0:T(8,128)(2,1)S(1)} %pad_maximum_fusion.refs_7_), channel_id=1, source_target_pairs={{0,1},{1,0},{2,3},{3,2},{4,5},{5,4},{6,7},{7,6},{8,9},{9,8},{10,11... | collective-permute-start | bytes 589832 | tf_op jit(solution)/shard_map/ppermute | solution.py:379
  18.1 7.3 %collective-permute-start.3 = (bf16[192,512]{1,0:T(8,128)(2,1)S(1)}, bf16[192,512]{1,0:T(8,128)(2,1)S(1)}, u32[]{:S(2)}, u32[]{:S(2)}) collective-permute-start(bf16[192,512]{1,0:T(8,128)(2,1)S(1)} %pad_maximum_fusion.refs_7_), channel_id=1, source_target_pairs={{0,2},{1,3},{2,0},{3,1},{4,6},{5,7},{6,4},{7,5},{8,10},{9,11},{10,... | collective-permute-start | bytes 589832 | tf_op jit(solution)/shard_map/ppermute | solution.py:379
  36.4 19.6 %collective-permute-start.12 = (bf16[2,384,512]{2,1,0:T(8,128)(2,1)S(1)}, bf16[2,384,512]{2,1,0:T(8,128)(2,1)S(1)}, u32[]{:S(2)}, u32[]{:S(2)}) collective-permute-start(bf16[2,384,512]{2,1,0:T(8,128)(2,1)S(1)} %get-tuple-element.102), channel_id=1, source_target_pairs={{0,2},{1,3},{2,0},{3,1},{4,6},{5,7},{6,4},{7,5},{8,10},{9,11},{10,... | collective-permute-start | bytes 2359304 | tf_op jit(solution)/shard_map/ppermute | solution.py:379
  56.2 3.1 %collective-permute-start.13 = (bf16[2,320,512]{2,1,0:T(8,128)(2,1)S(1)}, bf16[2,320,512]{2,1,0:T(8,128)(2,1)S(1)}, u32[]{:S(2)}, u32[]{:S(2)}) collective-permute-start(bf16[2,320,512]{2,1,0:T(8,128)(2,1)S(1)} %get-tuple-element.121), channel_id=1, source_target_pairs={{0,1},{1,0},{2,3},{3,2},{4,5},{5,4},{6,7},{7,6},{8,9},{9,8},{10,11... | collective-permute-start | bytes 1966088 | tf_op jit(solution)/shard_map/ppermute | solution.py:379
  57.0 3.3 %collective-permute-start.14 = (bf16[2,384,512]{2,1,0:T(8,128)(2,1)S(1)}, bf16[2,384,512]{2,1,0:T(8,128)(2,1)S(1)}, u32[]{:S(2)}, u32[]{:S(2)}) collective-permute-start(bf16[2,384,512]{2,1,0:T(8,128)(2,1)S(1)} %get-tuple-element.123), channel_id=1, source_target_pairs={{0,1},{1,0},{2,3},{3,2},{4,5},{5,4},{6,7},{7,6},{8,9},{9,8},{10,11... | collective-permute-start | bytes 2359304 | tf_op jit(solution)/shard_map/ppermute | solution.py:379
  57.5 3.1 %collective-permute-start.16 = (bf16[48,512]{1,0:T(8,128)(2,1)S(1)}, bf16[48,512]{1,0:T(8,128)(2,1)S(1)}, u32[]{:S(2)}, u32[]{:S(2)}) collective-permute-start(bf16[48,512]{1,0:T(8,128)(2,1)S(1)} %get-tuple-element.126), channel_id=1, source_target_pairs={{0,1},{1,0},{2,3},{3,2},{4,5},{5,4},{6,7},{7,6},{8,9},{9,8},{10,11... | collective-permute-start | bytes 147464 | tf_op jit(solution)/shard_map/ppermute | solution.py:379
  60.6 14.4 %collective-permute-start.19 = (bf16[48,512]{1,0:T(8,128)(2,1)S(1)}, bf16[48,512]{1,0:T(8,128)(2,1)S(1)}, u32[]{:S(2)}, u32[]{:S(2)}) collective-permute-start(bf16[48,512]{1,0:T(8,128)(2,1)S(1)} %get-tuple-element.135), channel_id=1, source_target_pairs={{0,13},{1,4},{2,15},{3,6},{4,1},{5,8},{6,3},{7,10},{8,5},{9,12},{1... | collective-permute-start | bytes 147464 | tf_op jit(solution)/shard_map/ppermute | solution.py:379
  64.4 10.5 %collective-permute-start.17 = (bf16[320,512]{1,0:T(8,128)(2,1)S(1)}, bf16[320,512]{1,0:T(8,128)(2,1)S(1)}, u32[]{:S(2)}, u32[]{:S(2)}) collective-permute-start(bf16[320,512]{1,0:T(8,128)(2,1)S(1)} %get-tuple-element.133), channel_id=1, source_target_pairs={{0,2},{1,3},{2,0},{3,1},{4,6},{5,7},{6,4},{7,5},{8,10},{9,11},{10,... | collective-permute-start | bytes 983048 | tf_op jit(solution)/shard_map/ppermute | solution.py:379
  64.8 6.3 %collective-permute-start.18 = (bf16[192,512]{1,0:T(8,128)(2,1)S(1)}, bf16[192,512]{1,0:T(8,128)(2,1)S(1)}, u32[]{:S(2)}, u32[]{:S(2)}) collective-permute-start(bf16[192,512]{1,0:T(8,128)(2,1)S(1)} %bitcast.40), channel_id=1, source_target_pairs={{0,4},{1,5},{2,6},{3,7},{4,0},{5,1},{6,2},{7,3},{8,12},{9,13},{10,... | collective-permute-start | bytes 589832 | tf_op jit(solution)/shard_map/ppermute | solution.py:379
  64.8 14.3 %collective-permute-start.21 = (bf16[384,512]{1,0:T(8,128)(2,1)S(1)}, bf16[384,512]{1,0:T(8,128)(2,1)S(1)}, u32[]{:S(2)}, u32[]{:S(2)}) collective-permute-start(bf16[384,512]{1,0:T(8,128)(2,1)S(1)} %get-tuple-element.139), channel_id=1, source_target_pairs={{0,2},{1,3},{2,0},{3,1},{4,6},{5,7},{6,4},{7,5},{8,10},{9,11},{10,... | collective-permute-start | bytes 1179656 | tf_op jit(solution)/shard_map/ppermute | solution.py:379
  75.1 6.5 %collective-permute-start.20 = (bf16[160,512]{1,0:T(8,128)(2,1)S(1)}, bf16[160,512]{1,0:T(8,128)(2,1)S(1)}, u32[]{:S(2)}, u32[]{:S(2)}) collective-permute-start(bf16[160,512]{1,0:T(8,128)(2,1)S(1)} %bitcast.41), channel_id=1, source_target_pairs={{0,4},{1,5},{2,6},{3,7},{4,0},{5,1},{6,2},{7,3},{8,12},{9,13},{10,... | collective-permute-start | bytes 491528 | tf_op jit(solution)/shard_map/ppermute | solution.py:379
  75.2 6.4 %collective-permute-start.22 = (bf16[96,512]{1,0:T(8,128)(2,1)S(1)}, bf16[96,512]{1,0:T(8,128)(2,1)S(1)}, u32[]{:S(2)}, u32[]{:S(2)}) collective-permute-start(bf16[96,512]{1,0:T(8,128)(2,1)S(1)} %get-tuple-element.177), channel_id=1, source_target_pairs={{0,8},{1,9},{2,10},{3,11},{4,12},{5,13},{6,14},{7,15},{8,0},{9,1},... | collective-permute-start | bytes 294920 | tf_op jit(solution)/shard_map/ppermute | solution.py:379
  81.6 9.8 %collective-permute-start.30 = (bf16[80,512]{1,0:T(8,128)(2,1)S(1)}, bf16[80,512]{1,0:T(8,128)(2,1)S(1)}, u32[]{:S(2)}, u32[]{:S(2)}) collective-permute-start(bf16[80,512]{1,0:T(8,128)(2,1)S(1)} %get-tuple-element.179), channel_id=1, source_target_pairs={{0,8},{1,9},{2,10},{3,11},{4,12},{5,13},{6,14},{7,15},{8,0},{9,1},... | collective-permute-start | bytes 245768 | tf_op jit(solution)/shard_map/ppermute | solution.py:379
  82.5 17.5 %collective-permute-start.25 = (bf16[96,512]{1,0:T(8,128)(2,1)S(1)}, bf16[96,512]{1,0:T(8,128)(2,1)S(1)}, u32[]{:S(2)}, u32[]{:S(2)}) collective-permute-start(bf16[96,512]{1,0:T(8,128)(2,1)S(1)} %get-tuple-element.169), channel_id=1, source_target_pairs={{0,12},{1,13},{2,14},{3,15},{4,8},{5,9},{6,10},{7,11},{8,4},{9,5},... | collective-permute-start | bytes 294920 | tf_op jit(solution)/shard_map/ppermute | solution.py:379
  85.4 14.6 %collective-permute-start.24 = (bf16[96,512]{1,0:T(8,128)(2,1)S(1)}, bf16[96,512]{1,0:T(8,128)(2,1)S(1)}, u32[]{:S(2)}, u32[]{:S(2)}) collective-permute-start(bf16[96,512]{1,0:T(8,128)(2,1)S(1)} %get-tuple-element.170), channel_id=1, source_target_pairs={{0,8},{1,9},{2,10},{3,11},{4,12},{5,13},{6,14},{7,15},{8,0},{9,1},... | collective-permute-start | bytes 294920 | tf_op jit(solution)/shard_map/ppermute | solution.py:379
  85.4 14.6 %collective-permute-start.23 = (bf16[96,512]{1,0:T(8,128)(2,1)S(1)}, bf16[96,512]{1,0:T(8,128)(2,1)S(1)}, u32[]{:S(2)}, u32[]{:S(2)}) collective-permute-start(bf16[96,512]{1,0:T(8,128)(2,1)S(1)} %get-tuple-element.171), channel_id=1, source_target_pairs={{0,4},{1,5},{2,6},{3,7},{4,0},{5,1},{6,2},{7,3},{8,12},{9,13},{10,... | collective-permute-start | bytes 294920 | tf_op jit(solution)/shard_map/ppermute | solution.py:379
  87.0 7.4 %collective-permute-start.26 = (bf16[96,512]{1,0:T(8,128)(2,1)S(1)}, bf16[96,512]{1,0:T(8,128)(2,1)S(1)}, u32[]{:S(2)}, u32[]{:S(2)}) collective-permute-start(bf16[96,512]{1,0:T(8,128)(2,1)S(1)} %get-tuple-element.146), channel_id=1, source_target_pairs={{0,2},{1,3},{2,4},{3,5},{4,6},{5,7},{6,8},{7,9},{8,10},{9,11},{10,... | collective-permute-start | bytes 294920 | tf_op jit(solution)/shard_map/ppermute | solution.py:379
  91.4 4.6 %collective-permute-start.27 = (bf16[96,512]{1,0:T(8,128)(2,1)S(1)}, bf16[96,512]{1,0:T(8,128)(2,1)S(1)}, u32[]{:S(2)}, u32[]{:S(2)}) collective-permute-start(bf16[96,512]{1,0:T(8,128)(2,1)S(1)} %get-tuple-element.147), channel_id=1, source_target_pairs={{0,14},{1,15},{2,0},{3,1},{4,2},{5,3},{6,4},{7,5},{8,6},{9,7},{10,... | collective-permute-start | bytes 294920 | tf_op jit(solution)/shard_map/ppermute | solution.py:379
  (19 other events, 174.2 us)

commit v12 on v10

--- a/solution.py
+++ b/solution.py
@@ -11,6 +11,7 @@
 STEP = 1024
 SUB = 512
 LANES = 128
+BLOCK = 256
 GRID_PARTS = 4
 NEAR = 3
 BF16 = jnp.bfloat16
@@ -74,15 +75,34 @@
     return jnp.concatenate(rows, axis=1)
 
 
+def in_block(indices, first):
+    place = indices - first
+    return jnp.where((place >= 0) & (place < BLOCK), place, -1).astype(F32).astype(BF16)
+
+
 def hot_rows(row, width, first=0):
-    column = as_column(row).astype(jnp.int32) - first
-    along = lax.broadcasted_iota(jnp.int32, (row.shape[1], width), 1)
-    return (column == along).astype(F32).astype(BF16)
+    column = as_column(row).astype(jnp.int32)
+    count = row.shape[1]
+    one = jnp.ones((), BF16)
+    zero = jnp.zeros((), BF16)
+    blocks = []
+    for start in range(0, width, BLOCK):
+        size = min(BLOCK, width - start)
+        along = lax.broadcasted_iota(jnp.int32, (count, size), 1).astype(F32).astype(BF16)
+        blocks.append(jnp.where(in_block(column, first + start) == along, one, zero))
+    return jnp.concatenate(blocks, axis=1)
 
 
 def hot_columns(row, height):
-    down = lax.broadcasted_iota(jnp.int32, (height, row.shape[1]), 0)
-    return (row == down).astype(F32).astype(BF16)
+    count = row.shape[1]
+    one = jnp.ones((), BF16)
+    zero = jnp.zeros((), BF16)
+    blocks = []
+    for start in range(0, height, BLOCK):
+        size = min(BLOCK, height - start)
+        down = lax.broadcasted_iota(jnp.int32, (size, count), 0).astype(F32).astype(BF16)
+        blocks.append(jnp.where(in_block(row, start) == down, one, zero))
+    return jnp.concatenate(blocks, axis=0)
 
 
 def live_only(row, first, count):
@@ -216,8 +236,8 @@
     near_refs, far_refs = refs[:7], refs[7:11]
     (w_sender_ref, w_out_ref, w_node_in_ref, w_node_out_ref, mesh_ref, cotangent_ref) = refs[11:17]
     (received_ref, hidden_ref, slope_ref, norm_ref, inverse_ref) = refs[17:22]
-    (send_ref, keep_ref, d_aggregate_ref, d_mesh_ref) = refs[22:26]
-    (slot_proj, aggregate, grad_in, grad_out) = refs[26:]
+    (send_ref, keep_ref, d_aggregate_ref, d_centred_ref, d_mesh_ref) = refs[22:27]
+    (slot_proj, aggregate, grad_in, grad_out, w_centred) = refs[27:]
     step = pl.program_id(0)
     me = me_ref[0]
     cap = near_refs[0].shape[0]
@@ -226,6 +246,8 @@
     @pl.when(step == 0)
     def _():
         aggregate[...] = jnp.zeros_like(aggregate)
+        w_out = w_out_ref[...].astype(F32)
+        w_centred[...] = (w_out - jnp.mean(w_out, axis=1, keepdims=True)).astype(BF16)
         w_sender = w_sender_ref[...]
 
         def place(owner, rows, projected):
@@ -257,9 +279,10 @@
             hidden = hidden.astype(BF16)
             hidden_ref[part, :] = hidden
             slope_ref[part, :] = slope.astype(BF16)
-            projs.append(dot(hidden, w_out_ref[...]))
+            projs.append(dot(hidden, w_centred[...]))
         for (start, part), proj in zip(parts, projs):
-            normed, inverse = layer_norm(proj)
+            inverse = lax.rsqrt(jnp.mean(proj * proj, axis=1, keepdims=True) + 1e-05)
+            normed = proj * inverse
             norm_ref[part, :] = normed.astype(BF16)
             inverse_ref[0, :, part] = as_row(inverse)
             edge_new = (edge_ref[part, :].astype(F32) + normed).astype(BF16)
@@ -278,7 +301,10 @@
         d_proj = norm_back(normed, inverse, upstream).astype(BF16)
         d_pre = (contract_cols(d_proj, w_node_out_ref[...]) * slope).astype(BF16)
         d_mesh_ref[...] = upstream + contract_cols(d_pre, w_node_in_ref[:width, :])
-        d_aggregate_ref[...] = contract_cols(d_pre, w_node_in_ref[width:, :]).astype(BF16)
+        d_aggregate = contract_cols(d_pre, w_node_in_ref[width:, :]).astype(BF16)
+        d_aggregate_ref[...] = d_aggregate
+        d_aggregate = d_aggregate.astype(F32)
+        d_centred_ref[...] = (d_aggregate - jnp.mean(d_aggregate, axis=1, keepdims=True)).astype(BF16)
         grad_out[...] = contract_rows(hidden, d_proj)
         grad_in[:width, :] = contract_rows(mesh, d_pre)
         grad_in[width:, :] = contract_rows(summed, d_pre)
@@ -294,7 +320,7 @@
 
 def backward_kernel(peers, me_ref, count_ref, src_ref, dst_ref, inverse_ref, *refs):
     (hidden_ref, slope_ref, norm_ref, edge_ref) = refs[:4]
-    (d_aggregate_ref, received_ref, mesh_ref, d_mesh_ref) = refs[4:8]
+    (d_centred_ref, received_ref, mesh_ref, d_mesh_ref) = refs[4:8]
     (w_sender_ref, w_receiver_ref, w_out_ref) = refs[8:11]
     (d_pre_ref, mesh_grad_ref, slot_send_ref, slot_keep_ref, edge_send_ref, edge_keep_ref) = refs[11:17]
     near_refs = refs[17:22]
@@ -319,7 +345,7 @@
             first = step * STEP + start
             live = count_ref[0] * TILE
             receivers = live_only(dst_ref[0, :, part], first, live)
-            upstreams.append(dot(hot_rows(receivers, mesh_count), d_aggregate_ref[...]))
+            upstreams.append(dot(hot_rows(receivers, mesh_count), d_centred_ref[...]))
             senders = live_only(src_ref[0, :, part], first, live)
             columns.append(
                 jnp.concatenate([hot_columns(senders, slots), hot_columns(receivers, mesh_count)], axis=0)
@@ -328,7 +354,9 @@
         d_hiddens = []
         for (start, part), upstream in zip(parts, upstreams):
             inverse = as_column(inverse_ref[0, :, part])
-            d_proj = norm_back(norm_ref[part, :].astype(F32), inverse, upstream).astype(BF16)
+            norm = norm_ref[part, :].astype(F32)
+            second = jnp.mean(upstream * norm, axis=1, keepdims=True)
+            d_proj = (inverse * (upstream - norm * second)).astype(BF16)
             d_projs.append(d_proj)
             d_hiddens.append(contract_cols(d_proj, w_out_ref[...]))
         for (start, part), d_proj, d_hidden, column in zip(parts, d_projs, d_hiddens, columns):
@@ -551,7 +579,7 @@
     far_both = send(far_next, by_xor(peers, 1))
 
     node_shape, node_spec = halves(w_node_in.shape[0] // peers + w_node_out.shape[0] // peers)
-    (received, hidden, slope, norm, inverse, node_send, node_keep, d_aggregate, d_mesh) = pl.pallas_call(
+    (received, hidden, slope, norm, inverse, node_send, node_keep, d_aggregate, d_centred, d_mesh) = pl.pallas_call(
         functools.partial(forward_kernel, peers),
         grid=(tiles,),
         in_specs=[smem, smem, index_tile, index_tile, tile_of(width), tile_of(width)]
@@ -563,17 +591,19 @@
         + [tile_of(width)] * 3
         + [index_tile]
         + node_spec
-        + [whole((mesh_count, width))] * 2,
+        + [whole((mesh_count, width))] * 3,
         out_shape=[jax.ShapeDtypeStruct((slots, width), BF16)]
         + [jax.ShapeDtypeStruct((edges, width), BF16)] * 3
         + [jax.ShapeDtypeStruct((tiles, 1, STEP), F32)]
         + node_shape
-        + [jax.ShapeDtypeStruct((mesh_count, width), BF16), jax.ShapeDtypeStruct((mesh_count, width), F32)],
+        + [jax.ShapeDtypeStruct((mesh_count, width), BF16)] * 2
+        + [jax.ShapeDtypeStruct((mesh_count, width), F32)],
         scratch_shapes=[
             pltpu.VMEM((slots, width), BF16),
             pltpu.VMEM((mesh_count, width), F32),
             pltpu.VMEM(w_node_in.shape, F32),
             pltpu.VMEM(w_node_out.shape, F32),
+            pltpu.VMEM(w_edge_out.shape, BF16),
         ],
         compiler_params=params,
         name="forward",
@@ -639,7 +669,7 @@
         slope,
         norm,
         edge_latent,
-        d_aggregate,
+        d_centred,
         received,
         mesh_latent,
         d_mesh,
@@ -648,20 +678,20 @@
         w_edge_out,
     )
     (d_pre, mesh_grad, slot_send, slot_keep, edge_send, edge_keep), returns = results[:6], results[6:]
-    (node_next, node_kept, slot_send, slot_keep, edge_send, edge_keep, returns, d_pre) = lax.optimization_barrier(
-        (node_next, node_kept, slot_send, slot_keep, edge_send, edge_keep, returns, d_pre)
-    )
     slot_next, slot_kept = first_sum(peers, 1, slot_send, slot_keep)
     edge_next, edge_kept = first_sum(peers, 1, edge_send, edge_keep)
     node_pieces = next_sum(peers, 1, node_next, node_kept)
-    bundles = [send(returns[2], by_shift(peers, 2)), send(returns[3], by_shift(peers, -2))]
     other = send(returns[1], by_xor(peers, 1))
-    (slot_next, slot_kept, edge_next, edge_kept, node_pieces, bundles, other, d_pre) = lax.optimization_barrier(
-        (slot_next, slot_kept, edge_next, edge_kept, node_pieces, bundles, other, d_pre)
+    slot_pieces = next_sum(peers, 2, slot_next, slot_kept)
+    (node_pieces, edge_next, edge_kept, other, across) = lax.optimization_barrier(
+        (node_pieces, edge_next, edge_kept, other, returns[4])
     )
-    slot_pieces = next_sum(peers, 2, slot_next, slot_kept)
+    node_pieces = halve_sum(peers, node_pieces)
+    (slot_pieces, edge_next, edge_kept, across, node_pieces, d_pre) = lax.optimization_barrier(
+        (slot_pieces, edge_next, edge_kept, across, node_pieces, d_pre)
+    )
     edge_pieces = next_sum(peers, 2, edge_next, edge_kept)
-    node_terms = last_terms(peers, node_pieces)
+    slot_half = halve_sum(peers, slot_pieces)
     edge_grad = pl.pallas_call(
         edges_kernel,
         grid=(tiles,),
@@ -674,13 +704,15 @@
         ),
         name="edge_grad",
     )(tile_count, dst, d_pre, d_aggregate, w_edge_in)
-    (slot_pieces, node_terms, across, bundles, edge_grad) = lax.optimization_barrier(
-        (slot_pieces, node_terms, returns[4], bundles, edge_grad)
+    slot_half, node_pieces, across, edge_grad, to_after, to_before = lax.optimization_barrier(
+        (slot_half, node_pieces, across, edge_grad, returns[2], returns[3])
     )
-    returned = [returns[0], other, *bundles, send(across, across_chips(peers))] + core_bundles(peers, bundles)
-    slot_half = halve_sum(peers, slot_pieces)
-    slot_half, edge_pieces, returned = lax.optimization_barrier((slot_half, edge_pieces, returned))
+    bundles = [send(to_after, by_shift(peers, 2)), send(to_before, by_shift(peers, -2))]
+    across = send(across, across_chips(peers))
+    node_terms = rest_terms(peers, node_pieces)
     slot_terms = rest_terms(peers, slot_half)
+    returned = [returns[0], other, *bundles, across] + core_bundles(peers, bundles)
+    edge_pieces, returned = lax.optimization_barrier((edge_pieces, returned))
     edge_terms = last_terms(peers, edge_pieces)
     node_terms, slot_terms = lax.optimization_barrier((node_terms, slot_terms))
     node_rows = w_node_in.shape[0] // peers

time: 104 us -> 103 us (level); the launches traced: 103 us -> 103 us
  waiting for transfers between devices: 23 us -> 25 us
    ppermute x32 -> x31, waiting for transfers between devices: 23 us -> 25 us  [send(): return lax.ppermute(values, 'lon', perm)]
    ppermute x32 -> x31, starting transfers between devices: 33.9 us -> 32.9 us  [send(): return lax.ppermute(values, 'lon', perm)]
  transfers between devices with their start and end apart: 32 -> 31, of which waited for: 9 -> 7; matrix products, arithmetic and copies ran while one was open for 3% -> 3% of each run, Pallas kernels for 24% -> 24%
where the time goes in v12:
time: 103 us
  Pallas kernels  39.8 us (39%)
  starting transfers between devices  32.9 us (32%)
  waiting for transfers between devices  25 us (24%)
  other arithmetic  3.8 us (4%)
  between operations  1.71 us (2%)
    ppermute x31, starting transfers between devices, send(): return lax.ppermute(values, 'lon', perm)  32.9 us
    ppermute x31, waiting for transfers between devices, send(): return lax.ppermute(values, 'lon', perm)  25 us
    pallas_call x1, Pallas kernels, on_device(): pl.pallas_call(functools.partial(backward_kernel, peers), grid=(tiles,),...  14.3 us
    pallas_call x1, Pallas kernels, on_device(): pl.pallas_call(functools.partial(forward_kernel, peers), grid=(tiles,), i...  11.6 us
    pallas_call x1, Pallas kernels, on_device(): pl.pallas_call(edges_kernel, grid=(tiles,), in_specs=[smem, index_tile, t...  4.16 us
    pallas_call x1, Pallas kernels, on_device(): pl.pallas_call(gather_kernel, in_specs=[smem, hbm, hbm], out_specs=near_s...  3.55 us
    pallas_call x1, Pallas kernels, on_device(): pl.pallas_call(local_kernel, grid=(tiles,), in_specs=[index_tile, tile_of...  3.42 us
    pallas_call x1, Pallas kernels, on_device(): pl.pallas_call(functools.partial(scatter_kernel, out_rows), grid=(2,), in...  2.73 us
  transfers between devices with their start and end apart: 31, of which 7 were waited for; matrix products, arithmetic and copies ran while one was open for 3% of the time, Pallas kernels for 24%

profile of v12, /device:TPU:0, one launch (start us, length us, event | category | flops | bytes accessed | tf_op | source)
XLA Modules:
  0.0 103.3 jit_solution(213310349449947332)
XLA Ops:
  0.7 3.6 %gather_lists.1 = (bf16[48,512]{1,0:T(8,128)(2,1)}, bf16[48,512]{1,0:T(8,128)(2,1)}, bf16[96,512]{1,0:T(8,128)(2,1)}, bf16[96,512]{1,0:T(8,128)(2,1)}, bf16[48,512]{1,0:T(8,128)(2,1)}, /*index=5*/bf16[48,512]{1,0:T(8,128)(2,1)}) custom-call(s32[1]{0:T(128)} %bitcast.me_ref, s32[16,48]{1,0:T(8,128)} %bitcast.42, bf16[2048,512]{1,0:T(8,128)(2,1)} %grid_hbm.1), custom_call_target="tpu_custom_call" | custom-call | flops 32212254720 | bytes 2097152 | tf_op jit(solution)/shard_map/gather_lists/pallas_call | solution.py:536
  4.2 5.1 %collective-permute-start.2 = (bf16[48,512]{1,0:T(8,128)(2,1)}, bf16[48,512]{1,0:T(8,128)(2,1)S(1)}, u32[]{:S(2)}, u32[]{:S(2)}) collective-permute-start(bf16[48,512]{1,0:T(8,128)(2,1)} %get-tuple-element.78), channel_id=1, source_target_pairs={{0,12},{1,13},{2,14},{3,15},{4,8},{5,9},{6,10},{7,11},{8,4},{9,5},... | collective-permute-start | bytes 147464 | tf_op jit(solution)/shard_map/ppermute | solution.py:407
  10.0 2.3 %collective-permute-start.7 = (bf16[48,512]{1,0:T(8,128)(2,1)}, bf16[48,512]{1,0:T(8,128)(2,1)S(1)}, u32[]{:S(2)}, u32[]{:S(2)}) collective-permute-start(bf16[48,512]{1,0:T(8,128)(2,1)} %get-tuple-element.84), channel_id=1, source_target_pairs={{0,13},{1,4},{2,15},{3,6},{4,1},{5,8},{6,3},{7,10},{8,5},{9,12},{1... | collective-permute-start | bytes 147464 | tf_op jit(solution)/shard_map/ppermute | solution.py:407
  12.3 1.5 %collective-permute-start.5 = (bf16[96,512]{1,0:T(8,128)(2,1)}, bf16[96,512]{1,0:T(8,128)(2,1)S(1)}, u32[]{:S(2)}, u32[]{:S(2)}) collective-permute-start(bf16[96,512]{1,0:T(8,128)(2,1)} %get-tuple-element.82), channel_id=1, source_target_pairs={{0,2},{1,3},{2,4},{3,5},{4,6},{5,7},{6,8},{7,9},{8,10},{9,11},{10,... | collective-permute-start | bytes 294920 | tf_op jit(solution)/shard_map/ppermute | solution.py:407
  13.9 3.2 %collective-permute-start.6 = (bf16[96,512]{1,0:T(8,128)(2,1)}, bf16[96,512]{1,0:T(8,128)(2,1)S(1)}, u32[]{:S(2)}, u32[]{:S(2)}) collective-permute-start(bf16[96,512]{1,0:T(8,128)(2,1)} %get-tuple-element.83), channel_id=1, source_target_pairs={{0,14},{1,15},{2,0},{3,1},{4,2},{5,3},{6,4},{7,5},{8,6},{9,7},{10,... | collective-permute-start | bytes 294920 | tf_op jit(solution)/shard_map/ppermute | solution.py:407
  18.2 3.4 %edge_local.1.local_ref = bf16[3072,512]{1,0:T(8,128)(2,1)S(1)} custom-call(s32[3,1,1024]{2,1,0:T(1,128)S(1)} %bitcast.36, bf16[3072,512]{1,0:T(8,128)(2,1)S(1)} %copy-done.1, bf16[256,512]{1,0:T(8,128)(2,1)S(1)} %copy-done.2, bf16[1536,512]{1,0:T(8,128)(2,1)S(1)} %copy-done, bf16[1536,512]{1,0:T(8,128)(2,1)S(1)} %copy-done), custom_call_target="tpu_custom_call" | custom-call | flops 2415919104 | bytes 6291456 | tf_op jit(solution)/shard_map/edge_local/pallas_call | solution.py:562
  21.6 3.7 %collective-permute-done.3.refs_9_ = bf16[192,512]{1,0:T(8,128)(2,1)S(1)} collective-permute-done((bf16[192,512]{1,0:T(8,128)(2,1)S(1)}, bf16[192,512]{1,0:T(8,128)(2,1)S(1)}, u32[]{:S(2)}, u32[]{:S(2)}) %collective-permute-start.3) | collective-permute-done | bytes 196640 | tf_op jit(solution)/shard_map/ppermute | solution.py:407
  27.3 11.6 %forward.1 = (bf16[768,512]{1,0:T(8,128)(2,1)S(1)}, bf16[3072,512]{1,0:T(8,128)(2,1)S(1)}, bf16[3072,512]{1,0:T(8,128)(2,1)S(1)}, bf16[3072,512]{1,0:T(8,128)(2,...) custom-call(s32[1]{0:T(128)} %bitcast.me_ref, ...), custom_call_target="tpu_custom_call" | custom-call | tf_op jit(solution)/shard_map/forward/pallas_call | solution.py:582
  39.3 14.3 %backward.1 = (bf16[3072,512]{1,0:T(8,128)(2,1)S(1)}, bf16[256,512]{1,0:T(8,128)(2,1)}, bf16[2,320,512]{2,1,0:T(8,128)(2,1)S(1)}, bf16[2,320,512]{2,1,0:T(8,128)...) custom-call(s32[1]{0:T(128)} %bitcast.me_ref, ...), custom_call_target="tpu_custom_call" | custom-call | flops 8858370048 | bytes 15728640 | tf_op jit(solution)/shard_map/backward/pallas_call | solution.py:633
  54.1 3.2 %collective-permute-done.14 = bf16[2,384,512]{2,1,0:T(8,128)(2,1)S(1)} collective-permute-done((bf16[2,384,512]{2,1,0:T(8,128)(2,1)S(1)}, bf16[2,384,512]{2,1,0:T(8,128)(2,1)S(1)}, u32[]{:S(2)}, u32[]{:S(2)}) %collective-permute-start.14) | collective-permute-done | bytes 786464 | tf_op jit(solution)/shard_map/ppermute | solution.py:407
  57.7 1.8 %collective-permute-start.13 = (bf16[320,512]{1,0:T(8,128)(2,1)S(1)}, bf16[320,512]{1,0:T(8,128)(2,1)S(1)}, u32[]{:S(2)}, u32[]{:S(2)}) collective-permute-start(bf16[320,512]{1,0:T(8,128)(2,1)S(1)} %fusion.8), channel_id=1, source_target_pairs={{0,2},{1,3},{2,0},{3,1},{4,6},{5,7},{6,4},{7,5},{8,10},{9,11},{10,... | collective-permute-start | bytes 983048 | tf_op jit(solution)/shard_map/ppermute | solution.py:407
  60.0 7.8 %collective-permute-done.13 = bf16[320,512]{1,0:T(8,128)(2,1)S(1)} collective-permute-done((bf16[320,512]{1,0:T(8,128)(2,1)S(1)}, bf16[320,512]{1,0:T(8,128)(2,1)S(1)}, u32[]{:S(2)}, u32[]{:S(2)}) %collective-permute-start.13) | collective-permute-done | bytes 327712 | tf_op jit(solution)/shard_map/ppermute | solution.py:407
  68.2 1.8 %collective-permute-start.19 = (bf16[384,512]{1,0:T(8,128)(2,1)S(1)}, bf16[384,512]{1,0:T(8,128)(2,1)S(1)}, u32[]{:S(2)}, u32[]{:S(2)}) collective-permute-start(bf16[384,512]{1,0:T(8,128)(2,1)S(1)} %get-tuple-element.115), channel_id=1, source_target_pairs={{0,2},{1,3},{2,0},{3,1},{4,6},{5,7},{6,4},{7,5},{8,10},{9,11},{10,... | collective-permute-start | bytes 1179656 | tf_op jit(solution)/shard_map/ppermute | solution.py:407
  70.0 4.2 %edge_grad.1 = bf16[3072,512]{1,0:T(8,128)(2,1)} custom-call(s32[1]{0:T(128)S(6)} %copy.23.count_ref, s32[3,1,1024]{2,1,0:T(1,128)S(1)} %bitcast.39, bf16[3072,512]{1,0:T(8,128)(2,1)S(1)} %get-tuple-element.121.d_pre_ref, bf16[256,512]{1,0:T(8,128)(2,1)S(1)} %get-tuple-element.122.d_aggregate_ref, bf16[1536,512]{1,0:T(8,128)(2,1)S(1)} %copy-done), custom_call_target="tpu_custom_call" | custom-call | flops 2415919104 | bytes 6291456 | tf_op jit(solution)/shard_map/edge_grad/pallas_call | solution.py:695
  74.2 1.6 %collective-permute-start.21 = (bf16[96,512]{1,0:T(8,128)(2,1)S(1)}, bf16[96,512]{1,0:T(8,128)(2,1)S(1)}, u32[]{:S(2)}, u32[]{:S(2)}) collective-permute-start(bf16[96,512]{1,0:T(8,128)(2,1)S(1)} %get-tuple-element.125), channel_id=1, source_target_pairs={{0,2},{1,3},{2,4},{3,5},{4,6},{5,7},{6,8},{7,9},{8,10},{9,11},{10,... | collective-permute-start | bytes 294920 | tf_op jit(solution)/shard_map/ppermute | solution.py:407
  75.8 3.2 %collective-permute-start.22 = (bf16[96,512]{1,0:T(8,128)(2,1)S(1)}, bf16[96,512]{1,0:T(8,128)(2,1)S(1)}, u32[]{:S(2)}, u32[]{:S(2)}) collective-permute-start(bf16[96,512]{1,0:T(8,128)(2,1)S(1)} %get-tuple-element.126), channel_id=1, source_target_pairs={{0,14},{1,15},{2,0},{3,1},{4,2},{5,3},{6,4},{7,5},{8,6},{9,7},{10,... | collective-permute-start | bytes 294920 | tf_op jit(solution)/shard_map/ppermute | solution.py:407
  79.1 3.0 %collective-permute-start.30 = (bf16[80,512]{1,0:T(8,128)(2,1)S(1)}, bf16[80,512]{1,0:T(8,128)(2,1)S(1)}, u32[]{:S(2)}, u32[]{:S(2)}) collective-permute-start(bf16[80,512]{1,0:T(8,128)(2,1)S(1)} %get-tuple-element.161), channel_id=1, source_target_pairs={{0,8},{1,9},{2,10},{3,11},{4,12},{5,13},{6,14},{7,15},{8,0},{9,1},... | collective-permute-start | bytes 245768 | tf_op jit(solution)/shard_map/ppermute | solution.py:407
  82.1 5.7 %collective-permute-done.30.refs_8_ = bf16[80,512]{1,0:T(8,128)(2,1)S(1)} collective-permute-done((bf16[80,512]{1,0:T(8,128)(2,1)S(1)}, bf16[80,512]{1,0:T(8,128)(2,1)S(1)}, u32[]{:S(2)}, u32[]{:S(2)}) %collective-permute-start.30) | collective-permute-done | bytes 81952 | tf_op jit(solution)/shard_map/ppermute | solution.py:407
  87.7 1.5 %collective-permute-start.23 = (bf16[48,512]{1,0:T(8,128)(2,1)S(1)}, bf16[48,512]{1,0:T(8,128)(2,1)S(1)}, u32[]{:S(2)}, u32[]{:S(2)}) collective-permute-start(bf16[48,512]{1,0:T(8,128)(2,1)S(1)} %get-tuple-element.127), channel_id=1, source_target_pairs={{0,13},{1,4},{2,15},{3,6},{4,1},{5,8},{6,3},{7,10},{8,5},{9,12},{1... | collective-permute-start | bytes 147464 | tf_op jit(solution)/shard_map/ppermute | solution.py:407
  90.5 2.6 %collective-permute-done.23.refs_4_ = bf16[48,512]{1,0:T(8,128)(2,1)S(1)} collective-permute-done((bf16[48,512]{1,0:T(8,128)(2,1)S(1)}, bf16[48,512]{1,0:T(8,128)(2,1)S(1)}, u32[]{:S(2)}, u32[]{:S(2)}) %collective-permute-start.23) | collective-permute-done | bytes 49184 | tf_op jit(solution)/shard_map/ppermute | solution.py:407
  93.2 1.0 collective-permute-start.28
  94.1 3.5 %collective-permute-start.26 = (bf16[96,512]{1,0:T(8,128)(2,1)S(1)}, bf16[96,512]{1,0:T(8,128)(2,1)S(1)}, u32[]{:S(2)}, u32[]{:S(2)}) collective-permute-start(bf16[96,512]{1,0:T(8,128)(2,1)S(1)} %get-tuple-element.153), channel_id=1, source_target_pairs={{0,4},{1,5},{2,6},{3,7},{4,0},{5,1},{6,2},{7,3},{8,12},{9,13},{10,... | collective-permute-start | bytes 294920 | tf_op jit(solution)/shard_map/ppermute | solution.py:407
  98.3 2.7 %scatter_lists.1 = bf16[2048,512]{1,0:T(8,128)(2,1)} custom-call(s32[1]{0:T(128)} %bitcast.me_ref, s32[16,48]{1,0:T(8,128)S(1)} %bitcast.43, bf16[48,512]{1,0:T(8,128)(2,1)S(1)} %get-tuple-element.129.refs_0_, bf16[48,512]{1,0:T(8,128)(2,1)S(1)} %collective-permute-done.17.refs_1_, bf16[96,512]{1,0:T(8,128)(2,1)S(1)} %collective-permute-done.21.refs_2_, ...), custom_call_target="tpu_custom_call" | custom-call | tf_op jit(solution)/shard_map/scatter_lists/pallas_call | solution.py:720
  101.0 1.6 %collective-permute-done.27 = bf16[96,512]{1,0:T(8,128)(2,1)S(1)} collective-permute-done((bf16[96,512]{1,0:T(8,128)(2,1)S(1)}, bf16[96,512]{1,0:T(8,128)(2,1)S(1)}, u32[]{:S(2)}, u32[]{:S(2)}) %collective-permute-start.27) | collective-permute-done | bytes 98336 | tf_op jit(solution)/shard_map/ppermute | solution.py:407
  (85 shorter events, 7.7 us)
Async XLA Ops:
  4.2 9.6 %collective-permute-start.2 = (bf16[48,512]{1,0:T(8,128)(2,1)}, bf16[48,512]{1,0:T(8,128)(2,1)S(1)}, u32[]{:S(2)}, u32[]{:S(2)}) collective-permute-start(bf16[48,512]{1,0:T(8,128)(2,1)} %get-tuple-element.78), channel_id=1, source_target_pairs={{0,12},{1,13},{2,14},{3,15},{4,8},{5,9},{6,10},{7,11},{8,4},{9,5},... | collective-permute-start | bytes 147464 | tf_op jit(solution)/shard_map/ppermute | solution.py:407
  9.3 7.7 %collective-permute-start.1 = (bf16[48,512]{1,0:T(8,128)(2,1)}, bf16[48,512]{1,0:T(8,128)(2,1)S(1)}, u32[]{:S(2)}, u32[]{:S(2)}) collective-permute-start(bf16[48,512]{1,0:T(8,128)(2,1)} %get-tuple-element.78), channel_id=1, source_target_pairs={{0,8},{1,9},{2,10},{3,11},{4,12},{5,13},{6,14},{7,15},{8,0},{9,1},... | collective-permute-start | bytes 147464 | tf_op jit(solution)/shard_map/ppermute | solution.py:407
  9.4 7.7 %collective-permute-start = (bf16[48,512]{1,0:T(8,128)(2,1)}, bf16[48,512]{1,0:T(8,128)(2,1)S(1)}, u32[]{:S(2)}, u32[]{:S(2)}) collective-permute-start(bf16[48,512]{1,0:T(8,128)(2,1)} %get-tuple-element.78), channel_id=1, source_target_pairs={{0,4},{1,5},{2,6},{3,7},{4,0},{5,1},{6,2},{7,3},{8,12},{9,13},{10,... | collective-permute-start | bytes 147464 | tf_op jit(solution)/shard_map/ppermute | solution.py:407
  10.0 11.6 %collective-permute-start.7 = (bf16[48,512]{1,0:T(8,128)(2,1)}, bf16[48,512]{1,0:T(8,128)(2,1)S(1)}, u32[]{:S(2)}, u32[]{:S(2)}) collective-permute-start(bf16[48,512]{1,0:T(8,128)(2,1)} %get-tuple-element.84), channel_id=1, source_target_pairs={{0,13},{1,4},{2,15},{3,6},{4,1},{5,8},{6,3},{7,10},{8,5},{9,12},{1... | collective-permute-start | bytes 147464 | tf_op jit(solution)/shard_map/ppermute | solution.py:407
  12.3 9.3 %collective-permute-start.5 = (bf16[96,512]{1,0:T(8,128)(2,1)}, bf16[96,512]{1,0:T(8,128)(2,1)S(1)}, u32[]{:S(2)}, u32[]{:S(2)}) collective-permute-start(bf16[96,512]{1,0:T(8,128)(2,1)} %get-tuple-element.82), channel_id=1, source_target_pairs={{0,2},{1,3},{2,4},{3,5},{4,6},{5,7},{6,8},{7,9},{8,10},{9,11},{10,... | collective-permute-start | bytes 294920 | tf_op jit(solution)/shard_map/ppermute | solution.py:407
  13.9 7.8 %collective-permute-start.6 = (bf16[96,512]{1,0:T(8,128)(2,1)}, bf16[96,512]{1,0:T(8,128)(2,1)S(1)}, u32[]{:S(2)}, u32[]{:S(2)}) collective-permute-start(bf16[96,512]{1,0:T(8,128)(2,1)} %get-tuple-element.83), channel_id=1, source_target_pairs={{0,14},{1,15},{2,0},{3,1},{4,2},{5,3},{6,4},{7,5},{8,6},{9,7},{10,... | collective-permute-start | bytes 294920 | tf_op jit(solution)/shard_map/ppermute | solution.py:407
  18.0 7.3 %collective-permute-start.3 = (bf16[192,512]{1,0:T(8,128)(2,1)S(1)}, bf16[192,512]{1,0:T(8,128)(2,1)S(1)}, u32[]{:S(2)}, u32[]{:S(2)}) collective-permute-start(bf16[192,512]{1,0:T(8,128)(2,1)S(1)} %pad_maximum_fusion.refs_7_), channel_id=1, source_target_pairs={{0,2},{1,3},{2,0},{3,1},{4,6},{5,7},{6,4},{7,5},{8,10},{9,11},{10,... | collective-permute-start | bytes 589832 | tf_op jit(solution)/shard_map/ppermute | solution.py:407
  39.0 18.4 %collective-permute-start.14 = (bf16[2,384,512]{2,1,0:T(8,128)(2,1)S(1)}, bf16[2,384,512]{2,1,0:T(8,128)(2,1)S(1)}, u32[]{:S(2)}, u32[]{:S(2)}) collective-permute-start(bf16[2,384,512]{2,1,0:T(8,128)(2,1)S(1)} %get-tuple-element.104), channel_id=1, source_target_pairs={{0,2},{1,3},{2,0},{3,1},{4,6},{5,7},{6,4},{7,5},{8,10},{9,11},{10,... | collective-permute-start | bytes 2359304 | tf_op jit(solution)/shard_map/ppermute | solution.py:407
  53.6 3.9 %collective-permute-start.12 = (bf16[2,320,512]{2,1,0:T(8,128)(2,1)S(1)}, bf16[2,320,512]{2,1,0:T(8,128)(2,1)S(1)}, u32[]{:S(2)}, u32[]{:S(2)}) collective-permute-start(bf16[2,320,512]{2,1,0:T(8,128)(2,1)S(1)} %get-tuple-element.102), channel_id=1, source_target_pairs={{0,1},{1,0},{2,3},{3,2},{4,5},{5,4},{6,7},{7,6},{8,9},{9,8},{10,11... | collective-permute-start | bytes 1966088 | tf_op jit(solution)/shard_map/ppermute | solution.py:407
  53.6 5.8 %collective-permute-start.16 = (bf16[2,384,512]{2,1,0:T(8,128)(2,1)S(1)}, bf16[2,384,512]{2,1,0:T(8,128)(2,1)S(1)}, u32[]{:S(2)}, u32[]{:S(2)}) collective-permute-start(bf16[2,384,512]{2,1,0:T(8,128)(2,1)S(1)} %get-tuple-element.106), channel_id=1, source_target_pairs={{0,1},{1,0},{2,3},{3,2},{4,5},{5,4},{6,7},{7,6},{8,9},{9,8},{10,11... | collective-permute-start | bytes 2359304 | tf_op jit(solution)/shard_map/ppermute | solution.py:407
  54.1 5.7 %collective-permute-start.17 = (bf16[48,512]{1,0:T(8,128)(2,1)S(1)}, bf16[48,512]{1,0:T(8,128)(2,1)S(1)}, u32[]{:S(2)}, u32[]{:S(2)}) collective-permute-start(bf16[48,512]{1,0:T(8,128)(2,1)S(1)} %get-tuple-element.107), channel_id=1, source_target_pairs={{0,1},{1,0},{2,3},{3,2},{4,5},{5,4},{6,7},{7,6},{8,9},{9,8},{10,11... | collective-permute-start | bytes 147464 | tf_op jit(solution)/shard_map/ppermute | solution.py:407
  57.7 10.2 %collective-permute-start.13 = (bf16[320,512]{1,0:T(8,128)(2,1)S(1)}, bf16[320,512]{1,0:T(8,128)(2,1)S(1)}, u32[]{:S(2)}, u32[]{:S(2)}) collective-permute-start(bf16[320,512]{1,0:T(8,128)(2,1)S(1)} %fusion.8), channel_id=1, source_target_pairs={{0,2},{1,3},{2,0},{3,1},{4,6},{5,7},{6,4},{7,5},{8,10},{9,11},{10,... | collective-permute-start | bytes 983048 | tf_op jit(solution)/shard_map/ppermute | solution.py:407
  59.9 8.1 %collective-permute-start.18 = (bf16[192,512]{1,0:T(8,128)(2,1)S(1)}, bf16[192,512]{1,0:T(8,128)(2,1)S(1)}, u32[]{:S(2)}, u32[]{:S(2)}) collective-permute-start(bf16[192,512]{1,0:T(8,128)(2,1)S(1)} %bitcast.46), channel_id=1, source_target_pairs={{0,4},{1,5},{2,6},{3,7},{4,0},{5,1},{6,2},{7,3},{8,12},{9,13},{10,... | collective-permute-start | bytes 589832 | tf_op jit(solution)/shard_map/ppermute | solution.py:407
  68.1 6.1 %collective-permute-start.20 = (bf16[160,512]{1,0:T(8,128)(2,1)S(1)}, bf16[160,512]{1,0:T(8,128)(2,1)S(1)}, u32[]{:S(2)}, u32[]{:S(2)}) collective-permute-start(bf16[160,512]{1,0:T(8,128)(2,1)S(1)} %bitcast.47), channel_id=1, source_target_pairs={{0,4},{1,5},{2,6},{3,7},{4,0},{5,1},{6,2},{7,3},{8,12},{9,13},{10,... | collective-permute-start | bytes 491528 | tf_op jit(solution)/shard_map/ppermute | solution.py:407
  68.2 22.2 %collective-permute-start.19 = (bf16[384,512]{1,0:T(8,128)(2,1)S(1)}, bf16[384,512]{1,0:T(8,128)(2,1)S(1)}, u32[]{:S(2)}, u32[]{:S(2)}) collective-permute-start(bf16[384,512]{1,0:T(8,128)(2,1)S(1)} %get-tuple-element.115), channel_id=1, source_target_pairs={{0,2},{1,3},{2,0},{3,1},{4,6},{5,7},{6,4},{7,5},{8,10},{9,11},{10,... | collective-permute-start | bytes 1179656 | tf_op jit(solution)/shard_map/ppermute | solution.py:407
  74.2 15.0 %collective-permute-start.21 = (bf16[96,512]{1,0:T(8,128)(2,1)S(1)}, bf16[96,512]{1,0:T(8,128)(2,1)S(1)}, u32[]{:S(2)}, u32[]{:S(2)}) collective-permute-start(bf16[96,512]{1,0:T(8,128)(2,1)S(1)} %get-tuple-element.125), channel_id=1, source_target_pairs={{0,2},{1,3},{2,4},{3,5},{4,6},{5,7},{6,8},{7,9},{8,10},{9,11},{10,... | collective-permute-start | bytes 294920 | tf_op jit(solution)/shard_map/ppermute | solution.py:407
  75.8 13.4 %collective-permute-start.22 = (bf16[96,512]{1,0:T(8,128)(2,1)S(1)}, bf16[96,512]{1,0:T(8,128)(2,1)S(1)}, u32[]{:S(2)}, u32[]{:S(2)}) collective-permute-start(bf16[96,512]{1,0:T(8,128)(2,1)S(1)} %get-tuple-element.126), channel_id=1, source_target_pairs={{0,14},{1,15},{2,0},{3,1},{4,2},{5,3},{6,4},{7,5},{8,6},{9,7},{10,... | collective-permute-start | bytes 294920 | tf_op jit(solution)/shard_map/ppermute | solution.py:407
  79.0 10.2 %collective-permute-start.29 = (bf16[96,512]{1,0:T(8,128)(2,1)S(1)}, bf16[96,512]{1,0:T(8,128)(2,1)S(1)}, u32[]{:S(2)}, u32[]{:S(2)}) collective-permute-start(bf16[96,512]{1,0:T(8,128)(2,1)S(1)} %get-tuple-element.159), channel_id=1, source_target_pairs={{0,8},{1,9},{2,10},{3,11},{4,12},{5,13},{6,14},{7,15},{8,0},{9,1},... | collective-permute-start | bytes 294920 | tf_op jit(solution)/shard_map/ppermute | solution.py:407
  79.1 8.6 %collective-permute-start.30 = (bf16[80,512]{1,0:T(8,128)(2,1)S(1)}, bf16[80,512]{1,0:T(8,128)(2,1)S(1)}, u32[]{:S(2)}, u32[]{:S(2)}) collective-permute-start(bf16[80,512]{1,0:T(8,128)(2,1)S(1)} %get-tuple-element.161), channel_id=1, source_target_pairs={{0,8},{1,9},{2,10},{3,11},{4,12},{5,13},{6,14},{7,15},{8,0},{9,1},... | collective-permute-start | bytes 245768 | tf_op jit(solution)/shard_map/ppermute | solution.py:407
  87.7 5.4 %collective-permute-start.23 = (bf16[48,512]{1,0:T(8,128)(2,1)S(1)}, bf16[48,512]{1,0:T(8,128)(2,1)S(1)}, u32[]{:S(2)}, u32[]{:S(2)}) collective-permute-start(bf16[48,512]{1,0:T(8,128)(2,1)S(1)} %get-tuple-element.127), channel_id=1, source_target_pairs={{0,13},{1,4},{2,15},{3,6},{4,1},{5,8},{6,3},{7,10},{8,5},{9,12},{1... | collective-permute-start | bytes 147464 | tf_op jit(solution)/shard_map/ppermute | solution.py:407
  89.2 3.9 %collective-permute-start.24 = (bf16[96,512]{1,0:T(8,128)(2,1)S(1)}, bf16[96,512]{1,0:T(8,128)(2,1)S(1)}, u32[]{:S(2)}, u32[]{:S(2)}) collective-permute-start(bf16[96,512]{1,0:T(8,128)(2,1)S(1)} %collective-permute-done.21.refs_2_), channel_id=1, source_target_pairs={{0,1},{1,0},{2,3},{3,2},{4,5},{5,4},{6,7},{7,6},{8,9},{9,8},{10,11... | collective-permute-start | bytes 294920 | tf_op jit(solution)/shard_map/ppermute | solution.py:407
  93.2 7.9 %collective-permute-start.28 = (bf16[96,512]{1,0:T(8,128)(2,1)S(1)}, bf16[96,512]{1,0:T(8,128)(2,1)S(1)}, u32[]{:S(2)}, u32[]{:S(2)}) collective-permute-start(bf16[96,512]{1,0:T(8,128)(2,1)S(1)} %get-tuple-element.151), channel_id=1, source_target_pairs={{0,12},{1,13},{2,14},{3,15},{4,8},{5,9},{6,10},{7,11},{8,4},{9,5},... | collective-permute-start | bytes 294920 | tf_op jit(solution)/shard_map/ppermute | solution.py:407
  94.1 8.5 %collective-permute-start.27 = (bf16[96,512]{1,0:T(8,128)(2,1)S(1)}, bf16[96,512]{1,0:T(8,128)(2,1)S(1)}, u32[]{:S(2)}, u32[]{:S(2)}) collective-permute-start(bf16[96,512]{1,0:T(8,128)(2,1)S(1)} %get-tuple-element.152), channel_id=1, source_target_pairs={{0,8},{1,9},{2,10},{3,11},{4,12},{5,13},{6,14},{7,15},{8,0},{9,1},... | collective-permute-start | bytes 294920 | tf_op jit(solution)/shard_map/ppermute | solution.py:407
  94.1 8.5 %collective-permute-start.26 = (bf16[96,512]{1,0:T(8,128)(2,1)S(1)}, bf16[96,512]{1,0:T(8,128)(2,1)S(1)}, u32[]{:S(2)}, u32[]{:S(2)}) collective-permute-start(bf16[96,512]{1,0:T(8,128)(2,1)S(1)} %get-tuple-element.153), channel_id=1, source_target_pairs={{0,4},{1,5},{2,6},{3,7},{4,0},{5,1},{6,2},{7,3},{8,12},{9,13},{10,... | collective-permute-start | bytes 294920 | tf_op jit(solution)/shard_map/ppermute | solution.py:407
  (19 other events, 174.8 us)

commit v13 on v12

--- a/solution.py
+++ b/solution.py
@@ -679,16 +679,20 @@
     )
     (d_pre, mesh_grad, slot_send, slot_keep, edge_send, edge_keep), returns = results[:6], results[6:]
     slot_next, slot_kept = first_sum(peers, 1, slot_send, slot_keep)
+    slot_pieces = next_sum(peers, 2, slot_next, slot_kept)
+    (node_next, node_kept, edge_send, edge_keep, returns) = lax.optimization_barrier(
+        (node_next, node_kept, edge_send, edge_keep, returns)
+    )
     edge_next, edge_kept = first_sum(peers, 1, edge_send, edge_keep)
+    other = send(returns[1], by_xor(peers, 1))
     node_pieces = next_sum(peers, 1, node_next, node_kept)
-    other = send(returns[1], by_xor(peers, 1))
-    slot_pieces = next_sum(peers, 2, slot_next, slot_kept)
-    (node_pieces, edge_next, edge_kept, other, across) = lax.optimization_barrier(
-        (node_pieces, edge_next, edge_kept, other, returns[4])
+    bundles = [send(returns[2], by_shift(peers, 2)), send(returns[3], by_shift(peers, -2))]
+    (node_pieces, edge_next, edge_kept, other, bundles) = lax.optimization_barrier(
+        (node_pieces, edge_next, edge_kept, other, bundles)
     )
     node_pieces = halve_sum(peers, node_pieces)
-    (slot_pieces, edge_next, edge_kept, across, node_pieces, d_pre) = lax.optimization_barrier(
-        (slot_pieces, edge_next, edge_kept, across, node_pieces, d_pre)
+    (slot_pieces, node_pieces, bundles, edge_next, edge_kept, d_pre) = lax.optimization_barrier(
+        (slot_pieces, node_pieces, bundles, edge_next, edge_kept, d_pre)
     )
     edge_pieces = next_sum(peers, 2, edge_next, edge_kept)
     slot_half = halve_sum(peers, slot_pieces)
@@ -704,16 +708,15 @@
         ),
         name="edge_grad",
     )(tile_count, dst, d_pre, d_aggregate, w_edge_in)
-    slot_half, node_pieces, across, edge_grad, to_after, to_before = lax.optimization_barrier(
-        (slot_half, node_pieces, across, edge_grad, returns[2], returns[3])
+    slot_half, node_pieces, across, edge_grad = lax.optimization_barrier(
+        (slot_half, node_pieces, returns[4], edge_grad)
     )
-    bundles = [send(to_after, by_shift(peers, 2)), send(to_before, by_shift(peers, -2))]
+    slot_terms = rest_terms(peers, slot_half)
+    node_terms = rest_terms(peers, node_pieces)
     across = send(across, across_chips(peers))
-    node_terms = rest_terms(peers, node_pieces)
-    slot_terms = rest_terms(peers, slot_half)
+    edge_pieces, across, bundles = lax.optimization_barrier((edge_pieces, across, bundles))
+    edge_terms = last_terms(peers, edge_pieces)
     returned = [returns[0], other, *bundles, across] + core_bundles(peers, bundles)
-    edge_pieces, returned = lax.optimization_barrier((edge_pieces, returned))
-    edge_terms = last_terms(peers, edge_pieces)
     node_terms, slot_terms = lax.optimization_barrier((node_terms, slot_terms))
     node_rows = w_node_in.shape[0] // peers
     out_rows = w_edge_out.shape[0] // peers

time: 103 us -> 106 us (1.029); the launches traced: 103 us -> 104 us
  starting transfers between devices: 32.9 us -> 49.6 us
  Pallas kernels: 39.8 us -> 25.2 us
  waiting for transfers between devices: 25 us -> 23.5 us
    ppermute x31, starting transfers between devices: 32.9 us -> 49.6 us  [send(): return lax.ppermute(values, 'lon', perm)]
    pallas_call x1, Pallas kernels: 14.3 us -> 6.45 us  [on_device(): pl.pallas_call(functools.partial(backward_kernel, peers), grid=(tiles,),...]
    pallas_call x1, Pallas kernels: 11.6 us -> 5.93 us  [on_device(): pl.pallas_call(functools.partial(forward_kernel, peers), grid=(tiles,), i...]
    ppermute x31, waiting for transfers between devices: 25 us -> 23.5 us  [send(): return lax.ppermute(values, 'lon', perm)]
    pallas_call x1, Pallas kernels: 4.16 us -> 3.06 us  [on_device(): pl.pallas_call(edges_kernel, grid=(tiles,), in_specs=[smem, index_tile, t...]
  transfers between devices with their start and end apart: 31 -> 31, of which waited for: 7 -> 9; matrix products, arithmetic and copies ran while one was open for 3% -> 3% of each run, Pallas kernels for 24% -> 15%
where the time goes in v13:
time: 106 us; the launch traced here: 104 us
  starting transfers between devices  49.6 us (47%)
  Pallas kernels  25.2 us (24%)
  waiting for transfers between devices  23.5 us (22%)
  other arithmetic  3.86 us (4%)
  between operations  1.63 us (2%)
    ppermute x31, starting transfers between devices, send(): return lax.ppermute(values, 'lon', perm)  49.6 us
    ppermute x31, waiting for transfers between devices, send(): return lax.ppermute(values, 'lon', perm)  23.5 us
    pallas_call x1, Pallas kernels, on_device(): pl.pallas_call(functools.partial(backward_kernel, peers), grid=(tiles,),...  6.45 us
    pallas_call x1, Pallas kernels, on_device(): pl.pallas_call(functools.partial(forward_kernel, peers), grid=(tiles,), i...  5.93 us
    pallas_call x1, Pallas kernels, on_device(): pl.pallas_call(gather_kernel, in_specs=[smem, hbm, hbm], out_specs=near_s...  3.55 us
    pallas_call x1, Pallas kernels, on_device(): pl.pallas_call(local_kernel, grid=(tiles,), in_specs=[index_tile, tile_of...  3.42 us
    pallas_call x1, Pallas kernels, on_device(): pl.pallas_call(edges_kernel, grid=(tiles,), in_specs=[smem, index_tile, t...  3.06 us
    pallas_call x1, Pallas kernels, on_device(): pl.pallas_call(functools.partial(scatter_kernel, out_rows), grid=(2,), in...  2.76 us
  transfers between devices with their start and end apart: 31, of which 9 were waited for; matrix products, arithmetic and copies ran while one was open for 3% of the time, Pallas kernels for 15%

profile of v13, /device:TPU:0, one launch (start us, length us, event | category | flops | bytes accessed | tf_op | source)
XLA Modules:
  0.0 104.0 jit_solution(8716856443720108162)
XLA Ops:
  0.7 3.6 %gather_lists.1 = (bf16[48,512]{1,0:T(8,128)(2,1)}, bf16[48,512]{1,0:T(8,128)(2,1)}, bf16[96,512]{1,0:T(8,128)(2,1)}, bf16[96,512]{1,0:T(8,128)(2,1)}, bf16[48,512]{1,0:T(8,128)(2,1)}, /*index=5*/bf16[48,512]{1,0:T(8,128)(2,1)}) custom-call(s32[1]{0:T(128)} %bitcast.me_ref, s32[16,48]{1,0:T(8,128)} %bitcast.39, bf16[2048,512]{1,0:T(8,128)(2,1)} %grid_hbm.1), custom_call_target="tpu_custom_call" | custom-call | flops 32212254720 | bytes 2097152 | tf_op jit(solution)/shard_map/gather_lists/pallas_call | solution.py:536
  4.2 3.1 %collective-permute-start = (bf16[48,512]{1,0:T(8,128)(2,1)}, bf16[48,512]{1,0:T(8,128)(2,1)S(1)}, u32[]{:S(2)}, u32[]{:S(2)}) collective-permute-start(bf16[48,512]{1,0:T(8,128)(2,1)} %get-tuple-element.83), channel_id=1, source_target_pairs={{0,4},{1,5},{2,6},{3,7},{4,0},{5,1},{6,2},{7,3},{8,12},{9,13},{10,... | collective-permute-start | bytes 147464 | tf_op jit(solution)/shard_map/ppermute | solution.py:407
  7.3 2.6 %collective-permute-start.1 = (bf16[48,512]{1,0:T(8,128)(2,1)}, bf16[48,512]{1,0:T(8,128)(2,1)S(1)}, u32[]{:S(2)}, u32[]{:S(2)}) collective-permute-start(bf16[48,512]{1,0:T(8,128)(2,1)} %get-tuple-element.83), channel_id=1, source_target_pairs={{0,8},{1,9},{2,10},{3,11},{4,12},{5,13},{6,14},{7,15},{8,0},{9,1},... | collective-permute-start | bytes 147464 | tf_op jit(solution)/shard_map/ppermute | solution.py:407
  9.9 1.7 %collective-permute-start.5 = (bf16[96,512]{1,0:T(8,128)(2,1)}, bf16[96,512]{1,0:T(8,128)(2,1)S(1)}, u32[]{:S(2)}, u32[]{:S(2)}) collective-permute-start(bf16[96,512]{1,0:T(8,128)(2,1)} %get-tuple-element.87), channel_id=1, source_target_pairs={{0,2},{1,3},{2,4},{3,5},{4,6},{5,7},{6,8},{7,9},{8,10},{9,11},{10,... | collective-permute-start | bytes 294920 | tf_op jit(solution)/shard_map/ppermute | solution.py:407
  11.7 3.0 %collective-permute-start.6 = (bf16[96,512]{1,0:T(8,128)(2,1)}, bf16[96,512]{1,0:T(8,128)(2,1)S(1)}, u32[]{:S(2)}, u32[]{:S(2)}) collective-permute-start(bf16[96,512]{1,0:T(8,128)(2,1)} %get-tuple-element.88), channel_id=1, source_target_pairs={{0,14},{1,15},{2,0},{3,1},{4,2},{5,3},{6,4},{7,5},{8,6},{9,7},{10,... | collective-permute-start | bytes 294920 | tf_op jit(solution)/shard_map/ppermute | solution.py:407
  17.0 1.6 %collective-permute-start.3 = (bf16[192,512]{1,0:T(8,128)(2,1)S(1)}, bf16[192,512]{1,0:T(8,128)(2,1)S(1)}, u32[]{:S(2)}, u32[]{:S(2)}) collective-permute-start(bf16[192,512]{1,0:T(8,128)(2,1)S(1)} %pad_maximum_fusion.refs_7_), channel_id=1, source_target_pairs={{0,2},{1,3},{2,0},{3,1},{4,6},{5,7},{6,4},{7,5},{8,10},{9,11},{10,... | collective-permute-start | bytes 589832 | tf_op jit(solution)/shard_map/ppermute | solution.py:407
  18.6 3.4 %edge_local.1.local_ref = bf16[3072,512]{1,0:T(8,128)(2,1)S(1)} custom-call(s32[3,1,1024]{2,1,0:T(1,128)S(1)} %bitcast.33, bf16[3072,512]{1,0:T(8,128)(2,1)S(1)} %copy-done.1, bf16[256,512]{1,0:T(8,128)(2,1)S(1)} %copy-done.2, bf16[1536,512]{1,0:T(8,128)(2,1)S(1)} %copy-done, bf16[1536,512]{1,0:T(8,128)(2,1)S(1)} %copy-done), custom_call_target="tpu_custom_call" | custom-call | flops 2415919104 | bytes 6291456 | tf_op jit(solution)/shard_map/edge_local/pallas_call | solution.py:562
  24.7 5.9 %forward.1 = (bf16[768,512]{1,0:T(8,128)(2,1)S(1)}, bf16[3072,512]{1,0:T(8,128)(2,1)S(1)}, bf16[3072,512]{1,0:T(8,128)(2,1)S(1)}, bf16[3072,512]{1,0:T(8,128)(2,...) custom-call(s32[1]{0:T(128)} %bitcast.me_ref, ...), custom_call_target="tpu_custom_call" | custom-call | tf_op jit(solution)/shard_map/forward/pallas_call | solution.py:582
  32.3 6.5 %backward.1 = (bf16[3072,512]{1,0:T(8,128)(2,1)S(1)}, bf16[256,512]{1,0:T(8,128)(2,1)}, bf16[2,320,512]{2,1,0:T(8,128)(2,1)S(1)}, bf16[2,320,512]{2,1,0:T(8,128)...) custom-call(s32[1]{0:T(128)} %bitcast.me_ref, ...), custom_call_target="tpu_custom_call" | custom-call | flops 8858370048 | bytes 15728640 | tf_op jit(solution)/shard_map/backward/pallas_call | solution.py:633
  38.7 9.7 %collective-permute-start.12 = (bf16[2,320,512]{2,1,0:T(8,128)(2,1)S(1)}, bf16[2,320,512]{2,1,0:T(8,128)(2,1)S(1)}, u32[]{:S(2)}, u32[]{:S(2)}) collective-permute-start(bf16[2,320,512]{2,1,0:T(8,128)(2,1)S(1)} %get-tuple-element.107), channel_id=1, source_target_pairs={{0,1},{1,0},{2,3},{3,2},{4,5},{5,4},{6,7},{7,6},{8,9},{9,8},{10,11... | collective-permute-start | bytes 1966088 | tf_op jit(solution)/shard_map/ppermute | solution.py:407
  48.6 2.6 %collective-permute-start.16 = (bf16[2,384,512]{2,1,0:T(8,128)(2,1)S(1)}, bf16[2,384,512]{2,1,0:T(8,128)(2,1)S(1)}, u32[]{:S(2)}, u32[]{:S(2)}) collective-permute-start(bf16[2,384,512]{2,1,0:T(8,128)(2,1)S(1)} %get-tuple-element.120), channel_id=1, source_target_pairs={{0,1},{1,0},{2,3},{3,2},{4,5},{5,4},{6,7},{7,6},{8,9},{9,8},{10,11... | collective-permute-start | bytes 2359304 | tf_op jit(solution)/shard_map/ppermute | solution.py:407
  51.4 3.1 %collective-permute-start.13 = (bf16[320,512]{1,0:T(8,128)(2,1)S(1)}, bf16[320,512]{1,0:T(8,128)(2,1)S(1)}, u32[]{:S(2)}, u32[]{:S(2)}) collective-permute-start(bf16[320,512]{1,0:T(8,128)(2,1)S(1)} %fusion.7), channel_id=1, source_target_pairs={{0,2},{1,3},{2,0},{3,1},{4,6},{5,7},{6,4},{7,5},{8,10},{9,11},{10,... | collective-permute-start | bytes 983048 | tf_op jit(solution)/shard_map/ppermute | solution.py:407
  54.6 4.7 %collective-permute-start.19 = (bf16[96,512]{1,0:T(8,128)(2,1)S(1)}, bf16[96,512]{1,0:T(8,128)(2,1)S(1)}, u32[]{:S(2)}, u32[]{:S(2)}) collective-permute-start(bf16[96,512]{1,0:T(8,128)(2,1)S(1)} %get-tuple-element.123), channel_id=1, source_target_pairs={{0,14},{1,15},{2,0},{3,1},{4,2},{5,3},{6,4},{7,5},{8,6},{9,7},{10,... | collective-permute-start | bytes 294920 | tf_op jit(solution)/shard_map/ppermute | solution.py:407
  60.5 5.7 %collective-permute-done.18.refs_2_ = bf16[96,512]{1,0:T(8,128)(2,1)S(1)} collective-permute-done((bf16[96,512]{1,0:T(8,128)(2,1)S(1)}, bf16[96,512]{1,0:T(8,128)(2,1)S(1)}, u32[]{:S(2)}, u32[]{:S(2)}) %collective-permute-start.18) | collective-permute-done | bytes 98336 | tf_op jit(solution)/shard_map/ppermute | solution.py:407
  67.0 3.6 %collective-permute-start.20 = (bf16[192,512]{1,0:T(8,128)(2,1)S(1)}, bf16[192,512]{1,0:T(8,128)(2,1)S(1)}, u32[]{:S(2)}, u32[]{:S(2)}) collective-permute-start(bf16[192,512]{1,0:T(8,128)(2,1)S(1)} %bitcast.43), channel_id=1, source_target_pairs={{0,4},{1,5},{2,6},{3,7},{4,0},{5,1},{6,2},{7,3},{8,12},{9,13},{10,... | collective-permute-start | bytes 589832 | tf_op jit(solution)/shard_map/ppermute | solution.py:407
  70.8 4.2 %collective-permute-done.20 = bf16[192,512]{1,0:T(8,128)(2,1)S(1)} collective-permute-done((bf16[192,512]{1,0:T(8,128)(2,1)S(1)}, bf16[192,512]{1,0:T(8,128)(2,1)S(1)}, u32[]{:S(2)}, u32[]{:S(2)}) %collective-permute-start.20) | collective-permute-done | bytes 196640 | tf_op jit(solution)/shard_map/ppermute | solution.py:407
  75.1 1.8 %collective-permute-start.22 = (bf16[160,512]{1,0:T(8,128)(2,1)S(1)}, bf16[160,512]{1,0:T(8,128)(2,1)S(1)}, u32[]{:S(2)}, u32[]{:S(2)}) collective-permute-start(bf16[160,512]{1,0:T(8,128)(2,1)S(1)} %bitcast.44), channel_id=1, source_target_pairs={{0,4},{1,5},{2,6},{3,7},{4,0},{5,1},{6,2},{7,3},{8,12},{9,13},{10,... | collective-permute-start | bytes 491528 | tf_op jit(solution)/shard_map/ppermute | solution.py:407
  78.1 3.1 %edge_grad.1 = bf16[3072,512]{1,0:T(8,128)(2,1)} custom-call(s32[1]{0:T(128)S(6)} %copy.23.count_ref, s32[3,1,1024]{2,1,0:T(1,128)S(1)} %bitcast.36, bf16[3072,512]{1,0:T(8,128)(2,1)S(1)} %get-tuple-element.135.d_pre_ref, bf16[256,512]{1,0:T(8,128)(2,1)S(1)} %get-tuple-element.136.d_aggregate_ref, bf16[1536,512]{1,0:T(8,128)(2,1)S(1)} %copy-done), custom_call_target="tpu_custom_call" | custom-call | flops 2415919104 | bytes 6291456 | tf_op jit(solution)/shard_map/edge_grad/pallas_call | solution.py:699
  82.0 2.4 %collective-permute-start.30 = (bf16[80,512]{1,0:T(8,128)(2,1)S(1)}, bf16[80,512]{1,0:T(8,128)(2,1)S(1)}, u32[]{:S(2)}, u32[]{:S(2)}) collective-permute-start(bf16[80,512]{1,0:T(8,128)(2,1)S(1)} %get-tuple-element.173), channel_id=1, source_target_pairs={{0,8},{1,9},{2,10},{3,11},{4,12},{5,13},{6,14},{7,15},{8,0},{9,1},... | collective-permute-start | bytes 245768 | tf_op jit(solution)/shard_map/ppermute | solution.py:407
  84.4 6.5 %collective-permute-done.30.refs_8_ = bf16[80,512]{1,0:T(8,128)(2,1)S(1)} collective-permute-done((bf16[80,512]{1,0:T(8,128)(2,1)S(1)}, bf16[80,512]{1,0:T(8,128)(2,1)S(1)}, u32[]{:S(2)}, u32[]{:S(2)}) %collective-permute-start.30) | collective-permute-done | bytes 81952 | tf_op jit(solution)/shard_map/ppermute | solution.py:407
  92.3 2.1 %collective-permute-start.25 = (bf16[96,512]{1,0:T(8,128)(2,1)S(1)}, bf16[96,512]{1,0:T(8,128)(2,1)S(1)}, u32[]{:S(2)}, u32[]{:S(2)}) collective-permute-start(bf16[96,512]{1,0:T(8,128)(2,1)S(1)} %get-tuple-element.164), channel_id=1, source_target_pairs={{0,8},{1,9},{2,10},{3,11},{4,12},{5,13},{6,14},{7,15},{8,0},{9,1},... | collective-permute-start | bytes 294920 | tf_op jit(solution)/shard_map/ppermute | solution.py:407
  94.4 2.3 %collective-permute-start.26 = (bf16[96,512]{1,0:T(8,128)(2,1)S(1)}, bf16[96,512]{1,0:T(8,128)(2,1)S(1)}, u32[]{:S(2)}, u32[]{:S(2)}) collective-permute-start(bf16[96,512]{1,0:T(8,128)(2,1)S(1)} %get-tuple-element.163), channel_id=1, source_target_pairs={{0,12},{1,13},{2,14},{3,15},{4,8},{5,9},{6,10},{7,11},{8,4},{9,5},... | collective-permute-start | bytes 294920 | tf_op jit(solution)/shard_map/ppermute | solution.py:407
  97.4 2.8 %scatter_lists.1 = bf16[2048,512]{1,0:T(8,128)(2,1)} custom-call(s32[1]{0:T(128)} %bitcast.me_ref, s32[16,48]{1,0:T(8,128)S(1)} %bitcast.40, bf16[48,512]{1,0:T(8,128)(2,1)S(1)} %get-tuple-element.141.refs_0_, bf16[48,512]{1,0:T(8,128)(2,1)S(1)} %collective-permute-done.17.refs_1_, bf16[96,512]{1,0:T(8,128)(2,1)S(1)} %collective-permute-done.18.refs_2_, ...), custom_call_target="tpu_custom_call" | custom-call | tf_op jit(solution)/shard_map/scatter_lists/pallas_call | solution.py:723
  100.2 3.1 %collective-permute-done.25 = bf16[96,512]{1,0:T(8,128)(2,1)S(1)} collective-permute-done((bf16[96,512]{1,0:T(8,128)(2,1)S(1)}, bf16[96,512]{1,0:T(8,128)(2,1)S(1)}, u32[]{:S(2)}, u32[]{:S(2)}) %collective-permute-start.25) | collective-permute-done | bytes 98336 | tf_op jit(solution)/shard_map/ppermute | solution.py:407
  (85 shorter events, 13.3 us)
Async XLA Ops:
  4.2 10.5 %collective-permute-start = (bf16[48,512]{1,0:T(8,128)(2,1)}, bf16[48,512]{1,0:T(8,128)(2,1)S(1)}, u32[]{:S(2)}, u32[]{:S(2)}) collective-permute-start(bf16[48,512]{1,0:T(8,128)(2,1)} %get-tuple-element.83), channel_id=1, source_target_pairs={{0,4},{1,5},{2,6},{3,7},{4,0},{5,1},{6,2},{7,3},{8,12},{9,13},{10,... | collective-permute-start | bytes 147464 | tf_op jit(solution)/shard_map/ppermute | solution.py:407
  7.3 7.4 %collective-permute-start.1 = (bf16[48,512]{1,0:T(8,128)(2,1)}, bf16[48,512]{1,0:T(8,128)(2,1)S(1)}, u32[]{:S(2)}, u32[]{:S(2)}) collective-permute-start(bf16[48,512]{1,0:T(8,128)(2,1)} %get-tuple-element.83), channel_id=1, source_target_pairs={{0,8},{1,9},{2,10},{3,11},{4,12},{5,13},{6,14},{7,15},{8,0},{9,1},... | collective-permute-start | bytes 147464 | tf_op jit(solution)/shard_map/ppermute | solution.py:407
  9.9 6.2 %collective-permute-start.2 = (bf16[48,512]{1,0:T(8,128)(2,1)}, bf16[48,512]{1,0:T(8,128)(2,1)S(1)}, u32[]{:S(2)}, u32[]{:S(2)}) collective-permute-start(bf16[48,512]{1,0:T(8,128)(2,1)} %get-tuple-element.83), channel_id=1, source_target_pairs={{0,12},{1,13},{2,14},{3,15},{4,8},{5,9},{6,10},{7,11},{8,4},{9,5},... | collective-permute-start | bytes 147464 | tf_op jit(solution)/shard_map/ppermute | solution.py:407
  9.9 12.2 %collective-permute-start.5 = (bf16[96,512]{1,0:T(8,128)(2,1)}, bf16[96,512]{1,0:T(8,128)(2,1)S(1)}, u32[]{:S(2)}, u32[]{:S(2)}) collective-permute-start(bf16[96,512]{1,0:T(8,128)(2,1)} %get-tuple-element.87), channel_id=1, source_target_pairs={{0,2},{1,3},{2,4},{3,5},{4,6},{5,7},{6,8},{7,9},{8,10},{9,11},{10,... | collective-permute-start | bytes 294920 | tf_op jit(solution)/shard_map/ppermute | solution.py:407
  11.7 10.4 %collective-permute-start.6 = (bf16[96,512]{1,0:T(8,128)(2,1)}, bf16[96,512]{1,0:T(8,128)(2,1)S(1)}, u32[]{:S(2)}, u32[]{:S(2)}) collective-permute-start(bf16[96,512]{1,0:T(8,128)(2,1)} %get-tuple-element.88), channel_id=1, source_target_pairs={{0,14},{1,15},{2,0},{3,1},{4,2},{5,3},{6,4},{7,5},{8,6},{9,7},{10,... | collective-permute-start | bytes 294920 | tf_op jit(solution)/shard_map/ppermute | solution.py:407
  14.7 7.4 %collective-permute-start.7 = (bf16[48,512]{1,0:T(8,128)(2,1)}, bf16[48,512]{1,0:T(8,128)(2,1)S(1)}, u32[]{:S(2)}, u32[]{:S(2)}) collective-permute-start(bf16[48,512]{1,0:T(8,128)(2,1)} %get-tuple-element.89), channel_id=1, source_target_pairs={{0,13},{1,4},{2,15},{3,6},{4,1},{5,8},{6,3},{7,10},{8,5},{9,12},{1... | collective-permute-start | bytes 147464 | tf_op jit(solution)/shard_map/ppermute | solution.py:407
  17.0 5.7 %collective-permute-start.3 = (bf16[192,512]{1,0:T(8,128)(2,1)S(1)}, bf16[192,512]{1,0:T(8,128)(2,1)S(1)}, u32[]{:S(2)}, u32[]{:S(2)}) collective-permute-start(bf16[192,512]{1,0:T(8,128)(2,1)S(1)} %pad_maximum_fusion.refs_7_), channel_id=1, source_target_pairs={{0,2},{1,3},{2,0},{3,1},{4,6},{5,7},{6,4},{7,5},{8,10},{9,11},{10,... | collective-permute-start | bytes 589832 | tf_op jit(solution)/shard_map/ppermute | solution.py:407
  30.7 17.7 %collective-permute-start.14 = (bf16[2,384,512]{2,1,0:T(8,128)(2,1)S(1)}, bf16[2,384,512]{2,1,0:T(8,128)(2,1)S(1)}, u32[]{:S(2)}, u32[]{:S(2)}) collective-permute-start(bf16[2,384,512]{2,1,0:T(8,128)(2,1)S(1)} %get-tuple-element.109), channel_id=1, source_target_pairs={{0,2},{1,3},{2,0},{3,1},{4,6},{5,7},{6,4},{7,5},{8,10},{9,11},{10,... | collective-permute-start | bytes 2359304 | tf_op jit(solution)/shard_map/ppermute | solution.py:407
  38.7 12.6 %collective-permute-start.12 = (bf16[2,320,512]{2,1,0:T(8,128)(2,1)S(1)}, bf16[2,320,512]{2,1,0:T(8,128)(2,1)S(1)}, u32[]{:S(2)}, u32[]{:S(2)}) collective-permute-start(bf16[2,320,512]{2,1,0:T(8,128)(2,1)S(1)} %get-tuple-element.107), channel_id=1, source_target_pairs={{0,1},{1,0},{2,3},{3,2},{4,5},{5,4},{6,7},{7,6},{8,9},{9,8},{10,11... | collective-permute-start | bytes 1966088 | tf_op jit(solution)/shard_map/ppermute | solution.py:407
  48.6 10.8 %collective-permute-start.16 = (bf16[2,384,512]{2,1,0:T(8,128)(2,1)S(1)}, bf16[2,384,512]{2,1,0:T(8,128)(2,1)S(1)}, u32[]{:S(2)}, u32[]{:S(2)}) collective-permute-start(bf16[2,384,512]{2,1,0:T(8,128)(2,1)S(1)} %get-tuple-element.120), channel_id=1, source_target_pairs={{0,1},{1,0},{2,3},{3,2},{4,5},{5,4},{6,7},{7,6},{8,9},{9,8},{10,11... | collective-permute-start | bytes 2359304 | tf_op jit(solution)/shard_map/ppermute | solution.py:407
  51.3 8.0 %collective-permute-start.15 = (bf16[384,512]{1,0:T(8,128)(2,1)S(1)}, bf16[384,512]{1,0:T(8,128)(2,1)S(1)}, u32[]{:S(2)}, u32[]{:S(2)}) collective-permute-start(bf16[384,512]{1,0:T(8,128)(2,1)S(1)} %get-tuple-element.118), channel_id=1, source_target_pairs={{0,1},{1,0},{2,3},{3,2},{4,5},{5,4},{6,7},{7,6},{8,9},{9,8},{10,11... | collective-permute-start | bytes 1179656 | tf_op jit(solution)/shard_map/ppermute | solution.py:407
  51.4 19.2 %collective-permute-start.13 = (bf16[320,512]{1,0:T(8,128)(2,1)S(1)}, bf16[320,512]{1,0:T(8,128)(2,1)S(1)}, u32[]{:S(2)}, u32[]{:S(2)}) collective-permute-start(bf16[320,512]{1,0:T(8,128)(2,1)S(1)} %fusion.7), channel_id=1, source_target_pairs={{0,2},{1,3},{2,0},{3,1},{4,6},{5,7},{6,4},{7,5},{8,10},{9,11},{10,... | collective-permute-start | bytes 983048 | tf_op jit(solution)/shard_map/ppermute | solution.py:407
  54.6 11.7 %collective-permute-start.18 = (bf16[96,512]{1,0:T(8,128)(2,1)S(1)}, bf16[96,512]{1,0:T(8,128)(2,1)S(1)}, u32[]{:S(2)}, u32[]{:S(2)}) collective-permute-start(bf16[96,512]{1,0:T(8,128)(2,1)S(1)} %get-tuple-element.122), channel_id=1, source_target_pairs={{0,2},{1,3},{2,4},{3,5},{4,6},{5,7},{6,8},{7,9},{8,10},{9,11},{10,... | collective-permute-start | bytes 294920 | tf_op jit(solution)/shard_map/ppermute | solution.py:407
  54.6 12.4 %collective-permute-start.19 = (bf16[96,512]{1,0:T(8,128)(2,1)S(1)}, bf16[96,512]{1,0:T(8,128)(2,1)S(1)}, u32[]{:S(2)}, u32[]{:S(2)}) collective-permute-start(bf16[96,512]{1,0:T(8,128)(2,1)S(1)} %get-tuple-element.123), channel_id=1, source_target_pairs={{0,14},{1,15},{2,0},{3,1},{4,2},{5,3},{6,4},{7,5},{8,6},{9,7},{10,... | collective-permute-start | bytes 294920 | tf_op jit(solution)/shard_map/ppermute | solution.py:407
  67.0 8.0 %collective-permute-start.20 = (bf16[192,512]{1,0:T(8,128)(2,1)S(1)}, bf16[192,512]{1,0:T(8,128)(2,1)S(1)}, u32[]{:S(2)}, u32[]{:S(2)}) collective-permute-start(bf16[192,512]{1,0:T(8,128)(2,1)S(1)} %bitcast.43), channel_id=1, source_target_pairs={{0,4},{1,5},{2,6},{3,7},{4,0},{5,1},{6,2},{7,3},{8,12},{9,13},{10,... | collective-permute-start | bytes 589832 | tf_op jit(solution)/shard_map/ppermute | solution.py:407
  75.1 6.1 %collective-permute-start.22 = (bf16[160,512]{1,0:T(8,128)(2,1)S(1)}, bf16[160,512]{1,0:T(8,128)(2,1)S(1)}, u32[]{:S(2)}, u32[]{:S(2)}) collective-permute-start(bf16[160,512]{1,0:T(8,128)(2,1)S(1)} %bitcast.44), channel_id=1, source_target_pairs={{0,4},{1,5},{2,6},{3,7},{4,0},{5,1},{6,2},{7,3},{8,12},{9,13},{10,... | collective-permute-start | bytes 491528 | tf_op jit(solution)/shard_map/ppermute | solution.py:407
  76.9 14.6 %collective-permute-start.21 = (bf16[384,512]{1,0:T(8,128)(2,1)S(1)}, bf16[384,512]{1,0:T(8,128)(2,1)S(1)}, u32[]{:S(2)}, u32[]{:S(2)}) collective-permute-start(bf16[384,512]{1,0:T(8,128)(2,1)S(1)} %get-tuple-element.131), channel_id=1, source_target_pairs={{0,2},{1,3},{2,0},{3,1},{4,6},{5,7},{6,4},{7,5},{8,10},{9,11},{10,... | collective-permute-start | bytes 1179656 | tf_op jit(solution)/shard_map/ppermute | solution.py:407
  81.3 9.6 %collective-permute-start.29 = (bf16[96,512]{1,0:T(8,128)(2,1)S(1)}, bf16[96,512]{1,0:T(8,128)(2,1)S(1)}, u32[]{:S(2)}, u32[]{:S(2)}) collective-permute-start(bf16[96,512]{1,0:T(8,128)(2,1)S(1)} %get-tuple-element.171), channel_id=1, source_target_pairs={{0,8},{1,9},{2,10},{3,11},{4,12},{5,13},{6,14},{7,15},{8,0},{9,1},... | collective-permute-start | bytes 294920 | tf_op jit(solution)/shard_map/ppermute | solution.py:407
  82.0 8.9 %collective-permute-start.30 = (bf16[80,512]{1,0:T(8,128)(2,1)S(1)}, bf16[80,512]{1,0:T(8,128)(2,1)S(1)}, u32[]{:S(2)}, u32[]{:S(2)}) collective-permute-start(bf16[80,512]{1,0:T(8,128)(2,1)S(1)} %get-tuple-element.173), channel_id=1, source_target_pairs={{0,8},{1,9},{2,10},{3,11},{4,12},{5,13},{6,14},{7,15},{8,0},{9,1},... | collective-permute-start | bytes 245768 | tf_op jit(solution)/shard_map/ppermute | solution.py:407
  84.4 7.3 %collective-permute-start.23 = (bf16[48,512]{1,0:T(8,128)(2,1)S(1)}, bf16[48,512]{1,0:T(8,128)(2,1)S(1)}, u32[]{:S(2)}, u32[]{:S(2)}) collective-permute-start(bf16[48,512]{1,0:T(8,128)(2,1)S(1)} %get-tuple-element.137), channel_id=1, source_target_pairs={{0,13},{1,4},{2,15},{3,6},{4,1},{5,8},{6,3},{7,10},{8,5},{9,12},{1... | collective-permute-start | bytes 147464 | tf_op jit(solution)/shard_map/ppermute | solution.py:407
  91.7 5.7 %collective-permute-start.27 = (bf16[96,512]{1,0:T(8,128)(2,1)S(1)}, bf16[96,512]{1,0:T(8,128)(2,1)S(1)}, u32[]{:S(2)}, u32[]{:S(2)}) collective-permute-start(bf16[96,512]{1,0:T(8,128)(2,1)S(1)} %collective-permute-done.18.refs_2_), channel_id=1, source_target_pairs={{0,1},{1,0},{2,3},{3,2},{4,5},{5,4},{6,7},{7,6},{8,9},{9,8},{10,11... | collective-permute-start | bytes 294920 | tf_op jit(solution)/shard_map/ppermute | solution.py:407
  92.3 7.9 %collective-permute-start.24 = (bf16[96,512]{1,0:T(8,128)(2,1)S(1)}, bf16[96,512]{1,0:T(8,128)(2,1)S(1)}, u32[]{:S(2)}, u32[]{:S(2)}) collective-permute-start(bf16[96,512]{1,0:T(8,128)(2,1)S(1)} %get-tuple-element.165), channel_id=1, source_target_pairs={{0,4},{1,5},{2,6},{3,7},{4,0},{5,1},{6,2},{7,3},{8,12},{9,13},{10,... | collective-permute-start | bytes 294920 | tf_op jit(solution)/shard_map/ppermute | solution.py:407
  92.3 10.9 %collective-permute-start.25 = (bf16[96,512]{1,0:T(8,128)(2,1)S(1)}, bf16[96,512]{1,0:T(8,128)(2,1)S(1)}, u32[]{:S(2)}, u32[]{:S(2)}) collective-permute-start(bf16[96,512]{1,0:T(8,128)(2,1)S(1)} %get-tuple-element.164), channel_id=1, source_target_pairs={{0,8},{1,9},{2,10},{3,11},{4,12},{5,13},{6,14},{7,15},{8,0},{9,1},... | collective-permute-start | bytes 294920 | tf_op jit(solution)/shard_map/ppermute | solution.py:407
  94.4 8.8 %collective-permute-start.26 = (bf16[96,512]{1,0:T(8,128)(2,1)S(1)}, bf16[96,512]{1,0:T(8,128)(2,1)S(1)}, u32[]{:S(2)}, u32[]{:S(2)}) collective-permute-start(bf16[96,512]{1,0:T(8,128)(2,1)S(1)} %get-tuple-element.163), channel_id=1, source_target_pairs={{0,12},{1,13},{2,14},{3,15},{4,8},{5,9},{6,10},{7,11},{8,4},{9,5},... | collective-permute-start | bytes 294920 | tf_op jit(solution)/shard_map/ppermute | solution.py:407
  (19 other events, 158.4 us)

commit v14 on v9

--- a/solution.py
+++ b/solution.py
@@ -11,6 +11,7 @@
 STEP = 1024
 SUB = 512
 LANES = 128
+BLOCK = 256
 GRID_PARTS = 4
 NEAR = 3
 BF16 = jnp.bfloat16
@@ -74,15 +75,34 @@
     return jnp.concatenate(rows, axis=1)
 
 
+def in_block(indices, first):
+    place = indices - first
+    return jnp.where((place >= 0) & (place < BLOCK), place, -1).astype(F32).astype(BF16)
+
+
 def hot_rows(row, width, first=0):
-    column = as_column(row).astype(jnp.int32) - first
-    along = lax.broadcasted_iota(jnp.int32, (row.shape[1], width), 1)
-    return (column == along).astype(F32).astype(BF16)
+    column = as_column(row).astype(jnp.int32)
+    count = row.shape[1]
+    one = jnp.ones((), BF16)
+    zero = jnp.zeros((), BF16)
+    blocks = []
+    for start in range(0, width, BLOCK):
+        size = min(BLOCK, width - start)
+        along = lax.broadcasted_iota(jnp.int32, (count, size), 1).astype(F32).astype(BF16)
+        blocks.append(jnp.where(in_block(column, first + start) == along, one, zero))
+    return jnp.concatenate(blocks, axis=1)
 
 
 def hot_columns(row, height):
-    down = lax.broadcasted_iota(jnp.int32, (height, row.shape[1]), 0)
-    return (row == down).astype(F32).astype(BF16)
+    count = row.shape[1]
+    one = jnp.ones((), BF16)
+    zero = jnp.zeros((), BF16)
+    blocks = []
+    for start in range(0, height, BLOCK):
+        size = min(BLOCK, height - start)
+        down = lax.broadcasted_iota(jnp.int32, (size, count), 0).astype(F32).astype(BF16)
+        blocks.append(jnp.where(in_block(row, start) == down, one, zero))
+    return jnp.concatenate(blocks, axis=0)
 
 
 def live_only(row, first, count):
@@ -240,7 +260,7 @@
     (w_sender_ref, w_out_ref, w_node_in_ref, w_node_out_ref, mesh_ref, cotangent_ref) = refs[11:17]
     (received_ref, hidden_ref, slope_ref, norm_ref, inverse_ref) = refs[17:22]
     (send_ref, keep_ref, d_aggregate_ref, d_mesh_ref) = refs[22:26]
-    (slot_proj, aggregate, grad_in, grad_out) = refs[26:]
+    (slot_proj, aggregate, grad_in, grad_out, w_centred) = refs[26:]
     step = pl.program_id(0)
     me = me_ref[0]
     cap = near_refs[0].shape[0]
@@ -249,6 +269,8 @@
     @pl.when(step == 0)
     def _():
         aggregate[...] = jnp.zeros_like(aggregate)
+        w_out = w_out_ref[...].astype(F32)
+        w_centred[...] = (w_out - jnp.mean(w_out, axis=1, keepdims=True)).astype(BF16)
         w_sender = w_sender_ref[...]
 
         def place(owner, rows, projected):
@@ -280,9 +302,10 @@
             hidden = hidden.astype(BF16)
             hidden_ref[part, :] = hidden
             slope_ref[part, :] = slope.astype(BF16)
-            projs.append(dot(hidden, w_out_ref[...]))
+            projs.append(dot(hidden, w_centred[...]))
         for (start, part), proj in zip(parts, projs):
-            normed, inverse = layer_norm(proj)
+            inverse = lax.rsqrt(jnp.mean(proj * proj, axis=1, keepdims=True) + 1e-05)
+            normed = proj * inverse
             norm_ref[part, :] = normed.astype(BF16)
             inverse_ref[0, :, part] = as_row(inverse)
             edge_new = (edge_ref[part, :].astype(F32) + normed).astype(BF16)
@@ -406,14 +429,8 @@
 
 
 def exchange_near(peers, lists):
-    mine, other, after, before, across = lists
-    return [
-        mine,
-        other,
-        send(after, by_shift(peers, 2)),
-        send(before, by_shift(peers, -2)),
-        send(across, across_chips(peers)),
-    ]
+    mine, other, after, before = lists
+    return [mine, other, send(after, by_shift(peers, 2)), send(before, by_shift(peers, -2))]
 
 
 def core_near(peers, near):
@@ -442,23 +459,6 @@
     for place in range(1, count):
         piece = pieces[place * share : (place + 1) * share]
         terms.append(send(piece, by_xor(peers, 4 * place)))
-    return terms
-
-
-def halve_sum(peers, pieces):
-    count = peers // 4
-    blocks = pieces.reshape(count // 2, 2, -1, pieces.shape[1])
-    kept, outgoing = [blocks[:, place].reshape(-1, pieces.shape[1]) for place in range(2)]
-    return add(kept, send(outgoing, by_xor(peers, 4)))
-
-
-def rest_terms(peers, pieces):
-    count = peers // 8
-    share = pieces.shape[0] // count
-    terms = [pieces[:share]]
-    for place in range(1, count):
-        piece = pieces[place * share : (place + 1) * share]
-        terms.append(send(piece, by_xor(peers, 8 * place)))
     return terms
 
 
@@ -546,7 +546,9 @@
     )(me, rows, grid_latent)
 
     hops = [send(lists[5], by_xor(peers, 4 * place)) for place in range(1, upper)]
-    near = exchange_near(peers, lists[:5])
+    near = exchange_near(peers, lists[:4])
+    hops[0], across = lax.optimization_barrier((hops[0], lists[4]))
+    near.append(send(across, across_chips(peers)))
     far_own = jnp.concatenate([lists[5]] + hops, axis=0)
     far_own, receivers = lax.optimization_barrier((far_own, dst))
     far_next = send(far_own, by_xor(peers, 2))
@@ -594,6 +596,7 @@
             pltpu.VMEM((mesh_count, width), F32),
             pltpu.VMEM(w_node_in.shape, F32),
             pltpu.VMEM(w_node_out.shape, F32),
+            pltpu.VMEM(w_edge_out.shape, BF16),
         ],
         compiler_params=params,
         name="forward",
@@ -680,23 +683,21 @@
     node_pieces, edge_next, edge_kept, swapped, across = lax.optimization_barrier(
         (node_pieces, edge_next, edge_kept, swapped, returns[4])
     )
-    node_pieces = halve_sum(peers, node_pieces)
+    node_terms = last_terms(peers, node_pieces)
     across = send(across, across_chips(peers))
     to_after = jnp.concatenate([returns[2], swapped[cap : 2 * cap]], axis=0)
     to_before = jnp.concatenate([returns[3], swapped[2 * cap :]], axis=0)
-    (slot_pieces, edge_next, edge_kept, across, node_pieces, to_after, to_before) = lax.optimization_barrier(
-        (slot_pieces, edge_next, edge_kept, across, node_pieces, to_after, to_before)
+    (slot_pieces, edge_next, edge_kept, across, node_terms, to_after, to_before) = lax.optimization_barrier(
+        (slot_pieces, edge_next, edge_kept, across, node_terms, to_after, to_before)
     )
     edge_pieces = next_sum(peers, 2, edge_next, edge_kept)
-    slot_half = halve_sum(peers, slot_pieces)
-    node_terms = rest_terms(peers, node_pieces)
-    (slot_half, edge_pieces, node_terms, to_after, to_before) = lax.optimization_barrier(
-        (slot_half, edge_pieces, node_terms, to_after, to_before)
+    slot_terms = last_terms(peers, slot_pieces)
+    (slot_terms, edge_pieces, to_after, to_before) = lax.optimization_barrier(
+        (slot_terms, edge_pieces, to_after, to_before)
     )
-    slot_terms = rest_terms(peers, slot_half)
     edge_terms = last_terms(peers, edge_pieces)
     bundles = [send(to_after, by_shift(peers, 2)), send(to_before, by_shift(peers, -2))]
-    node_terms, slot_terms = lax.optimization_barrier((node_terms, slot_terms))
+    node_terms, out_terms, bundles = lax.optimization_barrier((node_terms, slot_terms, bundles))
     returned = [returns[0], swapped, *bundles, across]
     node_rows = w_node_in.shape[0] // peers
     out_rows = w_edge_out.shape[0] // peers
@@ -705,7 +706,7 @@
         grid=(2,),
         in_specs=[smem, whole(rows.shape)]
         + return_specs
-        + [whole((out_rows + cap, width))] * (upper // 2),
+        + [whole((out_rows + cap, width))] * upper,
         out_specs=pl.BlockSpec((grid_part, width), lambda step: (step, 0)),
         out_shape=jax.ShapeDtypeStruct((grid_count, width), BF16),
         compiler_params=params,
@@ -717,7 +718,7 @@
         edge_grad,
         mesh_grad,
         total_of(edge_terms, 0, w_edge_in.shape[0] // peers),
-        total_of(slot_terms, 0, out_rows),
+        total_of(out_terms, 0, out_rows),
         total_of(node_terms, 0, node_rows),
         total_of(node_terms, node_rows, node_rows + w_node_out.shape[0] // peers),
     )

time: 102 us -> 101 us (level); the launches traced: 102 us -> 100 us
  Pallas kernels: 38.4 us -> 24.1 us
  starting transfers between devices: 35.9 us -> 43.5 us
  waiting for transfers between devices: 21.8 us -> 26.5 us
    pallas_call x1, Pallas kernels: 16.7 us -> 8.47 us  [on_device(): pl.pallas_call(functools.partial(backward_kernel, peers), grid=(tiles,),...]
    ppermute x29 -> x31, starting transfers between devices: 35.9 us -> 43.5 us  [send(): return lax.ppermute(values, 'lon', perm)]
    pallas_call x1, Pallas kernels: 11.9 us -> 5.92 us  [on_device(): pl.pallas_call(functools.partial(forward_kernel, peers), grid=(tiles,), i...]
    ppermute x29 -> x31, waiting for transfers between devices: 21.8 us -> 26.5 us  [send(): return lax.ppermute(values, 'lon', perm)]
  transfers between devices with their start and end apart: 29 -> 31, of which waited for: 9 -> 10; matrix products, arithmetic and copies ran while one was open for 4% -> 3% of each run, Pallas kernels for 22% -> 15%
where the time goes in v14:
time: 101 us; the launch traced here: 100 us
  starting transfers between devices  43.5 us (43%)
  waiting for transfers between devices  26.5 us (26%)
  Pallas kernels  24.1 us (24%)
  other arithmetic  4.37 us (4%)
  between operations  1.61 us (2%)
    ppermute x31, starting transfers between devices, send(): return lax.ppermute(values, 'lon', perm)  43.5 us
    ppermute x31, waiting for transfers between devices, send(): return lax.ppermute(values, 'lon', perm)  26.5 us
    pallas_call x1, Pallas kernels, on_device(): pl.pallas_call(functools.partial(backward_kernel, peers), grid=(tiles,),...  8.47 us
    pallas_call x1, Pallas kernels, on_device(): pl.pallas_call(functools.partial(forward_kernel, peers), grid=(tiles,), i...  5.92 us
    pallas_call x1, Pallas kernels, on_device(): pl.pallas_call(gather_kernel, in_specs=[smem, hbm, hbm], out_specs=near_s...  3.55 us
    pallas_call x1, Pallas kernels, on_device(): pl.pallas_call(local_kernel, grid=(tiles,), in_specs=[index_tile, tile_of...  3.42 us
    pallas_call x1, Pallas kernels, on_device(): pl.pallas_call(functools.partial(scatter_kernel, out_rows), grid=(2,), in...  2.75 us
    add x4, other arithmetic, total_of(): total = total + term[start:stop].astype(F32)  2.71 us
  transfers between devices with their start and end apart: 31, of which 10 were waited for; matrix products, arithmetic and copies ran while one was open for 3% of the time, Pallas kernels for 15%

profile of v14, /device:TPU:0, one launch (start us, length us, event | category | flops | bytes accessed | tf_op | source)
XLA Modules:
  0.0 100.2 jit_solution(9746872959585024952)
XLA Ops:
  0.7 3.6 %gather_lists.1 = (bf16[48,512]{1,0:T(8,128)(2,1)}, bf16[48,512]{1,0:T(8,128)(2,1)}, bf16[96,512]{1,0:T(8,128)(2,1)}, bf16[96,512]{1,0:T(8,128)(2,1)}, bf16[48,512]{1,0:T(8,128)(2,1)}, /*index=5*/bf16[48,512]{1,0:T(8,128)(2,1)}) custom-call(s32[1]{0:T(128)} %bitcast.me_ref, s32[16,48]{1,0:T(8,128)} %bitcast.24, bf16[2048,512]{1,0:T(8,128)(2,1)} %grid_hbm.1), custom_call_target="tpu_custom_call" | custom-call | flops 32212254720 | bytes 2097152 | tf_op jit(solution)/shard_map/gather_lists/pallas_call | solution.py:528
  4.2 3.1 %collective-permute-start = (bf16[48,512]{1,0:T(8,128)(2,1)}, bf16[48,512]{1,0:T(8,128)(2,1)S(1)}, u32[]{:S(2)}, u32[]{:S(2)}) collective-permute-start(bf16[48,512]{1,0:T(8,128)(2,1)} %get-tuple-element.93), channel_id=1, source_target_pairs={{0,4},{1,5},{2,6},{3,7},{4,0},{5,1},{6,2},{7,3},{8,12},{9,13},{10,... | collective-permute-start | bytes 147464 | tf_op jit(solution)/shard_map/ppermute | solution.py:416
  7.3 2.5 %collective-permute-start.2 = (bf16[48,512]{1,0:T(8,128)(2,1)}, bf16[48,512]{1,0:T(8,128)(2,1)S(1)}, u32[]{:S(2)}, u32[]{:S(2)}) collective-permute-start(bf16[48,512]{1,0:T(8,128)(2,1)} %get-tuple-element.93), channel_id=1, source_target_pairs={{0,12},{1,13},{2,14},{3,15},{4,8},{5,9},{6,10},{7,11},{8,4},{9,5},... | collective-permute-start | bytes 147464 | tf_op jit(solution)/shard_map/ppermute | solution.py:416
  11.4 3.2 %collective-permute-start.6 = (bf16[96,512]{1,0:T(8,128)(2,1)}, bf16[96,512]{1,0:T(8,128)(2,1)S(1)}, u32[]{:S(2)}, u32[]{:S(2)}) collective-permute-start(bf16[96,512]{1,0:T(8,128)(2,1)} %get-tuple-element.100), channel_id=1, source_target_pairs={{0,14},{1,15},{2,0},{3,1},{4,2},{5,3},{6,4},{7,5},{8,6},{9,7},{10,... | collective-permute-start | bytes 294920 | tf_op jit(solution)/shard_map/ppermute | solution.py:416
  16.8 3.3 %collective-permute-start.3 = (bf16[192,512]{1,0:T(8,128)(2,1)S(1)}, bf16[192,512]{1,0:T(8,128)(2,1)S(1)}, u32[]{:S(2)}, u32[]{:S(2)}) collective-permute-start(bf16[192,512]{1,0:T(8,128)(2,1)S(1)} %pad_maximum_fusion.refs_7_), channel_id=1, source_target_pairs={{0,2},{1,3},{2,0},{3,1},{4,6},{5,7},{6,4},{7,5},{8,10},{9,11},{10,... | collective-permute-start | bytes 589832 | tf_op jit(solution)/shard_map/ppermute | solution.py:416
  20.6 3.4 %edge_local.1.local_ref = bf16[3072,512]{1,0:T(8,128)(2,1)S(1)} custom-call(s32[3,1,1024]{2,1,0:T(1,128)S(1)} %bitcast.19, bf16[3072,512]{1,0:T(8,128)(2,1)S(1)} %copy-done.1, bf16[256,512]{1,0:T(8,128)(2,1)S(1)} %copy-done.2, bf16[1536,512]{1,0:T(8,128)(2,1)S(1)} %copy-done, bf16[1536,512]{1,0:T(8,128)(2,1)S(1)} %copy-done), custom_call_target="tpu_custom_call" | custom-call | flops 2415919104 | bytes 6291456 | tf_op jit(solution)/shard_map/edge_local/pallas_call | solution.py:556
  24.0 1.6 %collective-permute-done.7.refs_4_ = bf16[48,512]{1,0:T(8,128)(2,1)S(1)} collective-permute-done((bf16[48,512]{1,0:T(8,128)(2,1)}, bf16[48,512]{1,0:T(8,128)(2,1)S(1)}, u32[]{:S(2)}, u32[]{:S(2)}) %collective-permute-start.7) | collective-permute-done | bytes 49184 | tf_op jit(solution)/shard_map/ppermute | solution.py:416
  27.7 5.9 %forward.1 = (bf16[768,512]{1,0:T(8,128)(2,1)S(1)}, bf16[3072,512]{1,0:T(8,128)(2,1)S(1)}, bf16[3072,512]{1,0:T(8,128)(2,1)S(1)}, bf16[3072,512]{1,0:T(8,128)(2,...) custom-call(s32[1]{0:T(128)} %bitcast.me_ref, ...), custom_call_target="tpu_custom_call" | custom-call | tf_op jit(solution)/shard_map/forward/pallas_call | solution.py:576
  33.6 1.7 %collective-permute-start.12 = (bf16[2,384,512]{2,1,0:T(8,128)(2,1)S(1)}, bf16[2,384,512]{2,1,0:T(8,128)(2,1)S(1)}, u32[]{:S(2)}, u32[]{:S(2)}) collective-permute-start(bf16[2,384,512]{2,1,0:T(8,128)(2,1)S(1)} %get-tuple-element.112), channel_id=1, source_target_pairs={{0,2},{1,3},{2,0},{3,1},{4,6},{5,7},{6,4},{7,5},{8,10},{9,11},{10,... | collective-permute-start | bytes 2359304 | tf_op jit(solution)/shard_map/ppermute | solution.py:416
  35.3 8.5 %backward.1 = (bf16[3072,512]{1,0:T(8,128)(2,1)}, bf16[256,512]{1,0:T(8,128)(2,1)}, bf16[2,320,512]{2,1,0:T(8,128)(2,1)S(1)}, bf16[2,320,512]{2,1,0:T(8,128)(2,1...) custom-call(s32[1]{0:T(128)} %bitcast.me_ref, ...), custom_call_target="tpu_custom_call" | custom-call | flops 10468982784 | bytes 15728640 | tf_op jit(solution)/shard_map/backward/pallas_call | solution.py:626
  43.8 8.6 %collective-permute-done.12 = bf16[2,384,512]{2,1,0:T(8,128)(2,1)S(1)} collective-permute-done((bf16[2,384,512]{2,1,0:T(8,128)(2,1)S(1)}, bf16[2,384,512]{2,1,0:T(8,128)(2,1)S(1)}, u32[]{:S(2)}, u32[]{:S(2)}) %collective-permute-start.12) | collective-permute-done | bytes 786464 | tf_op jit(solution)/shard_map/ppermute | solution.py:416
  54.8 1.7 %collective-permute-done.15 = bf16[384,512]{1,0:T(8,128)(2,1)S(1)} collective-permute-done((bf16[384,512]{1,0:T(8,128)(2,1)S(1)}, bf16[384,512]{1,0:T(8,128)(2,1)S(1)}, u32[]{:S(2)}, u32[]{:S(2)}) %collective-permute-start.15) | collective-permute-done | bytes 393248 | tf_op jit(solution)/shard_map/ppermute | solution.py:416
  56.7 1.7 %collective-permute-start.14 = (bf16[320,512]{1,0:T(8,128)(2,1)S(1)}, bf16[320,512]{1,0:T(8,128)(2,1)S(1)}, u32[]{:S(2)}, u32[]{:S(2)}) collective-permute-start(bf16[320,512]{1,0:T(8,128)(2,1)S(1)} %fusion.6), channel_id=1, source_target_pairs={{0,2},{1,3},{2,0},{3,1},{4,6},{5,7},{6,4},{7,5},{8,10},{9,11},{10,... | collective-permute-start | bytes 983048 | tf_op jit(solution)/shard_map/ppermute | solution.py:416
  58.6 3.3 %collective-permute-start.18 = (bf16[48,512]{1,0:T(8,128)(2,1)S(1)}, bf16[48,512]{1,0:T(8,128)(2,1)S(1)}, u32[]{:S(2)}, u32[]{:S(2)}) collective-permute-start(bf16[48,512]{1,0:T(8,128)(2,1)S(1)} %get-tuple-element.139), channel_id=1, source_target_pairs={{0,13},{1,4},{2,15},{3,6},{4,1},{5,8},{6,3},{7,10},{8,5},{9,12},{1... | collective-permute-start | bytes 147464 | tf_op jit(solution)/shard_map/ppermute | solution.py:416
  61.9 2.4 %collective-permute-start.21 = (bf16[96,512]{1,0:T(8,128)(2,1)S(1)}, bf16[96,512]{1,0:T(8,128)(2,1)S(1)}, u32[]{:S(2)}, u32[]{:S(2)}) collective-permute-start(bf16[96,512]{1,0:T(8,128)(2,1)S(1)} %get-tuple-element.187), channel_id=1, source_target_pairs={{0,12},{1,13},{2,14},{3,15},{4,8},{5,9},{6,10},{7,11},{8,4},{9,5},... | collective-permute-start | bytes 294920 | tf_op jit(solution)/shard_map/ppermute | solution.py:416
  64.4 2.0 %collective-permute-start.19 = (bf16[96,512]{1,0:T(8,128)(2,1)S(1)}, bf16[96,512]{1,0:T(8,128)(2,1)S(1)}, u32[]{:S(2)}, u32[]{:S(2)}) collective-permute-start(bf16[96,512]{1,0:T(8,128)(2,1)S(1)} %get-tuple-element.189), channel_id=1, source_target_pairs={{0,4},{1,5},{2,6},{3,7},{4,0},{5,1},{6,2},{7,3},{8,12},{9,13},{10,... | collective-permute-start | bytes 294920 | tf_op jit(solution)/shard_map/ppermute | solution.py:416
  66.9 2.6 %collective-permute-done.21 = bf16[96,512]{1,0:T(8,128)(2,1)S(1)} collective-permute-done((bf16[96,512]{1,0:T(8,128)(2,1)S(1)}, bf16[96,512]{1,0:T(8,128)(2,1)S(1)}, u32[]{:S(2)}, u32[]{:S(2)}) %collective-permute-start.21) | collective-permute-done | bytes 98336 | tf_op jit(solution)/shard_map/ppermute | solution.py:416
  69.5 4.1 %collective-permute-done.20 = bf16[96,512]{1,0:T(8,128)(2,1)S(1)} collective-permute-done((bf16[96,512]{1,0:T(8,128)(2,1)S(1)}, bf16[96,512]{1,0:T(8,128)(2,1)S(1)}, u32[]{:S(2)}, u32[]{:S(2)}) %collective-permute-start.20) | collective-permute-done | bytes 98336 | tf_op jit(solution)/shard_map/ppermute | solution.py:416
  74.8 2.3 %collective-permute-start.24 = (bf16[80,512]{1,0:T(8,128)(2,1)S(1)}, bf16[80,512]{1,0:T(8,128)(2,1)S(1)}, u32[]{:S(2)}, u32[]{:S(2)}) collective-permute-start(bf16[80,512]{1,0:T(8,128)(2,1)S(1)} %get-tuple-element.191), channel_id=1, source_target_pairs={{0,12},{1,13},{2,14},{3,15},{4,8},{5,9},{6,10},{7,11},{8,4},{9,5},... | collective-permute-start | bytes 245768 | tf_op jit(solution)/shard_map/ppermute | solution.py:416
  77.1 2.2 %collective-permute-start.22 = (bf16[80,512]{1,0:T(8,128)(2,1)S(1)}, bf16[80,512]{1,0:T(8,128)(2,1)S(1)}, u32[]{:S(2)}, u32[]{:S(2)}) collective-permute-start(bf16[80,512]{1,0:T(8,128)(2,1)S(1)} %get-tuple-element.193), channel_id=1, source_target_pairs={{0,4},{1,5},{2,6},{3,7},{4,0},{5,1},{6,2},{7,3},{8,12},{9,13},{10,... | collective-permute-start | bytes 245768 | tf_op jit(solution)/shard_map/ppermute | solution.py:416
  79.2 5.4 %collective-permute-done.25 = bf16[384,512]{1,0:T(8,128)(2,1)S(1)} collective-permute-done((bf16[384,512]{1,0:T(8,128)(2,1)S(1)}, bf16[384,512]{1,0:T(8,128)(2,1)S(1)}, u32[]{:S(2)}, u32[]{:S(2)}) %collective-permute-start.25) | collective-permute-done | bytes 393248 | tf_op jit(solution)/shard_map/ppermute | solution.py:416
  86.1 3.5 %collective-permute-start.30 = (bf16[96,512]{1,0:T(8,128)(2,1)S(1)}, bf16[96,512]{1,0:T(8,128)(2,1)S(1)}, u32[]{:S(2)}, u32[]{:S(2)}) collective-permute-start(bf16[96,512]{1,0:T(8,128)(2,1)S(1)} %get-tuple-element.160), channel_id=1, source_target_pairs={{0,14},{1,15},{2,0},{3,1},{4,2},{5,3},{6,4},{7,5},{8,6},{9,7},{10,... | collective-permute-start | bytes 294920 | tf_op jit(solution)/shard_map/ppermute | solution.py:416
  90.5 3.5 %collective-permute-start.26 = (bf16[96,512]{1,0:T(8,128)(2,1)S(1)}, bf16[96,512]{1,0:T(8,128)(2,1)S(1)}, u32[]{:S(2)}, u32[]{:S(2)}) collective-permute-start(bf16[96,512]{1,0:T(8,128)(2,1)S(1)} %get-tuple-element.185), channel_id=1, source_target_pairs={{0,4},{1,5},{2,6},{3,7},{4,0},{5,1},{6,2},{7,3},{8,12},{9,13},{10,... | collective-permute-start | bytes 294920 | tf_op jit(solution)/shard_map/ppermute | solution.py:416
  95.3 2.8 %scatter_lists.1 = bf16[2048,512]{1,0:T(8,128)(2,1)} custom-call(s32[1]{0:T(128)} %bitcast.me_ref, s32[16,48]{1,0:T(8,128)S(1)} %bitcast.25, bf16[48,512]{1,0:T(8,128)(2,1)S(1)} %get-tuple-element.150.refs_0_, bf16[144,512]{1,0:T(8,128)(2,1)S(1)} %collective-permute-done.17.refs_1_, bf16[96,512]{1,0:T(8,128)(2,1)S(1)} %collective-permute-done.29.refs_2_, ...), custom_call_target="tpu_custom_call" | custom-call | tf_op jit(solution)/shard_map/scatter_lists/pallas_call | solution.py:704
  (83 shorter events, 15.9 us)
Async XLA Ops:
  4.2 10.4 %collective-permute-start = (bf16[48,512]{1,0:T(8,128)(2,1)}, bf16[48,512]{1,0:T(8,128)(2,1)S(1)}, u32[]{:S(2)}, u32[]{:S(2)}) collective-permute-start(bf16[48,512]{1,0:T(8,128)(2,1)} %get-tuple-element.93), channel_id=1, source_target_pairs={{0,4},{1,5},{2,6},{3,7},{4,0},{5,1},{6,2},{7,3},{8,12},{9,13},{10,... | collective-permute-start | bytes 147464 | tf_op jit(solution)/shard_map/ppermute | solution.py:416
  7.3 7.3 %collective-permute-start.2 = (bf16[48,512]{1,0:T(8,128)(2,1)}, bf16[48,512]{1,0:T(8,128)(2,1)S(1)}, u32[]{:S(2)}, u32[]{:S(2)}) collective-permute-start(bf16[48,512]{1,0:T(8,128)(2,1)} %get-tuple-element.93), channel_id=1, source_target_pairs={{0,12},{1,13},{2,14},{3,15},{4,8},{5,9},{6,10},{7,11},{8,4},{9,5},... | collective-permute-start | bytes 147464 | tf_op jit(solution)/shard_map/ppermute | solution.py:416
  9.8 6.0 %collective-permute-start.1 = (bf16[48,512]{1,0:T(8,128)(2,1)}, bf16[48,512]{1,0:T(8,128)(2,1)S(1)}, u32[]{:S(2)}, u32[]{:S(2)}) collective-permute-start(bf16[48,512]{1,0:T(8,128)(2,1)} %get-tuple-element.93), channel_id=1, source_target_pairs={{0,8},{1,9},{2,10},{3,11},{4,12},{5,13},{6,14},{7,15},{8,0},{9,1},... | collective-permute-start | bytes 147464 | tf_op jit(solution)/shard_map/ppermute | solution.py:416
  9.9 15.7 %collective-permute-start.5 = (bf16[96,512]{1,0:T(8,128)(2,1)}, bf16[96,512]{1,0:T(8,128)(2,1)S(1)}, u32[]{:S(2)}, u32[]{:S(2)}) collective-permute-start(bf16[96,512]{1,0:T(8,128)(2,1)} %get-tuple-element.99), channel_id=1, source_target_pairs={{0,2},{1,3},{2,4},{3,5},{4,6},{5,7},{6,8},{7,9},{8,10},{9,11},{10,... | collective-permute-start | bytes 294920 | tf_op jit(solution)/shard_map/ppermute | solution.py:416
  11.4 14.2 %collective-permute-start.6 = (bf16[96,512]{1,0:T(8,128)(2,1)}, bf16[96,512]{1,0:T(8,128)(2,1)S(1)}, u32[]{:S(2)}, u32[]{:S(2)}) collective-permute-start(bf16[96,512]{1,0:T(8,128)(2,1)} %get-tuple-element.100), channel_id=1, source_target_pairs={{0,14},{1,15},{2,0},{3,1},{4,2},{5,3},{6,4},{7,5},{8,6},{9,7},{10,... | collective-permute-start | bytes 294920 | tf_op jit(solution)/shard_map/ppermute | solution.py:416
  16.7 8.9 %collective-permute-start.4 = (bf16[192,512]{1,0:T(8,128)(2,1)S(1)}, bf16[192,512]{1,0:T(8,128)(2,1)S(1)}, u32[]{:S(2)}, u32[]{:S(2)}) collective-permute-start(bf16[192,512]{1,0:T(8,128)(2,1)S(1)} %pad_maximum_fusion.refs_7_), channel_id=1, source_target_pairs={{0,1},{1,0},{2,3},{3,2},{4,5},{5,4},{6,7},{7,6},{8,9},{9,8},{10,11... | collective-permute-start | bytes 589832 | tf_op jit(solution)/shard_map/ppermute | solution.py:416
  16.8 8.8 %collective-permute-start.3 = (bf16[192,512]{1,0:T(8,128)(2,1)S(1)}, bf16[192,512]{1,0:T(8,128)(2,1)S(1)}, u32[]{:S(2)}, u32[]{:S(2)}) collective-permute-start(bf16[192,512]{1,0:T(8,128)(2,1)S(1)} %pad_maximum_fusion.refs_7_), channel_id=1, source_target_pairs={{0,2},{1,3},{2,0},{3,1},{4,6},{5,7},{6,4},{7,5},{8,10},{9,11},{10,... | collective-permute-start | bytes 589832 | tf_op jit(solution)/shard_map/ppermute | solution.py:416
  20.1 5.5 %collective-permute-start.7 = (bf16[48,512]{1,0:T(8,128)(2,1)}, bf16[48,512]{1,0:T(8,128)(2,1)S(1)}, u32[]{:S(2)}, u32[]{:S(2)}) collective-permute-start(bf16[48,512]{1,0:T(8,128)(2,1)} %get-tuple-element.101), channel_id=1, source_target_pairs={{0,13},{1,4},{2,15},{3,6},{4,1},{5,8},{6,3},{7,10},{8,5},{9,12},{1... | collective-permute-start | bytes 147464 | tf_op jit(solution)/shard_map/ppermute | solution.py:416
  33.6 18.8 %collective-permute-start.12 = (bf16[2,384,512]{2,1,0:T(8,128)(2,1)S(1)}, bf16[2,384,512]{2,1,0:T(8,128)(2,1)S(1)}, u32[]{:S(2)}, u32[]{:S(2)}) collective-permute-start(bf16[2,384,512]{2,1,0:T(8,128)(2,1)S(1)} %get-tuple-element.112), channel_id=1, source_target_pairs={{0,2},{1,3},{2,0},{3,1},{4,6},{5,7},{6,4},{7,5},{8,10},{9,11},{10,... | collective-permute-start | bytes 2359304 | tf_op jit(solution)/shard_map/ppermute | solution.py:416
  54.3 4.1 %collective-permute-start.16 = (bf16[2,384,512]{2,1,0:T(8,128)(2,1)S(1)}, bf16[2,384,512]{2,1,0:T(8,128)(2,1)S(1)}, u32[]{:S(2)}, u32[]{:S(2)}) collective-permute-start(bf16[2,384,512]{2,1,0:T(8,128)(2,1)S(1)} %get-tuple-element.134), channel_id=1, source_target_pairs={{0,1},{1,0},{2,3},{3,2},{4,5},{5,4},{6,7},{7,6},{8,9},{9,8},{10,11... | collective-permute-start | bytes 2359304 | tf_op jit(solution)/shard_map/ppermute | solution.py:416
  56.7 10.1 %collective-permute-start.14 = (bf16[320,512]{1,0:T(8,128)(2,1)S(1)}, bf16[320,512]{1,0:T(8,128)(2,1)S(1)}, u32[]{:S(2)}, u32[]{:S(2)}) collective-permute-start(bf16[320,512]{1,0:T(8,128)(2,1)S(1)} %fusion.6), channel_id=1, source_target_pairs={{0,2},{1,3},{2,0},{3,1},{4,6},{5,7},{6,4},{7,5},{8,10},{9,11},{10,... | collective-permute-start | bytes 983048 | tf_op jit(solution)/shard_map/ppermute | solution.py:416
  58.6 8.2 %collective-permute-start.18 = (bf16[48,512]{1,0:T(8,128)(2,1)S(1)}, bf16[48,512]{1,0:T(8,128)(2,1)S(1)}, u32[]{:S(2)}, u32[]{:S(2)}) collective-permute-start(bf16[48,512]{1,0:T(8,128)(2,1)S(1)} %get-tuple-element.139), channel_id=1, source_target_pairs={{0,13},{1,4},{2,15},{3,6},{4,1},{5,8},{6,3},{7,10},{8,5},{9,12},{1... | collective-permute-start | bytes 147464 | tf_op jit(solution)/shard_map/ppermute | solution.py:416
  61.9 7.5 %collective-permute-start.21 = (bf16[96,512]{1,0:T(8,128)(2,1)S(1)}, bf16[96,512]{1,0:T(8,128)(2,1)S(1)}, u32[]{:S(2)}, u32[]{:S(2)}) collective-permute-start(bf16[96,512]{1,0:T(8,128)(2,1)S(1)} %get-tuple-element.187), channel_id=1, source_target_pairs={{0,12},{1,13},{2,14},{3,15},{4,8},{5,9},{6,10},{7,11},{8,4},{9,5},... | collective-permute-start | bytes 294920 | tf_op jit(solution)/shard_map/ppermute | solution.py:416
  64.4 9.2 %collective-permute-start.20 = (bf16[96,512]{1,0:T(8,128)(2,1)S(1)}, bf16[96,512]{1,0:T(8,128)(2,1)S(1)}, u32[]{:S(2)}, u32[]{:S(2)}) collective-permute-start(bf16[96,512]{1,0:T(8,128)(2,1)S(1)} %get-tuple-element.188), channel_id=1, source_target_pairs={{0,8},{1,9},{2,10},{3,11},{4,12},{5,13},{6,14},{7,15},{8,0},{9,1},... | collective-permute-start | bytes 294920 | tf_op jit(solution)/shard_map/ppermute | solution.py:416
  64.4 9.2 %collective-permute-start.19 = (bf16[96,512]{1,0:T(8,128)(2,1)S(1)}, bf16[96,512]{1,0:T(8,128)(2,1)S(1)}, u32[]{:S(2)}, u32[]{:S(2)}) collective-permute-start(bf16[96,512]{1,0:T(8,128)(2,1)S(1)} %get-tuple-element.189), channel_id=1, source_target_pairs={{0,4},{1,5},{2,6},{3,7},{4,0},{5,1},{6,2},{7,3},{8,12},{9,13},{10,... | collective-permute-start | bytes 294920 | tf_op jit(solution)/shard_map/ppermute | solution.py:416
  73.6 11.0 %collective-permute-start.25 = (bf16[384,512]{1,0:T(8,128)(2,1)S(1)}, bf16[384,512]{1,0:T(8,128)(2,1)S(1)}, u32[]{:S(2)}, u32[]{:S(2)}) collective-permute-start(bf16[384,512]{1,0:T(8,128)(2,1)S(1)} %get-tuple-element.146), channel_id=1, source_target_pairs={{0,2},{1,3},{2,0},{3,1},{4,6},{5,7},{6,4},{7,5},{8,10},{9,11},{10,... | collective-permute-start | bytes 1179656 | tf_op jit(solution)/shard_map/ppermute | solution.py:416
  74.8 9.9 %collective-permute-start.24 = (bf16[80,512]{1,0:T(8,128)(2,1)S(1)}, bf16[80,512]{1,0:T(8,128)(2,1)S(1)}, u32[]{:S(2)}, u32[]{:S(2)}) collective-permute-start(bf16[80,512]{1,0:T(8,128)(2,1)S(1)} %get-tuple-element.191), channel_id=1, source_target_pairs={{0,12},{1,13},{2,14},{3,15},{4,8},{5,9},{6,10},{7,11},{8,4},{9,5},... | collective-permute-start | bytes 245768 | tf_op jit(solution)/shard_map/ppermute | solution.py:416
  77.1 7.7 %collective-permute-start.23 = (bf16[80,512]{1,0:T(8,128)(2,1)S(1)}, bf16[80,512]{1,0:T(8,128)(2,1)S(1)}, u32[]{:S(2)}, u32[]{:S(2)}) collective-permute-start(bf16[80,512]{1,0:T(8,128)(2,1)S(1)} %get-tuple-element.192), channel_id=1, source_target_pairs={{0,8},{1,9},{2,10},{3,11},{4,12},{5,13},{6,14},{7,15},{8,0},{9,1},... | collective-permute-start | bytes 245768 | tf_op jit(solution)/shard_map/ppermute | solution.py:416
  77.1 7.7 %collective-permute-start.22 = (bf16[80,512]{1,0:T(8,128)(2,1)S(1)}, bf16[80,512]{1,0:T(8,128)(2,1)S(1)}, u32[]{:S(2)}, u32[]{:S(2)}) collective-permute-start(bf16[80,512]{1,0:T(8,128)(2,1)S(1)} %get-tuple-element.193), channel_id=1, source_target_pairs={{0,4},{1,5},{2,6},{3,7},{4,0},{5,1},{6,2},{7,3},{8,12},{9,13},{10,... | collective-permute-start | bytes 245768 | tf_op jit(solution)/shard_map/ppermute | solution.py:416
  84.7 9.3 %collective-permute-start.29 = (bf16[96,512]{1,0:T(8,128)(2,1)S(1)}, bf16[96,512]{1,0:T(8,128)(2,1)S(1)}, u32[]{:S(2)}, u32[]{:S(2)}) collective-permute-start(bf16[96,512]{1,0:T(8,128)(2,1)S(1)} %get-tuple-element.159), channel_id=1, source_target_pairs={{0,2},{1,3},{2,4},{3,5},{4,6},{5,7},{6,8},{7,9},{8,10},{9,11},{10,... | collective-permute-start | bytes 294920 | tf_op jit(solution)/shard_map/ppermute | solution.py:416
  86.1 7.9 %collective-permute-start.30 = (bf16[96,512]{1,0:T(8,128)(2,1)S(1)}, bf16[96,512]{1,0:T(8,128)(2,1)S(1)}, u32[]{:S(2)}, u32[]{:S(2)}) collective-permute-start(bf16[96,512]{1,0:T(8,128)(2,1)S(1)} %get-tuple-element.160), channel_id=1, source_target_pairs={{0,14},{1,15},{2,0},{3,1},{4,2},{5,3},{6,4},{7,5},{8,6},{9,7},{10,... | collective-permute-start | bytes 294920 | tf_op jit(solution)/shard_map/ppermute | solution.py:416
  89.5 8.6 %collective-permute-start.28 = (bf16[96,512]{1,0:T(8,128)(2,1)S(1)}, bf16[96,512]{1,0:T(8,128)(2,1)S(1)}, u32[]{:S(2)}, u32[]{:S(2)}) collective-permute-start(bf16[96,512]{1,0:T(8,128)(2,1)S(1)} %get-tuple-element.183), channel_id=1, source_target_pairs={{0,12},{1,13},{2,14},{3,15},{4,8},{5,9},{6,10},{7,11},{8,4},{9,5},... | collective-permute-start | bytes 294920 | tf_op jit(solution)/shard_map/ppermute | solution.py:416
  90.5 8.3 %collective-permute-start.27 = (bf16[96,512]{1,0:T(8,128)(2,1)S(1)}, bf16[96,512]{1,0:T(8,128)(2,1)S(1)}, u32[]{:S(2)}, u32[]{:S(2)}) collective-permute-start(bf16[96,512]{1,0:T(8,128)(2,1)S(1)} %get-tuple-element.184), channel_id=1, source_target_pairs={{0,8},{1,9},{2,10},{3,11},{4,12},{5,13},{6,14},{7,15},{8,0},{9,1},... | collective-permute-start | bytes 294920 | tf_op jit(solution)/shard_map/ppermute | solution.py:416
  90.5 8.3 %collective-permute-start.26 = (bf16[96,512]{1,0:T(8,128)(2,1)S(1)}, bf16[96,512]{1,0:T(8,128)(2,1)S(1)}, u32[]{:S(2)}, u32[]{:S(2)}) collective-permute-start(bf16[96,512]{1,0:T(8,128)(2,1)S(1)} %get-tuple-element.185), channel_id=1, source_target_pairs={{0,4},{1,5},{2,6},{3,7},{4,0},{5,1},{6,2},{7,3},{8,12},{9,13},{10,... | collective-permute-start | bytes 294920 | tf_op jit(solution)/shard_map/ppermute | solution.py:416
  (19 other events, 208.4 us)

commit v15 on v14

--- a/solution.py
+++ b/solution.py
@@ -459,6 +459,23 @@
     for place in range(1, count):
         piece = pieces[place * share : (place + 1) * share]
         terms.append(send(piece, by_xor(peers, 4 * place)))
+    return terms
+
+
+def halve_sum(peers, pieces):
+    count = peers // 4
+    blocks = pieces.reshape(count // 2, 2, -1, pieces.shape[1])
+    kept, outgoing = [blocks[:, place].reshape(-1, pieces.shape[1]) for place in range(2)]
+    return add(kept, send(outgoing, by_xor(peers, 4)))
+
+
+def rest_terms(peers, pieces):
+    count = peers // 8
+    share = pieces.shape[0] // count
+    terms = [pieces[:share]]
+    for place in range(1, count):
+        piece = pieces[place * share : (place + 1) * share]
+        terms.append(send(piece, by_xor(peers, 8 * place)))
     return terms
 
 
@@ -683,21 +700,21 @@
     node_pieces, edge_next, edge_kept, swapped, across = lax.optimization_barrier(
         (node_pieces, edge_next, edge_kept, swapped, returns[4])
     )
-    node_terms = last_terms(peers, node_pieces)
+    node_pieces = halve_sum(peers, node_pieces)
     across = send(across, across_chips(peers))
     to_after = jnp.concatenate([returns[2], swapped[cap : 2 * cap]], axis=0)
     to_before = jnp.concatenate([returns[3], swapped[2 * cap :]], axis=0)
-    (slot_pieces, edge_next, edge_kept, across, node_terms, to_after, to_before) = lax.optimization_barrier(
-        (slot_pieces, edge_next, edge_kept, across, node_terms, to_after, to_before)
+    (slot_pieces, edge_next, edge_kept, across, node_pieces, to_after, to_before) = lax.optimization_barrier(
+        (slot_pieces, edge_next, edge_kept, across, node_pieces, to_after, to_before)
     )
     edge_pieces = next_sum(peers, 2, edge_next, edge_kept)
     slot_terms = last_terms(peers, slot_pieces)
-    (slot_terms, edge_pieces, to_after, to_before) = lax.optimization_barrier(
-        (slot_terms, edge_pieces, to_after, to_before)
+    node_terms = rest_terms(peers, node_pieces)
+    (slot_terms, node_terms, edge_pieces, to_after, to_before) = lax.optimization_barrier(
+        (slot_terms, node_terms, edge_pieces, to_after, to_before)
     )
     edge_terms = last_terms(peers, edge_pieces)
     bundles = [send(to_after, by_shift(peers, 2)), send(to_before, by_shift(peers, -2))]
-    node_terms, out_terms, bundles = lax.optimization_barrier((node_terms, slot_terms, bundles))
     returned = [returns[0], swapped, *bundles, across]
     node_rows = w_node_in.shape[0] // peers
     out_rows = w_edge_out.shape[0] // peers
@@ -712,6 +729,7 @@
         compiler_params=params,
         name="scatter_lists",
     )(me, rows, *returned, *slot_terms)
+    node_terms, out_terms, grid_grad = lax.optimization_barrier((node_terms, slot_terms, grid_grad))
     edge_terms, grid_grad = lax.optimization_barrier((edge_terms, grid_grad))
     return (
         grid_grad,

time: 101 us -> 102 us (level); the launches traced: 100 us -> 102 us
  Pallas kernels: 24.1 us -> 38.1 us
  starting transfers between devices: 43.5 us -> 36.9 us
  waiting for transfers between devices: 26.5 us -> 21 us
    pallas_call x1, Pallas kernels: 8.47 us -> 16.7 us  [on_device(): pl.pallas_call(functools.partial(backward_kernel, peers), grid=(tiles,),...]
    ppermute x31 -> x30, starting transfers between devices: 43.5 us -> 36.9 us  [send(): return lax.ppermute(values, 'lon', perm)]
    pallas_call x1, Pallas kernels: 5.92 us -> 11.6 us  [on_device(): pl.pallas_call(functools.partial(forward_kernel, peers), grid=(tiles,), i...]
    ppermute x31 -> x30, waiting for transfers between devices: 26.5 us -> 21 us  [send(): return lax.ppermute(values, 'lon', perm)]
  transfers between devices with their start and end apart: 31 -> 30, of which waited for: 10 -> 10; matrix products, arithmetic and copies ran while one was open for 3% -> 3% of each run, Pallas kernels for 15% -> 22%
where the time goes in v15:
time: 102 us
  Pallas kernels  38.1 us (37%)
  starting transfers between devices  36.9 us (36%)
  waiting for transfers between devices  21 us (21%)
  other arithmetic  4.43 us (4%)
  between operations  1.65 us (2%)
    ppermute x30, starting transfers between devices, send(): return lax.ppermute(values, 'lon', perm)  36.9 us
    ppermute x30, waiting for transfers between devices, send(): return lax.ppermute(values, 'lon', perm)  21 us
    pallas_call x1, Pallas kernels, on_device(): pl.pallas_call(functools.partial(backward_kernel, peers), grid=(tiles,),...  16.7 us
    pallas_call x1, Pallas kernels, on_device(): pl.pallas_call(functools.partial(forward_kernel, peers), grid=(tiles,), i...  11.6 us
    pallas_call x1, Pallas kernels, on_device(): pl.pallas_call(gather_kernel, in_specs=[smem, hbm, hbm], out_specs=near_s...  3.55 us
    pallas_call x1, Pallas kernels, on_device(): pl.pallas_call(local_kernel, grid=(tiles,), in_specs=[index_tile, tile_of...  3.42 us
    pallas_call x1, Pallas kernels, on_device(): pl.pallas_call(functools.partial(scatter_kernel, out_rows), grid=(2,), in...  2.77 us
    add x4, other arithmetic, total_of(): total = total + term[start:stop].astype(F32)  2.68 us
  transfers between devices with their start and end apart: 30, of which 10 were waited for; matrix products, arithmetic and copies ran while one was open for 3% of the time, Pallas kernels for 22%

profile of v15, /device:TPU:0, one launch (start us, length us, event | category | flops | bytes accessed | tf_op | source)
XLA Modules:
  0.0 102.3 jit_solution(9983249871047745130)
XLA Ops:
  0.7 3.6 %gather_lists.1 = (bf16[48,512]{1,0:T(8,128)(2,1)}, bf16[48,512]{1,0:T(8,128)(2,1)}, bf16[96,512]{1,0:T(8,128)(2,1)}, bf16[96,512]{1,0:T(8,128)(2,1)}, bf16[48,512]{1,0:T(8,128)(2,1)}, /*index=5*/bf16[48,512]{1,0:T(8,128)(2,1)}) custom-call(s32[1]{0:T(128)} %bitcast.me_ref, s32[16,48]{1,0:T(8,128)} %bitcast.29, bf16[2048,512]{1,0:T(8,128)(2,1)} %grid_hbm.1), custom_call_target="tpu_custom_call" | custom-call | flops 32212254720 | bytes 2097152 | tf_op jit(solution)/shard_map/gather_lists/pallas_call | solution.py:545
  4.2 3.1 %collective-permute-start = (bf16[48,512]{1,0:T(8,128)(2,1)}, bf16[48,512]{1,0:T(8,128)(2,1)S(1)}, u32[]{:S(2)}, u32[]{:S(2)}) collective-permute-start(bf16[48,512]{1,0:T(8,128)(2,1)} %get-tuple-element.89), channel_id=1, source_target_pairs={{0,4},{1,5},{2,6},{3,7},{4,0},{5,1},{6,2},{7,3},{8,12},{9,13},{10,... | collective-permute-start | bytes 147464 | tf_op jit(solution)/shard_map/ppermute | solution.py:416
  7.3 2.5 %collective-permute-start.2 = (bf16[48,512]{1,0:T(8,128)(2,1)}, bf16[48,512]{1,0:T(8,128)(2,1)S(1)}, u32[]{:S(2)}, u32[]{:S(2)}) collective-permute-start(bf16[48,512]{1,0:T(8,128)(2,1)} %get-tuple-element.89), channel_id=1, source_target_pairs={{0,12},{1,13},{2,14},{3,15},{4,8},{5,9},{6,10},{7,11},{8,4},{9,5},... | collective-permute-start | bytes 147464 | tf_op jit(solution)/shard_map/ppermute | solution.py:416
  9.9 1.5 %collective-permute-start.5 = (bf16[96,512]{1,0:T(8,128)(2,1)}, bf16[96,512]{1,0:T(8,128)(2,1)S(1)}, u32[]{:S(2)}, u32[]{:S(2)}) collective-permute-start(bf16[96,512]{1,0:T(8,128)(2,1)} %get-tuple-element.95), channel_id=1, source_target_pairs={{0,2},{1,3},{2,4},{3,5},{4,6},{5,7},{6,8},{7,9},{8,10},{9,11},{10,... | collective-permute-start | bytes 294920 | tf_op jit(solution)/shard_map/ppermute | solution.py:416
  11.4 3.2 %collective-permute-start.6 = (bf16[96,512]{1,0:T(8,128)(2,1)}, bf16[96,512]{1,0:T(8,128)(2,1)S(1)}, u32[]{:S(2)}, u32[]{:S(2)}) collective-permute-start(bf16[96,512]{1,0:T(8,128)(2,1)} %get-tuple-element.96), channel_id=1, source_target_pairs={{0,14},{1,15},{2,0},{3,1},{4,2},{5,3},{6,4},{7,5},{8,6},{9,7},{10,... | collective-permute-start | bytes 294920 | tf_op jit(solution)/shard_map/ppermute | solution.py:416
  16.8 3.3 %collective-permute-start.3 = (bf16[192,512]{1,0:T(8,128)(2,1)S(1)}, bf16[192,512]{1,0:T(8,128)(2,1)S(1)}, u32[]{:S(2)}, u32[]{:S(2)}) collective-permute-start(bf16[192,512]{1,0:T(8,128)(2,1)S(1)} %pad_maximum_fusion.refs_7_), channel_id=1, source_target_pairs={{0,2},{1,3},{2,0},{3,1},{4,6},{5,7},{6,4},{7,5},{8,10},{9,11},{10,... | collective-permute-start | bytes 589832 | tf_op jit(solution)/shard_map/ppermute | solution.py:416
  20.6 3.4 %edge_local.1.local_ref = bf16[3072,512]{1,0:T(8,128)(2,1)S(1)} custom-call(s32[3,1,1024]{2,1,0:T(1,128)S(1)} %bitcast.24, bf16[3072,512]{1,0:T(8,128)(2,1)S(1)} %copy-done.1, bf16[256,512]{1,0:T(8,128)(2,1)S(1)} %copy-done.2, bf16[1536,512]{1,0:T(8,128)(2,1)S(1)} %copy-done, bf16[1536,512]{1,0:T(8,128)(2,1)S(1)} %copy-done), custom_call_target="tpu_custom_call" | custom-call | flops 2415919104 | bytes 6291456 | tf_op jit(solution)/shard_map/edge_local/pallas_call | solution.py:573
  24.0 1.6 %collective-permute-done.7.refs_4_ = bf16[48,512]{1,0:T(8,128)(2,1)S(1)} collective-permute-done((bf16[48,512]{1,0:T(8,128)(2,1)}, bf16[48,512]{1,0:T(8,128)(2,1)S(1)}, u32[]{:S(2)}, u32[]{:S(2)}) %collective-permute-start.7) | collective-permute-done | bytes 49184 | tf_op jit(solution)/shard_map/ppermute | solution.py:416
  27.7 11.6 %forward.1 = (bf16[768,512]{1,0:T(8,128)(2,1)S(1)}, bf16[3072,512]{1,0:T(8,128)(2,1)S(1)}, bf16[3072,512]{1,0:T(8,128)(2,1)S(1)}, bf16[3072,512]{1,0:T(8,128)(2,...) custom-call(s32[1]{0:T(128)} %bitcast.me_ref, ...), custom_call_target="tpu_custom_call" | custom-call | tf_op jit(solution)/shard_map/forward/pallas_call | solution.py:593
  39.3 1.7 %collective-permute-start.12 = (bf16[2,384,512]{2,1,0:T(8,128)(2,1)S(1)}, bf16[2,384,512]{2,1,0:T(8,128)(2,1)S(1)}, u32[]{:S(2)}, u32[]{:S(2)}) collective-permute-start(bf16[2,384,512]{2,1,0:T(8,128)(2,1)S(1)} %get-tuple-element.108), channel_id=1, source_target_pairs={{0,2},{1,3},{2,0},{3,1},{4,6},{5,7},{6,4},{7,5},{8,10},{9,11},{10,... | collective-permute-start | bytes 2359304 | tf_op jit(solution)/shard_map/ppermute | solution.py:416
  41.0 16.7 %backward.1 = (bf16[3072,512]{1,0:T(8,128)(2,1)}, bf16[256,512]{1,0:T(8,128)(2,1)}, bf16[2,320,512]{2,1,0:T(8,128)(2,1)S(1)}, bf16[2,320,512]{2,1,0:T(8,128)(2,1...) custom-call(s32[1]{0:T(128)} %bitcast.me_ref, ...), custom_call_target="tpu_custom_call" | custom-call | flops 10468982784 | bytes 15728640 | tf_op jit(solution)/shard_map/backward/pallas_call | solution.py:643
  57.7 1.3 %collective-permute-done.12 = bf16[2,384,512]{2,1,0:T(8,128)(2,1)S(1)} collective-permute-done((bf16[2,384,512]{2,1,0:T(8,128)(2,1)S(1)}, bf16[2,384,512]{2,1,0:T(8,128)(2,1)S(1)}, u32[]{:S(2)}, u32[]{:S(2)}) %collective-permute-start.12) | collective-permute-done | bytes 786464 | tf_op jit(solution)/shard_map/ppermute | solution.py:416
  60.4 1.6 %collective-permute-done.15 = bf16[384,512]{1,0:T(8,128)(2,1)S(1)} collective-permute-done((bf16[384,512]{1,0:T(8,128)(2,1)S(1)}, bf16[384,512]{1,0:T(8,128)(2,1)S(1)}, u32[]{:S(2)}, u32[]{:S(2)}) %collective-permute-start.15) | collective-permute-done | bytes 393248 | tf_op jit(solution)/shard_map/ppermute | solution.py:416
  62.2 1.8 %collective-permute-start.14 = (bf16[320,512]{1,0:T(8,128)(2,1)S(1)}, bf16[320,512]{1,0:T(8,128)(2,1)S(1)}, u32[]{:S(2)}, u32[]{:S(2)}) collective-permute-start(bf16[320,512]{1,0:T(8,128)(2,1)S(1)} %fusion.7), channel_id=1, source_target_pairs={{0,2},{1,3},{2,0},{3,1},{4,6},{5,7},{6,4},{7,5},{8,10},{9,11},{10,... | collective-permute-start | bytes 983048 | tf_op jit(solution)/shard_map/ppermute | solution.py:416
  64.4 1.5 %collective-permute-start.19 = (bf16[192,512]{1,0:T(8,128)(2,1)S(1)}, bf16[192,512]{1,0:T(8,128)(2,1)S(1)}, u32[]{:S(2)}, u32[]{:S(2)}) collective-permute-start(bf16[192,512]{1,0:T(8,128)(2,1)S(1)} %bitcast.32), channel_id=1, source_target_pairs={{0,4},{1,5},{2,6},{3,7},{4,0},{5,1},{6,2},{7,3},{8,12},{9,13},{10,... | collective-permute-start | bytes 589832 | tf_op jit(solution)/shard_map/ppermute | solution.py:416
  65.9 6.1 %collective-permute-done.14 = bf16[320,512]{1,0:T(8,128)(2,1)S(1)} collective-permute-done((bf16[320,512]{1,0:T(8,128)(2,1)S(1)}, bf16[320,512]{1,0:T(8,128)(2,1)S(1)}, u32[]{:S(2)}, u32[]{:S(2)}) %collective-permute-start.14) | collective-permute-done | bytes 327712 | tf_op jit(solution)/shard_map/ppermute | solution.py:416
  72.3 1.8 %collective-permute-start.24 = (bf16[384,512]{1,0:T(8,128)(2,1)S(1)}, bf16[384,512]{1,0:T(8,128)(2,1)S(1)}, u32[]{:S(2)}, u32[]{:S(2)}) collective-permute-start(bf16[384,512]{1,0:T(8,128)(2,1)S(1)} %get-tuple-element.143), channel_id=1, source_target_pairs={{0,2},{1,3},{2,0},{3,1},{4,6},{5,7},{6,4},{7,5},{8,10},{9,11},{10,... | collective-permute-start | bytes 1179656 | tf_op jit(solution)/shard_map/ppermute | solution.py:416
  75.2 3.4 %collective-permute-start.20 = (bf16[80,512]{1,0:T(8,128)(2,1)S(1)}, bf16[80,512]{1,0:T(8,128)(2,1)S(1)}, u32[]{:S(2)}, u32[]{:S(2)}) collective-permute-start(bf16[80,512]{1,0:T(8,128)(2,1)S(1)} %get-tuple-element.183), channel_id=1, source_target_pairs={{0,4},{1,5},{2,6},{3,7},{4,0},{5,1},{6,2},{7,3},{8,12},{9,13},{10,... | collective-permute-start | bytes 245768 | tf_op jit(solution)/shard_map/ppermute | solution.py:416
  78.6 4.0 %collective-permute-done.24 = bf16[384,512]{1,0:T(8,128)(2,1)S(1)} collective-permute-done((bf16[384,512]{1,0:T(8,128)(2,1)S(1)}, bf16[384,512]{1,0:T(8,128)(2,1)S(1)}, u32[]{:S(2)}, u32[]{:S(2)}) %collective-permute-start.24) | collective-permute-done | bytes 393248 | tf_op jit(solution)/shard_map/ppermute | solution.py:416
  82.8 2.6 %collective-permute-done.21.refs_7_ = bf16[80,512]{1,0:T(8,128)(2,1)S(1)} collective-permute-done((bf16[80,512]{1,0:T(8,128)(2,1)S(1)}, bf16[80,512]{1,0:T(8,128)(2,1)S(1)}, u32[]{:S(2)}, u32[]{:S(2)}) %collective-permute-start.21) | collective-permute-done | bytes 81952 | tf_op jit(solution)/shard_map/ppermute | solution.py:416
  85.4 1.7 %collective-permute-done.23 = bf16[96,512]{1,0:T(8,128)(2,1)S(1)} collective-permute-done((bf16[96,512]{1,0:T(8,128)(2,1)S(1)}, bf16[96,512]{1,0:T(8,128)(2,1)S(1)}, u32[]{:S(2)}, u32[]{:S(2)}) %collective-permute-start.23) | collective-permute-done | bytes 98336 | tf_op jit(solution)/shard_map/ppermute | solution.py:416
  87.9 3.8 %collective-permute-start.29 = (bf16[96,512]{1,0:T(8,128)(2,1)S(1)}, bf16[96,512]{1,0:T(8,128)(2,1)S(1)}, u32[]{:S(2)}, u32[]{:S(2)}) collective-permute-start(bf16[96,512]{1,0:T(8,128)(2,1)S(1)} %get-tuple-element.155), channel_id=1, source_target_pairs={{0,14},{1,15},{2,0},{3,1},{4,2},{5,3},{6,4},{7,5},{8,6},{9,7},{10,... | collective-permute-start | bytes 294920 | tf_op jit(solution)/shard_map/ppermute | solution.py:416
  92.0 4.3 %collective-permute-start.25 = (bf16[96,512]{1,0:T(8,128)(2,1)S(1)}, bf16[96,512]{1,0:T(8,128)(2,1)S(1)}, u32[]{:S(2)}, u32[]{:S(2)}) collective-permute-start(bf16[96,512]{1,0:T(8,128)(2,1)S(1)} %get-tuple-element.177), channel_id=1, source_target_pairs={{0,4},{1,5},{2,6},{3,7},{4,0},{5,1},{6,2},{7,3},{8,12},{9,13},{10,... | collective-permute-start | bytes 294920 | tf_op jit(solution)/shard_map/ppermute | solution.py:416
  96.3 2.8 %scatter_lists.1 = bf16[2048,512]{1,0:T(8,128)(2,1)} custom-call(s32[1]{0:T(128)} %bitcast.me_ref, s32[16,48]{1,0:T(8,128)S(1)} %bitcast.30, bf16[48,512]{1,0:T(8,128)(2,1)S(1)} %get-tuple-element.153.refs_0_, bf16[144,512]{1,0:T(8,128)(2,1)S(1)} %collective-permute-done.17.refs_1_, bf16[96,512]{1,0:T(8,128)(2,1)S(1)} %collective-permute-done.28.refs_2_, ...), custom_call_target="tpu_custom_call" | custom-call | tf_op jit(solution)/shard_map/scatter_lists/pallas_call | solution.py:721
  (83 shorter events, 11.6 us)
Async XLA Ops:
  4.2 10.4 %collective-permute-start = (bf16[48,512]{1,0:T(8,128)(2,1)}, bf16[48,512]{1,0:T(8,128)(2,1)S(1)}, u32[]{:S(2)}, u32[]{:S(2)}) collective-permute-start(bf16[48,512]{1,0:T(8,128)(2,1)} %get-tuple-element.89), channel_id=1, source_target_pairs={{0,4},{1,5},{2,6},{3,7},{4,0},{5,1},{6,2},{7,3},{8,12},{9,13},{10,... | collective-permute-start | bytes 147464 | tf_op jit(solution)/shard_map/ppermute | solution.py:416
  7.3 7.3 %collective-permute-start.2 = (bf16[48,512]{1,0:T(8,128)(2,1)}, bf16[48,512]{1,0:T(8,128)(2,1)S(1)}, u32[]{:S(2)}, u32[]{:S(2)}) collective-permute-start(bf16[48,512]{1,0:T(8,128)(2,1)} %get-tuple-element.89), channel_id=1, source_target_pairs={{0,12},{1,13},{2,14},{3,15},{4,8},{5,9},{6,10},{7,11},{8,4},{9,5},... | collective-permute-start | bytes 147464 | tf_op jit(solution)/shard_map/ppermute | solution.py:416
  9.8 6.0 %collective-permute-start.1 = (bf16[48,512]{1,0:T(8,128)(2,1)}, bf16[48,512]{1,0:T(8,128)(2,1)S(1)}, u32[]{:S(2)}, u32[]{:S(2)}) collective-permute-start(bf16[48,512]{1,0:T(8,128)(2,1)} %get-tuple-element.89), channel_id=1, source_target_pairs={{0,8},{1,9},{2,10},{3,11},{4,12},{5,13},{6,14},{7,15},{8,0},{9,1},... | collective-permute-start | bytes 147464 | tf_op jit(solution)/shard_map/ppermute | solution.py:416
  9.9 15.7 %collective-permute-start.5 = (bf16[96,512]{1,0:T(8,128)(2,1)}, bf16[96,512]{1,0:T(8,128)(2,1)S(1)}, u32[]{:S(2)}, u32[]{:S(2)}) collective-permute-start(bf16[96,512]{1,0:T(8,128)(2,1)} %get-tuple-element.95), channel_id=1, source_target_pairs={{0,2},{1,3},{2,4},{3,5},{4,6},{5,7},{6,8},{7,9},{8,10},{9,11},{10,... | collective-permute-start | bytes 294920 | tf_op jit(solution)/shard_map/ppermute | solution.py:416
  11.4 14.2 %collective-permute-start.6 = (bf16[96,512]{1,0:T(8,128)(2,1)}, bf16[96,512]{1,0:T(8,128)(2,1)S(1)}, u32[]{:S(2)}, u32[]{:S(2)}) collective-permute-start(bf16[96,512]{1,0:T(8,128)(2,1)} %get-tuple-element.96), channel_id=1, source_target_pairs={{0,14},{1,15},{2,0},{3,1},{4,2},{5,3},{6,4},{7,5},{8,6},{9,7},{10,... | collective-permute-start | bytes 294920 | tf_op jit(solution)/shard_map/ppermute | solution.py:416
  16.7 8.9 %collective-permute-start.4 = (bf16[192,512]{1,0:T(8,128)(2,1)S(1)}, bf16[192,512]{1,0:T(8,128)(2,1)S(1)}, u32[]{:S(2)}, u32[]{:S(2)}) collective-permute-start(bf16[192,512]{1,0:T(8,128)(2,1)S(1)} %pad_maximum_fusion.refs_7_), channel_id=1, source_target_pairs={{0,1},{1,0},{2,3},{3,2},{4,5},{5,4},{6,7},{7,6},{8,9},{9,8},{10,11... | collective-permute-start | bytes 589832 | tf_op jit(solution)/shard_map/ppermute | solution.py:416
  16.8 8.8 %collective-permute-start.3 = (bf16[192,512]{1,0:T(8,128)(2,1)S(1)}, bf16[192,512]{1,0:T(8,128)(2,1)S(1)}, u32[]{:S(2)}, u32[]{:S(2)}) collective-permute-start(bf16[192,512]{1,0:T(8,128)(2,1)S(1)} %pad_maximum_fusion.refs_7_), channel_id=1, source_target_pairs={{0,2},{1,3},{2,0},{3,1},{4,6},{5,7},{6,4},{7,5},{8,10},{9,11},{10,... | collective-permute-start | bytes 589832 | tf_op jit(solution)/shard_map/ppermute | solution.py:416
  20.1 5.5 %collective-permute-start.7 = (bf16[48,512]{1,0:T(8,128)(2,1)}, bf16[48,512]{1,0:T(8,128)(2,1)S(1)}, u32[]{:S(2)}, u32[]{:S(2)}) collective-permute-start(bf16[48,512]{1,0:T(8,128)(2,1)} %get-tuple-element.97), channel_id=1, source_target_pairs={{0,13},{1,4},{2,15},{3,6},{4,1},{5,8},{6,3},{7,10},{8,5},{9,12},{1... | collective-permute-start | bytes 147464 | tf_op jit(solution)/shard_map/ppermute | solution.py:416
  39.3 19.8 %collective-permute-start.12 = (bf16[2,384,512]{2,1,0:T(8,128)(2,1)S(1)}, bf16[2,384,512]{2,1,0:T(8,128)(2,1)S(1)}, u32[]{:S(2)}, u32[]{:S(2)}) collective-permute-start(bf16[2,384,512]{2,1,0:T(8,128)(2,1)S(1)} %get-tuple-element.108), channel_id=1, source_target_pairs={{0,2},{1,3},{2,0},{3,1},{4,6},{5,7},{6,4},{7,5},{8,10},{9,11},{10,... | collective-permute-start | bytes 2359304 | tf_op jit(solution)/shard_map/ppermute | solution.py:416
  59.9 4.2 %collective-permute-start.16 = (bf16[2,384,512]{2,1,0:T(8,128)(2,1)S(1)}, bf16[2,384,512]{2,1,0:T(8,128)(2,1)S(1)}, u32[]{:S(2)}, u32[]{:S(2)}) collective-permute-start(bf16[2,384,512]{2,1,0:T(8,128)(2,1)S(1)} %get-tuple-element.130), channel_id=1, source_target_pairs={{0,1},{1,0},{2,3},{3,2},{4,5},{5,4},{6,7},{7,6},{8,9},{9,8},{10,11... | collective-permute-start | bytes 2359304 | tf_op jit(solution)/shard_map/ppermute | solution.py:416
  59.9 4.3 %collective-permute-start.17 = (bf16[144,512]{1,0:T(8,128)(2,1)S(1)}, bf16[144,512]{1,0:T(8,128)(2,1)S(1)}, u32[]{:S(2)}, u32[]{:S(2)}) collective-permute-start(bf16[144,512]{1,0:T(8,128)(2,1)S(1)} %get-tuple-element.131), channel_id=1, source_target_pairs={{0,1},{1,0},{2,3},{3,2},{4,5},{5,4},{6,7},{7,6},{8,9},{9,8},{10,11... | collective-permute-start | bytes 442376 | tf_op jit(solution)/shard_map/ppermute | solution.py:416
  62.2 9.8 %collective-permute-start.14 = (bf16[320,512]{1,0:T(8,128)(2,1)S(1)}, bf16[320,512]{1,0:T(8,128)(2,1)S(1)}, u32[]{:S(2)}, u32[]{:S(2)}) collective-permute-start(bf16[320,512]{1,0:T(8,128)(2,1)S(1)} %fusion.7), channel_id=1, source_target_pairs={{0,2},{1,3},{2,0},{3,1},{4,6},{5,7},{6,4},{7,5},{8,10},{9,11},{10,... | collective-permute-start | bytes 983048 | tf_op jit(solution)/shard_map/ppermute | solution.py:416
  64.2 8.0 %collective-permute-start.18 = (bf16[48,512]{1,0:T(8,128)(2,1)S(1)}, bf16[48,512]{1,0:T(8,128)(2,1)S(1)}, u32[]{:S(2)}, u32[]{:S(2)}) collective-permute-start(bf16[48,512]{1,0:T(8,128)(2,1)S(1)} %get-tuple-element.135), channel_id=1, source_target_pairs={{0,13},{1,4},{2,15},{3,6},{4,1},{5,8},{6,3},{7,10},{8,5},{9,12},{1... | collective-permute-start | bytes 147464 | tf_op jit(solution)/shard_map/ppermute | solution.py:416
  64.4 7.8 %collective-permute-start.19 = (bf16[192,512]{1,0:T(8,128)(2,1)S(1)}, bf16[192,512]{1,0:T(8,128)(2,1)S(1)}, u32[]{:S(2)}, u32[]{:S(2)}) collective-permute-start(bf16[192,512]{1,0:T(8,128)(2,1)S(1)} %bitcast.32), channel_id=1, source_target_pairs={{0,4},{1,5},{2,6},{3,7},{4,0},{5,1},{6,2},{7,3},{8,12},{9,13},{10,... | collective-permute-start | bytes 589832 | tf_op jit(solution)/shard_map/ppermute | solution.py:416
  72.3 10.4 %collective-permute-start.24 = (bf16[384,512]{1,0:T(8,128)(2,1)S(1)}, bf16[384,512]{1,0:T(8,128)(2,1)S(1)}, u32[]{:S(2)}, u32[]{:S(2)}) collective-permute-start(bf16[384,512]{1,0:T(8,128)(2,1)S(1)} %get-tuple-element.143), channel_id=1, source_target_pairs={{0,2},{1,3},{2,0},{3,1},{4,6},{5,7},{6,4},{7,5},{8,10},{9,11},{10,... | collective-permute-start | bytes 1179656 | tf_op jit(solution)/shard_map/ppermute | solution.py:416
  74.1 8.7 %collective-permute-start.22 = (bf16[80,512]{1,0:T(8,128)(2,1)S(1)}, bf16[80,512]{1,0:T(8,128)(2,1)S(1)}, u32[]{:S(2)}, u32[]{:S(2)}) collective-permute-start(bf16[80,512]{1,0:T(8,128)(2,1)S(1)} %get-tuple-element.181), channel_id=1, source_target_pairs={{0,12},{1,13},{2,14},{3,15},{4,8},{5,9},{6,10},{7,11},{8,4},{9,5},... | collective-permute-start | bytes 245768 | tf_op jit(solution)/shard_map/ppermute | solution.py:416
  74.3 11.0 %collective-permute-start.21 = (bf16[80,512]{1,0:T(8,128)(2,1)S(1)}, bf16[80,512]{1,0:T(8,128)(2,1)S(1)}, u32[]{:S(2)}, u32[]{:S(2)}) collective-permute-start(bf16[80,512]{1,0:T(8,128)(2,1)S(1)} %get-tuple-element.182), channel_id=1, source_target_pairs={{0,8},{1,9},{2,10},{3,11},{4,12},{5,13},{6,14},{7,15},{8,0},{9,1},... | collective-permute-start | bytes 245768 | tf_op jit(solution)/shard_map/ppermute | solution.py:416
  75.2 10.2 %collective-permute-start.20 = (bf16[80,512]{1,0:T(8,128)(2,1)S(1)}, bf16[80,512]{1,0:T(8,128)(2,1)S(1)}, u32[]{:S(2)}, u32[]{:S(2)}) collective-permute-start(bf16[80,512]{1,0:T(8,128)(2,1)S(1)} %get-tuple-element.183), channel_id=1, source_target_pairs={{0,4},{1,5},{2,6},{3,7},{4,0},{5,1},{6,2},{7,3},{8,12},{9,13},{10,... | collective-permute-start | bytes 245768 | tf_op jit(solution)/shard_map/ppermute | solution.py:416
  78.6 8.5 %collective-permute-start.23 = (bf16[96,512]{1,0:T(8,128)(2,1)S(1)}, bf16[96,512]{1,0:T(8,128)(2,1)S(1)}, u32[]{:S(2)}, u32[]{:S(2)}) collective-permute-start(bf16[96,512]{1,0:T(8,128)(2,1)S(1)} %get-tuple-element.185), channel_id=1, source_target_pairs={{0,8},{1,9},{2,10},{3,11},{4,12},{5,13},{6,14},{7,15},{8,0},{9,1},... | collective-permute-start | bytes 294920 | tf_op jit(solution)/shard_map/ppermute | solution.py:416
  87.1 9.2 %collective-permute-start.28 = (bf16[96,512]{1,0:T(8,128)(2,1)S(1)}, bf16[96,512]{1,0:T(8,128)(2,1)S(1)}, u32[]{:S(2)}, u32[]{:S(2)}) collective-permute-start(bf16[96,512]{1,0:T(8,128)(2,1)S(1)} %get-tuple-element.154), channel_id=1, source_target_pairs={{0,2},{1,3},{2,4},{3,5},{4,6},{5,7},{6,8},{7,9},{8,10},{9,11},{10,... | collective-permute-start | bytes 294920 | tf_op jit(solution)/shard_map/ppermute | solution.py:416
  87.9 8.3 %collective-permute-start.29 = (bf16[96,512]{1,0:T(8,128)(2,1)S(1)}, bf16[96,512]{1,0:T(8,128)(2,1)S(1)}, u32[]{:S(2)}, u32[]{:S(2)}) collective-permute-start(bf16[96,512]{1,0:T(8,128)(2,1)S(1)} %get-tuple-element.155), channel_id=1, source_target_pairs={{0,14},{1,15},{2,0},{3,1},{4,2},{5,3},{6,4},{7,5},{8,6},{9,7},{10,... | collective-permute-start | bytes 294920 | tf_op jit(solution)/shard_map/ppermute | solution.py:416
  91.8 8.6 %collective-permute-start.27 = (bf16[96,512]{1,0:T(8,128)(2,1)S(1)}, bf16[96,512]{1,0:T(8,128)(2,1)S(1)}, u32[]{:S(2)}, u32[]{:S(2)}) collective-permute-start(bf16[96,512]{1,0:T(8,128)(2,1)S(1)} %get-tuple-element.175), channel_id=1, source_target_pairs={{0,12},{1,13},{2,14},{3,15},{4,8},{5,9},{6,10},{7,11},{8,4},{9,5},... | collective-permute-start | bytes 294920 | tf_op jit(solution)/shard_map/ppermute | solution.py:416
  91.9 9.0 %collective-permute-start.26 = (bf16[96,512]{1,0:T(8,128)(2,1)S(1)}, bf16[96,512]{1,0:T(8,128)(2,1)S(1)}, u32[]{:S(2)}, u32[]{:S(2)}) collective-permute-start(bf16[96,512]{1,0:T(8,128)(2,1)S(1)} %get-tuple-element.176), channel_id=1, source_target_pairs={{0,8},{1,9},{2,10},{3,11},{4,12},{5,13},{6,14},{7,15},{8,0},{9,1},... | collective-permute-start | bytes 294920 | tf_op jit(solution)/shard_map/ppermute | solution.py:416
  92.0 8.9 %collective-permute-start.25 = (bf16[96,512]{1,0:T(8,128)(2,1)S(1)}, bf16[96,512]{1,0:T(8,128)(2,1)S(1)}, u32[]{:S(2)}, u32[]{:S(2)}) collective-permute-start(bf16[96,512]{1,0:T(8,128)(2,1)S(1)} %get-tuple-element.177), channel_id=1, source_target_pairs={{0,4},{1,5},{2,6},{3,7},{4,0},{5,1},{6,2},{7,3},{8,12},{9,13},{10,... | collective-permute-start | bytes 294920 | tf_op jit(solution)/shard_map/ppermute | solution.py:416
  (18 other events, 198.9 us)

commit v16 on v15

--- a/solution.py
+++ b/solution.py
@@ -205,16 +205,31 @@
     far_ref[...] = lists[7]
 
 
-def scatter_kernel(skip, me_ref, rows_ref, *refs):
-    near_refs, far_refs, out_ref = refs[:5], refs[5:-1], refs[-1]
+def scatter_kernel(skip, slot_count, me_ref, rows_ref, *refs):
+    near_refs, refs = refs[:5], refs[5:]
+    out_ref, grad_out_ref, node_in_ref, node_out_ref = refs[-4:]
+    terms = refs[:-4]
     part = out_ref.shape[0]
     cap = rows_ref.shape[1]
+    far_refs, node_refs = terms[:slot_count], terms[slot_count:]
+    node_rows = node_in_ref.shape[0]
+
+    def total(term_refs, start, stop):
+        result = term_refs[0][start:stop, :].astype(F32)
+        for ref in term_refs[1:]:
+            result = result + ref[start:stop, :].astype(F32)
+        return result
+
     hots = list_hots(me_ref[0], rows_ref, part, pl.program_id(0) * part)
-    far = far_refs[0][skip:, :].astype(F32)
-    for ref in far_refs[1:]:
-        far = far + ref[skip:, :].astype(F32)
+    far = total(far_refs, skip, skip + cap)
     values = jnp.concatenate(read_back(near_refs, cap) + [far.astype(BF16)], axis=0)
     out_ref[...] = contract_rows(hots, values).astype(BF16)
+
+    @pl.when(pl.program_id(0) == 0)
+    def _():
+        grad_out_ref[...] = total(far_refs, 0, skip)
+        node_in_ref[...] = total(node_refs, 0, node_rows)
+        node_out_ref[...] = total(node_refs, node_rows, node_rows + node_out_ref.shape[0])
 
 
 def halves_of(ref):
@@ -693,10 +708,10 @@
         (node_next, node_kept, slot_send, slot_keep, edge_send, edge_keep, returns)
     )
     slot_next, slot_kept = first_sum(peers, 1, slot_send, slot_keep)
+    slot_pieces = next_sum(peers, 2, slot_next, slot_kept)
     edge_next, edge_kept = first_sum(peers, 1, edge_send, edge_keep)
     node_pieces = next_sum(peers, 1, node_next, node_kept)
     swapped = send(returns[1], by_xor(peers, 1))
-    slot_pieces = next_sum(peers, 2, slot_next, slot_kept)
     node_pieces, edge_next, edge_kept, swapped, across = lax.optimization_barrier(
         (node_pieces, edge_next, edge_kept, swapped, returns[4])
     )
@@ -717,28 +732,31 @@
     bundles = [send(to_after, by_shift(peers, 2)), send(to_before, by_shift(peers, -2))]
     returned = [returns[0], swapped, *bundles, across]
     node_rows = w_node_in.shape[0] // peers
+    node_out_rows = w_node_out.shape[0] // peers
     out_rows = w_edge_out.shape[0] // peers
-    grid_grad = pl.pallas_call(
-        functools.partial(scatter_kernel, out_rows),
+    grid_grad, grad_edge_out, grad_node_in, grad_node_out = pl.pallas_call(
+        functools.partial(scatter_kernel, out_rows, len(slot_terms)),
         grid=(2,),
         in_specs=[smem, whole(rows.shape)]
         + return_specs
-        + [whole((out_rows + cap, width))] * upper,
-        out_specs=pl.BlockSpec((grid_part, width), lambda step: (step, 0)),
-        out_shape=jax.ShapeDtypeStruct((grid_count, width), BF16),
+        + [whole((out_rows + cap, width))] * len(slot_terms)
+        + [whole((node_rows + node_out_rows, width))] * len(node_terms),
+        out_specs=[pl.BlockSpec((grid_count // 2, width), lambda step: (step, 0))]
+        + [whole((count, width)) for count in (out_rows, node_rows, node_out_rows)],
+        out_shape=[jax.ShapeDtypeStruct((grid_count, width), BF16)]
+        + [jax.ShapeDtypeStruct((count, width), F32) for count in (out_rows, node_rows, node_out_rows)],
         compiler_params=params,
         name="scatter_lists",
-    )(me, rows, *returned, *slot_terms)
-    node_terms, out_terms, grid_grad = lax.optimization_barrier((node_terms, slot_terms, grid_grad))
+    )(me, rows, *returned, *slot_terms, *node_terms)
     edge_terms, grid_grad = lax.optimization_barrier((edge_terms, grid_grad))
     return (
         grid_grad,
         edge_grad,
         mesh_grad,
         total_of(edge_terms, 0, w_edge_in.shape[0] // peers),
-        total_of(out_terms, 0, out_rows),
-        total_of(node_terms, 0, node_rows),
-        total_of(node_terms, node_rows, node_rows + w_node_out.shape[0] // peers),
+        grad_edge_out,
+        grad_node_in,
+        grad_node_out,
     )
 
 

time: 102 us -> 100 us (0.980)
  other arithmetic: 4.43 us -> 2.47 us
  waiting for transfers between devices: 21 us -> 22.6 us
  starting transfers between devices: 36.9 us -> 35.5 us
    add x4 -> x1, other arithmetic: 2.68 us -> 0.73 us  [total_of(): total = total + term[start:stop].astype(F32)]
    ppermute x30, waiting for transfers between devices: 21 us -> 22.6 us  [send(): return lax.ppermute(values, 'lon', perm)]
    ppermute x30, starting transfers between devices: 36.9 us -> 35.5 us  [send(): return lax.ppermute(values, 'lon', perm)]
  transfers between devices with their start and end apart: 30 -> 30, of which waited for: 10 -> 11; matrix products, arithmetic and copies ran while one was open for 3% -> 2% of each run, Pallas kernels for 22% -> 23%
where the time goes in v16:
time: 100 us; the launch traced here: 101 us
  Pallas kernels  38.2 us (38%)
  starting transfers between devices  35.5 us (36%)
  waiting for transfers between devices  22.6 us (23%)
  other arithmetic  2.47 us (2%)
  between operations  1.62 us (2%)
    ppermute x30, starting transfers between devices, send(): return lax.ppermute(values, 'lon', perm)  35.5 us
    ppermute x30, waiting for transfers between devices, send(): return lax.ppermute(values, 'lon', perm)  22.6 us
    pallas_call x1, Pallas kernels, on_device(): pl.pallas_call(functools.partial(backward_kernel, peers), grid=(tiles,),...  16.7 us
    pallas_call x1, Pallas kernels, on_device(): pl.pallas_call(functools.partial(forward_kernel, peers), grid=(tiles,), i...  11.6 us
    pallas_call x1, Pallas kernels, on_device(): pl.pallas_call(gather_kernel, in_specs=[smem, hbm, hbm], out_specs=near_s...  3.55 us
    pallas_call x1, Pallas kernels, on_device(): pl.pallas_call(local_kernel, grid=(tiles,), in_specs=[index_tile, tile_of...  3.42 us
    pallas_call x1, Pallas kernels, on_device(): pl.pallas_call(functools.partial(scatter_kernel, out_rows, len(slot_terms...  2.89 us
  transfers between devices with their start and end apart: 30, of which 11 were waited for; matrix products, arithmetic and copies ran while one was open for 2% of the time, Pallas kernels for 23%

profile of v16, /device:TPU:0, one launch (start us, length us, event | category | flops | bytes accessed | tf_op | source)
XLA Modules:
  0.0 100.6 jit_solution(9041919760156957404)
XLA Ops:
  0.7 3.6 %gather_lists.1 = (bf16[48,512]{1,0:T(8,128)(2,1)}, bf16[48,512]{1,0:T(8,128)(2,1)}, bf16[96,512]{1,0:T(8,128)(2,1)}, bf16[96,512]{1,0:T(8,128)(2,1)}, bf16[48,512]{1,0:T(8,128)(2,1)}, /*index=5*/bf16[48,512]{1,0:T(8,128)(2,1)}) custom-call(s32[1]{0:T(128)} %bitcast.me_ref, s32[16,48]{1,0:T(8,128)} %bitcast.33, bf16[2048,512]{1,0:T(8,128)(2,1)} %grid_hbm.1), custom_call_target="tpu_custom_call" | custom-call | flops 32212254720 | bytes 2097152 | tf_op jit(solution)/shard_map/gather_lists/pallas_call | solution.py:560
  4.2 3.1 %collective-permute-start = (bf16[48,512]{1,0:T(8,128)(2,1)}, bf16[48,512]{1,0:T(8,128)(2,1)S(1)}, u32[]{:S(2)}, u32[]{:S(2)}) collective-permute-start(bf16[48,512]{1,0:T(8,128)(2,1)} %get-tuple-element.86), channel_id=1, source_target_pairs={{0,4},{1,5},{2,6},{3,7},{4,0},{5,1},{6,2},{7,3},{8,12},{9,13},{10,... | collective-permute-start | bytes 147464 | tf_op jit(solution)/shard_map/ppermute | solution.py:431
  7.3 2.5 %collective-permute-start.2 = (bf16[48,512]{1,0:T(8,128)(2,1)}, bf16[48,512]{1,0:T(8,128)(2,1)S(1)}, u32[]{:S(2)}, u32[]{:S(2)}) collective-permute-start(bf16[48,512]{1,0:T(8,128)(2,1)} %get-tuple-element.86), channel_id=1, source_target_pairs={{0,12},{1,13},{2,14},{3,15},{4,8},{5,9},{6,10},{7,11},{8,4},{9,5},... | collective-permute-start | bytes 147464 | tf_op jit(solution)/shard_map/ppermute | solution.py:431
  9.9 1.5 %collective-permute-start.5 = (bf16[96,512]{1,0:T(8,128)(2,1)}, bf16[96,512]{1,0:T(8,128)(2,1)S(1)}, u32[]{:S(2)}, u32[]{:S(2)}) collective-permute-start(bf16[96,512]{1,0:T(8,128)(2,1)} %get-tuple-element.92), channel_id=1, source_target_pairs={{0,2},{1,3},{2,4},{3,5},{4,6},{5,7},{6,8},{7,9},{8,10},{9,11},{10,... | collective-permute-start | bytes 294920 | tf_op jit(solution)/shard_map/ppermute | solution.py:431
  11.4 3.2 %collective-permute-start.6 = (bf16[96,512]{1,0:T(8,128)(2,1)}, bf16[96,512]{1,0:T(8,128)(2,1)S(1)}, u32[]{:S(2)}, u32[]{:S(2)}) collective-permute-start(bf16[96,512]{1,0:T(8,128)(2,1)} %get-tuple-element.93), channel_id=1, source_target_pairs={{0,14},{1,15},{2,0},{3,1},{4,2},{5,3},{6,4},{7,5},{8,6},{9,7},{10,... | collective-permute-start | bytes 294920 | tf_op jit(solution)/shard_map/ppermute | solution.py:431
  16.8 3.3 %collective-permute-start.3 = (bf16[192,512]{1,0:T(8,128)(2,1)S(1)}, bf16[192,512]{1,0:T(8,128)(2,1)S(1)}, u32[]{:S(2)}, u32[]{:S(2)}) collective-permute-start(bf16[192,512]{1,0:T(8,128)(2,1)S(1)} %pad_maximum_fusion.refs_7_), channel_id=1, source_target_pairs={{0,2},{1,3},{2,0},{3,1},{4,6},{5,7},{6,4},{7,5},{8,10},{9,11},{10,... | collective-permute-start | bytes 589832 | tf_op jit(solution)/shard_map/ppermute | solution.py:431
  20.6 3.4 %edge_local.1.local_ref = bf16[3072,512]{1,0:T(8,128)(2,1)S(1)} custom-call(s32[3,1,1024]{2,1,0:T(1,128)S(1)} %bitcast.28, bf16[3072,512]{1,0:T(8,128)(2,1)S(1)} %copy-done.1, bf16[256,512]{1,0:T(8,128)(2,1)S(1)} %copy-done.2, bf16[1536,512]{1,0:T(8,128)(2,1)S(1)} %copy-done, bf16[1536,512]{1,0:T(8,128)(2,1)S(1)} %copy-done), custom_call_target="tpu_custom_call" | custom-call | flops 2415919104 | bytes 6291456 | tf_op jit(solution)/shard_map/edge_local/pallas_call | solution.py:588
  24.0 1.6 %collective-permute-done.7.refs_4_ = bf16[48,512]{1,0:T(8,128)(2,1)S(1)} collective-permute-done((bf16[48,512]{1,0:T(8,128)(2,1)}, bf16[48,512]{1,0:T(8,128)(2,1)S(1)}, u32[]{:S(2)}, u32[]{:S(2)}) %collective-permute-start.7) | collective-permute-done | bytes 49184 | tf_op jit(solution)/shard_map/ppermute | solution.py:431
  27.7 11.6 %forward.1 = (bf16[768,512]{1,0:T(8,128)(2,1)S(1)}, bf16[3072,512]{1,0:T(8,128)(2,1)S(1)}, bf16[3072,512]{1,0:T(8,128)(2,1)S(1)}, bf16[3072,512]{1,0:T(8,128)(2,...) custom-call(s32[1]{0:T(128)} %bitcast.me_ref, ...), custom_call_target="tpu_custom_call" | custom-call | tf_op jit(solution)/shard_map/forward/pallas_call | solution.py:608
  39.3 1.7 %collective-permute-start.12 = (bf16[2,384,512]{2,1,0:T(8,128)(2,1)S(1)}, bf16[2,384,512]{2,1,0:T(8,128)(2,1)S(1)}, u32[]{:S(2)}, u32[]{:S(2)}) collective-permute-start(bf16[2,384,512]{2,1,0:T(8,128)(2,1)S(1)} %get-tuple-element.105), channel_id=1, source_target_pairs={{0,2},{1,3},{2,0},{3,1},{4,6},{5,7},{6,4},{7,5},{8,10},{9,11},{10,... | collective-permute-start | bytes 2359304 | tf_op jit(solution)/shard_map/ppermute | solution.py:431
  41.0 16.7 %backward.1 = (bf16[3072,512]{1,0:T(8,128)(2,1)}, bf16[256,512]{1,0:T(8,128)(2,1)}, bf16[2,320,512]{2,1,0:T(8,128)(2,1)S(1)}, bf16[2,320,512]{2,1,0:T(8,128)(2,1...) custom-call(s32[1]{0:T(128)} %bitcast.me_ref, ...), custom_call_target="tpu_custom_call" | custom-call | flops 10468982784 | bytes 15728640 | tf_op jit(solution)/shard_map/backward/pallas_call | solution.py:658
  59.1 1.6 %collective-permute-done.15 = bf16[384,512]{1,0:T(8,128)(2,1)S(1)} collective-permute-done((bf16[384,512]{1,0:T(8,128)(2,1)S(1)}, bf16[384,512]{1,0:T(8,128)(2,1)S(1)}, u32[]{:S(2)}, u32[]{:S(2)}) %collective-permute-start.15) | collective-permute-done | bytes 393248 | tf_op jit(solution)/shard_map/ppermute | solution.py:431
  62.6 1.4 %collective-permute-start.19 = (bf16[192,512]{1,0:T(8,128)(2,1)S(1)}, bf16[192,512]{1,0:T(8,128)(2,1)S(1)}, u32[]{:S(2)}, u32[]{:S(2)}) collective-permute-start(bf16[192,512]{1,0:T(8,128)(2,1)S(1)} %bitcast.36), channel_id=1, source_target_pairs={{0,4},{1,5},{2,6},{3,7},{4,0},{5,1},{6,2},{7,3},{8,12},{9,13},{10,... | collective-permute-start | bytes 589832 | tf_op jit(solution)/shard_map/ppermute | solution.py:431
  64.0 6.7 %collective-permute-done.14 = bf16[320,512]{1,0:T(8,128)(2,1)S(1)} collective-permute-done((bf16[320,512]{1,0:T(8,128)(2,1)S(1)}, bf16[320,512]{1,0:T(8,128)(2,1)S(1)}, u32[]{:S(2)}, u32[]{:S(2)}) %collective-permute-start.14) | collective-permute-done | bytes 327712 | tf_op jit(solution)/shard_map/ppermute | solution.py:431
  73.0 1.3 %collective-permute-start.21 = (bf16[80,512]{1,0:T(8,128)(2,1)S(1)}, bf16[80,512]{1,0:T(8,128)(2,1)S(1)}, u32[]{:S(2)}, u32[]{:S(2)}) collective-permute-start(bf16[80,512]{1,0:T(8,128)(2,1)S(1)} %get-tuple-element.176), channel_id=1, source_target_pairs={{0,8},{1,9},{2,10},{3,11},{4,12},{5,13},{6,14},{7,15},{8,0},{9,1},... | collective-permute-start | bytes 245768 | tf_op jit(solution)/shard_map/ppermute | solution.py:431
  74.3 2.4 %collective-permute-start.20 = (bf16[80,512]{1,0:T(8,128)(2,1)S(1)}, bf16[80,512]{1,0:T(8,128)(2,1)S(1)}, u32[]{:S(2)}, u32[]{:S(2)}) collective-permute-start(bf16[80,512]{1,0:T(8,128)(2,1)S(1)} %get-tuple-element.177), channel_id=1, source_target_pairs={{0,4},{1,5},{2,6},{3,7},{4,0},{5,1},{6,2},{7,3},{8,12},{9,13},{10,... | collective-permute-start | bytes 245768 | tf_op jit(solution)/shard_map/ppermute | solution.py:431
  77.0 5.0 %collective-permute-done.24 = bf16[384,512]{1,0:T(8,128)(2,1)S(1)} collective-permute-done((bf16[384,512]{1,0:T(8,128)(2,1)S(1)}, bf16[384,512]{1,0:T(8,128)(2,1)S(1)}, u32[]{:S(2)}, u32[]{:S(2)}) %collective-permute-start.24) | collective-permute-done | bytes 393248 | tf_op jit(solution)/shard_map/ppermute | solution.py:431
  82.1 2.5 %collective-permute-done.21.refs_7_ = bf16[80,512]{1,0:T(8,128)(2,1)S(1)} collective-permute-done((bf16[80,512]{1,0:T(8,128)(2,1)S(1)}, bf16[80,512]{1,0:T(8,128)(2,1)S(1)}, u32[]{:S(2)}, u32[]{:S(2)}) %collective-permute-start.21) | collective-permute-done | bytes 81952 | tf_op jit(solution)/shard_map/ppermute | solution.py:431
  84.6 1.6 %collective-permute-done.23.refs_10_ = bf16[96,512]{1,0:T(8,128)(2,1)S(1)} collective-permute-done((bf16[96,512]{1,0:T(8,128)(2,1)S(1)}, bf16[96,512]{1,0:T(8,128)(2,1)S(1)}, u32[]{:S(2)}, u32[]{:S(2)}) %collective-permute-start.23) | collective-permute-done | bytes 98336 | tf_op jit(solution)/shard_map/ppermute | solution.py:431
  86.2 1.4 %collective-permute-start.28 = (bf16[96,512]{1,0:T(8,128)(2,1)S(1)}, bf16[96,512]{1,0:T(8,128)(2,1)S(1)}, u32[]{:S(2)}, u32[]{:S(2)}) collective-permute-start(bf16[96,512]{1,0:T(8,128)(2,1)S(1)} %get-tuple-element.145), channel_id=1, source_target_pairs={{0,2},{1,3},{2,4},{3,5},{4,6},{5,7},{6,8},{7,9},{8,10},{9,11},{10,... | collective-permute-start | bytes 294920 | tf_op jit(solution)/shard_map/ppermute | solution.py:431
  87.5 3.4 %collective-permute-start.29 = (bf16[96,512]{1,0:T(8,128)(2,1)S(1)}, bf16[96,512]{1,0:T(8,128)(2,1)S(1)}, u32[]{:S(2)}, u32[]{:S(2)}) collective-permute-start(bf16[96,512]{1,0:T(8,128)(2,1)S(1)} %get-tuple-element.146), channel_id=1, source_target_pairs={{0,14},{1,15},{2,0},{3,1},{4,2},{5,3},{6,4},{7,5},{8,6},{9,7},{10,... | collective-permute-start | bytes 294920 | tf_op jit(solution)/shard_map/ppermute | solution.py:431
  91.1 4.3 %collective-permute-start.25 = (bf16[96,512]{1,0:T(8,128)(2,1)S(1)}, bf16[96,512]{1,0:T(8,128)(2,1)S(1)}, u32[]{:S(2)}, u32[]{:S(2)}) collective-permute-start(bf16[96,512]{1,0:T(8,128)(2,1)S(1)} %get-tuple-element.171), channel_id=1, source_target_pairs={{0,4},{1,5},{2,6},{3,7},{4,0},{5,1},{6,2},{7,3},{8,12},{9,13},{10,... | collective-permute-start | bytes 294920 | tf_op jit(solution)/shard_map/ppermute | solution.py:431
  95.4 2.9 %scatter_lists.1 = (bf16[2048,512]{1,0:T(8,128)(2,1)}, f32[32,512]{1,0:T(8,128)}, f32[64,512]{1,0:T(8,128)}, f32[32,512]{1,0:T(8,128)}) custom-call(s32[1]{0:T(128)} %bitcast.me_ref, s32[16,48]{1,0:T(8,128)S(1)} %bitcast.34, bf16[48,512]{1,0:T(8,128)(2,1)S(1)} %get-tuple-element.144.refs_0_, bf16[144,512]{1,0:T(8,128)(2,1)S(1)} %collective-permute-done.17.refs_1_, ...), custom_call_target="tpu_custom_call" | custom-call | tf_op jit(solution)/shard_map/scatter_lists/pallas_call | solution.py:737
  98.6 1.3 %collective-permute-done.26 = bf16[96,512]{1,0:T(8,128)(2,1)S(1)} collective-permute-done((bf16[96,512]{1,0:T(8,128)(2,1)S(1)}, bf16[96,512]{1,0:T(8,128)(2,1)S(1)}, u32[]{:S(2)}, u32[]{:S(2)}) %collective-permute-start.26) | collective-permute-done | bytes 98336 | tf_op jit(solution)/shard_map/ppermute | solution.py:431
  (80 shorter events, 11.2 us)
Async XLA Ops:
  4.2 10.4 %collective-permute-start = (bf16[48,512]{1,0:T(8,128)(2,1)}, bf16[48,512]{1,0:T(8,128)(2,1)S(1)}, u32[]{:S(2)}, u32[]{:S(2)}) collective-permute-start(bf16[48,512]{1,0:T(8,128)(2,1)} %get-tuple-element.86), channel_id=1, source_target_pairs={{0,4},{1,5},{2,6},{3,7},{4,0},{5,1},{6,2},{7,3},{8,12},{9,13},{10,... | collective-permute-start | bytes 147464 | tf_op jit(solution)/shard_map/ppermute | solution.py:431
  7.3 7.3 %collective-permute-start.2 = (bf16[48,512]{1,0:T(8,128)(2,1)}, bf16[48,512]{1,0:T(8,128)(2,1)S(1)}, u32[]{:S(2)}, u32[]{:S(2)}) collective-permute-start(bf16[48,512]{1,0:T(8,128)(2,1)} %get-tuple-element.86), channel_id=1, source_target_pairs={{0,12},{1,13},{2,14},{3,15},{4,8},{5,9},{6,10},{7,11},{8,4},{9,5},... | collective-permute-start | bytes 147464 | tf_op jit(solution)/shard_map/ppermute | solution.py:431
  9.8 6.0 %collective-permute-start.1 = (bf16[48,512]{1,0:T(8,128)(2,1)}, bf16[48,512]{1,0:T(8,128)(2,1)S(1)}, u32[]{:S(2)}, u32[]{:S(2)}) collective-permute-start(bf16[48,512]{1,0:T(8,128)(2,1)} %get-tuple-element.86), channel_id=1, source_target_pairs={{0,8},{1,9},{2,10},{3,11},{4,12},{5,13},{6,14},{7,15},{8,0},{9,1},... | collective-permute-start | bytes 147464 | tf_op jit(solution)/shard_map/ppermute | solution.py:431
  9.9 15.7 %collective-permute-start.5 = (bf16[96,512]{1,0:T(8,128)(2,1)}, bf16[96,512]{1,0:T(8,128)(2,1)S(1)}, u32[]{:S(2)}, u32[]{:S(2)}) collective-permute-start(bf16[96,512]{1,0:T(8,128)(2,1)} %get-tuple-element.92), channel_id=1, source_target_pairs={{0,2},{1,3},{2,4},{3,5},{4,6},{5,7},{6,8},{7,9},{8,10},{9,11},{10,... | collective-permute-start | bytes 294920 | tf_op jit(solution)/shard_map/ppermute | solution.py:431
  11.4 14.2 %collective-permute-start.6 = (bf16[96,512]{1,0:T(8,128)(2,1)}, bf16[96,512]{1,0:T(8,128)(2,1)S(1)}, u32[]{:S(2)}, u32[]{:S(2)}) collective-permute-start(bf16[96,512]{1,0:T(8,128)(2,1)} %get-tuple-element.93), channel_id=1, source_target_pairs={{0,14},{1,15},{2,0},{3,1},{4,2},{5,3},{6,4},{7,5},{8,6},{9,7},{10,... | collective-permute-start | bytes 294920 | tf_op jit(solution)/shard_map/ppermute | solution.py:431
  16.7 8.9 %collective-permute-start.4 = (bf16[192,512]{1,0:T(8,128)(2,1)S(1)}, bf16[192,512]{1,0:T(8,128)(2,1)S(1)}, u32[]{:S(2)}, u32[]{:S(2)}) collective-permute-start(bf16[192,512]{1,0:T(8,128)(2,1)S(1)} %pad_maximum_fusion.refs_7_), channel_id=1, source_target_pairs={{0,1},{1,0},{2,3},{3,2},{4,5},{5,4},{6,7},{7,6},{8,9},{9,8},{10,11... | collective-permute-start | bytes 589832 | tf_op jit(solution)/shard_map/ppermute | solution.py:431
  16.8 8.8 %collective-permute-start.3 = (bf16[192,512]{1,0:T(8,128)(2,1)S(1)}, bf16[192,512]{1,0:T(8,128)(2,1)S(1)}, u32[]{:S(2)}, u32[]{:S(2)}) collective-permute-start(bf16[192,512]{1,0:T(8,128)(2,1)S(1)} %pad_maximum_fusion.refs_7_), channel_id=1, source_target_pairs={{0,2},{1,3},{2,0},{3,1},{4,6},{5,7},{6,4},{7,5},{8,10},{9,11},{10,... | collective-permute-start | bytes 589832 | tf_op jit(solution)/shard_map/ppermute | solution.py:431
  20.1 5.5 %collective-permute-start.7 = (bf16[48,512]{1,0:T(8,128)(2,1)}, bf16[48,512]{1,0:T(8,128)(2,1)S(1)}, u32[]{:S(2)}, u32[]{:S(2)}) collective-permute-start(bf16[48,512]{1,0:T(8,128)(2,1)} %get-tuple-element.94), channel_id=1, source_target_pairs={{0,13},{1,4},{2,15},{3,6},{4,1},{5,8},{6,3},{7,10},{8,5},{9,12},{1... | collective-permute-start | bytes 147464 | tf_op jit(solution)/shard_map/ppermute | solution.py:431
  39.3 18.5 %collective-permute-start.12 = (bf16[2,384,512]{2,1,0:T(8,128)(2,1)S(1)}, bf16[2,384,512]{2,1,0:T(8,128)(2,1)S(1)}, u32[]{:S(2)}, u32[]{:S(2)}) collective-permute-start(bf16[2,384,512]{2,1,0:T(8,128)(2,1)S(1)} %get-tuple-element.105), channel_id=1, source_target_pairs={{0,2},{1,3},{2,0},{3,1},{4,6},{5,7},{6,4},{7,5},{8,10},{9,11},{10,... | collective-permute-start | bytes 2359304 | tf_op jit(solution)/shard_map/ppermute | solution.py:431
  58.6 3.3 %collective-permute-start.16 = (bf16[2,384,512]{2,1,0:T(8,128)(2,1)S(1)}, bf16[2,384,512]{2,1,0:T(8,128)(2,1)S(1)}, u32[]{:S(2)}, u32[]{:S(2)}) collective-permute-start(bf16[2,384,512]{2,1,0:T(8,128)(2,1)S(1)} %get-tuple-element.127), channel_id=1, source_target_pairs={{0,1},{1,0},{2,3},{3,2},{4,5},{5,4},{6,7},{7,6},{8,9},{9,8},{10,11... | collective-permute-start | bytes 2359304 | tf_op jit(solution)/shard_map/ppermute | solution.py:431
  58.6 3.4 %collective-permute-start.17 = (bf16[144,512]{1,0:T(8,128)(2,1)S(1)}, bf16[144,512]{1,0:T(8,128)(2,1)S(1)}, u32[]{:S(2)}, u32[]{:S(2)}) collective-permute-start(bf16[144,512]{1,0:T(8,128)(2,1)S(1)} %get-tuple-element.128), channel_id=1, source_target_pairs={{0,1},{1,0},{2,3},{3,2},{4,5},{5,4},{6,7},{7,6},{8,9},{9,8},{10,11... | collective-permute-start | bytes 442376 | tf_op jit(solution)/shard_map/ppermute | solution.py:431
  60.9 9.8 %collective-permute-start.14 = (bf16[320,512]{1,0:T(8,128)(2,1)S(1)}, bf16[320,512]{1,0:T(8,128)(2,1)S(1)}, u32[]{:S(2)}, u32[]{:S(2)}) collective-permute-start(bf16[320,512]{1,0:T(8,128)(2,1)S(1)} %fusion.7), channel_id=1, source_target_pairs={{0,2},{1,3},{2,0},{3,1},{4,6},{5,7},{6,4},{7,5},{8,10},{9,11},{10,... | collective-permute-start | bytes 983048 | tf_op jit(solution)/shard_map/ppermute | solution.py:431
  62.0 8.9 %collective-permute-start.18 = (bf16[48,512]{1,0:T(8,128)(2,1)S(1)}, bf16[48,512]{1,0:T(8,128)(2,1)S(1)}, u32[]{:S(2)}, u32[]{:S(2)}) collective-permute-start(bf16[48,512]{1,0:T(8,128)(2,1)S(1)} %get-tuple-element.132), channel_id=1, source_target_pairs={{0,13},{1,4},{2,15},{3,6},{4,1},{5,8},{6,3},{7,10},{8,5},{9,12},{1... | collective-permute-start | bytes 147464 | tf_op jit(solution)/shard_map/ppermute | solution.py:431
  62.6 8.2 %collective-permute-start.19 = (bf16[192,512]{1,0:T(8,128)(2,1)S(1)}, bf16[192,512]{1,0:T(8,128)(2,1)S(1)}, u32[]{:S(2)}, u32[]{:S(2)}) collective-permute-start(bf16[192,512]{1,0:T(8,128)(2,1)S(1)} %bitcast.36), channel_id=1, source_target_pairs={{0,4},{1,5},{2,6},{3,7},{4,0},{5,1},{6,2},{7,3},{8,12},{9,13},{10,... | collective-permute-start | bytes 589832 | tf_op jit(solution)/shard_map/ppermute | solution.py:431
  71.0 11.0 %collective-permute-start.24 = (bf16[384,512]{1,0:T(8,128)(2,1)S(1)}, bf16[384,512]{1,0:T(8,128)(2,1)S(1)}, u32[]{:S(2)}, u32[]{:S(2)}) collective-permute-start(bf16[384,512]{1,0:T(8,128)(2,1)S(1)} %get-tuple-element.140), channel_id=1, source_target_pairs={{0,2},{1,3},{2,0},{3,1},{4,6},{5,7},{6,4},{7,5},{8,10},{9,11},{10,... | collective-permute-start | bytes 1179656 | tf_op jit(solution)/shard_map/ppermute | solution.py:431
  72.2 9.9 %collective-permute-start.22 = (bf16[80,512]{1,0:T(8,128)(2,1)S(1)}, bf16[80,512]{1,0:T(8,128)(2,1)S(1)}, u32[]{:S(2)}, u32[]{:S(2)}) collective-permute-start(bf16[80,512]{1,0:T(8,128)(2,1)S(1)} %get-tuple-element.175), channel_id=1, source_target_pairs={{0,12},{1,13},{2,14},{3,15},{4,8},{5,9},{6,10},{7,11},{8,4},{9,5},... | collective-permute-start | bytes 245768 | tf_op jit(solution)/shard_map/ppermute | solution.py:431
  73.0 11.6 %collective-permute-start.21 = (bf16[80,512]{1,0:T(8,128)(2,1)S(1)}, bf16[80,512]{1,0:T(8,128)(2,1)S(1)}, u32[]{:S(2)}, u32[]{:S(2)}) collective-permute-start(bf16[80,512]{1,0:T(8,128)(2,1)S(1)} %get-tuple-element.176), channel_id=1, source_target_pairs={{0,8},{1,9},{2,10},{3,11},{4,12},{5,13},{6,14},{7,15},{8,0},{9,1},... | collective-permute-start | bytes 245768 | tf_op jit(solution)/shard_map/ppermute | solution.py:431
  74.3 10.3 %collective-permute-start.20 = (bf16[80,512]{1,0:T(8,128)(2,1)S(1)}, bf16[80,512]{1,0:T(8,128)(2,1)S(1)}, u32[]{:S(2)}, u32[]{:S(2)}) collective-permute-start(bf16[80,512]{1,0:T(8,128)(2,1)S(1)} %get-tuple-element.177), channel_id=1, source_target_pairs={{0,4},{1,5},{2,6},{3,7},{4,0},{5,1},{6,2},{7,3},{8,12},{9,13},{10,... | collective-permute-start | bytes 245768 | tf_op jit(solution)/shard_map/ppermute | solution.py:431
  76.6 9.5 %collective-permute-start.23 = (bf16[96,512]{1,0:T(8,128)(2,1)S(1)}, bf16[96,512]{1,0:T(8,128)(2,1)S(1)}, u32[]{:S(2)}, u32[]{:S(2)}) collective-permute-start(bf16[96,512]{1,0:T(8,128)(2,1)S(1)} %get-tuple-element.179), channel_id=1, source_target_pairs={{0,8},{1,9},{2,10},{3,11},{4,12},{5,13},{6,14},{7,15},{8,0},{9,1},... | collective-permute-start | bytes 294920 | tf_op jit(solution)/shard_map/ppermute | solution.py:431
  86.2 9.2 %collective-permute-start.28 = (bf16[96,512]{1,0:T(8,128)(2,1)S(1)}, bf16[96,512]{1,0:T(8,128)(2,1)S(1)}, u32[]{:S(2)}, u32[]{:S(2)}) collective-permute-start(bf16[96,512]{1,0:T(8,128)(2,1)S(1)} %get-tuple-element.145), channel_id=1, source_target_pairs={{0,2},{1,3},{2,4},{3,5},{4,6},{5,7},{6,8},{7,9},{8,10},{9,11},{10,... | collective-permute-start | bytes 294920 | tf_op jit(solution)/shard_map/ppermute | solution.py:431
  87.5 7.9 %collective-permute-start.29 = (bf16[96,512]{1,0:T(8,128)(2,1)S(1)}, bf16[96,512]{1,0:T(8,128)(2,1)S(1)}, u32[]{:S(2)}, u32[]{:S(2)}) collective-permute-start(bf16[96,512]{1,0:T(8,128)(2,1)S(1)} %get-tuple-element.146), channel_id=1, source_target_pairs={{0,14},{1,15},{2,0},{3,1},{4,2},{5,3},{6,4},{7,5},{8,6},{9,7},{10,... | collective-permute-start | bytes 294920 | tf_op jit(solution)/shard_map/ppermute | solution.py:431
  90.9 7.7 %collective-permute-start.27 = (bf16[96,512]{1,0:T(8,128)(2,1)S(1)}, bf16[96,512]{1,0:T(8,128)(2,1)S(1)}, u32[]{:S(2)}, u32[]{:S(2)}) collective-permute-start(bf16[96,512]{1,0:T(8,128)(2,1)S(1)} %get-tuple-element.169), channel_id=1, source_target_pairs={{0,12},{1,13},{2,14},{3,15},{4,8},{5,9},{6,10},{7,11},{8,4},{9,5},... | collective-permute-start | bytes 294920 | tf_op jit(solution)/shard_map/ppermute | solution.py:431
  91.0 8.9 %collective-permute-start.26 = (bf16[96,512]{1,0:T(8,128)(2,1)S(1)}, bf16[96,512]{1,0:T(8,128)(2,1)S(1)}, u32[]{:S(2)}, u32[]{:S(2)}) collective-permute-start(bf16[96,512]{1,0:T(8,128)(2,1)S(1)} %get-tuple-element.170), channel_id=1, source_target_pairs={{0,8},{1,9},{2,10},{3,11},{4,12},{5,13},{6,14},{7,15},{8,0},{9,1},... | collective-permute-start | bytes 294920 | tf_op jit(solution)/shard_map/ppermute | solution.py:431
  91.1 8.8 %collective-permute-start.25 = (bf16[96,512]{1,0:T(8,128)(2,1)S(1)}, bf16[96,512]{1,0:T(8,128)(2,1)S(1)}, u32[]{:S(2)}, u32[]{:S(2)}) collective-permute-start(bf16[96,512]{1,0:T(8,128)(2,1)S(1)} %get-tuple-element.171), channel_id=1, source_target_pairs={{0,4},{1,5},{2,6},{3,7},{4,0},{5,1},{6,2},{7,3},{8,12},{9,13},{10,... | collective-permute-start | bytes 294920 | tf_op jit(solution)/shard_map/ppermute | solution.py:431
  (18 other events, 199.8 us)

commit v17 on v16

--- a/solution.py
+++ b/solution.py
@@ -444,8 +444,14 @@
 
 
 def exchange_near(peers, lists):
-    mine, other, after, before = lists
-    return [mine, other, send(after, by_shift(peers, 2)), send(before, by_shift(peers, -2))]
+    mine, other, after, before, across = lists
+    return [
+        mine,
+        other,
+        send(after, by_shift(peers, 2)),
+        send(before, by_shift(peers, -2)),
+        send(across, across_chips(peers)),
+    ]
 
 
 def core_near(peers, near):
@@ -578,9 +584,7 @@
     )(me, rows, grid_latent)
 
     hops = [send(lists[5], by_xor(peers, 4 * place)) for place in range(1, upper)]
-    near = exchange_near(peers, lists[:4])
-    hops[0], across = lax.optimization_barrier((hops[0], lists[4]))
-    near.append(send(across, across_chips(peers)))
+    near = exchange_near(peers, lists[:5])
     far_own = jnp.concatenate([lists[5]] + hops, axis=0)
     far_own, receivers = lax.optimization_barrier((far_own, dst))
     far_next = send(far_own, by_xor(peers, 2))

time: 100 us -> 99.9 us (level)
  transfers between devices with their start and end apart: 30 -> 30, of which waited for: 11 -> 12; matrix products, arithmetic and copies ran while one was open for 2% -> 2% of each run, Pallas kernels for 23% -> 23%
where the time goes in v17:
time: 99.9 us; the launch traced here: 99.7 us
  Pallas kernels  38.3 us (38%)
  starting transfers between devices  35.4 us (35%)
  waiting for transfers between devices  21.7 us (22%)
  other arithmetic  2.47 us (2%)
  between operations  1.67 us (2%)
    ppermute x30, starting transfers between devices, send(): return lax.ppermute(values, 'lon', perm)  35.4 us
    ppermute x30, waiting for transfers between devices, send(): return lax.ppermute(values, 'lon', perm)  21.7 us
    pallas_call x1, Pallas kernels, on_device(): pl.pallas_call(functools.partial(backward_kernel, peers), grid=(tiles,),...  16.8 us
    pallas_call x1, Pallas kernels, on_device(): pl.pallas_call(functools.partial(forward_kernel, peers), grid=(tiles,), i...  11.6 us
    pallas_call x1, Pallas kernels, on_device(): pl.pallas_call(gather_kernel, in_specs=[smem, hbm, hbm], out_specs=near_s...  3.55 us
    pallas_call x1, Pallas kernels, on_device(): pl.pallas_call(local_kernel, grid=(tiles,), in_specs=[index_tile, tile_of...  3.42 us
    pallas_call x1, Pallas kernels, on_device(): pl.pallas_call(functools.partial(scatter_kernel, out_rows, len(slot_terms...  2.89 us
  transfers between devices with their start and end apart: 30, of which 12 were waited for; matrix products, arithmetic and copies ran while one was open for 2% of the time, Pallas kernels for 23%

profile of v17, /device:TPU:0, one launch (start us, length us, event | category | flops | bytes accessed | tf_op | source)
XLA Modules:
  0.0 99.7 jit_solution(16023152282907143745)
XLA Ops:
  0.7 3.6 %gather_lists.1 = (bf16[48,512]{1,0:T(8,128)(2,1)}, bf16[48,512]{1,0:T(8,128)(2,1)}, bf16[96,512]{1,0:T(8,128)(2,1)}, bf16[96,512]{1,0:T(8,128)(2,1)}, bf16[48,512]{1,0:T(8,128)(2,1)}, /*index=5*/bf16[48,512]{1,0:T(8,128)(2,1)}) custom-call(s32[1]{0:T(128)} %bitcast.me_ref, s32[16,48]{1,0:T(8,128)} %bitcast.33, bf16[2048,512]{1,0:T(8,128)(2,1)} %grid_hbm.1), custom_call_target="tpu_custom_call" | custom-call | flops 32212254720 | bytes 2097152 | tf_op jit(solution)/shard_map/gather_lists/pallas_call | solution.py:566
  4.2 5.1 %collective-permute-start.2 = (bf16[48,512]{1,0:T(8,128)(2,1)}, bf16[48,512]{1,0:T(8,128)(2,1)S(1)}, u32[]{:S(2)}, u32[]{:S(2)}) collective-permute-start(bf16[48,512]{1,0:T(8,128)(2,1)} %get-tuple-element.84), channel_id=1, source_target_pairs={{0,12},{1,13},{2,14},{3,15},{4,8},{5,9},{6,10},{7,11},{8,4},{9,5},... | collective-permute-start | bytes 147464 | tf_op jit(solution)/shard_map/ppermute | solution.py:431
  10.0 2.3 %collective-permute-start.7 = (bf16[48,512]{1,0:T(8,128)(2,1)}, bf16[48,512]{1,0:T(8,128)(2,1)S(1)}, u32[]{:S(2)}, u32[]{:S(2)}) collective-permute-start(bf16[48,512]{1,0:T(8,128)(2,1)} %get-tuple-element.90), channel_id=1, source_target_pairs={{0,13},{1,4},{2,15},{3,6},{4,1},{5,8},{6,3},{7,10},{8,5},{9,12},{1... | collective-permute-start | bytes 147464 | tf_op jit(solution)/shard_map/ppermute | solution.py:431
  12.3 1.5 %collective-permute-start.5 = (bf16[96,512]{1,0:T(8,128)(2,1)}, bf16[96,512]{1,0:T(8,128)(2,1)S(1)}, u32[]{:S(2)}, u32[]{:S(2)}) collective-permute-start(bf16[96,512]{1,0:T(8,128)(2,1)} %get-tuple-element.88), channel_id=1, source_target_pairs={{0,2},{1,3},{2,4},{3,5},{4,6},{5,7},{6,8},{7,9},{8,10},{9,11},{10,... | collective-permute-start | bytes 294920 | tf_op jit(solution)/shard_map/ppermute | solution.py:431
  13.9 3.2 %collective-permute-start.6 = (bf16[96,512]{1,0:T(8,128)(2,1)}, bf16[96,512]{1,0:T(8,128)(2,1)S(1)}, u32[]{:S(2)}, u32[]{:S(2)}) collective-permute-start(bf16[96,512]{1,0:T(8,128)(2,1)} %get-tuple-element.89), channel_id=1, source_target_pairs={{0,14},{1,15},{2,0},{3,1},{4,2},{5,3},{6,4},{7,5},{8,6},{9,7},{10,... | collective-permute-start | bytes 294920 | tf_op jit(solution)/shard_map/ppermute | solution.py:431
  18.2 3.4 %edge_local.1.local_ref = bf16[3072,512]{1,0:T(8,128)(2,1)S(1)} custom-call(s32[3,1,1024]{2,1,0:T(1,128)S(1)} %bitcast.28, bf16[3072,512]{1,0:T(8,128)(2,1)S(1)} %copy-done.1, bf16[256,512]{1,0:T(8,128)(2,1)S(1)} %copy-done.2, bf16[1536,512]{1,0:T(8,128)(2,1)S(1)} %copy-done, bf16[1536,512]{1,0:T(8,128)(2,1)S(1)} %copy-done), custom_call_target="tpu_custom_call" | custom-call | flops 2415919104 | bytes 6291456 | tf_op jit(solution)/shard_map/edge_local/pallas_call | solution.py:592
  21.6 3.7 %collective-permute-done.3.refs_9_ = bf16[192,512]{1,0:T(8,128)(2,1)S(1)} collective-permute-done((bf16[192,512]{1,0:T(8,128)(2,1)S(1)}, bf16[192,512]{1,0:T(8,128)(2,1)S(1)}, u32[]{:S(2)}, u32[]{:S(2)}) %collective-permute-start.3) | collective-permute-done | bytes 196640 | tf_op jit(solution)/shard_map/ppermute | solution.py:431
  27.3 11.6 %forward.1 = (bf16[768,512]{1,0:T(8,128)(2,1)S(1)}, bf16[3072,512]{1,0:T(8,128)(2,1)S(1)}, bf16[3072,512]{1,0:T(8,128)(2,1)S(1)}, bf16[3072,512]{1,0:T(8,128)(2,...) custom-call(s32[1]{0:T(128)} %bitcast.me_ref, ...), custom_call_target="tpu_custom_call" | custom-call | tf_op jit(solution)/shard_map/forward/pallas_call | solution.py:612
  39.1 16.8 %backward.1 = (bf16[3072,512]{1,0:T(8,128)(2,1)}, bf16[256,512]{1,0:T(8,128)(2,1)}, bf16[2,320,512]{2,1,0:T(8,128)(2,1)S(1)}, bf16[2,320,512]{2,1,0:T(8,128)(2,1...) custom-call(s32[1]{0:T(128)} %bitcast.me_ref, ...), custom_call_target="tpu_custom_call" | custom-call | flops 10468982784 | bytes 15728640 | tf_op jit(solution)/shard_map/backward/pallas_call | solution.py:662
  57.3 1.6 %collective-permute-done.15 = bf16[384,512]{1,0:T(8,128)(2,1)S(1)} collective-permute-done((bf16[384,512]{1,0:T(8,128)(2,1)S(1)}, bf16[384,512]{1,0:T(8,128)(2,1)S(1)}, u32[]{:S(2)}, u32[]{:S(2)}) %collective-permute-start.15) | collective-permute-done | bytes 393248 | tf_op jit(solution)/shard_map/ppermute | solution.py:431
  60.3 3.9 %collective-permute-start.18 = (bf16[48,512]{1,0:T(8,128)(2,1)S(1)}, bf16[48,512]{1,0:T(8,128)(2,1)S(1)}, u32[]{:S(2)}, u32[]{:S(2)}) collective-permute-start(bf16[48,512]{1,0:T(8,128)(2,1)S(1)} %get-tuple-element.128), channel_id=1, source_target_pairs={{0,13},{1,4},{2,15},{3,6},{4,1},{5,8},{6,3},{7,10},{8,5},{9,12},{1... | collective-permute-start | bytes 147464 | tf_op jit(solution)/shard_map/ppermute | solution.py:431
  64.3 4.6 %collective-permute-done.14 = bf16[320,512]{1,0:T(8,128)(2,1)S(1)} collective-permute-done((bf16[320,512]{1,0:T(8,128)(2,1)S(1)}, bf16[320,512]{1,0:T(8,128)(2,1)S(1)}, u32[]{:S(2)}, u32[]{:S(2)}) %collective-permute-start.14) | collective-permute-done | bytes 327712 | tf_op jit(solution)/shard_map/ppermute | solution.py:431
  69.1 1.1 %collective-permute-done.19 = bf16[192,512]{1,0:T(8,128)(2,1)S(1)} collective-permute-done((bf16[192,512]{1,0:T(8,128)(2,1)S(1)}, bf16[192,512]{1,0:T(8,128)(2,1)S(1)}, u32[]{:S(2)}, u32[]{:S(2)}) %collective-permute-start.19) | collective-permute-done | bytes 196640 | tf_op jit(solution)/shard_map/ppermute | solution.py:431
  71.3 2.8 %collective-permute-start.22 = (bf16[80,512]{1,0:T(8,128)(2,1)S(1)}, bf16[80,512]{1,0:T(8,128)(2,1)S(1)}, u32[]{:S(2)}, u32[]{:S(2)}) collective-permute-start(bf16[80,512]{1,0:T(8,128)(2,1)S(1)} %get-tuple-element.171), channel_id=1, source_target_pairs={{0,12},{1,13},{2,14},{3,15},{4,8},{5,9},{6,10},{7,11},{8,4},{9,5},... | collective-permute-start | bytes 245768 | tf_op jit(solution)/shard_map/ppermute | solution.py:431
  74.1 1.6 %collective-permute-start.20 = (bf16[80,512]{1,0:T(8,128)(2,1)S(1)}, bf16[80,512]{1,0:T(8,128)(2,1)S(1)}, u32[]{:S(2)}, u32[]{:S(2)}) collective-permute-start(bf16[80,512]{1,0:T(8,128)(2,1)S(1)} %get-tuple-element.173), channel_id=1, source_target_pairs={{0,4},{1,5},{2,6},{3,7},{4,0},{5,1},{6,2},{7,3},{8,12},{9,13},{10,... | collective-permute-start | bytes 245768 | tf_op jit(solution)/shard_map/ppermute | solution.py:431
  75.7 1.4 %collective-permute-start.23 = (bf16[96,512]{1,0:T(8,128)(2,1)S(1)}, bf16[96,512]{1,0:T(8,128)(2,1)S(1)}, u32[]{:S(2)}, u32[]{:S(2)}) collective-permute-start(bf16[96,512]{1,0:T(8,128)(2,1)S(1)} %get-tuple-element.175), channel_id=1, source_target_pairs={{0,8},{1,9},{2,10},{3,11},{4,12},{5,13},{6,14},{7,15},{8,0},{9,1},... | collective-permute-start | bytes 294920 | tf_op jit(solution)/shard_map/ppermute | solution.py:431
  77.1 2.5 %collective-permute-done.24 = bf16[384,512]{1,0:T(8,128)(2,1)S(1)} collective-permute-done((bf16[384,512]{1,0:T(8,128)(2,1)S(1)}, bf16[384,512]{1,0:T(8,128)(2,1)S(1)}, u32[]{:S(2)}, u32[]{:S(2)}) %collective-permute-start.24) | collective-permute-done | bytes 393248 | tf_op jit(solution)/shard_map/ppermute | solution.py:431
  79.7 3.8 %collective-permute-done.21.refs_7_ = bf16[80,512]{1,0:T(8,128)(2,1)S(1)} collective-permute-done((bf16[80,512]{1,0:T(8,128)(2,1)S(1)}, bf16[80,512]{1,0:T(8,128)(2,1)S(1)}, u32[]{:S(2)}, u32[]{:S(2)}) %collective-permute-start.21) | collective-permute-done | bytes 81952 | tf_op jit(solution)/shard_map/ppermute | solution.py:431
  83.5 1.6 %collective-permute-done.23.refs_10_ = bf16[96,512]{1,0:T(8,128)(2,1)S(1)} collective-permute-done((bf16[96,512]{1,0:T(8,128)(2,1)S(1)}, bf16[96,512]{1,0:T(8,128)(2,1)S(1)}, u32[]{:S(2)}, u32[]{:S(2)}) %collective-permute-start.23) | collective-permute-done | bytes 98336 | tf_op jit(solution)/shard_map/ppermute | solution.py:431
  85.0 1.3 %collective-permute-start.28 = (bf16[96,512]{1,0:T(8,128)(2,1)S(1)}, bf16[96,512]{1,0:T(8,128)(2,1)S(1)}, u32[]{:S(2)}, u32[]{:S(2)}) collective-permute-start(bf16[96,512]{1,0:T(8,128)(2,1)S(1)} %get-tuple-element.141), channel_id=1, source_target_pairs={{0,2},{1,3},{2,4},{3,5},{4,6},{5,7},{6,8},{7,9},{8,10},{9,11},{10,... | collective-permute-start | bytes 294920 | tf_op jit(solution)/shard_map/ppermute | solution.py:431
  86.3 3.4 %collective-permute-start.29 = (bf16[96,512]{1,0:T(8,128)(2,1)S(1)}, bf16[96,512]{1,0:T(8,128)(2,1)S(1)}, u32[]{:S(2)}, u32[]{:S(2)}) collective-permute-start(bf16[96,512]{1,0:T(8,128)(2,1)S(1)} %get-tuple-element.142), channel_id=1, source_target_pairs={{0,14},{1,15},{2,0},{3,1},{4,2},{5,3},{6,4},{7,5},{8,6},{9,7},{10,... | collective-permute-start | bytes 294920 | tf_op jit(solution)/shard_map/ppermute | solution.py:431
  90.6 3.6 %collective-permute-start.25 = (bf16[96,512]{1,0:T(8,128)(2,1)S(1)}, bf16[96,512]{1,0:T(8,128)(2,1)S(1)}, u32[]{:S(2)}, u32[]{:S(2)}) collective-permute-start(bf16[96,512]{1,0:T(8,128)(2,1)S(1)} %get-tuple-element.167), channel_id=1, source_target_pairs={{0,4},{1,5},{2,6},{3,7},{4,0},{5,1},{6,2},{7,3},{8,12},{9,13},{10,... | collective-permute-start | bytes 294920 | tf_op jit(solution)/shard_map/ppermute | solution.py:431
  94.2 2.9 %scatter_lists.1 = (bf16[2048,512]{1,0:T(8,128)(2,1)}, f32[32,512]{1,0:T(8,128)}, f32[64,512]{1,0:T(8,128)}, f32[32,512]{1,0:T(8,128)}) custom-call(s32[1]{0:T(128)} %bitcast.me_ref, s32[16,48]{1,0:T(8,128)S(1)} %bitcast.34, bf16[48,512]{1,0:T(8,128)(2,1)S(1)} %get-tuple-element.140.refs_0_, bf16[144,512]{1,0:T(8,128)(2,1)S(1)} %collective-permute-done.17.refs_1_, ...), custom_call_target="tpu_custom_call" | custom-call | tf_op jit(solution)/shard_map/scatter_lists/pallas_call | solution.py:741
  97.4 1.5 %collective-permute-done.26 = bf16[96,512]{1,0:T(8,128)(2,1)S(1)} collective-permute-done((bf16[96,512]{1,0:T(8,128)(2,1)S(1)}, bf16[96,512]{1,0:T(8,128)(2,1)S(1)}, u32[]{:S(2)}, u32[]{:S(2)}) %collective-permute-start.26) | collective-permute-done | bytes 98336 | tf_op jit(solution)/shard_map/ppermute | solution.py:431
  (80 shorter events, 9.1 us)
Async XLA Ops:
  4.2 9.6 %collective-permute-start.2 = (bf16[48,512]{1,0:T(8,128)(2,1)}, bf16[48,512]{1,0:T(8,128)(2,1)S(1)}, u32[]{:S(2)}, u32[]{:S(2)}) collective-permute-start(bf16[48,512]{1,0:T(8,128)(2,1)} %get-tuple-element.84), channel_id=1, source_target_pairs={{0,12},{1,13},{2,14},{3,15},{4,8},{5,9},{6,10},{7,11},{8,4},{9,5},... | collective-permute-start | bytes 147464 | tf_op jit(solution)/shard_map/ppermute | solution.py:431
  9.3 7.7 %collective-permute-start.1 = (bf16[48,512]{1,0:T(8,128)(2,1)}, bf16[48,512]{1,0:T(8,128)(2,1)S(1)}, u32[]{:S(2)}, u32[]{:S(2)}) collective-permute-start(bf16[48,512]{1,0:T(8,128)(2,1)} %get-tuple-element.84), channel_id=1, source_target_pairs={{0,8},{1,9},{2,10},{3,11},{4,12},{5,13},{6,14},{7,15},{8,0},{9,1},... | collective-permute-start | bytes 147464 | tf_op jit(solution)/shard_map/ppermute | solution.py:431
  9.4 7.7 %collective-permute-start = (bf16[48,512]{1,0:T(8,128)(2,1)}, bf16[48,512]{1,0:T(8,128)(2,1)S(1)}, u32[]{:S(2)}, u32[]{:S(2)}) collective-permute-start(bf16[48,512]{1,0:T(8,128)(2,1)} %get-tuple-element.84), channel_id=1, source_target_pairs={{0,4},{1,5},{2,6},{3,7},{4,0},{5,1},{6,2},{7,3},{8,12},{9,13},{10,... | collective-permute-start | bytes 147464 | tf_op jit(solution)/shard_map/ppermute | solution.py:431
  10.0 11.6 %collective-permute-start.7 = (bf16[48,512]{1,0:T(8,128)(2,1)}, bf16[48,512]{1,0:T(8,128)(2,1)S(1)}, u32[]{:S(2)}, u32[]{:S(2)}) collective-permute-start(bf16[48,512]{1,0:T(8,128)(2,1)} %get-tuple-element.90), channel_id=1, source_target_pairs={{0,13},{1,4},{2,15},{3,6},{4,1},{5,8},{6,3},{7,10},{8,5},{9,12},{1... | collective-permute-start | bytes 147464 | tf_op jit(solution)/shard_map/ppermute | solution.py:431
  12.3 9.3 %collective-permute-start.5 = (bf16[96,512]{1,0:T(8,128)(2,1)}, bf16[96,512]{1,0:T(8,128)(2,1)S(1)}, u32[]{:S(2)}, u32[]{:S(2)}) collective-permute-start(bf16[96,512]{1,0:T(8,128)(2,1)} %get-tuple-element.88), channel_id=1, source_target_pairs={{0,2},{1,3},{2,4},{3,5},{4,6},{5,7},{6,8},{7,9},{8,10},{9,11},{10,... | collective-permute-start | bytes 294920 | tf_op jit(solution)/shard_map/ppermute | solution.py:431
  13.9 7.8 %collective-permute-start.6 = (bf16[96,512]{1,0:T(8,128)(2,1)}, bf16[96,512]{1,0:T(8,128)(2,1)S(1)}, u32[]{:S(2)}, u32[]{:S(2)}) collective-permute-start(bf16[96,512]{1,0:T(8,128)(2,1)} %get-tuple-element.89), channel_id=1, source_target_pairs={{0,14},{1,15},{2,0},{3,1},{4,2},{5,3},{6,4},{7,5},{8,6},{9,7},{10,... | collective-permute-start | bytes 294920 | tf_op jit(solution)/shard_map/ppermute | solution.py:431
  18.0 3.7 %collective-permute-start.4 = (bf16[192,512]{1,0:T(8,128)(2,1)S(1)}, bf16[192,512]{1,0:T(8,128)(2,1)S(1)}, u32[]{:S(2)}, u32[]{:S(2)}) collective-permute-start(bf16[192,512]{1,0:T(8,128)(2,1)S(1)} %pad_maximum_fusion.refs_7_), channel_id=1, source_target_pairs={{0,1},{1,0},{2,3},{3,2},{4,5},{5,4},{6,7},{7,6},{8,9},{9,8},{10,11... | collective-permute-start | bytes 589832 | tf_op jit(solution)/shard_map/ppermute | solution.py:431
  18.0 7.3 %collective-permute-start.3 = (bf16[192,512]{1,0:T(8,128)(2,1)S(1)}, bf16[192,512]{1,0:T(8,128)(2,1)S(1)}, u32[]{:S(2)}, u32[]{:S(2)}) collective-permute-start(bf16[192,512]{1,0:T(8,128)(2,1)S(1)} %pad_maximum_fusion.refs_7_), channel_id=1, source_target_pairs={{0,2},{1,3},{2,0},{3,1},{4,6},{5,7},{6,4},{7,5},{8,10},{9,11},{10,... | collective-permute-start | bytes 589832 | tf_op jit(solution)/shard_map/ppermute | solution.py:431
  39.0 17.0 %collective-permute-start.12 = (bf16[2,384,512]{2,1,0:T(8,128)(2,1)S(1)}, bf16[2,384,512]{2,1,0:T(8,128)(2,1)S(1)}, u32[]{:S(2)}, u32[]{:S(2)}) collective-permute-start(bf16[2,384,512]{2,1,0:T(8,128)(2,1)S(1)} %get-tuple-element.101), channel_id=1, source_target_pairs={{0,2},{1,3},{2,0},{3,1},{4,6},{5,7},{6,4},{7,5},{8,10},{9,11},{10,... | collective-permute-start | bytes 2359304 | tf_op jit(solution)/shard_map/ppermute | solution.py:431
  56.8 3.3 %collective-permute-start.16 = (bf16[2,384,512]{2,1,0:T(8,128)(2,1)S(1)}, bf16[2,384,512]{2,1,0:T(8,128)(2,1)S(1)}, u32[]{:S(2)}, u32[]{:S(2)}) collective-permute-start(bf16[2,384,512]{2,1,0:T(8,128)(2,1)S(1)} %get-tuple-element.123), channel_id=1, source_target_pairs={{0,1},{1,0},{2,3},{3,2},{4,5},{5,4},{6,7},{7,6},{8,9},{9,8},{10,11... | collective-permute-start | bytes 2359304 | tf_op jit(solution)/shard_map/ppermute | solution.py:431
  56.9 3.4 %collective-permute-start.17 = (bf16[144,512]{1,0:T(8,128)(2,1)S(1)}, bf16[144,512]{1,0:T(8,128)(2,1)S(1)}, u32[]{:S(2)}, u32[]{:S(2)}) collective-permute-start(bf16[144,512]{1,0:T(8,128)(2,1)S(1)} %get-tuple-element.124), channel_id=1, source_target_pairs={{0,1},{1,0},{2,3},{3,2},{4,5},{5,4},{6,7},{7,6},{8,9},{9,8},{10,11... | collective-permute-start | bytes 442376 | tf_op jit(solution)/shard_map/ppermute | solution.py:431
  59.1 9.8 %collective-permute-start.14 = (bf16[320,512]{1,0:T(8,128)(2,1)S(1)}, bf16[320,512]{1,0:T(8,128)(2,1)S(1)}, u32[]{:S(2)}, u32[]{:S(2)}) collective-permute-start(bf16[320,512]{1,0:T(8,128)(2,1)S(1)} %fusion.7), channel_id=1, source_target_pairs={{0,2},{1,3},{2,0},{3,1},{4,6},{5,7},{6,4},{7,5},{8,10},{9,11},{10,... | collective-permute-start | bytes 983048 | tf_op jit(solution)/shard_map/ppermute | solution.py:431
  60.3 10.0 %collective-permute-start.18 = (bf16[48,512]{1,0:T(8,128)(2,1)S(1)}, bf16[48,512]{1,0:T(8,128)(2,1)S(1)}, u32[]{:S(2)}, u32[]{:S(2)}) collective-permute-start(bf16[48,512]{1,0:T(8,128)(2,1)S(1)} %get-tuple-element.128), channel_id=1, source_target_pairs={{0,13},{1,4},{2,15},{3,6},{4,1},{5,8},{6,3},{7,10},{8,5},{9,12},{1... | collective-permute-start | bytes 147464 | tf_op jit(solution)/shard_map/ppermute | solution.py:431
  64.2 6.0 %collective-permute-start.19 = (bf16[192,512]{1,0:T(8,128)(2,1)S(1)}, bf16[192,512]{1,0:T(8,128)(2,1)S(1)}, u32[]{:S(2)}, u32[]{:S(2)}) collective-permute-start(bf16[192,512]{1,0:T(8,128)(2,1)S(1)} %bitcast.36), channel_id=1, source_target_pairs={{0,4},{1,5},{2,6},{3,7},{4,0},{5,1},{6,2},{7,3},{8,12},{9,13},{10,... | collective-permute-start | bytes 589832 | tf_op jit(solution)/shard_map/ppermute | solution.py:431
  70.2 9.3 %collective-permute-start.24 = (bf16[384,512]{1,0:T(8,128)(2,1)S(1)}, bf16[384,512]{1,0:T(8,128)(2,1)S(1)}, u32[]{:S(2)}, u32[]{:S(2)}) collective-permute-start(bf16[384,512]{1,0:T(8,128)(2,1)S(1)} %get-tuple-element.136), channel_id=1, source_target_pairs={{0,2},{1,3},{2,0},{3,1},{4,6},{5,7},{6,4},{7,5},{8,10},{9,11},{10,... | collective-permute-start | bytes 1179656 | tf_op jit(solution)/shard_map/ppermute | solution.py:431
  71.3 8.4 %collective-permute-start.22 = (bf16[80,512]{1,0:T(8,128)(2,1)S(1)}, bf16[80,512]{1,0:T(8,128)(2,1)S(1)}, u32[]{:S(2)}, u32[]{:S(2)}) collective-permute-start(bf16[80,512]{1,0:T(8,128)(2,1)S(1)} %get-tuple-element.171), channel_id=1, source_target_pairs={{0,12},{1,13},{2,14},{3,15},{4,8},{5,9},{6,10},{7,11},{8,4},{9,5},... | collective-permute-start | bytes 245768 | tf_op jit(solution)/shard_map/ppermute | solution.py:431
  74.1 9.4 %collective-permute-start.21 = (bf16[80,512]{1,0:T(8,128)(2,1)S(1)}, bf16[80,512]{1,0:T(8,128)(2,1)S(1)}, u32[]{:S(2)}, u32[]{:S(2)}) collective-permute-start(bf16[80,512]{1,0:T(8,128)(2,1)S(1)} %get-tuple-element.172), channel_id=1, source_target_pairs={{0,8},{1,9},{2,10},{3,11},{4,12},{5,13},{6,14},{7,15},{8,0},{9,1},... | collective-permute-start | bytes 245768 | tf_op jit(solution)/shard_map/ppermute | solution.py:431
  74.1 9.4 %collective-permute-start.20 = (bf16[80,512]{1,0:T(8,128)(2,1)S(1)}, bf16[80,512]{1,0:T(8,128)(2,1)S(1)}, u32[]{:S(2)}, u32[]{:S(2)}) collective-permute-start(bf16[80,512]{1,0:T(8,128)(2,1)S(1)} %get-tuple-element.173), channel_id=1, source_target_pairs={{0,4},{1,5},{2,6},{3,7},{4,0},{5,1},{6,2},{7,3},{8,12},{9,13},{10,... | collective-permute-start | bytes 245768 | tf_op jit(solution)/shard_map/ppermute | solution.py:431
  75.7 9.3 %collective-permute-start.23 = (bf16[96,512]{1,0:T(8,128)(2,1)S(1)}, bf16[96,512]{1,0:T(8,128)(2,1)S(1)}, u32[]{:S(2)}, u32[]{:S(2)}) collective-permute-start(bf16[96,512]{1,0:T(8,128)(2,1)S(1)} %get-tuple-element.175), channel_id=1, source_target_pairs={{0,8},{1,9},{2,10},{3,11},{4,12},{5,13},{6,14},{7,15},{8,0},{9,1},... | collective-permute-start | bytes 294920 | tf_op jit(solution)/shard_map/ppermute | solution.py:431
  85.0 9.2 %collective-permute-start.28 = (bf16[96,512]{1,0:T(8,128)(2,1)S(1)}, bf16[96,512]{1,0:T(8,128)(2,1)S(1)}, u32[]{:S(2)}, u32[]{:S(2)}) collective-permute-start(bf16[96,512]{1,0:T(8,128)(2,1)S(1)} %get-tuple-element.141), channel_id=1, source_target_pairs={{0,2},{1,3},{2,4},{3,5},{4,6},{5,7},{6,8},{7,9},{8,10},{9,11},{10,... | collective-permute-start | bytes 294920 | tf_op jit(solution)/shard_map/ppermute | solution.py:431
  86.3 7.9 %collective-permute-start.29 = (bf16[96,512]{1,0:T(8,128)(2,1)S(1)}, bf16[96,512]{1,0:T(8,128)(2,1)S(1)}, u32[]{:S(2)}, u32[]{:S(2)}) collective-permute-start(bf16[96,512]{1,0:T(8,128)(2,1)S(1)} %get-tuple-element.142), channel_id=1, source_target_pairs={{0,14},{1,15},{2,0},{3,1},{4,2},{5,3},{6,4},{7,5},{8,6},{9,7},{10,... | collective-permute-start | bytes 294920 | tf_op jit(solution)/shard_map/ppermute | solution.py:431
  89.8 7.7 %collective-permute-start.27 = (bf16[96,512]{1,0:T(8,128)(2,1)S(1)}, bf16[96,512]{1,0:T(8,128)(2,1)S(1)}, u32[]{:S(2)}, u32[]{:S(2)}) collective-permute-start(bf16[96,512]{1,0:T(8,128)(2,1)S(1)} %get-tuple-element.165), channel_id=1, source_target_pairs={{0,12},{1,13},{2,14},{3,15},{4,8},{5,9},{6,10},{7,11},{8,4},{9,5},... | collective-permute-start | bytes 294920 | tf_op jit(solution)/shard_map/ppermute | solution.py:431
  90.6 8.4 %collective-permute-start.26 = (bf16[96,512]{1,0:T(8,128)(2,1)S(1)}, bf16[96,512]{1,0:T(8,128)(2,1)S(1)}, u32[]{:S(2)}, u32[]{:S(2)}) collective-permute-start(bf16[96,512]{1,0:T(8,128)(2,1)S(1)} %get-tuple-element.166), channel_id=1, source_target_pairs={{0,8},{1,9},{2,10},{3,11},{4,12},{5,13},{6,14},{7,15},{8,0},{9,1},... | collective-permute-start | bytes 294920 | tf_op jit(solution)/shard_map/ppermute | solution.py:431
  90.6 8.4 %collective-permute-start.25 = (bf16[96,512]{1,0:T(8,128)(2,1)S(1)}, bf16[96,512]{1,0:T(8,128)(2,1)S(1)}, u32[]{:S(2)}, u32[]{:S(2)}) collective-permute-start(bf16[96,512]{1,0:T(8,128)(2,1)S(1)} %get-tuple-element.167), channel_id=1, source_target_pairs={{0,4},{1,5},{2,6},{3,7},{4,0},{5,1},{6,2},{7,3},{8,12},{9,13},{10,... | collective-permute-start | bytes 294920 | tf_op jit(solution)/shard_map/ppermute | solution.py:431
  (18 other events, 176.4 us)
